TPU v7x, 32 devices: a whole 2x2x4 slice. The times are simulated.
32 devices in a mesh: runs: 2 (over x), tp: 8 (over z, y), dp: 2 (over core).
Axes of the slice: x: 2, y: 2, z: 4, core: 2. Of those that a mesh axis runs over, the one named last changes fastest.
Arguments:
- grad_out: bfloat16 [4, 256, 4096], P(('runs', 'dp'), 'tp'), parts along dimension 0, may hold values from -1 to 1
- hidden: bfloat16 [4, 256, 3584], P(('runs', 'dp'), None, 'tp'), parts along dimension 0, may hold values from -6 to 6
- feedback: bfloat16 [4, 3584, 4096], P(('runs', 'dp'), 'tp'), parts along dimension 0, may hold values from -100 to 100
- right_factor: float32 [64, 4096], replicated, may hold values from -6 to 6
Outputs:
- new_feedback: bfloat16 [4, 3584, 4096], P(('runs', 'dp'), 'tp'), parts along dimension 0
- new_factor: float32 [128, 4096], P('runs'), parts along dimension 0
There are 2 independent parts, one for each index of `runs`. A program takes and returns all parts, laid end to end along the dimension named above; an argument that names none is the same for every part. Nothing has to cross between parts.
All inputs are finite; a program needn't handle non-finite values.
Results may differ from a plain program's by a relative error of at most 0.0004.
Values may be sent and summed in bfloat16 or wider, within the bound.
No kernel may reach another device: no remote copies, remote signals or barrier semaphores. Data moves between devices by JAX's collectives and lax.ppermute only.
A program may use at most 64 MiB of HBM per device.

v0:
```python
import jax
import jax.numpy as jnp
from jax import lax
from jax.sharding import PartitionSpec as P

HIGHEST = lax.Precision.HIGHEST


def contract_first(left_side, right_side):
    return lax.dot_general(
        left_side,
        right_side,
        (((0,), (0,)), ((), ())),
        preferred_element_type=jnp.float32,
        precision=HIGHEST,
    )


def contract_last(left_side, right_side):
    return lax.dot_general(
        left_side,
        right_side,
        (((1,), (1,)), ((), ())),
        preferred_element_type=jnp.float32,
        precision=HIGHEST,
    )


def orthonormal(left_sum):
    gram_local = jnp.dot(left_sum.T, left_sum, precision=HIGHEST)
    gram_matrix = lax.psum(gram_local, "tp")
    lower_factor = jnp.linalg.cholesky(gram_matrix)
    return lax.linalg.triangular_solve(
        lower_factor, left_sum, left_side=False, lower=True, transpose_a=True
    )


def local(grad_out, hidden, feedback, right_factor):
    rows_here = grad_out[0]
    activations = hidden[0]
    residue = feedback[0].astype(jnp.float32)
    replicas = lax.axis_size("dp")
    gathered = lax.all_gather(rows_here, "tp", axis=0, tiled=True)
    product = lax.dot_general(
        activations, gathered, (((0,), (0,)), ((), ())), preferred_element_type=jnp.float32
    )
    merged = product + residue
    left_local = contract_last(merged, right_factor)
    left_sum = lax.psum(left_local, "dp")
    left_orth = orthonormal(left_sum)
    right_local = contract_first(left_orth, merged)
    right_total = lax.psum(right_local, ("tp", "dp"))
    new_factor = right_total / replicas
    approx = jnp.dot(left_orth, new_factor, precision=HIGHEST)
    new_feedback = (merged - approx).astype(jnp.bfloat16)
    return (new_feedback[None], new_factor)


def solution(mesh):
    return jax.shard_map(
        local,
        mesh=mesh,
        in_specs=(
            P(("runs", "dp"), "tp", None),
            P(("runs", "dp"), None, "tp"),
            P(("runs", "dp"), "tp", None),
            P(),
        ),
        out_specs=(P(("runs", "dp"), "tp", None), P("runs", None)),
        check_vma=False,
    )
```

profile of v0, /device:TPU:0, one launch (start us, length us, event | category | flops | bytes accessed | tf_op | source)
XLA Modules:
  0.0 262.2 jit_solution(15526046611157581308)
XLA Ops:
  7.2 0.0 copy-start
  7.2 0.0 all-gather.3.cloned.1.call-start
  7.2 0.7 all-gather.3.cloned.1.call-update
  7.9 0.0 all-reduce.3.cloned.1.call-start
  8.0 54.2 %all-gather.3.cloned.1.call-done = bf16[1,256,4096]{2,1,0:T(8,128)(2,1)} async-done(((bf16[1,32,4096]{2,1,0:T(8,128)(2,1)}), bf16[1,256,4096]{2,1,0:T(8,128)(2,1)}) %all-gather.3.cloned.1.call-update) | async-done | bytes 2097168 | tf_op jit(solution)/shard_map/all_gather | solution.py:43
  62.2 3.9 %convert_add_fusion = f32[448,4096]{1,0:T(8,128)S(1)} fusion(bf16[1,448,4096]{2,1,0:T(8,128)(2,1)} %param.6, bf16[1,256,4096]{2,1,0:T(8,128)(2,1)} %all-gather.3.cloned.1.call-done, bf16[1,256,448]{1,2,0:T(8,128)(2,1)} %param.5), kind=kOutput, calls=%fused_computation | convolution fusion | flops 943194112 | bytes 13336576 | tf_op jit(solution)/shard_map/dot_general | solution.py:44
  66.0 0.0 copy-start.1
  66.1 3.0 %copy-done.1 = f32[448,4096]{1,0:T(8,128)} copy-done((f32[448,4096]{1,0:T(8,128)}, f32[448,4096]{1,0:T(8,128)S(1)}, u32[]{:S(2)}) %copy-start.1) | copy-done | bytes 7340056
  69.0 0.0 copy-done
  69.0 7.4 %fusion.7 = f32[448,64]{0,1:T(8,128)} fusion(f32[448,4096]{1,0:T(8,128)S(1)} %convert_add_fusion, f32[64,4096]{1,0:T(8,128)S(1)} %copy-done), kind=kOutput, calls=%fused_computation.16 | convolution fusion | flops 1409286144 | bytes 8503296 | tf_op jit(solution)/shard_map/dot_general | solution.py:20
  76.5 0.0 all-reduce.3.cloned.1.call-update
  76.5 0.0 all-reduce.5.cloned.1.call-start
  76.5 16.5 %all-reduce.3.cloned.1.call-done = f32[448,64]{0,1:T(8,128)} async-done(((f32[448,64]{0,1:T(8,128)}), f32[448,64]{0,1:T(8,128)}) %all-reduce.3.cloned.1.call-update) | async-done | bytes 114704 | tf_op jit(solution)/shard_map/psum | solution.py:49
  93.0 1.2 fusion.8
  94.3 37.4 %psum.22 = f32[64,64]{0,1:T(8,128)S(1)} all-reduce(f32[64,64]{0,1:T(8,128)S(1)} %fusion.8), channel_id=1, replica_groups=mesh['runs'=2,'tp'=8,'dp'=2] {'tp'}, use_global_device_ids=true, to_apply=%region_1.0 | all-reduce | flops 4096 | bytes 32768 | tf_op jit(solution)/shard_map/psum | solution.py:31
  131.7 0.1 copy.7
  131.8 5.8 %cholesky.16 = f32[64,64]{1,0:T(8,128)S(1)} custom-call(f32[64,64]{1,0:T(8,128)S(1)} %fusion.6), custom_call_target="Cholesky" | custom-call | tf_op jit(solution)/shard_map/jit(cholesky)/cholesky | solution.py:32
  137.6 0.6 compare_reduce_fusion
  138.3 0.7 fusion.3
  139.0 4.9 %custom-call.6 = f32[1,64,64]{1,2,0:T(8,128)S(1)} custom-call(f32[1,64,64]{2,1,0:T(8,128)S(1)} %fusion.3), custom_call_target="InvertDiagBlocksLowerTriangular" | custom-call | tf_op jit(solution)/shard_map/triangular_solve | solution.py:33
  143.9 1.2 fusion.4
  145.1 8.6 %fusion.9 = f32[64,4096]{1,0:T(8,128)} fusion(f32[448,64]{0,1:T(8,128)S(1)} %fusion.4, f32[448,4096]{1,0:T(8,128)} %copy-done.1), kind=kOutput, calls=%fused_computation.18 | convolution fusion | flops 1409286144 | bytes 8503296 | tf_op jit(solution)/shard_map/dot_general | solution.py:10
  153.6 0.0 all-reduce.5.cloned.1.call-update
  153.7 90.7 %all-reduce.5.cloned.1.call-done = f32[64,4096]{1,0:T(8,128)} async-done(((f32[64,4096]{1,0:T(8,128)}), f32[64,4096]{1,0:T(8,128)}) %all-reduce.5.cloned.1.call-update) | async-done | bytes 1048592 | tf_op jit(solution)/shard_map/psum | solution.py:52
  244.4 1.3 broadcast_multiply_fusion
  245.7 0.0 copy-start.2
  245.7 9.9 %fusion = bf16[1,448,4096]{2,1,0:T(8,128)(2,1)} fusion(f32[448,4096]{1,0:T(8,128)} %copy-done.1, f32[448,64]{0,1:T(8,128)S(1)} %fusion.4, f32[64,4096]{1,0:T(8,128)S(1)} %broadcast_multiply_fusion), kind=kOutput, calls=%fused_computation.2 | convolution fusion | flops 1412956160 | bytes 12173312 | tf_op jit(solution)/shard_map/dot_general | solution.py:54
  255.7 0.0 copy-done.2
  (2 shorter events, 0.0 us)
Async XLA Ops:
  7.2 61.8 %copy-start = (f32[64,4096]{1,0:T(8,128)S(1)}, f32[64,4096]{1,0:T(8,128)}, u32[]{:S(2)}) copy-start(f32[64,4096]{1,0:T(8,128)} %param.7) | copy-start | bytes 3145732
  7.2 55.0 %all-gather.3.cloned.1.call-start = ((), (), s32[]{:S(2)}) async-start(), calls=%async_computation.2 | async-start | bytes 2359296 | tf_op jit(solution)/shard_map/all_gather | solution.py:43
  7.9 85.1 %all-reduce.3.cloned.1.call-start = ((), (), s32[]{:S(2)}) async-start(), calls=%async_computation | async-start | bytes 262144 | tf_op jit(solution)/shard_map/psum | solution.py:49
  66.0 3.0 %copy-start.1 = (f32[448,4096]{1,0:T(8,128)}, f32[448,4096]{1,0:T(8,128)S(1)}, u32[]{:S(2)}) copy-start(f32[448,4096]{1,0:T(8,128)S(1)} %convert_add_fusion) | copy-start | bytes 22020100
  76.5 167.9 %all-reduce.5.cloned.1.call-start = ((), (), s32[]{:S(2)}) async-start(), calls=%async_computation.1 | async-start | bytes 2097152 | tf_op jit(solution)/shard_map/psum | solution.py:52
  245.7 10.0 %copy-start.2 = (f32[64,4096]{1,0:T(8,128)}, f32[64,4096]{1,0:T(8,128)S(1)}, u32[]{:S(2)}) copy-start(f32[64,4096]{1,0:T(8,128)S(1)} %broadcast_multiply_fusion) | copy-start | bytes 3145732
Sparse Core Ops, SparseCore 0:
  10.1 51.9 all-gather.2
  76.6 16.3 all-reduce.2
  153.8 90.5 all-reduce.4
where the time goes:
time: 262 us
  waiting for transfers between devices  162 us (62%)
  blocking collectives  37.4 us (14%)
  matrix products  32.3 us (12%)
  between operations  13.8 us (5%)
  other arithmetic  13.4 us (5%)
  local copies, waits for them, and re-layouts  3.05 us (1%)
    psum x1, waiting for transfers between devices, local(): right_total = lax.psum(right_local, ('tp', 'dp'))  90.7 us
    all_gather x1, waiting for transfers between devices, local(): gathered = lax.all_gather(rows_here, 'tp', axis=0, tiled=True)  54.2 us
    psum x1, blocking collectives, orthonormal(): gram_matrix = lax.psum(gram_local, 'tp')  37.4 us
    psum x1, waiting for transfers between devices, local(): left_sum = lax.psum(left_local, 'dp')  16.5 us
    dot_general x1, matrix products, local(): approx = jnp.dot(left_orth, new_factor, precision=HIGHEST)  9.94 us
    dot_general x1, matrix products, contract_first(): lax.dot_general(left_side, right_side, (((0,), (0,)), ((), ())), preferre...  8.55 us
    dot_general x1, matrix products, contract_last(): lax.dot_general(left_side, right_side, (((1,), (1,)), ((), ())), preferre...  7.45 us
    another operation x3, other arithmetic, orthonormal(): lower_factor = jnp.linalg.cholesky(gram_matrix)  6.52 us
  transfers between devices with their start and end apart: 3, of which 3 were waited for; matrix products, arithmetic and copies ran while one was open for 0% of the time, Pallas kernels for 0%

commit v1 on v0

v1 whole, which is shorter than its diff:
```python
import functools

import jax
import jax.numpy as jnp
import numpy as np
from jax import lax
from jax.experimental import pallas as pl
from jax.experimental.pallas import tpu as pltpu
from jax.sharding import PartitionSpec as P

F32 = jnp.float32
BF16 = jnp.bfloat16
HIGHEST = lax.Precision.HIGHEST
VMEM_LIMIT = 40 * 1024 * 1024


def split3(value):
    high = value.astype(BF16)
    rest = value - high.astype(F32)
    middle = rest.astype(BF16)
    low = (rest - middle.astype(F32)).astype(BF16)
    return high, middle, low


def fold3(stacked):
    rank = stacked.shape[0] // 3
    return stacked[:rank] + stacked[rank : 2 * rank] + stacked[2 * rank :]


def nn(a, b):
    return lax.dot_general(a, b, (((1,), (0,)), ((), ())), preferred_element_type=F32)


def nt(a, b):
    return lax.dot_general(a, b, (((1,), (1,)), ((), ())), preferred_element_type=F32)


def params(semantics=None):
    return pltpu.CompilerParams(vmem_limit_bytes=VMEM_LIMIT, dimension_semantics=semantics)


def whole(shape):
    return pl.BlockSpec(shape, lambda *_: (0,) * len(shape))


def residue_kernel(right, feedback, terms, left_t, total):
    step = pl.program_id(0)
    stacked = jnp.concatenate(split3(right[...]), axis=0)
    terms[...] = stacked
    part = nt(stacked, feedback[...])

    @pl.when(step == 0)
    def _():
        total[...] = part

    @pl.when(step > 0)
    def _():
        total[...] += part

    @pl.when(step == pl.num_programs(0) - 1)
    def _():
        left_t[...] = fold3(total[...])


def residue_left(right, feedback):
    rank, width = right.shape
    rows = feedback.shape[0]
    steps = 4
    cols = width // steps
    return pl.pallas_call(
        residue_kernel,
        grid=(steps,),
        in_specs=[
            pl.BlockSpec((rank, cols), lambda j: (0, j)),
            pl.BlockSpec((rows, cols), lambda j: (0, j)),
        ],
        out_specs=[pl.BlockSpec((3 * rank, cols), lambda j: (0, j)), whole((rank, rows))],
        out_shape=[
            jax.ShapeDtypeStruct((3 * rank, width), BF16),
            jax.ShapeDtypeStruct((rank, rows), F32),
        ],
        scratch_shapes=[pltpu.VMEM((3 * rank, rows), F32)],
        compiler_params=params(("arbitrary",)),
        name="residue_left",
    )(right, feedback)


def left_kernel(places, *refs):
    count = places.shape[1]
    pieces, (terms, residue_t, hidden_t, tokens, left_t) = refs[:count], refs[count:]
    here = lax.axis_index("tp")
    for index, piece in enumerate(pieces):
        size = piece.shape[0]
        tokens[pl.ds(pl.multiple_of(places[here, index] * size, size), size), :] = piece[...]
    projected = fold3(nt(terms[...], tokens[...]))
    stacked = jnp.concatenate(split3(projected), axis=0)
    left_t[...] = residue_t[...] + fold3(nt(stacked, hidden_t[...]))


def left_factor(places, pieces, terms, residue_t, hidden_t):
    rows, count = hidden_t.shape
    width = terms.shape[1]
    operands = [*pieces, terms, residue_t, hidden_t]
    return pl.pallas_call(
        left_kernel,
        in_specs=[pl.BlockSpec(memory_space=pltpu.SMEM)]
        + [pl.BlockSpec(memory_space=pltpu.VMEM)] * len(operands),
        out_specs=[pl.BlockSpec(memory_space=pltpu.VMEM)] * 2,
        out_shape=[
            jax.ShapeDtypeStruct((count, width), BF16),
            jax.ShapeDtypeStruct(residue_t.shape, F32),
        ],
        compiler_params=params(),
        name="left_factor",
    )(jnp.asarray(places), *operands)


def right_kernel(here_l, other_l, hidden_t, feedback, tokens, keep, give, gram, left_sum, lhs, rhs):
    step = pl.program_id(0)
    chip, core = lax.axis_index("tp"), lax.axis_index("dp")
    half = keep.shape[2]

    @pl.when(step == 0)
    def _():
        left_t = here_l[...] + other_l[...]
        left_sum[...] = left_t
        gram[...] = lax.dot_general(
            left_t, left_t, (((1,), (1,)), ((), ())), precision=HIGHEST, preferred_element_type=F32
        )
        stacked = jnp.concatenate(split3(left_t), axis=0)
        lhs[...] = stacked
        seen_t = fold3(nn(stacked, hidden_t[...]))
        rhs[...] = jnp.concatenate(split3(seen_t), axis=0)

    block = fold3(nn(lhs[...], feedback[...]) + nn(rhs[...], tokens[...]))
    first, second = block[:, :half], block[:, half:]
    place = step ^ chip
    keep[place] = jnp.where(core == 0, first, second)
    give[place] = jnp.where(core == 0, second, first)


def right_factor_terms(here_l, other_l, hidden_t, feedback, tokens, chips):
    rank, rows = here_l.shape
    count, width = tokens.shape
    cols = width // chips
    half = cols // 2
    return pl.pallas_call(
        right_kernel,
        grid=(chips,),
        in_specs=[
            whole((rank, rows)),
            whole((rank, rows)),
            whole((rows, count)),
            pl.BlockSpec((rows, cols), lambda j: (0, j)),
            pl.BlockSpec((count, cols), lambda j: (0, j)),
        ],
        out_specs=[
            whole((chips, rank, half)),
            whole((chips, rank, half)),
            whole((rank, rank)),
            whole((rank, rows)),
        ],
        out_shape=[
            jax.ShapeDtypeStruct((chips, rank, half), F32),
            jax.ShapeDtypeStruct((chips, rank, half), F32),
            jax.ShapeDtypeStruct((rank, rank), F32),
            jax.ShapeDtypeStruct((rank, rows), F32),
        ],
        scratch_shapes=[pltpu.VMEM((3 * rank, rows), BF16), pltpu.VMEM((3 * rank, count), BF16)],
        compiler_params=params(("arbitrary",)),
        name="right_terms",
    )(here_l, other_l, hidden_t, feedback, tokens)


def message_kernel(keep, got, gram, *messages):
    chips, rank, half = keep.shape
    blocks = half // rank
    rows = rank // blocks
    for index, message in enumerate(messages):
        message[:rank, :] = keep[index] + got[index]
        for block in range(blocks):
            message[rank:, block * rank : (block + 1) * rank] = gram[block * rows : (block + 1) * rows, :]


def messages_for(keep, got, gram):
    chips, rank, half = keep.shape
    rows = rank + rank // (half // rank)
    return pl.pallas_call(
        message_kernel,
        in_specs=[pl.BlockSpec(memory_space=pltpu.VMEM)] * 3,
        out_specs=[pl.BlockSpec(memory_space=pltpu.VMEM)] * chips,
        out_shape=[jax.ShapeDtypeStruct((rows, half), F32)] * chips,
        compiler_params=params(),
        name="messages",
    )(keep, got, gram)


def sum_kernel(*refs):
    messages, (share, gram) = refs[:-2], refs[-2:]
    parts = [message[...] for message in messages]
    while len(parts) > 1:
        parts = [a + b for a, b in zip(parts[::2], parts[1::2])]
    total = parts[0]
    rank, half = share.shape
    blocks = half // rank
    rows = rank // blocks
    share[...] = total[:rank]
    for block in range(blocks):
        gram[block * rows : (block + 1) * rows, :] = total[rank:, block * rank : (block + 1) * rank]


def summed(messages, rank):
    half = messages[0].shape[1]
    return pl.pallas_call(
        sum_kernel,
        in_specs=[pl.BlockSpec(memory_space=pltpu.VMEM)] * len(messages),
        out_specs=[pl.BlockSpec(memory_space=pltpu.VMEM)] * 2,
        out_shape=[jax.ShapeDtypeStruct((rank, half), F32), jax.ShapeDtypeStruct((rank, rank), F32)],
        compiler_params=params(),
        name="sum_messages",
    )(*messages)


def inverse_kernel(gram, inverse):
    rank = gram.shape[0]
    row = lax.broadcasted_iota(jnp.int32, (rank, 2 * rank), 0)
    lane = lax.broadcasted_iota(jnp.int32, (rank, 2 * rank), 1)
    eye = (lane[:, rank:] == row[:, rank:] + rank).astype(F32)
    table = jnp.concatenate([gram[...], eye], axis=1)
    scale = jnp.zeros((rank, 1), F32)
    for pivot in range(rank):
        line = table[pivot : pivot + 1, :]
        column = table[:, pivot : pivot + 1]
        top = line[:, pivot : pivot + 1]
        scale = jnp.where(row[:, :1] == pivot, lax.rsqrt(top), scale)
        if pivot + 1 < rank:
            factor = jnp.where(row[:, :1] > pivot, column / top, 0.0)
            table = table - factor * line
    inverse[...] = table[:, rank:] * scale


def cholesky_inverse(gram):
    return pl.pallas_call(
        inverse_kernel,
        in_specs=[pl.BlockSpec(memory_space=pltpu.VMEM)],
        out_specs=pl.BlockSpec(memory_space=pltpu.VMEM),
        out_shape=jax.ShapeDtypeStruct(gram.shape, F32),
        compiler_params=params(),
        name="cholesky_inverse",
    )(gram)


def final_kernel(replicas, mine, theirs, inverse, left_sum, hidden_t, feedback, tokens, out, factor, lhs, rhs):
    step = pl.program_id(0)
    chip, core = lax.axis_index("tp"), lax.axis_index("dp")
    rows, count = hidden_t.shape
    rank = inverse.shape[0]

    @pl.when(step == 0)
    def _():
        orth_t = jnp.dot(inverse[...], left_sum[...], precision=HIGHEST, preferred_element_type=F32)
        high, middle, low = split3(-orth_t.T)
        lhs[:, :count] = hidden_t[...]
        for place, term in enumerate((high, high, high, middle, middle, low)):
            lhs[:, count + place * rank : count + (place + 1) * rank] = term

    place = step ^ chip
    here, there = mine[place], theirs[place]
    block = jnp.concatenate(
        [jnp.where(core == 0, here, there), jnp.where(core == 0, there, here)], axis=1
    )
    new = jnp.dot(inverse[...], block, precision=HIGHEST, preferred_element_type=F32) * (1.0 / replicas)
    factor[...] = new
    high, middle, low = split3(new)
    rhs[:count, :] = tokens[...]
    for place, term in enumerate((high, middle, low, high, middle, high)):
        rhs[count + place * rank : count + (place + 1) * rank, :] = term
    out[...] = (nn(lhs[...], rhs[...]) + feedback[...].astype(F32)).astype(BF16)


def finish(mine, theirs, inverse, left_sum, hidden_t, feedback, tokens, replicas):
    chips, rank, half = mine.shape
    rows, count = hidden_t.shape
    width = tokens.shape[1]
    cols = width // chips
    depth = count + 6 * rank
    return pl.pallas_call(
        functools.partial(final_kernel, replicas),
        grid=(chips,),
        in_specs=[
            whole(mine.shape),
            whole(mine.shape),
            whole((rank, rank)),
            whole((rank, rows)),
            whole((rows, count)),
            pl.BlockSpec((rows, cols), lambda j: (0, j)),
            pl.BlockSpec((count, cols), lambda j: (0, j)),
        ],
        out_specs=[
            pl.BlockSpec((rows, cols), lambda j: (0, j)),
            pl.BlockSpec((rank, cols), lambda j: (0, j)),
        ],
        out_shape=[
            jax.ShapeDtypeStruct((rows, width), BF16),
            jax.ShapeDtypeStruct((rank, width), F32),
        ],
        scratch_shapes=[pltpu.VMEM((rows, depth), BF16), pltpu.VMEM((depth, cols), BF16)],
        compiler_params=params(("arbitrary",)),
        name="finish",
    )(mine, theirs, inverse, left_sum, hidden_t, feedback, tokens)


def ring_order(chips):
    if chips == 8:
        return [0, 1, 3, 5, 7, 6, 4, 2]
    return list(range(chips))


def ring_gather(shard, chips):
    order = ring_order(chips)
    position = {chip: place for place, chip in enumerate(order)}
    right = [(order[i], order[(i + 1) % chips]) for i in range(chips)]
    left = [(b, a) for a, b in right]
    size = shard.shape[0] // 2
    halves = [shard[:size], shard[size:]]
    pieces = list(halves)
    origin = [(0, 0), (0, 1)]
    going = {(way, half): halves[half] for way in (1, -1) for half in (0, 1)}
    far = chips // 2
    for hop in range(1, far + 1):
        for way, pairs in ((1, right), (-1, left)):
            for half in (0, 1):
                if hop == far and (half == 0) != (way == 1):
                    continue
                going[way, half] = lax.ppermute(going[way, half], "tp", pairs)
                pieces.append(going[way, half])
                origin.append((-way * hop, half))
    places = np.zeros((chips, len(pieces)), np.int32)
    for chip in range(chips):
        for index, (shift, half) in enumerate(origin):
            places[chip, index] = 2 * order[(position[chip] + shift) % chips] + half
    return pieces, places


def swap(value):
    return lax.ppermute(value, "dp", [(0, 1), (1, 0)])


def local(grad_out, hidden, feedback, right_factor):
    shard, residue = grad_out[0], feedback[0]
    hidden_t = hidden[0].T
    chips, replicas = lax.axis_size("tp"), lax.axis_size("dp")
    rank = right_factor.shape[0]
    pairs = [[(i, i ^ k) for i in range(chips)] for k in range(chips)]

    pieces, places = ring_gather(shard, chips)
    terms, residue_t = residue_left(right_factor, residue)
    tokens, left_t = left_factor(places, pieces, terms, residue_t, hidden_t)
    keep, give, gram, left_sum = right_factor_terms(
        left_t, swap(left_t), hidden_t, residue, tokens, chips
    )
    messages = messages_for(keep, swap(give), gram)
    received = [messages[0]] + [lax.ppermute(messages[k], "tp", pairs[k]) for k in range(1, chips)]
    share, gram_matrix = summed(received, rank)
    shares = [share] + [lax.ppermute(share, "tp", pairs[k]) for k in range(1, chips)]
    inverse = cholesky_inverse(gram_matrix)
    mine = jnp.stack(shares)
    new_feedback, new_factor = finish(
        mine, swap(mine), inverse, left_sum, hidden_t, residue, tokens, replicas
    )
    return new_feedback[None], new_factor


def solution(mesh):
    return jax.shard_map(
        local,
        mesh=mesh,
        in_specs=(
            P(("runs", "dp"), "tp", None),
            P(("runs", "dp"), None, "tp"),
            P(("runs", "dp"), "tp", None),
            P(),
        ),
        out_specs=(P(("runs", "dp"), "tp", None), P("runs", None)),
        check_vma=False,
    )
```

time: 262 us -> 93.7 us (0.36)
  waiting for transfers between devices: 162 us -> 28.2 us
  starting transfers between devices: 0.12 us -> 39 us
  blocking collectives: 37.4 us -> 0 us
  matrix products: 32.3 us -> 0 us
  Pallas kernels: 0 us -> 21 us
  other arithmetic: 13.4 us -> 0 us
  between operations: 13.8 us -> 0.83 us
    psum x2 -> x0, waiting for transfers between devices: 107 us -> none  [the longest x1 90.7 us: local(): right_total = lax.psum(right_local, ('tp', 'dp'))]
    all_gather x1 -> x0, waiting for transfers between devices: 54.2 us -> none  [local(): gathered = lax.all_gather(rows_here, 'tp', axis=0, tiled=True)]
    ppermute x0 -> x31, starting transfers between devices: none -> 39 us  [the longest x14 15.7 us: ring_gather(): going[way, half] = lax.ppermute(going[way, half], 'tp', pairs)]
    psum x1 -> x0, blocking collectives: 37.4 us -> none  [orthonormal(): gram_matrix = lax.psum(gram_local, 'tp')]
    dot_general x5 -> x0, matrix products: 31 us -> none  [the longest x1 9.94 us: local(): approx = jnp.dot(left_orth, new_factor, precision=HIGHEST)]
    ppermute x0 -> x31, waiting for transfers between devices: none -> 28.2 us  [the longest x7 10.3 us: local(): lax.ppermute(share, 'tp', pairs[k])]
    pallas_call x0 -> x7, Pallas kernels: none -> 21 us  [the longest x1 7.36 us: finish(): pl.pallas_call(functools.partial(final_kernel, replicas), grid=(chips,),...]
    another operation x5 -> x0, other arithmetic: 12.1 us -> none  [the longest x3 6.52 us: orthonormal(): lower_factor = jnp.linalg.cholesky(gram_matrix)]
  transfers between devices with their start and end apart: 3 -> 31, of which waited for: 3 -> 10; matrix products, arithmetic and copies ran while one was open for 0% -> 0% of each run, Pallas kernels for 0% -> 9%
where the time goes in v1:
time: 93.7 us; the launch traced here: 93.4 us
  starting transfers between devices  39 us (42%)
  waiting for transfers between devices  28.2 us (30%)
  Pallas kernels  21 us (22%)
  local copies, waits for them, and re-layouts  4.35 us (5%)
    ppermute x14, starting transfers between devices, ring_gather(): going[way, half] = lax.ppermute(going[way, half], 'tp', pairs)  15.7 us
    ppermute x7, starting transfers between devices, local(): lax.ppermute(share, 'tp', pairs[k])  11.7 us
    ppermute x7, starting transfers between devices, local(): lax.ppermute(messages[k], 'tp', pairs[k])  11.2 us
    ppermute x7, waiting for transfers between devices, local(): lax.ppermute(share, 'tp', pairs[k])  10.3 us
    ppermute x7, waiting for transfers between devices, local(): lax.ppermute(messages[k], 'tp', pairs[k])  8.15 us
    pallas_call x1, Pallas kernels, finish(): pl.pallas_call(functools.partial(final_kernel, replicas), grid=(chips,),...  7.36 us
    ppermute x14, waiting for transfers between devices, ring_gather(): going[way, half] = lax.ppermute(going[way, half], 'tp', pairs)  6.73 us
    pallas_call x1, Pallas kernels, cholesky_inverse(): pl.pallas_call(inverse_kernel, in_specs=[pl.BlockSpec(memory_space=pltpu....  5.61 us
  transfers between devices with their start and end apart: 31, of which 10 were waited for; matrix products, arithmetic and copies ran while one was open for 0% of the time, Pallas kernels for 9%

profile of v1, /device:TPU:0, one launch (start us, length us, event | category | flops | bytes accessed | tf_op | source)
XLA Modules:
  0.0 93.4 jit_solution(5383016608314586257)
XLA Ops:
  0.7 1.0 %slice_bitcast_fusion = (bf16[16,4096]{1,0:T(8,128)(2,1)S(1)}, bf16[16,4096]{1,0:T(8,128)(2,1)S(1)}) fusion(bf16[1,32,4096]{2,1,0:T(8,128)(2,1)} %param.5), kind=kLoop, calls=%fused_computation | loop fusion | bytes 524288 | tf_op jit(solution)/shard_map/slice | solution.py:325
  1.7 3.1 %collective-permute-start.3 = (bf16[16,4096]{1,0:T(8,128)(2,1)S(1)}, bf16[16,4096]{1,0:T(8,128)(2,1)S(1)}, u32[]{:S(2)}, u32[]{:S(2)}) collective-permute-start(bf16[16,4096]{1,0:T(8,128)(2,1)S(1)} %get-tuple-element.42.refs_1_), channel_id=1, source_target_pairs={{2,0},{6,2},{10,6},{14,10},{12,14},{8,12},{4,8},{0,4},{3,1},{7,3},... | collective-permute-start | bytes 393224 | tf_op jit(solution)/shard_map/ppermute | solution.py:335
  4.8 2.0 %collective-permute-start.1 = (bf16[16,4096]{1,0:T(8,128)(2,1)S(1)}, bf16[16,4096]{1,0:T(8,128)(2,1)S(1)}, u32[]{:S(2)}, u32[]{:S(2)}) collective-permute-start(bf16[16,4096]{1,0:T(8,128)(2,1)S(1)} %get-tuple-element.42.refs_1_), channel_id=1, source_target_pairs={{0,2},{2,6},{6,10},{10,14},{14,12},{12,8},{8,4},{4,0},{1,3},{3,7},... | collective-permute-start | bytes 393224 | tf_op jit(solution)/shard_map/ppermute | solution.py:335
  6.7 0.1 collective-permute-start.2
  6.8 1.8 %collective-permute-done.3.refs_5_ = bf16[16,4096]{1,0:T(8,128)(2,1)S(1)} collective-permute-done((bf16[16,4096]{1,0:T(8,128)(2,1)S(1)}, bf16[16,4096]{1,0:T(8,128)(2,1)S(1)}, u32[]{:S(2)}, u32[]{:S(2)}) %collective-permute-start.3) | collective-permute-done | bytes 131104 | tf_op jit(solution)/shard_map/ppermute | solution.py:335
  8.7 2.5 %collective-permute-start.7 = (bf16[16,4096]{1,0:T(8,128)(2,1)S(1)}, bf16[16,4096]{1,0:T(8,128)(2,1)S(1)}, u32[]{:S(2)}, u32[]{:S(2)}) collective-permute-start(bf16[16,4096]{1,0:T(8,128)(2,1)S(1)} %collective-permute-done.3.refs_5_), channel_id=1, source_target_pairs={{2,0},{6,2},{10,6},{14,10},{12,14},{8,12},{4,8},{0,4},{3,1},{7,3},... | collective-permute-start | bytes 393224 | tf_op jit(solution)/shard_map/ppermute | solution.py:335
  11.2 2.6 %collective-permute-done.1.refs_3_ = bf16[16,4096]{1,0:T(8,128)(2,1)S(1)} collective-permute-done((bf16[16,4096]{1,0:T(8,128)(2,1)S(1)}, bf16[16,4096]{1,0:T(8,128)(2,1)S(1)}, u32[]{:S(2)}, u32[]{:S(2)}) %collective-permute-start.1) | collective-permute-done | bytes 131104 | tf_op jit(solution)/shard_map/ppermute | solution.py:335
  13.7 0.0 collective-permute-start.5
  13.7 2.0 %collective-permute-start.6 = (bf16[16,4096]{1,0:T(8,128)(2,1)S(1)}, bf16[16,4096]{1,0:T(8,128)(2,1)S(1)}, u32[]{:S(2)}, u32[]{:S(2)}) collective-permute-start(bf16[16,4096]{1,0:T(8,128)(2,1)S(1)} %collective-permute-done.2.refs_4_), channel_id=1, source_target_pairs={{2,0},{6,2},{10,6},{14,10},{12,14},{8,12},{4,8},{0,4},{3,1},{7,3},... | collective-permute-start | bytes 393224 | tf_op jit(solution)/shard_map/ppermute | solution.py:335
  15.7 1.6 %collective-permute-start.11 = (bf16[16,4096]{1,0:T(8,128)(2,1)S(1)}, bf16[16,4096]{1,0:T(8,128)(2,1)S(1)}, u32[]{:S(2)}, u32[]{:S(2)}) collective-permute-start(bf16[16,4096]{1,0:T(8,128)(2,1)S(1)} %collective-permute-done.7.refs_9_), channel_id=1, source_target_pairs={{2,0},{6,2},{10,6},{14,10},{12,14},{8,12},{4,8},{0,4},{3,1},{7,3},... | collective-permute-start | bytes 393224 | tf_op jit(solution)/shard_map/ppermute | solution.py:335
  17.3 0.4 collective-permute-start.8
  17.8 2.2 %collective-permute-done.5.refs_7_ = bf16[16,4096]{1,0:T(8,128)(2,1)S(1)} collective-permute-done((bf16[16,4096]{1,0:T(8,128)(2,1)S(1)}, bf16[16,4096]{1,0:T(8,128)(2,1)S(1)}, u32[]{:S(2)}, u32[]{:S(2)}) %collective-permute-start.5) | collective-permute-done | bytes 131104 | tf_op jit(solution)/shard_map/ppermute | solution.py:335
  20.0 0.1 collective-permute-start.9
  20.1 1.9 %collective-permute-start.10 = (bf16[16,4096]{1,0:T(8,128)(2,1)S(1)}, bf16[16,4096]{1,0:T(8,128)(2,1)S(1)}, u32[]{:S(2)}, u32[]{:S(2)}) collective-permute-start(bf16[16,4096]{1,0:T(8,128)(2,1)S(1)} %collective-permute-done.6.refs_8_), channel_id=1, source_target_pairs={{2,0},{6,2},{10,6},{14,10},{12,14},{8,12},{4,8},{0,4},{3,1},{7,3},... | collective-permute-start | bytes 393224 | tf_op jit(solution)/shard_map/ppermute | solution.py:335
  22.1 0.1 collective-permute-done.11.refs_13_
  22.1 1.7 %collective-permute-start.13 = (bf16[16,4096]{1,0:T(8,128)(2,1)S(1)}, bf16[16,4096]{1,0:T(8,128)(2,1)S(1)}, u32[]{:S(2)}, u32[]{:S(2)}) collective-permute-start(bf16[16,4096]{1,0:T(8,128)(2,1)S(1)} %collective-permute-done.11.refs_13_), channel_id=1, source_target_pairs={{2,0},{6,2},{10,6},{14,10},{12,14},{8,12},{4,8},{0,4},{3,1},{7,3},... | collective-permute-start | bytes 393224 | tf_op jit(solution)/shard_map/ppermute | solution.py:335
  23.9 0.3 collective-permute-start.12
  24.1 2.0 %copy-done = bf16[1,448,4096]{2,1,0:T(8,128)(2,1)S(1)} copy-done((bf16[1,448,4096]{2,1,0:T(8,128)(2,1)S(1)}, bf16[1,448,4096]{2,1,0:T(8,128)(2,1)}, u32[]{:S(2)}) %copy-start) | copy-done | bytes 3670040
  26.2 1.2 %copy-done.3 = f32[64,4096]{1,0:T(8,128)S(1)} copy-done((f32[64,4096]{1,0:T(8,128)S(1)}, f32[64,4096]{1,0:T(8,128)}, u32[]{:S(2)}) %copy-start.3) | copy-done | bytes 1048600
  27.4 2.5 %residue_left.1 = (bf16[192,4096]{1,0:T(8,128)(2,1)S(1)}, f32[64,448]{1,0:T(8,128)S(1)}) custom-call(f32[64,4096]{1,0:T(8,128)S(1)} %copy-done.3, bf16[448,4096]{1,0:T(8,128)(2,1)S(1)} %bitcast.25), custom_call_target="tpu_custom_call" | custom-call | tf_op jit(solution)/shard_map/residue_left/pallas_call | solution.py:70
  30.0 1.8 %left_factor.1 = (bf16[256,4096]{1,0:T(8,128)(2,1)S(1)}, f32[64,448]{1,0:T(8,128)S(1)}) custom-call(s32[8,16]{1,0:T(8,128)S(1)} %copy-done.4, bf16[16,4096]{1,0:T(8,128)(2,1)S(1)} %get-tuple-element.43.refs_0_, bf16[16,4096]{1,0:T(8,128)(2,1)S(1)} %get-tuple-element.42.refs_1_, bf16[16,4096]{1,0:T(8,128)(2,1)S(1)} %collective-permute-done.refs_2_, ...), custom_call_target="tpu_custom_call" | custom-call | tf_op jit(solution)/shard_map/left_factor/pallas_call | solution.py:104
  31.8 0.1 collective-permute-start.14
  31.9 1.3 %collective-permute-done.14.other_l = f32[64,448]{1,0:T(8,128)S(1)} collective-permute-done((f32[64,448]{1,0:T(8,128)S(1)}, f32[64,448]{1,0:T(8,128)S(1)}, u32[]{:S(2)}, u32[]{:S(2)}) %collective-permute-start.14) | collective-permute-done | bytes 114720 | tf_op jit(solution)/shard_map/ppermute | solution.py:346
  33.2 3.5 %right_terms.1 = (f32[8,64,256]{2,1,0:T(8,128)S(1)}, f32[8,64,256]{2,1,0:T(8,128)S(1)}, f32[64,64]{1,0:T(8,128)S(1)}, f32[64,448]{1,0:T(8,128)S(1)}) custom-call(f32[64,448]{1,0:T(8,128)S(1)} %get-tuple-element.24.here_l, f32[64,448]{1,0:T(8,128)S(1)} %collective-permute-done.14.other_l, bf16[448,256]{1,0:T(8,128)(2,1)S(1)} %bitcast.29, ...), custom_call_target="tpu_custom_call" | custom-call | tf_op jit(solution)/shard_map/right_terms/pallas_call | solution.py:147
  36.7 0.2 collective-permute-start.15
  36.9 1.8 %collective-permute-done.15.got = f32[8,64,256]{2,1,0:T(8,128)S(1)} collective-permute-done((f32[8,64,256]{2,1,0:T(8,128)S(1)}, f32[8,64,256]{2,1,0:T(8,128)S(1)}, u32[]{:S(2)}, u32[]{:S(2)}) %collective-permute-start.15) | collective-permute-done | bytes 524320 | tf_op jit(solution)/shard_map/ppermute | solution.py:346
  38.7 0.1 messages.1
  38.8 1.7 %collective-permute-start.16 = (f32[80,256]{1,0:T(8,128)S(1)}, f32[80,256]{1,0:T(8,128)S(1)}, u32[]{:S(2)}, u32[]{:S(2)}) collective-permute-start(f32[80,256]{1,0:T(8,128)S(1)} %get-tuple-element.30), channel_id=1, source_target_pairs={{0,2},{2,0},{4,6},{6,4},{8,10},{10,8},{12,14},{14,12},{1,3},{3,1},... | collective-permute-start | bytes 245768 | tf_op jit(solution)/shard_map/ppermute | solution.py:363
  40.5 1.6 %collective-permute-start.17 = (f32[80,256]{1,0:T(8,128)S(1)}, f32[80,256]{1,0:T(8,128)S(1)}, u32[]{:S(2)}, u32[]{:S(2)}) collective-permute-start(f32[80,256]{1,0:T(8,128)S(1)} %get-tuple-element.31), channel_id=1, source_target_pairs={{0,4},{2,6},{4,0},{6,2},{8,12},{10,14},{12,8},{14,10},{1,5},{3,7},... | collective-permute-start | bytes 245768 | tf_op jit(solution)/shard_map/ppermute | solution.py:363
  42.1 0.3 collective-permute-start.18
  42.4 2.8 %collective-permute-start.19 = (f32[80,256]{1,0:T(8,128)S(1)}, f32[80,256]{1,0:T(8,128)S(1)}, u32[]{:S(2)}, u32[]{:S(2)}) collective-permute-start(f32[80,256]{1,0:T(8,128)S(1)} %get-tuple-element.33), channel_id=1, source_target_pairs={{0,8},{2,10},{4,12},{6,14},{8,0},{10,2},{12,4},{14,6},{1,9},{3,11}... | collective-permute-start | bytes 245768 | tf_op jit(solution)/shard_map/ppermute | solution.py:363
  45.1 1.3 %collective-permute-start.20 = (f32[80,256]{1,0:T(8,128)S(1)}, f32[80,256]{1,0:T(8,128)S(1)}, u32[]{:S(2)}, u32[]{:S(2)}) collective-permute-start(f32[80,256]{1,0:T(8,128)S(1)} %get-tuple-element.34), channel_id=1, source_target_pairs={{0,10},{2,8},{4,14},{6,12},{8,2},{10,0},{12,6},{14,4},{1,11},{3,9}... | collective-permute-start | bytes 245768 | tf_op jit(solution)/shard_map/ppermute | solution.py:363
  46.4 3.6 %collective-permute-start.21 = (f32[80,256]{1,0:T(8,128)S(1)}, f32[80,256]{1,0:T(8,128)S(1)}, u32[]{:S(2)}, u32[]{:S(2)}) collective-permute-start(f32[80,256]{1,0:T(8,128)S(1)} %get-tuple-element.35), channel_id=1, source_target_pairs={{0,12},{2,14},{4,8},{6,10},{8,4},{10,6},{12,0},{14,2},{1,13},{3,15... | collective-permute-start | bytes 245768 | tf_op jit(solution)/shard_map/ppermute | solution.py:363
  50.0 0.1 collective-permute-start.22
  50.0 8.1 %collective-permute-done.20.refs_5_ = f32[80,256]{1,0:T(8,128)S(1)} collective-permute-done((f32[80,256]{1,0:T(8,128)S(1)}, f32[80,256]{1,0:T(8,128)S(1)}, u32[]{:S(2)}, u32[]{:S(2)}) %collective-permute-start.20) | collective-permute-done | bytes 81952 | tf_op jit(solution)/shard_map/ppermute | solution.py:363
  58.2 0.1 sum_messages.1
  58.3 3.1 %collective-permute-start.29 = (f32[64,256]{1,0:T(8,128)S(1)}, f32[64,256]{1,0:T(8,128)S(1)}, u32[]{:S(2)}, u32[]{:S(2)}) collective-permute-start(f32[64,256]{1,0:T(8,128)S(1)} %get-tuple-element.37), channel_id=1, source_target_pairs={{0,14},{2,12},{4,10},{6,8},{8,6},{10,4},{12,2},{14,0},{1,15},{3,13... | collective-permute-start | bytes 196616 | tf_op jit(solution)/shard_map/ppermute | solution.py:365
  61.3 1.2 %collective-permute-start.28 = (f32[64,256]{1,0:T(8,128)S(1)}, f32[64,256]{1,0:T(8,128)S(1)}, u32[]{:S(2)}, u32[]{:S(2)}) collective-permute-start(f32[64,256]{1,0:T(8,128)S(1)} %get-tuple-element.37), channel_id=1, source_target_pairs={{0,12},{2,14},{4,8},{6,10},{8,4},{10,6},{12,0},{14,2},{1,13},{3,15... | collective-permute-start | bytes 196616 | tf_op jit(solution)/shard_map/ppermute | solution.py:365
  62.5 3.5 %collective-permute-start.27 = (f32[64,256]{1,0:T(8,128)S(1)}, f32[64,256]{1,0:T(8,128)S(1)}, u32[]{:S(2)}, u32[]{:S(2)}) collective-permute-start(f32[64,256]{1,0:T(8,128)S(1)} %get-tuple-element.37), channel_id=1, source_target_pairs={{0,10},{2,8},{4,14},{6,12},{8,2},{10,0},{12,6},{14,4},{1,11},{3,9}... | collective-permute-start | bytes 196616 | tf_op jit(solution)/shard_map/ppermute | solution.py:365
  66.0 0.9 collective-permute-start.23
  66.9 3.4 %collective-permute-done.23 = f32[64,256]{1,0:T(8,128)S(1)} collective-permute-done((f32[64,256]{1,0:T(8,128)S(1)}, f32[64,256]{1,0:T(8,128)S(1)}, u32[]{:S(2)}, u32[]{:S(2)}) %collective-permute-start.23) | collective-permute-done | bytes 65568 | tf_op jit(solution)/shard_map/ppermute | solution.py:365
  70.3 1.6 %collective-permute-start.24 = (f32[64,256]{1,0:T(8,128)S(1)}, f32[64,256]{1,0:T(8,128)S(1)}, u32[]{:S(2)}, u32[]{:S(2)}) collective-permute-start(f32[64,256]{1,0:T(8,128)S(1)} %get-tuple-element.37), channel_id=1, source_target_pairs={{0,4},{2,6},{4,0},{6,2},{8,12},{10,14},{12,8},{14,10},{1,5},{3,7},... | collective-permute-start | bytes 196616 | tf_op jit(solution)/shard_map/ppermute | solution.py:365
  71.9 3.2 %collective-permute-done.24 = f32[64,256]{1,0:T(8,128)S(1)} collective-permute-done((f32[64,256]{1,0:T(8,128)S(1)}, f32[64,256]{1,0:T(8,128)S(1)}, u32[]{:S(2)}, u32[]{:S(2)}) %collective-permute-start.24) | collective-permute-done | bytes 65568 | tf_op jit(solution)/shard_map/ppermute | solution.py:365
  75.1 1.5 %collective-permute-start.25 = (f32[64,256]{1,0:T(8,128)S(1)}, f32[64,256]{1,0:T(8,128)S(1)}, u32[]{:S(2)}, u32[]{:S(2)}) collective-permute-start(f32[64,256]{1,0:T(8,128)S(1)} %get-tuple-element.37), channel_id=1, source_target_pairs={{0,6},{2,4},{4,2},{6,0},{8,14},{10,12},{12,10},{14,8},{1,7},{3,5},... | collective-permute-start | bytes 196616 | tf_op jit(solution)/shard_map/ppermute | solution.py:365
  76.6 3.7 %collective-permute-done.25 = f32[64,256]{1,0:T(8,128)S(1)} collective-permute-done((f32[64,256]{1,0:T(8,128)S(1)}, f32[64,256]{1,0:T(8,128)S(1)}, u32[]{:S(2)}, u32[]{:S(2)}) %collective-permute-start.25) | collective-permute-done | bytes 65568 | tf_op jit(solution)/shard_map/ppermute | solution.py:365
  80.4 0.1 collective-permute-start.30
  80.5 5.6 %cholesky_inverse.1.inverse = f32[64,64]{1,0:T(8,128)S(1)} custom-call(f32[64,64]{1,0:T(8,128)S(1)} %get-tuple-element.38.gram), custom_call_target="tpu_custom_call" | custom-call | tf_op jit(solution)/shard_map/cholesky_inverse/pallas_call | solution.py:243
  86.1 7.4 %finish.1 = (bf16[448,4096]{1,0:T(8,128)(2,1)}, f32[64,4096]{1,0:T(8,128)}) custom-call(f32[8,64,256]{2,1,0:T(8,128)S(1)} %bitcast_dynamic-update-slice_fusion.mine, f32[8,64,256]{2,1,0:T(8,128)S(1)} %collective-permute-done.30.theirs, f32[64,64]{1,0:T(8,128)S(1)} %cholesky_inverse.1.inverse, f32[64,448]{1,0:T(8,128)S(1)} %get-tuple-element.39.left_sum, ...), custom_call_target="tpu_custom_call" | custom-call | tf_op jit(solution)/shard_map/finish/pallas_call | solution.py:287
  (40 shorter events, 0.1 us)
Async XLA Ops:
  0.6 29.3 %copy-start.4 = (s32[8,16]{1,0:T(8,128)S(1)}, s32[8,16]{1,0:T(8,128)}, u32[]{:S(2)}) copy-start(s32[8,16]{1,0:T(8,128)} %constant.2.clone.places) | copy-start | bytes 1540
  0.6 29.3 %copy-start.2 = (bf16[1,256,448]{1,2,0:T(8,128)(2,1)S(1)}, bf16[1,256,448]{1,2,0:T(8,128)(2,1)}, u32[]{:S(2)}) copy-start(bf16[1,256,448]{1,2,0:T(8,128)(2,1)} %param.6) | copy-start | bytes 688132
  1.7 7.0 %collective-permute-start.3 = (bf16[16,4096]{1,0:T(8,128)(2,1)S(1)}, bf16[16,4096]{1,0:T(8,128)(2,1)S(1)}, u32[]{:S(2)}, u32[]{:S(2)}) collective-permute-start(bf16[16,4096]{1,0:T(8,128)(2,1)S(1)} %get-tuple-element.42.refs_1_), channel_id=1, source_target_pairs={{2,0},{6,2},{10,6},{14,10},{12,14},{8,12},{4,8},{0,4},{3,1},{7,3},... | collective-permute-start | bytes 393224 | tf_op jit(solution)/shard_map/ppermute | solution.py:335
  4.8 6.4 %collective-permute-start = (bf16[16,4096]{1,0:T(8,128)(2,1)S(1)}, bf16[16,4096]{1,0:T(8,128)(2,1)S(1)}, u32[]{:S(2)}, u32[]{:S(2)}) collective-permute-start(bf16[16,4096]{1,0:T(8,128)(2,1)S(1)} %get-tuple-element.43.refs_0_), channel_id=1, source_target_pairs={{0,2},{2,6},{6,10},{10,14},{14,12},{12,8},{8,4},{4,0},{1,3},{3,7},... | collective-permute-start | bytes 393224 | tf_op jit(solution)/shard_map/ppermute | solution.py:335
  4.8 8.9 %collective-permute-start.1 = (bf16[16,4096]{1,0:T(8,128)(2,1)S(1)}, bf16[16,4096]{1,0:T(8,128)(2,1)S(1)}, u32[]{:S(2)}, u32[]{:S(2)}) collective-permute-start(bf16[16,4096]{1,0:T(8,128)(2,1)S(1)} %get-tuple-element.42.refs_1_), channel_id=1, source_target_pairs={{0,2},{2,6},{6,10},{10,14},{14,12},{12,8},{8,4},{4,0},{1,3},{3,7},... | collective-permute-start | bytes 393224 | tf_op jit(solution)/shard_map/ppermute | solution.py:335
  6.7 7.0 %collective-permute-start.2 = (bf16[16,4096]{1,0:T(8,128)(2,1)S(1)}, bf16[16,4096]{1,0:T(8,128)(2,1)S(1)}, u32[]{:S(2)}, u32[]{:S(2)}) collective-permute-start(bf16[16,4096]{1,0:T(8,128)(2,1)S(1)} %get-tuple-element.43.refs_0_), channel_id=1, source_target_pairs={{2,0},{6,2},{10,6},{14,10},{12,14},{8,12},{4,8},{0,4},{3,1},{7,3},... | collective-permute-start | bytes 393224 | tf_op jit(solution)/shard_map/ppermute | solution.py:335
  8.7 7.1 %collective-permute-start.7 = (bf16[16,4096]{1,0:T(8,128)(2,1)S(1)}, bf16[16,4096]{1,0:T(8,128)(2,1)S(1)}, u32[]{:S(2)}, u32[]{:S(2)}) collective-permute-start(bf16[16,4096]{1,0:T(8,128)(2,1)S(1)} %collective-permute-done.3.refs_5_), channel_id=1, source_target_pairs={{2,0},{6,2},{10,6},{14,10},{12,14},{8,12},{4,8},{0,4},{3,1},{7,3},... | collective-permute-start | bytes 393224 | tf_op jit(solution)/shard_map/ppermute | solution.py:335
  11.1 6.2 %collective-permute-start.4 = (bf16[16,4096]{1,0:T(8,128)(2,1)S(1)}, bf16[16,4096]{1,0:T(8,128)(2,1)S(1)}, u32[]{:S(2)}, u32[]{:S(2)}) collective-permute-start(bf16[16,4096]{1,0:T(8,128)(2,1)S(1)} %collective-permute-done.refs_2_), channel_id=1, source_target_pairs={{0,2},{2,6},{6,10},{10,14},{14,12},{12,8},{8,4},{4,0},{1,3},{3,7},... | collective-permute-start | bytes 393224 | tf_op jit(solution)/shard_map/ppermute | solution.py:335
  13.7 6.3 %collective-permute-start.5 = (bf16[16,4096]{1,0:T(8,128)(2,1)S(1)}, bf16[16,4096]{1,0:T(8,128)(2,1)S(1)}, u32[]{:S(2)}, u32[]{:S(2)}) collective-permute-start(bf16[16,4096]{1,0:T(8,128)(2,1)S(1)} %collective-permute-done.1.refs_3_), channel_id=1, source_target_pairs={{0,2},{2,6},{6,10},{10,14},{14,12},{12,8},{8,4},{4,0},{1,3},{3,7},... | collective-permute-start | bytes 393224 | tf_op jit(solution)/shard_map/ppermute | solution.py:335
  13.7 6.4 %collective-permute-start.6 = (bf16[16,4096]{1,0:T(8,128)(2,1)S(1)}, bf16[16,4096]{1,0:T(8,128)(2,1)S(1)}, u32[]{:S(2)}, u32[]{:S(2)}) collective-permute-start(bf16[16,4096]{1,0:T(8,128)(2,1)S(1)} %collective-permute-done.2.refs_4_), channel_id=1, source_target_pairs={{2,0},{6,2},{10,6},{14,10},{12,14},{8,12},{4,8},{0,4},{3,1},{7,3},... | collective-permute-start | bytes 393224 | tf_op jit(solution)/shard_map/ppermute | solution.py:335
  15.7 6.4 %collective-permute-start.11 = (bf16[16,4096]{1,0:T(8,128)(2,1)S(1)}, bf16[16,4096]{1,0:T(8,128)(2,1)S(1)}, u32[]{:S(2)}, u32[]{:S(2)}) collective-permute-start(bf16[16,4096]{1,0:T(8,128)(2,1)S(1)} %collective-permute-done.7.refs_9_), channel_id=1, source_target_pairs={{2,0},{6,2},{10,6},{14,10},{12,14},{8,12},{4,8},{0,4},{3,1},{7,3},... | collective-permute-start | bytes 393224 | tf_op jit(solution)/shard_map/ppermute | solution.py:335
  17.3 6.5 %collective-permute-start.8 = (bf16[16,4096]{1,0:T(8,128)(2,1)S(1)}, bf16[16,4096]{1,0:T(8,128)(2,1)S(1)}, u32[]{:S(2)}, u32[]{:S(2)}) collective-permute-start(bf16[16,4096]{1,0:T(8,128)(2,1)S(1)} %collective-permute-done.4.refs_6_), channel_id=1, source_target_pairs={{0,2},{2,6},{6,10},{10,14},{14,12},{12,8},{8,4},{4,0},{1,3},{3,7},... | collective-permute-start | bytes 393224 | tf_op jit(solution)/shard_map/ppermute | solution.py:335
  20.0 9.9 %collective-permute-start.9 = (bf16[16,4096]{1,0:T(8,128)(2,1)S(1)}, bf16[16,4096]{1,0:T(8,128)(2,1)S(1)}, u32[]{:S(2)}, u32[]{:S(2)}) collective-permute-start(bf16[16,4096]{1,0:T(8,128)(2,1)S(1)} %collective-permute-done.5.refs_7_), channel_id=1, source_target_pairs={{0,2},{2,6},{6,10},{10,14},{14,12},{12,8},{8,4},{4,0},{1,3},{3,7},... | collective-permute-start | bytes 393224 | tf_op jit(solution)/shard_map/ppermute | solution.py:335
  20.1 9.8 %collective-permute-start.10 = (bf16[16,4096]{1,0:T(8,128)(2,1)S(1)}, bf16[16,4096]{1,0:T(8,128)(2,1)S(1)}, u32[]{:S(2)}, u32[]{:S(2)}) collective-permute-start(bf16[16,4096]{1,0:T(8,128)(2,1)S(1)} %collective-permute-done.6.refs_8_), channel_id=1, source_target_pairs={{2,0},{6,2},{10,6},{14,10},{12,14},{8,12},{4,8},{0,4},{3,1},{7,3},... | collective-permute-start | bytes 393224 | tf_op jit(solution)/shard_map/ppermute | solution.py:335
  22.1 7.8 %collective-permute-start.13 = (bf16[16,4096]{1,0:T(8,128)(2,1)S(1)}, bf16[16,4096]{1,0:T(8,128)(2,1)S(1)}, u32[]{:S(2)}, u32[]{:S(2)}) collective-permute-start(bf16[16,4096]{1,0:T(8,128)(2,1)S(1)} %collective-permute-done.11.refs_13_), channel_id=1, source_target_pairs={{2,0},{6,2},{10,6},{14,10},{12,14},{8,12},{4,8},{0,4},{3,1},{7,3},... | collective-permute-start | bytes 393224 | tf_op jit(solution)/shard_map/ppermute | solution.py:335
  23.9 6.1 %collective-permute-start.12 = (bf16[16,4096]{1,0:T(8,128)(2,1)S(1)}, bf16[16,4096]{1,0:T(8,128)(2,1)S(1)}, u32[]{:S(2)}, u32[]{:S(2)}) collective-permute-start(bf16[16,4096]{1,0:T(8,128)(2,1)S(1)} %collective-permute-done.8.refs_10_), channel_id=1, source_target_pairs={{0,2},{2,6},{6,10},{10,14},{14,12},{12,8},{8,4},{4,0},{1,3},{3,7},... | collective-permute-start | bytes 393224 | tf_op jit(solution)/shard_map/ppermute | solution.py:335
  24.1 2.0 %copy-start = (bf16[1,448,4096]{2,1,0:T(8,128)(2,1)S(1)}, bf16[1,448,4096]{2,1,0:T(8,128)(2,1)}, u32[]{:S(2)}) copy-start(bf16[1,448,4096]{2,1,0:T(8,128)(2,1)} %param.7) | copy-start | bytes 11010052
  26.2 1.2 %copy-start.3 = (f32[64,4096]{1,0:T(8,128)S(1)}, f32[64,4096]{1,0:T(8,128)}, u32[]{:S(2)}) copy-start(f32[64,4096]{1,0:T(8,128)} %right.1) | copy-start | bytes 3145732
  27.4 5.8 %copy-start.1 = (bf16[1,448,4096]{2,1,0:T(8,128)(2,1)S(1)}, bf16[1,448,4096]{2,1,0:T(8,128)(2,1)}, u32[]{:S(2)}) copy-start(bf16[1,448,4096]{2,1,0:T(8,128)(2,1)} %param.7) | copy-start | bytes 11010052
  31.8 1.4 %collective-permute-start.14 = (f32[64,448]{1,0:T(8,128)S(1)}, f32[64,448]{1,0:T(8,128)S(1)}, u32[]{:S(2)}, u32[]{:S(2)}) collective-permute-start(f32[64,448]{1,0:T(8,128)S(1)} %get-tuple-element.24.here_l), channel_id=1, source_target_pairs={{0,1},{1,0},{2,3},{3,2},{4,5},{5,4},{6,7},{7,6},{8,9},{9,8},{10,11... | collective-permute-start | bytes 344072 | tf_op jit(solution)/shard_map/ppermute | solution.py:346
  36.7 2.0 %collective-permute-start.15 = (f32[8,64,256]{2,1,0:T(8,128)S(1)}, f32[8,64,256]{2,1,0:T(8,128)S(1)}, u32[]{:S(2)}, u32[]{:S(2)}) collective-permute-start(f32[8,64,256]{2,1,0:T(8,128)S(1)} %get-tuple-element.27), channel_id=1, source_target_pairs={{0,1},{1,0},{2,3},{3,2},{4,5},{5,4},{6,7},{7,6},{8,9},{9,8},{10,11... | collective-permute-start | bytes 1572872 | tf_op jit(solution)/shard_map/ppermute | solution.py:346
  38.8 7.6 %collective-permute-start.16 = (f32[80,256]{1,0:T(8,128)S(1)}, f32[80,256]{1,0:T(8,128)S(1)}, u32[]{:S(2)}, u32[]{:S(2)}) collective-permute-start(f32[80,256]{1,0:T(8,128)S(1)} %get-tuple-element.30), channel_id=1, source_target_pairs={{0,2},{2,0},{4,6},{6,4},{8,10},{10,8},{12,14},{14,12},{1,3},{3,1},... | collective-permute-start | bytes 245768 | tf_op jit(solution)/shard_map/ppermute | solution.py:363
  40.5 9.5 %collective-permute-start.17 = (f32[80,256]{1,0:T(8,128)S(1)}, f32[80,256]{1,0:T(8,128)S(1)}, u32[]{:S(2)}, u32[]{:S(2)}) collective-permute-start(f32[80,256]{1,0:T(8,128)S(1)} %get-tuple-element.31), channel_id=1, source_target_pairs={{0,4},{2,6},{4,0},{6,2},{8,12},{10,14},{12,8},{14,10},{1,5},{3,7},... | collective-permute-start | bytes 245768 | tf_op jit(solution)/shard_map/ppermute | solution.py:363
  42.1 7.9 %collective-permute-start.18 = (f32[80,256]{1,0:T(8,128)S(1)}, f32[80,256]{1,0:T(8,128)S(1)}, u32[]{:S(2)}, u32[]{:S(2)}) collective-permute-start(f32[80,256]{1,0:T(8,128)S(1)} %get-tuple-element.32), channel_id=1, source_target_pairs={{0,6},{2,4},{4,2},{6,0},{8,14},{10,12},{12,10},{14,8},{1,7},{3,5},... | collective-permute-start | bytes 245768 | tf_op jit(solution)/shard_map/ppermute | solution.py:363
  42.4 7.7 %collective-permute-start.19 = (f32[80,256]{1,0:T(8,128)S(1)}, f32[80,256]{1,0:T(8,128)S(1)}, u32[]{:S(2)}, u32[]{:S(2)}) collective-permute-start(f32[80,256]{1,0:T(8,128)S(1)} %get-tuple-element.33), channel_id=1, source_target_pairs={{0,8},{2,10},{4,12},{6,14},{8,0},{10,2},{12,4},{14,6},{1,9},{3,11}... | collective-permute-start | bytes 245768 | tf_op jit(solution)/shard_map/ppermute | solution.py:363
  45.1 13.1 %collective-permute-start.20 = (f32[80,256]{1,0:T(8,128)S(1)}, f32[80,256]{1,0:T(8,128)S(1)}, u32[]{:S(2)}, u32[]{:S(2)}) collective-permute-start(f32[80,256]{1,0:T(8,128)S(1)} %get-tuple-element.34), channel_id=1, source_target_pairs={{0,10},{2,8},{4,14},{6,12},{8,2},{10,0},{12,6},{14,4},{1,11},{3,9}... | collective-permute-start | bytes 245768 | tf_op jit(solution)/shard_map/ppermute | solution.py:363
  46.4 11.8 %collective-permute-start.21 = (f32[80,256]{1,0:T(8,128)S(1)}, f32[80,256]{1,0:T(8,128)S(1)}, u32[]{:S(2)}, u32[]{:S(2)}) collective-permute-start(f32[80,256]{1,0:T(8,128)S(1)} %get-tuple-element.35), channel_id=1, source_target_pairs={{0,12},{2,14},{4,8},{6,10},{8,4},{10,6},{12,0},{14,2},{1,13},{3,15... | collective-permute-start | bytes 245768 | tf_op jit(solution)/shard_map/ppermute | solution.py:363
  50.0 8.2 %collective-permute-start.22 = (f32[80,256]{1,0:T(8,128)S(1)}, f32[80,256]{1,0:T(8,128)S(1)}, u32[]{:S(2)}, u32[]{:S(2)}) collective-permute-start(f32[80,256]{1,0:T(8,128)S(1)} %get-tuple-element.36), channel_id=1, source_target_pairs={{0,14},{2,12},{4,10},{6,8},{8,6},{10,4},{12,2},{14,0},{1,15},{3,13... | collective-permute-start | bytes 245768 | tf_op jit(solution)/shard_map/ppermute | solution.py:363
  58.3 22.1 %collective-permute-start.29 = (f32[64,256]{1,0:T(8,128)S(1)}, f32[64,256]{1,0:T(8,128)S(1)}, u32[]{:S(2)}, u32[]{:S(2)}) collective-permute-start(f32[64,256]{1,0:T(8,128)S(1)} %get-tuple-element.37), channel_id=1, source_target_pairs={{0,14},{2,12},{4,10},{6,8},{8,6},{10,4},{12,2},{14,0},{1,15},{3,13... | collective-permute-start | bytes 196616 | tf_op jit(solution)/shard_map/ppermute | solution.py:365
  61.3 19.0 %collective-permute-start.28 = (f32[64,256]{1,0:T(8,128)S(1)}, f32[64,256]{1,0:T(8,128)S(1)}, u32[]{:S(2)}, u32[]{:S(2)}) collective-permute-start(f32[64,256]{1,0:T(8,128)S(1)} %get-tuple-element.37), channel_id=1, source_target_pairs={{0,12},{2,14},{4,8},{6,10},{8,4},{10,6},{12,0},{14,2},{1,13},{3,15... | collective-permute-start | bytes 196616 | tf_op jit(solution)/shard_map/ppermute | solution.py:365
  62.5 17.8 %collective-permute-start.27 = (f32[64,256]{1,0:T(8,128)S(1)}, f32[64,256]{1,0:T(8,128)S(1)}, u32[]{:S(2)}, u32[]{:S(2)}) collective-permute-start(f32[64,256]{1,0:T(8,128)S(1)} %get-tuple-element.37), channel_id=1, source_target_pairs={{0,10},{2,8},{4,14},{6,12},{8,2},{10,0},{12,6},{14,4},{1,11},{3,9}... | collective-permute-start | bytes 196616 | tf_op jit(solution)/shard_map/ppermute | solution.py:365
  66.0 14.3 %collective-permute-start.26 = (f32[64,256]{1,0:T(8,128)S(1)}, f32[64,256]{1,0:T(8,128)S(1)}, u32[]{:S(2)}, u32[]{:S(2)}) collective-permute-start(f32[64,256]{1,0:T(8,128)S(1)} %get-tuple-element.37), channel_id=1, source_target_pairs={{0,8},{2,10},{4,12},{6,14},{8,0},{10,2},{12,4},{14,6},{1,9},{3,11}... | collective-permute-start | bytes 196616 | tf_op jit(solution)/shard_map/ppermute | solution.py:365
  66.0 4.3 %collective-permute-start.23 = (f32[64,256]{1,0:T(8,128)S(1)}, f32[64,256]{1,0:T(8,128)S(1)}, u32[]{:S(2)}, u32[]{:S(2)}) collective-permute-start(f32[64,256]{1,0:T(8,128)S(1)} %get-tuple-element.37), channel_id=1, source_target_pairs={{0,2},{2,0},{4,6},{6,4},{8,10},{10,8},{12,14},{14,12},{1,3},{3,1},... | collective-permute-start | bytes 196616 | tf_op jit(solution)/shard_map/ppermute | solution.py:365
  70.3 4.8 %collective-permute-start.24 = (f32[64,256]{1,0:T(8,128)S(1)}, f32[64,256]{1,0:T(8,128)S(1)}, u32[]{:S(2)}, u32[]{:S(2)}) collective-permute-start(f32[64,256]{1,0:T(8,128)S(1)} %get-tuple-element.37), channel_id=1, source_target_pairs={{0,4},{2,6},{4,0},{6,2},{8,12},{10,14},{12,8},{14,10},{1,5},{3,7},... | collective-permute-start | bytes 196616 | tf_op jit(solution)/shard_map/ppermute | solution.py:365
  75.1 5.2 %collective-permute-start.25 = (f32[64,256]{1,0:T(8,128)S(1)}, f32[64,256]{1,0:T(8,128)S(1)}, u32[]{:S(2)}, u32[]{:S(2)}) collective-permute-start(f32[64,256]{1,0:T(8,128)S(1)} %get-tuple-element.37), channel_id=1, source_target_pairs={{0,6},{2,4},{4,2},{6,0},{8,14},{10,12},{12,10},{14,8},{1,7},{3,5},... | collective-permute-start | bytes 196616 | tf_op jit(solution)/shard_map/ppermute | solution.py:365
  80.4 5.7 %collective-permute-start.30 = (f32[8,64,256]{2,1,0:T(8,128)S(1)}, f32[8,64,256]{2,1,0:T(8,128)S(1)}, u32[]{:S(2)}, u32[]{:S(2)}) collective-permute-start(f32[8,64,256]{2,1,0:T(8,128)S(1)} %bitcast_dynamic-update-slice_fusion.mine), channel_id=1, source_target_pairs={{0,1},{1,0},{2,3},{3,2},{4,5},{5,4},{6,7},{7,6},{8,9},{9,8},{10,11... | collective-permute-start | bytes 1572872 | tf_op jit(solution)/shard_map/ppermute | solution.py:346

commit v2 on v1

v2 whole, which is shorter than its diff:
```python
import functools

import jax
import jax.numpy as jnp
import numpy as np
from jax import lax
from jax.experimental import pallas as pl
from jax.experimental.pallas import tpu as pltpu
from jax.sharding import PartitionSpec as P

F32 = jnp.float32
BF16 = jnp.bfloat16
HIGHEST = lax.Precision.HIGHEST
VMEM_LIMIT = 40 * 1024 * 1024
GROUP = 2


def split3(value):
    high = value.astype(BF16)
    rest = value - high.astype(F32)
    middle = rest.astype(BF16)
    low = (rest - middle.astype(F32)).astype(BF16)
    return high, middle, low


def split2(value):
    high = value.astype(BF16)
    return high, (value - high.astype(F32)).astype(BF16)


def fold3(stacked):
    rank = stacked.shape[0] // 3
    return stacked[:rank] + stacked[rank : 2 * rank] + stacked[2 * rank :]


def nn(a, b):
    return lax.dot_general(a, b, (((1,), (0,)), ((), ())), preferred_element_type=F32)


def nt(a, b):
    return lax.dot_general(a, b, (((1,), (1,)), ((), ())), preferred_element_type=F32)


def params(semantics=None, limit=VMEM_LIMIT):
    return pltpu.CompilerParams(vmem_limit_bytes=limit, dimension_semantics=semantics)


def cost(microseconds):
    return pl.CostEstimate(flops=int(microseconds * 1.15e9), bytes_accessed=0, transcendentals=0)


def whole(shape):
    return pl.BlockSpec(shape, lambda *_: (0,) * len(shape))


def residue_kernel(right, feedback, terms, left_t, right_here, feedback_here, sems):
    width = right.shape[1]
    steps = sems.shape[0]
    cols = width // steps
    copies = []
    for step in range(steps):
        span = slice(step * cols, (step + 1) * cols)
        copies.append(
            [
                pltpu.make_async_copy(right.at[:, span], right_here.at[:, span], sems.at[step, 0]),
                pltpu.make_async_copy(feedback.at[:, span], feedback_here.at[:, span], sems.at[step, 1]),
            ]
        )
    for pair in copies:
        for copy in pair:
            copy.start()
    total = None
    for step, pair in enumerate(copies):
        span = slice(step * cols, (step + 1) * cols)
        for copy in pair:
            copy.wait()
        stacked = jnp.concatenate(split3(right_here[:, span]), axis=0)
        terms[:, span] = stacked
        part = nt(stacked, feedback_here[:, span])
        total = part if total is None else total + part
    left_t[...] = fold3(total)


def residue_left(right, feedback):
    rank, width = right.shape
    rows = feedback.shape[0]
    return pl.pallas_call(
        residue_kernel,
        in_specs=[pl.BlockSpec(memory_space=pltpu.HBM)] * 2,
        out_specs=[pl.BlockSpec(memory_space=pltpu.VMEM)] * 2,
        out_shape=[
            jax.ShapeDtypeStruct((3 * rank, width), BF16),
            jax.ShapeDtypeStruct((rank, rows), F32),
        ],
        scratch_shapes=[
            pltpu.VMEM((rank, width), F32),
            pltpu.VMEM((rows, width), BF16),
            pltpu.SemaphoreType.DMA((4, 2)),
        ],
        compiler_params=params(),
        cost_estimate=cost(2.2),
        name="residue_left",
    )(right, feedback)


def left_kernel(places, *refs):
    count = places.shape[1]
    pieces, (terms, residue_t, hidden_t, tokens, left_t) = refs[:count], refs[count:]
    here = lax.axis_index("tp")
    for index, piece in enumerate(pieces):
        size = piece.shape[0]
        tokens[pl.ds(pl.multiple_of(places[here, index] * size, size), size), :] = piece[...]
    projected = fold3(nt(terms[...], tokens[...]))
    stacked = jnp.concatenate(split3(projected), axis=0)
    left_t[...] = residue_t[...] + fold3(nt(stacked, hidden_t[...]))


def left_factor(places, pieces, terms, residue_t, hidden_t):
    rows, count = hidden_t.shape
    width = terms.shape[1]
    operands = [*pieces, terms, residue_t, hidden_t]
    return pl.pallas_call(
        left_kernel,
        in_specs=[pl.BlockSpec(memory_space=pltpu.SMEM)]
        + [pl.BlockSpec(memory_space=pltpu.VMEM)] * len(operands),
        out_specs=[pl.BlockSpec(memory_space=pltpu.VMEM)] * 2,
        out_shape=[
            jax.ShapeDtypeStruct((count, width), BF16),
            jax.ShapeDtypeStruct(residue_t.shape, F32),
        ],
        compiler_params=params(),
        cost_estimate=cost(1.8),
        name="left_factor",
    )(jnp.asarray(places), *operands)


def core_of(place):
    return (place >> 1) & 1


def index_of(place):
    return (place >> 2) * 2 + (place & 1)


def right_kernel(here_l, other_l, hidden_t, feedback, tokens, keep, give, gram, left_sum, lhs, rhs):
    step = pl.program_id(0)
    chip, core = lax.axis_index("tp"), lax.axis_index("dp")
    cols = keep.shape[2]

    @pl.when(step == 0)
    def _():
        left_t = here_l[...] + other_l[...]
        left_sum[...] = left_t
        gram[...] = lax.dot_general(
            left_t, left_t, (((1,), (1,)), ((), ())), precision=HIGHEST, preferred_element_type=F32
        )
        stacked = jnp.concatenate(split3(left_t), axis=0)
        lhs[...] = stacked
        seen_t = fold3(nn(stacked, hidden_t[...]))
        rhs[...] = jnp.concatenate(split3(seen_t), axis=0)

    block = fold3(nn(lhs[...], feedback[...]) + nn(rhs[...], tokens[...]))
    for part in range(GROUP):
        value = block[:, part * cols : (part + 1) * cols]
        place = (GROUP * step + part) ^ chip
        ours = core_of(place) == core

        @pl.when(ours)
        def _():
            keep[index_of(place)] = value

        @pl.when(jnp.logical_not(ours))
        def _():
            give[index_of(place)] = value


def right_factor_terms(here_l, other_l, hidden_t, feedback, tokens, chips):
    rank, rows = here_l.shape
    count, width = tokens.shape
    cols = width // chips
    return pl.pallas_call(
        right_kernel,
        grid=(chips // GROUP,),
        in_specs=[
            whole((rank, rows)),
            whole((rank, rows)),
            whole((rows, count)),
            pl.BlockSpec((rows, GROUP * cols), lambda j: (0, j)),
            pl.BlockSpec((count, GROUP * cols), lambda j: (0, j)),
        ],
        out_specs=[
            whole((chips // 2, rank, cols)),
            whole((chips // 2, rank, cols)),
            whole((rank, rank)),
            whole((rank, rows)),
        ],
        out_shape=[
            jax.ShapeDtypeStruct((chips // 2, rank, cols), F32),
            jax.ShapeDtypeStruct((chips // 2, rank, cols), F32),
            jax.ShapeDtypeStruct((rank, rank), F32),
            jax.ShapeDtypeStruct((rank, rows), F32),
        ],
        scratch_shapes=[pltpu.VMEM((3 * rank, rows), BF16), pltpu.VMEM((3 * rank, count), BF16)],
        compiler_params=params(("arbitrary",)),
        cost_estimate=cost(2.8),
        name="right_terms",
    )(here_l, other_l, hidden_t, feedback, tokens)


def message_kernel(keep, got, gram, *messages):
    rank, cols = keep.shape[1:]
    blocks = cols // rank
    rows = rank // blocks
    for index, message in enumerate(messages):
        message[:rank, :] = keep[index] + got[index]
        for block in range(blocks):
            message[rank:, block * rank : (block + 1) * rank] = gram[block * rows : (block + 1) * rows, :]


def messages_for(keep, got, gram):
    places, rank, cols = keep.shape
    rows = rank + rank // (cols // rank)
    return pl.pallas_call(
        message_kernel,
        in_specs=[pl.BlockSpec(memory_space=pltpu.VMEM)] * 3,
        out_specs=[pl.BlockSpec(memory_space=pltpu.VMEM)] * places,
        out_shape=[jax.ShapeDtypeStruct((rows, cols), F32)] * places,
        compiler_params=params(),
        cost_estimate=cost(0.3),
        name="messages",
    )(keep, got, gram)


def core_sum_kernel(own, second, *refs):
    messages, total = refs[:-1], refs[-1]
    first = jnp.where(lax.axis_index("dp") == 0, own[...], second[...])
    parts = [first + messages[0][...]] + [message[...] for message in messages[1:]]
    while len(parts) > 1:
        parts = [a + b for a, b in zip(parts[::2], parts[1::2])]
    total[...] = parts[0]


def core_sum(own, first, second, across):
    operands = [own, first, second, *across]
    return pl.pallas_call(
        core_sum_kernel,
        in_specs=[pl.BlockSpec(memory_space=pltpu.VMEM)] * len(operands),
        out_specs=pl.BlockSpec(memory_space=pltpu.VMEM),
        out_shape=jax.ShapeDtypeStruct(own.shape, F32),
        compiler_params=params(),
        cost_estimate=cost(0.3),
        name="core_sum",
    )(*operands)


def chip_sum_kernel(here, other, share, gram):
    total = here[...] + other[...]
    rank, cols = share.shape
    blocks = cols // rank
    rows = rank // blocks
    share[...] = total[:rank]
    for block in range(blocks):
        gram[block * rows : (block + 1) * rows, :] = total[rank:, block * rank : (block + 1) * rank]


def chip_sum(here, other, rank):
    return pl.pallas_call(
        chip_sum_kernel,
        in_specs=[pl.BlockSpec(memory_space=pltpu.VMEM)] * 2,
        out_specs=[pl.BlockSpec(memory_space=pltpu.VMEM)] * 2,
        out_shape=[
            jax.ShapeDtypeStruct((rank, here.shape[1]), F32),
            jax.ShapeDtypeStruct((rank, rank), F32),
        ],
        compiler_params=params(),
        cost_estimate=cost(0.3),
        name="chip_sum",
    )(here, other)


def inverse_kernel(gram, inverse):
    rank = gram.shape[0]
    row = lax.broadcasted_iota(jnp.int32, (rank, 2 * rank), 0)
    lane = lax.broadcasted_iota(jnp.int32, (rank, 2 * rank), 1)
    eye = (lane[:, rank:] == row[:, rank:] + rank).astype(F32)
    table = jnp.concatenate([gram[...], eye], axis=1)
    scale = jnp.zeros((rank, 1), F32)
    for pivot in range(rank):
        line = table[pivot : pivot + 1, :]
        column = table[:, pivot : pivot + 1]
        top = line[:, pivot : pivot + 1]
        scale = jnp.where(row[:, :1] == pivot, lax.rsqrt(top), scale)
        if pivot + 1 < rank:
            factor = jnp.where(row[:, :1] > pivot, column / top, 0.0)
            table = table - factor * line
    inverse[...] = table[:, rank:] * scale


def cholesky_inverse(gram):
    return pl.pallas_call(
        inverse_kernel,
        in_specs=[pl.BlockSpec(memory_space=pltpu.VMEM)],
        out_specs=pl.BlockSpec(memory_space=pltpu.VMEM),
        out_shape=jax.ShapeDtypeStruct(gram.shape, F32),
        compiler_params=params(),
        cost_estimate=cost(5.0),
        name="cholesky_inverse",
    )(gram)


def spread(target, rows, start, value):
    rank = value.shape[1]
    high, low = split2(value)
    for place, term in enumerate((high, high, low, low)):
        target[rows, start + place * rank : start + (place + 1) * rank] = term


def operand_kernel(replicas, inverse, left_sum, hidden_t, lhs):
    rank = inverse.shape[0]
    rows, count = hidden_t.shape
    orth_t = jnp.dot(inverse[...], left_sum[...], precision=HIGHEST, preferred_element_type=F32)
    share = inverse[...] * (1.0 / replicas)
    weight_t = lax.dot_general(
        share, orth_t, (((0,), (0,)), ((), ())), precision=HIGHEST, preferred_element_type=F32
    )
    lhs[:rows, :count] = hidden_t[...]
    lhs[rows:, :count] = jnp.zeros((rank, count), BF16)
    spread(lhs, slice(0, rows), count, -weight_t.T)
    spread(lhs, slice(rows, rows + rank), count, share)


def last_operand(inverse, left_sum, hidden_t, replicas):
    rank = inverse.shape[0]
    rows, count = hidden_t.shape
    return pl.pallas_call(
        functools.partial(operand_kernel, replicas),
        in_specs=[pl.BlockSpec(memory_space=pltpu.VMEM)] * 3,
        out_specs=pl.BlockSpec(memory_space=pltpu.VMEM),
        out_shape=jax.ShapeDtypeStruct((rows + rank, count + 4 * rank), BF16),
        compiler_params=params(),
        cost_estimate=cost(1.5),
        name="last_operand",
    )(inverse, left_sum, hidden_t)


def final_kernel(mine, theirs, lhs, feedback, tokens, out, factor, rhs):
    step = pl.program_id(0)
    chip, core = lax.axis_index("tp"), lax.axis_index("dp")
    count = tokens.shape[0]
    rows = feedback.shape[0]
    rank, width = mine.shape[1:]
    rhs[:count, :] = tokens[...]
    for part in range(GROUP):
        place = (GROUP * step + part) ^ chip
        index = index_of(place)
        high, low = split2(jnp.where(core_of(place) == core, mine[index], theirs[index]))
        cols = slice(part * width, (part + 1) * width)
        for order, term in enumerate((high, low, high, low)):
            rhs[count + order * rank : count + (order + 1) * rank, cols] = term
    product = nn(lhs[...], rhs[...])
    factor[...] = product[rows:]
    out[...] = (product[:rows] + feedback[...].astype(F32)).astype(BF16)


def finish(mine, theirs, lhs, feedback, tokens):
    rank = mine.shape[1]
    count, width = tokens.shape
    rows = feedback.shape[0]
    cols = GROUP * mine.shape[2]
    return pl.pallas_call(
        final_kernel,
        grid=(width // cols,),
        in_specs=[
            whole(mine.shape),
            whole(mine.shape),
            whole(lhs.shape),
            pl.BlockSpec((rows, cols), lambda j: (0, j)),
            pl.BlockSpec((count, cols), lambda j: (0, j)),
        ],
        out_specs=[
            pl.BlockSpec((rows, cols), lambda j: (0, j)),
            pl.BlockSpec((rank, cols), lambda j: (0, j)),
        ],
        out_shape=[
            jax.ShapeDtypeStruct((rows, width), BF16),
            jax.ShapeDtypeStruct((rank, width), F32),
        ],
        scratch_shapes=[pltpu.VMEM((lhs.shape[1], cols), BF16)],
        compiler_params=params(("arbitrary",)),
        cost_estimate=cost(4.4),
        name="finish",
    )(mine, theirs, lhs, feedback, tokens)


def ring_order(chips):
    if chips == 8:
        return [0, 1, 3, 5, 7, 6, 4, 2]
    return list(range(chips))


def ring_gather(shard, chips, beside):
    order = ring_order(chips)
    position = {chip: place for place, chip in enumerate(order)}
    right = [(order[i], order[(i + 1) % chips]) for i in range(chips)]
    left = [(b, a) for a, b in right]
    size = shard.shape[0] // 2
    halves = [shard[:size], shard[size:]]
    pieces = list(halves)
    origin = [(0, 0), (0, 1)]
    going = {(way, half): halves[half] for way in (1, -1) for half in (0, 1)}
    far = chips // 2
    for hop in range(1, far + 1):
        for way, pairs in ((1, right), (-1, left)):
            for half in (0, 1):
                if hop == far and (half == 0) != (way == 1):
                    continue
                going[way, half] = lax.ppermute(going[way, half], "tp", pairs)
                if hop == 1 and (way, half) == (1, 0):
                    going[way, half], beside = lax.optimization_barrier((going[way, half], beside))
                pieces.append(going[way, half])
                origin.append((-way * hop, half))
    places = np.zeros((chips, len(pieces)), np.int32)
    for chip in range(chips):
        for index, (shift, half) in enumerate(origin):
            places[chip, index] = 2 * order[(position[chip] + shift) % chips] + half
    return pieces, places, beside


def swap(value):
    return lax.ppermute(value, "dp", [(0, 1), (1, 0)])


def local(grad_out, hidden, feedback, right_factor):
    shard, residue = grad_out[0], feedback[0]
    hidden_t = hidden[0].T
    chips, replicas = lax.axis_size("tp"), lax.axis_size("dp")
    rank = right_factor.shape[0]

    half = chips // 2

    def exchange(value, index, place=None):
        pairs = []
        for chip in range(chips):
            for core in range(2):
                to = (index >> 1) * 4 + core * 2 + (index & 1) if place is None else place
                if to:
                    pairs.append((2 * chip + core, 2 * (chip ^ to) + core))
        return lax.ppermute(value, ("tp", "dp"), pairs)

    pieces, places, (terms, residue_t) = ring_gather(shard, chips, residue_left(right_factor, residue))
    tokens, left_t = left_factor(places, pieces, terms, residue_t, hidden_t)
    keep, give, gram, left_sum = right_factor_terms(
        left_t, swap(left_t), hidden_t, residue, tokens, chips
    )

    messages = messages_for(keep, swap(give), gram)
    passed = [exchange(messages[index + 1], index + 1, 1) for index in range(2, half, 2)]
    beside = exchange(messages[1], 1), exchange(messages[0], 0)
    across = [exchange(messages[2 * i + 2] + value, 2 * i + 2) for i, value in enumerate(passed)]
    partial = core_sum(messages[0], beside[1], beside[0], across)
    share, gram_matrix = chip_sum(partial, swap(partial), rank)

    across = [exchange(share, index) for index in range(2, half, 2)]
    beside = exchange(share, 1), exchange(share, 0)
    inverse = cholesky_inverse(gram_matrix)
    across[0], inverse = lax.optimization_barrier((across[0], inverse))
    passed = [exchange(value, 2 * i + 3, 1) for i, value in enumerate(across)]
    lhs = last_operand(inverse, left_sum, hidden_t, replicas)
    first = jnp.where(lax.axis_index("dp") == 0, share, beside[1])
    mine = jnp.stack([first, beside[0]] + [value for pair in zip(across, passed) for value in pair])
    mine, lhs = lax.optimization_barrier((mine, lhs))
    new_feedback, new_factor = finish(mine, swap(mine), lhs, residue, tokens)
    return new_feedback[None], new_factor


def solution(mesh):
    return jax.shard_map(
        local,
        mesh=mesh,
        in_specs=(
            P(("runs", "dp"), "tp", None),
            P(("runs", "dp"), None, "tp"),
            P(("runs", "dp"), "tp", None),
            P(),
        ),
        out_specs=(P(("runs", "dp"), "tp", None), P("runs", None)),
        check_vma=False,
    )
```

time: 93.7 us -> 79.9 us (0.85)
  starting transfers between devices: 39 us -> 26 us
  Pallas kernels: 21 us -> 17.9 us
  waiting for transfers between devices: 28.2 us -> 30.6 us
    ppermute x14 -> x8, starting transfers between devices: 22.9 us -> 8.15 us  [exchange(): return lax.ppermute(value, ('tp', 'dp'), pairs)]
    pallas_call x4 -> x6, Pallas kernels: 13.4 us -> 10.3 us  [the longest x1 4.46 us: finish(): pl.pallas_call(final_kernel, grid=(width // cols,), in_specs=[whole(mine....]
    ppermute x3 -> x4, waiting for transfers between devices: 3.1 us -> 5.98 us  [swap(): return lax.ppermute(value, 'dp', [(0, 1), (1, 0)])]
    ppermute x14 -> x8, waiting for transfers between devices: 18.4 us -> 15.8 us  [exchange(): return lax.ppermute(value, ('tp', 'dp'), pairs)]
    ppermute x3 -> x4, starting transfers between devices: 0.36 us -> 2.6 us  [swap(): return lax.ppermute(value, 'dp', [(0, 1), (1, 0)])]
    ppermute x14, waiting for transfers between devices: 6.73 us -> 8.79 us  [ring_gather(): going[way, half] = lax.ppermute(going[way, half], 'tp', pairs)]
    unnamed x17 -> x12, local copies, waits for them, and re-layouts: 3.32 us -> 3.28 us
  transfers between devices with their start and end apart: 31 -> 26, of which waited for: 10 -> 15; matrix products, arithmetic and copies ran while one was open for 0% -> 0% of each run, Pallas kernels for 9% -> 11%
where the time goes in v2:
time: 79.9 us; the launch traced here: 79.6 us
  waiting for transfers between devices  30.6 us (38%)
  starting transfers between devices  26 us (33%)
  Pallas kernels  17.9 us (22%)
  local copies, waits for them, and re-layouts  4.27 us (5%)
    ppermute x8, waiting for transfers between devices, exchange(): return lax.ppermute(value, ('tp', 'dp'), pairs)  15.8 us
    ppermute x14, starting transfers between devices, ring_gather(): going[way, half] = lax.ppermute(going[way, half], 'tp', pairs)  15.3 us
    ppermute x14, waiting for transfers between devices, ring_gather(): going[way, half] = lax.ppermute(going[way, half], 'tp', pairs)  8.79 us
    ppermute x8, starting transfers between devices, exchange(): return lax.ppermute(value, ('tp', 'dp'), pairs)  8.15 us
    ppermute x4, waiting for transfers between devices, swap(): return lax.ppermute(value, 'dp', [(0, 1), (1, 0)])  5.98 us
    pallas_call x1, Pallas kernels, cholesky_inverse(): pl.pallas_call(inverse_kernel, in_specs=[pl.BlockSpec(memory_space=pltpu....  5.61 us
    pallas_call x1, Pallas kernels, finish(): pl.pallas_call(final_kernel, grid=(width // cols,), in_specs=[whole(mine....  4.46 us
    unnamed x12, local copies, waits for them, and re-layouts  3.28 us
  transfers between devices with their start and end apart: 26, of which 15 were waited for; matrix products, arithmetic and copies ran while one was open for 0% of the time, Pallas kernels for 11%

profile of v2, /device:TPU:0, one launch (start us, length us, event | category | flops | bytes accessed | tf_op | source)
XLA Modules:
  0.0 79.6 jit_solution(18378786383779900426)
XLA Ops:
  0.6 1.0 %slice_bitcast_fusion = (bf16[16,4096]{1,0:T(8,128)(2,1)S(1)}, bf16[16,4096]{1,0:T(8,128)(2,1)S(1)}) fusion(bf16[1,32,4096]{2,1,0:T(8,128)(2,1)} %param.5), kind=kLoop, calls=%fused_computation.2 | loop fusion | bytes 524288 | tf_op jit(solution)/shard_map/slice | solution.py:407
  1.6 3.1 %collective-permute-start.3 = (bf16[16,4096]{1,0:T(8,128)(2,1)S(1)}, bf16[16,4096]{1,0:T(8,128)(2,1)S(1)}, u32[]{:S(2)}, u32[]{:S(2)}) collective-permute-start(bf16[16,4096]{1,0:T(8,128)(2,1)S(1)} %get-tuple-element.48.refs_1_), channel_id=1, source_target_pairs={{2,0},{6,2},{10,6},{14,10},{12,14},{8,12},{4,8},{0,4},{3,1},{7,3},... | collective-permute-start | bytes 393224 | tf_op jit(solution)/shard_map/ppermute | solution.py:417
  4.7 2.0 %collective-permute-start.2 = (bf16[16,4096]{1,0:T(8,128)(2,1)S(1)}, bf16[16,4096]{1,0:T(8,128)(2,1)S(1)}, u32[]{:S(2)}, u32[]{:S(2)}) collective-permute-start(bf16[16,4096]{1,0:T(8,128)(2,1)S(1)} %get-tuple-element.49.refs_0_), channel_id=1, source_target_pairs={{2,0},{6,2},{10,6},{14,10},{12,14},{8,12},{4,8},{0,4},{3,1},{7,3},... | collective-permute-start | bytes 393224 | tf_op jit(solution)/shard_map/ppermute | solution.py:417
  6.7 2.0 %copy-done = bf16[1,448,4096]{2,1,0:T(8,128)(2,1)S(1)} copy-done((bf16[1,448,4096]{2,1,0:T(8,128)(2,1)S(1)}, bf16[1,448,4096]{2,1,0:T(8,128)(2,1)}, u32[]{:S(2)}) %copy-start) | copy-done | bytes 3670040
  8.8 1.2 %copy-done.3 = f32[64,4096]{1,0:T(8,128)S(1)} copy-done((f32[64,4096]{1,0:T(8,128)S(1)}, f32[64,4096]{1,0:T(8,128)}, u32[]{:S(2)}) %copy-start.3) | copy-done | bytes 1048600
  10.0 2.1 %residue_left.1 = (bf16[192,4096]{1,0:T(8,128)(2,1)S(1)}, f32[64,448]{1,0:T(8,128)S(1)}) custom-call(f32[64,4096]{1,0:T(8,128)S(1)} %copy-done.3, bf16[448,4096]{1,0:T(8,128)(2,1)S(1)} %bitcast.14), custom_call_target="tpu_custom_call" | custom-call | flops 2529999872 | tf_op jit(solution)/shard_map/residue_left/pallas_call | solution.py:87
  12.1 0.3 collective-permute-done.refs_2_
  12.5 1.8 %collective-permute-start.7 = (bf16[16,4096]{1,0:T(8,128)(2,1)S(1)}, bf16[16,4096]{1,0:T(8,128)(2,1)S(1)}, u32[]{:S(2)}, u32[]{:S(2)}) collective-permute-start(bf16[16,4096]{1,0:T(8,128)(2,1)S(1)} %collective-permute-done.3.refs_5_), channel_id=1, source_target_pairs={{2,0},{6,2},{10,6},{14,10},{12,14},{8,12},{4,8},{0,4},{3,1},{7,3},... | collective-permute-start | bytes 393224 | tf_op jit(solution)/shard_map/ppermute | solution.py:417
  14.2 0.3 collective-permute-start.4
  14.5 1.7 %collective-permute-start.5 = (bf16[16,4096]{1,0:T(8,128)(2,1)S(1)}, bf16[16,4096]{1,0:T(8,128)(2,1)S(1)}, u32[]{:S(2)}, u32[]{:S(2)}) collective-permute-start(bf16[16,4096]{1,0:T(8,128)(2,1)S(1)} %collective-permute-done.1.refs_3_), channel_id=1, source_target_pairs={{0,2},{2,6},{6,10},{10,14},{14,12},{12,8},{8,4},{4,0},{1,3},{3,7},... | collective-permute-start | bytes 393224 | tf_op jit(solution)/shard_map/ppermute | solution.py:417
  16.2 0.3 collective-permute-start.6
  16.5 1.7 %collective-permute-done.7.refs_9_ = bf16[16,4096]{1,0:T(8,128)(2,1)S(1)} collective-permute-done((bf16[16,4096]{1,0:T(8,128)(2,1)S(1)}, bf16[16,4096]{1,0:T(8,128)(2,1)S(1)}, u32[]{:S(2)}, u32[]{:S(2)}) %collective-permute-start.7) | collective-permute-done | bytes 131104 | tf_op jit(solution)/shard_map/ppermute | solution.py:417
  18.3 2.1 %collective-permute-start.11 = (bf16[16,4096]{1,0:T(8,128)(2,1)S(1)}, bf16[16,4096]{1,0:T(8,128)(2,1)S(1)}, u32[]{:S(2)}, u32[]{:S(2)}) collective-permute-start(bf16[16,4096]{1,0:T(8,128)(2,1)S(1)} %collective-permute-done.7.refs_9_), channel_id=1, source_target_pairs={{2,0},{6,2},{10,6},{14,10},{12,14},{8,12},{4,8},{0,4},{3,1},{7,3},... | collective-permute-start | bytes 393224 | tf_op jit(solution)/shard_map/ppermute | solution.py:417
  20.3 2.0 %collective-permute-done.5.refs_7_ = bf16[16,4096]{1,0:T(8,128)(2,1)S(1)} collective-permute-done((bf16[16,4096]{1,0:T(8,128)(2,1)S(1)}, bf16[16,4096]{1,0:T(8,128)(2,1)S(1)}, u32[]{:S(2)}, u32[]{:S(2)}) %collective-permute-start.5) | collective-permute-done | bytes 131104 | tf_op jit(solution)/shard_map/ppermute | solution.py:417
  22.3 0.4 collective-permute-start.9
  22.7 1.7 %collective-permute-start.10 = (bf16[16,4096]{1,0:T(8,128)(2,1)S(1)}, bf16[16,4096]{1,0:T(8,128)(2,1)S(1)}, u32[]{:S(2)}, u32[]{:S(2)}) collective-permute-start(bf16[16,4096]{1,0:T(8,128)(2,1)S(1)} %collective-permute-done.6.refs_8_), channel_id=1, source_target_pairs={{2,0},{6,2},{10,6},{14,10},{12,14},{8,12},{4,8},{0,4},{3,1},{7,3},... | collective-permute-start | bytes 393224 | tf_op jit(solution)/shard_map/ppermute | solution.py:417
  24.3 0.3 collective-permute-done.11.refs_13_
  24.6 1.5 %collective-permute-start.13 = (bf16[16,4096]{1,0:T(8,128)(2,1)S(1)}, bf16[16,4096]{1,0:T(8,128)(2,1)S(1)}, u32[]{:S(2)}, u32[]{:S(2)}) collective-permute-start(bf16[16,4096]{1,0:T(8,128)(2,1)S(1)} %collective-permute-done.11.refs_13_), channel_id=1, source_target_pairs={{2,0},{6,2},{10,6},{14,10},{12,14},{8,12},{4,8},{0,4},{3,1},{7,3},... | collective-permute-start | bytes 393224 | tf_op jit(solution)/shard_map/ppermute | solution.py:417
  26.1 0.5 collective-permute-start.12
  26.7 1.4 %collective-permute-done.9.refs_11_ = bf16[16,4096]{1,0:T(8,128)(2,1)S(1)} collective-permute-done((bf16[16,4096]{1,0:T(8,128)(2,1)S(1)}, bf16[16,4096]{1,0:T(8,128)(2,1)S(1)}, u32[]{:S(2)}, u32[]{:S(2)}) %collective-permute-start.9) | collective-permute-done | bytes 131104 | tf_op jit(solution)/shard_map/ppermute | solution.py:417
  28.1 1.5 %collective-permute-done.13.refs_15_ = bf16[16,4096]{1,0:T(8,128)(2,1)S(1)} collective-permute-done((bf16[16,4096]{1,0:T(8,128)(2,1)S(1)}, bf16[16,4096]{1,0:T(8,128)(2,1)S(1)}, u32[]{:S(2)}, u32[]{:S(2)}) %collective-permute-start.13) | collective-permute-done | bytes 131104 | tf_op jit(solution)/shard_map/ppermute | solution.py:417
  29.6 1.5 %collective-permute-done.12.refs_14_ = bf16[16,4096]{1,0:T(8,128)(2,1)S(1)} collective-permute-done((bf16[16,4096]{1,0:T(8,128)(2,1)S(1)}, bf16[16,4096]{1,0:T(8,128)(2,1)S(1)}, u32[]{:S(2)}, u32[]{:S(2)}) %collective-permute-start.12) | collective-permute-done | bytes 131104 | tf_op jit(solution)/shard_map/ppermute | solution.py:417
  31.1 1.9 %left_factor.1 = (bf16[256,4096]{1,0:T(8,128)(2,1)S(1)}, f32[64,448]{1,0:T(8,128)S(1)}) custom-call(s32[8,16]{1,0:T(8,128)S(1)} %copy-done.5, bf16[16,4096]{1,0:T(8,128)(2,1)S(1)} %get-tuple-element.49.refs_0_, bf16[16,4096]{1,0:T(8,128)(2,1)S(1)} %get-tuple-element.48.refs_1_, bf16[16,4096]{1,0:T(8,128)(2,1)S(1)} %collective-permute-done.refs_2_, ...), custom_call_target="tpu_custom_call" | custom-call | flops 2070000000 | tf_op jit(solution)/shard_map/left_factor/pallas_call | solution.py:122
  33.0 0.1 collective-permute-start.14
  33.1 1.3 %collective-permute-done.14.other_l = f32[64,448]{1,0:T(8,128)S(1)} collective-permute-done((f32[64,448]{1,0:T(8,128)S(1)}, f32[64,448]{1,0:T(8,128)S(1)}, u32[]{:S(2)}, u32[]{:S(2)}) %collective-permute-start.14) | collective-permute-done | bytes 114720 | tf_op jit(solution)/shard_map/ppermute | solution.py:430
  34.4 2.8 %right_terms.1 = (f32[4,64,512]{2,1,0:T(8,128)S(1)}, f32[4,64,512]{2,1,0:T(8,128)S(1)}, f32[64,64]{1,0:T(8,128)S(1)}, f32[64,448]{1,0:T(8,128)S(1)}) custom-call(f32[64,448]{1,0:T(8,128)S(1)} %get-tuple-element.30.here_l, f32[64,448]{1,0:T(8,128)S(1)} %collective-permute-done.14.other_l, bf16[448,256]{1,0:T(8,128)(2,1)S(1)} %bitcast.18, ...), custom_call_target="tpu_custom_call" | custom-call | flops 3220000000 | tf_op jit(solution)/shard_map/right_terms/pallas_call | solution.py:181
  37.3 0.2 collective-permute-start.15
  37.5 1.8 %collective-permute-done.15.got = f32[4,64,512]{2,1,0:T(8,128)S(1)} collective-permute-done((f32[4,64,512]{2,1,0:T(8,128)S(1)}, f32[4,64,512]{2,1,0:T(8,128)S(1)}, u32[]{:S(2)}, u32[]{:S(2)}) %collective-permute-start.15) | collective-permute-done | bytes 524320 | tf_op jit(solution)/shard_map/ppermute | solution.py:430
  39.2 0.1 messages.1
  39.3 0.6 collective-permute-start.18
  39.9 1.5 %collective-permute-start.17 = (f32[72,512]{1,0:T(8,128)S(1)}, f32[72,512]{1,0:T(8,128)S(1)}, u32[]{:S(2)}, u32[]{:S(2)}) collective-permute-start(f32[72,512]{1,0:T(8,128)S(1)} %get-tuple-element.36), channel_id=1, source_target_pairs={{0,2},{1,7},{2,0},{3,5},{4,6},{5,3},{6,4},{7,1},{8,10},{9,15},{10,... | collective-permute-start | bytes 442376 | tf_op jit(solution)/shard_map/ppermute | solution.py:448
  41.4 0.7 collective-permute-start.16
  42.1 4.8 %collective-permute-done.18 = f32[72,512]{1,0:T(8,128)S(1)} collective-permute-done((f32[72,512]{1,0:T(8,128)S(1)}, f32[72,512]{1,0:T(8,128)S(1)}, u32[]{:S(2)}, u32[]{:S(2)}) %collective-permute-start.18) | collective-permute-done | bytes 147488 | tf_op jit(solution)/shard_map/ppermute | solution.py:448
  46.9 2.8 %collective-permute-start.19 = (f32[72,512]{1,0:T(8,128)S(1)}, f32[72,512]{1,0:T(8,128)S(1)}, u32[]{:S(2)}, u32[]{:S(2)}) collective-permute-start(f32[72,512]{1,0:T(8,128)S(1)} %add.3), channel_id=1, source_target_pairs={{0,8},{1,13},{2,10},{3,15},{4,12},{5,9},{6,14},{7,11},{8,0},{9,5},... | collective-permute-start | bytes 442376 | tf_op jit(solution)/shard_map/ppermute | solution.py:448
  49.7 6.6 %collective-permute-done.19.refs_1_ = f32[72,512]{1,0:T(8,128)S(1)} collective-permute-done((f32[72,512]{1,0:T(8,128)S(1)}, f32[72,512]{1,0:T(8,128)S(1)}, u32[]{:S(2)}, u32[]{:S(2)}) %collective-permute-start.19) | collective-permute-done | bytes 147488 | tf_op jit(solution)/shard_map/ppermute | solution.py:448
  56.5 1.4 %collective-permute-done.20.other = f32[72,512]{1,0:T(8,128)S(1)} collective-permute-done((f32[72,512]{1,0:T(8,128)S(1)}, f32[72,512]{1,0:T(8,128)S(1)}, u32[]{:S(2)}, u32[]{:S(2)}) %collective-permute-start.20) | collective-permute-done | bytes 147488 | tf_op jit(solution)/shard_map/ppermute | solution.py:430
  57.8 0.1 chip_sum.1
  57.9 0.3 collective-permute-start.23
  58.2 0.7 collective-permute-start.22
  59.0 0.7 collective-permute-start.21
  59.6 5.6 %cholesky_inverse.1.inverse = f32[64,64]{1,0:T(8,128)S(1)} custom-call(f32[64,64]{1,0:T(8,128)S(1)} %get-tuple-element.40.gram), custom_call_target="tpu_custom_call" | custom-call | flops 5750000128 | tf_op jit(solution)/shard_map/cholesky_inverse/pallas_call | solution.py:300
  65.3 1.1 %collective-permute-done.23 = f32[64,512]{1,0:T(8,128)S(1)} collective-permute-done((f32[64,512]{1,0:T(8,128)S(1)}, f32[64,512]{1,0:T(8,128)S(1)}, u32[]{:S(2)}, u32[]{:S(2)}) %collective-permute-start.23) | collective-permute-done | bytes 131104 | tf_op jit(solution)/shard_map/ppermute | solution.py:448
  66.4 0.8 %collective-permute-start.24 = (f32[64,512]{1,0:T(8,128)S(1)}, f32[64,512]{1,0:T(8,128)S(1)}, u32[]{:S(2)}, u32[]{:S(2)}) collective-permute-start(f32[64,512]{1,0:T(8,128)S(1)} %collective-permute-done.23), channel_id=1, source_target_pairs={{0,2},{1,3},{2,0},{3,1},{4,6},{5,7},{6,4},{7,5},{8,10},{9,11},{10,... | collective-permute-start | bytes 393224 | tf_op jit(solution)/shard_map/ppermute | solution.py:448
  67.3 0.8 last_operand.1.lhs
  68.1 3.3 %collective-permute-done.24 = f32[64,512]{1,0:T(8,128)S(1)} collective-permute-done((f32[64,512]{1,0:T(8,128)S(1)}, f32[64,512]{1,0:T(8,128)S(1)}, u32[]{:S(2)}, u32[]{:S(2)}) %collective-permute-start.24) | collective-permute-done | bytes 131104 | tf_op jit(solution)/shard_map/ppermute | solution.py:448
  71.4 2.2 %collective-permute-start.25 = (f32[4,64,512]{2,1,0:T(8,128)S(1)}, f32[4,64,512]{2,1,0:T(8,128)S(1)}, u32[]{:S(2)}, u32[]{:S(2)}) collective-permute-start(f32[4,64,512]{2,1,0:T(8,128)S(1)} %pad_maximum_fusion.mine), channel_id=1, source_target_pairs={{0,1},{1,0},{2,3},{3,2},{4,5},{5,4},{6,7},{7,6},{8,9},{9,8},{10,11... | collective-permute-start | bytes 1572872 | tf_op jit(solution)/shard_map/ppermute | solution.py:430
  73.6 1.5 %collective-permute-done.25.theirs = f32[4,64,512]{2,1,0:T(8,128)S(1)} collective-permute-done((f32[4,64,512]{2,1,0:T(8,128)S(1)}, f32[4,64,512]{2,1,0:T(8,128)S(1)}, u32[]{:S(2)}, u32[]{:S(2)}) %collective-permute-start.25) | collective-permute-done | bytes 524320 | tf_op jit(solution)/shard_map/ppermute | solution.py:430
  75.2 4.5 %finish.1 = (bf16[448,4096]{1,0:T(8,128)(2,1)}, f32[64,4096]{1,0:T(8,128)}) custom-call(f32[4,64,512]{2,1,0:T(8,128)S(1)} %pad_maximum_fusion.mine, f32[4,64,512]{2,1,0:T(8,128)S(1)} %collective-permute-done.25.theirs, bf16[512,512]{1,0:T(8,128)(2,1)S(1)} %last_operand.1.lhs, bf16[448,4096]{1,0:T(8,128)(2,1)S(1)} %bitcast.16, ...), custom_call_target="tpu_custom_call" | custom-call | flops 5059999744 | tf_op jit(solution)/shard_map/finish/pallas_call | solution.py:370
  (29 shorter events, 0.2 us)
Async XLA Ops:
  1.6 10.9 %collective-permute-start.3 = (bf16[16,4096]{1,0:T(8,128)(2,1)S(1)}, bf16[16,4096]{1,0:T(8,128)(2,1)S(1)}, u32[]{:S(2)}, u32[]{:S(2)}) collective-permute-start(bf16[16,4096]{1,0:T(8,128)(2,1)S(1)} %get-tuple-element.48.refs_1_), channel_id=1, source_target_pairs={{2,0},{6,2},{10,6},{14,10},{12,14},{8,12},{4,8},{0,4},{3,1},{7,3},... | collective-permute-start | bytes 393224 | tf_op jit(solution)/shard_map/ppermute | solution.py:417
  4.7 9.8 %collective-permute-start.1 = (bf16[16,4096]{1,0:T(8,128)(2,1)S(1)}, bf16[16,4096]{1,0:T(8,128)(2,1)S(1)}, u32[]{:S(2)}, u32[]{:S(2)}) collective-permute-start(bf16[16,4096]{1,0:T(8,128)(2,1)S(1)} %get-tuple-element.48.refs_1_), channel_id=1, source_target_pairs={{0,2},{2,6},{6,10},{10,14},{14,12},{12,8},{8,4},{4,0},{1,3},{3,7},... | collective-permute-start | bytes 393224 | tf_op jit(solution)/shard_map/ppermute | solution.py:417
  4.7 11.5 %collective-permute-start.2 = (bf16[16,4096]{1,0:T(8,128)(2,1)S(1)}, bf16[16,4096]{1,0:T(8,128)(2,1)S(1)}, u32[]{:S(2)}, u32[]{:S(2)}) collective-permute-start(bf16[16,4096]{1,0:T(8,128)(2,1)S(1)} %get-tuple-element.49.refs_0_), channel_id=1, source_target_pairs={{2,0},{6,2},{10,6},{14,10},{12,14},{8,12},{4,8},{0,4},{3,1},{7,3},... | collective-permute-start | bytes 393224 | tf_op jit(solution)/shard_map/ppermute | solution.py:417
  6.7 5.8 %collective-permute-start = (bf16[16,4096]{1,0:T(8,128)(2,1)S(1)}, bf16[16,4096]{1,0:T(8,128)(2,1)S(1)}, u32[]{:S(2)}, u32[]{:S(2)}) collective-permute-start(bf16[16,4096]{1,0:T(8,128)(2,1)S(1)} %get-tuple-element.49.refs_0_), channel_id=1, source_target_pairs={{0,2},{2,6},{6,10},{10,14},{14,12},{12,8},{8,4},{4,0},{1,3},{3,7},... | collective-permute-start | bytes 393224 | tf_op jit(solution)/shard_map/ppermute | solution.py:417
  6.7 2.0 %copy-start = (bf16[1,448,4096]{2,1,0:T(8,128)(2,1)S(1)}, bf16[1,448,4096]{2,1,0:T(8,128)(2,1)}, u32[]{:S(2)}) copy-start(bf16[1,448,4096]{2,1,0:T(8,128)(2,1)} %param.7) | copy-start | bytes 11010052
  8.8 1.2 %copy-start.3 = (f32[64,4096]{1,0:T(8,128)S(1)}, f32[64,4096]{1,0:T(8,128)}, u32[]{:S(2)}) copy-start(f32[64,4096]{1,0:T(8,128)} %right.1) | copy-start | bytes 3145732
  10.0 21.1 %copy-start.4 = (bf16[1,256,448]{1,2,0:T(8,128)(2,1)S(1)}, bf16[1,256,448]{1,2,0:T(8,128)(2,1)}, u32[]{:S(2)}) copy-start(bf16[1,256,448]{1,2,0:T(8,128)(2,1)} %param.6) | copy-start | bytes 688132
  10.0 21.1 %copy-start.5 = (s32[8,16]{1,0:T(8,128)S(1)}, s32[8,16]{1,0:T(8,128)}, u32[]{:S(2)}) copy-start(s32[8,16]{1,0:T(8,128)} %constant.8.clone.places) | copy-start | bytes 1540
  12.5 5.8 %collective-permute-start.7 = (bf16[16,4096]{1,0:T(8,128)(2,1)S(1)}, bf16[16,4096]{1,0:T(8,128)(2,1)S(1)}, u32[]{:S(2)}, u32[]{:S(2)}) collective-permute-start(bf16[16,4096]{1,0:T(8,128)(2,1)S(1)} %collective-permute-done.3.refs_5_), channel_id=1, source_target_pairs={{2,0},{6,2},{10,6},{14,10},{12,14},{8,12},{4,8},{0,4},{3,1},{7,3},... | collective-permute-start | bytes 393224 | tf_op jit(solution)/shard_map/ppermute | solution.py:417
  14.2 6.1 %collective-permute-start.4 = (bf16[16,4096]{1,0:T(8,128)(2,1)S(1)}, bf16[16,4096]{1,0:T(8,128)(2,1)S(1)}, u32[]{:S(2)}, u32[]{:S(2)}) collective-permute-start(bf16[16,4096]{1,0:T(8,128)(2,1)S(1)} %collective-permute-done.refs_2_), channel_id=1, source_target_pairs={{0,2},{2,6},{6,10},{10,14},{14,12},{12,8},{8,4},{4,0},{1,3},{3,7},... | collective-permute-start | bytes 393224 | tf_op jit(solution)/shard_map/ppermute | solution.py:417
  14.5 7.8 %collective-permute-start.5 = (bf16[16,4096]{1,0:T(8,128)(2,1)S(1)}, bf16[16,4096]{1,0:T(8,128)(2,1)S(1)}, u32[]{:S(2)}, u32[]{:S(2)}) collective-permute-start(bf16[16,4096]{1,0:T(8,128)(2,1)S(1)} %collective-permute-done.1.refs_3_), channel_id=1, source_target_pairs={{0,2},{2,6},{6,10},{10,14},{14,12},{12,8},{8,4},{4,0},{1,3},{3,7},... | collective-permute-start | bytes 393224 | tf_op jit(solution)/shard_map/ppermute | solution.py:417
  16.2 6.5 %collective-permute-start.6 = (bf16[16,4096]{1,0:T(8,128)(2,1)S(1)}, bf16[16,4096]{1,0:T(8,128)(2,1)S(1)}, u32[]{:S(2)}, u32[]{:S(2)}) collective-permute-start(bf16[16,4096]{1,0:T(8,128)(2,1)S(1)} %collective-permute-done.2.refs_4_), channel_id=1, source_target_pairs={{2,0},{6,2},{10,6},{14,10},{12,14},{8,12},{4,8},{0,4},{3,1},{7,3},... | collective-permute-start | bytes 393224 | tf_op jit(solution)/shard_map/ppermute | solution.py:417
  18.3 6.4 %collective-permute-start.11 = (bf16[16,4096]{1,0:T(8,128)(2,1)S(1)}, bf16[16,4096]{1,0:T(8,128)(2,1)S(1)}, u32[]{:S(2)}, u32[]{:S(2)}) collective-permute-start(bf16[16,4096]{1,0:T(8,128)(2,1)S(1)} %collective-permute-done.7.refs_9_), channel_id=1, source_target_pairs={{2,0},{6,2},{10,6},{14,10},{12,14},{8,12},{4,8},{0,4},{3,1},{7,3},... | collective-permute-start | bytes 393224 | tf_op jit(solution)/shard_map/ppermute | solution.py:417
  20.3 5.8 %collective-permute-start.8 = (bf16[16,4096]{1,0:T(8,128)(2,1)S(1)}, bf16[16,4096]{1,0:T(8,128)(2,1)S(1)}, u32[]{:S(2)}, u32[]{:S(2)}) collective-permute-start(bf16[16,4096]{1,0:T(8,128)(2,1)S(1)} %collective-permute-done.4.refs_6_), channel_id=1, source_target_pairs={{0,2},{2,6},{6,10},{10,14},{14,12},{12,8},{8,4},{4,0},{1,3},{3,7},... | collective-permute-start | bytes 393224 | tf_op jit(solution)/shard_map/ppermute | solution.py:417
  22.3 5.8 %collective-permute-start.9 = (bf16[16,4096]{1,0:T(8,128)(2,1)S(1)}, bf16[16,4096]{1,0:T(8,128)(2,1)S(1)}, u32[]{:S(2)}, u32[]{:S(2)}) collective-permute-start(bf16[16,4096]{1,0:T(8,128)(2,1)S(1)} %collective-permute-done.5.refs_7_), channel_id=1, source_target_pairs={{0,2},{2,6},{6,10},{10,14},{14,12},{12,8},{8,4},{4,0},{1,3},{3,7},... | collective-permute-start | bytes 393224 | tf_op jit(solution)/shard_map/ppermute | solution.py:417
  22.7 5.4 %collective-permute-start.10 = (bf16[16,4096]{1,0:T(8,128)(2,1)S(1)}, bf16[16,4096]{1,0:T(8,128)(2,1)S(1)}, u32[]{:S(2)}, u32[]{:S(2)}) collective-permute-start(bf16[16,4096]{1,0:T(8,128)(2,1)S(1)} %collective-permute-done.6.refs_8_), channel_id=1, source_target_pairs={{2,0},{6,2},{10,6},{14,10},{12,14},{8,12},{4,8},{0,4},{3,1},{7,3},... | collective-permute-start | bytes 393224 | tf_op jit(solution)/shard_map/ppermute | solution.py:417
  24.6 5.0 %collective-permute-start.13 = (bf16[16,4096]{1,0:T(8,128)(2,1)S(1)}, bf16[16,4096]{1,0:T(8,128)(2,1)S(1)}, u32[]{:S(2)}, u32[]{:S(2)}) collective-permute-start(bf16[16,4096]{1,0:T(8,128)(2,1)S(1)} %collective-permute-done.11.refs_13_), channel_id=1, source_target_pairs={{2,0},{6,2},{10,6},{14,10},{12,14},{8,12},{4,8},{0,4},{3,1},{7,3},... | collective-permute-start | bytes 393224 | tf_op jit(solution)/shard_map/ppermute | solution.py:417
  26.1 5.0 %collective-permute-start.12 = (bf16[16,4096]{1,0:T(8,128)(2,1)S(1)}, bf16[16,4096]{1,0:T(8,128)(2,1)S(1)}, u32[]{:S(2)}, u32[]{:S(2)}) collective-permute-start(bf16[16,4096]{1,0:T(8,128)(2,1)S(1)} %collective-permute-done.8.refs_10_), channel_id=1, source_target_pairs={{0,2},{2,6},{6,10},{10,14},{14,12},{12,8},{8,4},{4,0},{1,3},{3,7},... | collective-permute-start | bytes 393224 | tf_op jit(solution)/shard_map/ppermute | solution.py:417
  31.1 3.3 %copy-start.1 = (bf16[1,448,4096]{2,1,0:T(8,128)(2,1)S(1)}, bf16[1,448,4096]{2,1,0:T(8,128)(2,1)}, u32[]{:S(2)}) copy-start(bf16[1,448,4096]{2,1,0:T(8,128)(2,1)} %param.7) | copy-start | bytes 11010052
  33.0 1.4 %collective-permute-start.14 = (f32[64,448]{1,0:T(8,128)S(1)}, f32[64,448]{1,0:T(8,128)S(1)}, u32[]{:S(2)}, u32[]{:S(2)}) collective-permute-start(f32[64,448]{1,0:T(8,128)S(1)} %get-tuple-element.30.here_l), channel_id=1, source_target_pairs={{0,1},{1,0},{2,3},{3,2},{4,5},{5,4},{6,7},{7,6},{8,9},{9,8},{10,11... | collective-permute-start | bytes 344072 | tf_op jit(solution)/shard_map/ppermute | solution.py:430
  37.3 2.0 %collective-permute-start.15 = (f32[4,64,512]{2,1,0:T(8,128)S(1)}, f32[4,64,512]{2,1,0:T(8,128)S(1)}, u32[]{:S(2)}, u32[]{:S(2)}) collective-permute-start(f32[4,64,512]{2,1,0:T(8,128)S(1)} %get-tuple-element.33), channel_id=1, source_target_pairs={{0,1},{1,0},{2,3},{3,2},{4,5},{5,4},{6,7},{7,6},{8,9},{9,8},{10,11... | collective-permute-start | bytes 1572872 | tf_op jit(solution)/shard_map/ppermute | solution.py:430
  39.3 7.5 %collective-permute-start.18 = (f32[72,512]{1,0:T(8,128)S(1)}, f32[72,512]{1,0:T(8,128)S(1)}, u32[]{:S(2)}, u32[]{:S(2)}) collective-permute-start(f32[72,512]{1,0:T(8,128)S(1)} %get-tuple-element.38), channel_id=1, source_target_pairs={{0,2},{1,3},{2,0},{3,1},{4,6},{5,7},{6,4},{7,5},{8,10},{9,11},{10,... | collective-permute-start | bytes 442376 | tf_op jit(solution)/shard_map/ppermute | solution.py:448
  39.9 9.8 %collective-permute-start.17 = (f32[72,512]{1,0:T(8,128)S(1)}, f32[72,512]{1,0:T(8,128)S(1)}, u32[]{:S(2)}, u32[]{:S(2)}) collective-permute-start(f32[72,512]{1,0:T(8,128)S(1)} %get-tuple-element.36), channel_id=1, source_target_pairs={{0,2},{1,7},{2,0},{3,5},{4,6},{5,3},{6,4},{7,1},{8,10},{9,15},{10,... | collective-permute-start | bytes 442376 | tf_op jit(solution)/shard_map/ppermute | solution.py:448
  41.4 8.3 %collective-permute-start.16 = (f32[72,512]{1,0:T(8,128)S(1)}, f32[72,512]{1,0:T(8,128)S(1)}, u32[]{:S(2)}, u32[]{:S(2)}) collective-permute-start(f32[72,512]{1,0:T(8,128)S(1)} %get-tuple-element.35.own), channel_id=1, source_target_pairs={{1,5},{3,7},{5,1},{7,3},{9,13},{11,15},{13,9},{15,11},{17,21},{19,... | collective-permute-start | bytes 442376 | tf_op jit(solution)/shard_map/ppermute | solution.py:448
  46.9 9.4 %collective-permute-start.19 = (f32[72,512]{1,0:T(8,128)S(1)}, f32[72,512]{1,0:T(8,128)S(1)}, u32[]{:S(2)}, u32[]{:S(2)}) collective-permute-start(f32[72,512]{1,0:T(8,128)S(1)} %add.3), channel_id=1, source_target_pairs={{0,8},{1,13},{2,10},{3,15},{4,12},{5,9},{6,14},{7,11},{8,0},{9,5},... | collective-permute-start | bytes 442376 | tf_op jit(solution)/shard_map/ppermute | solution.py:448
  56.4 1.4 %collective-permute-start.20 = (f32[72,512]{1,0:T(8,128)S(1)}, f32[72,512]{1,0:T(8,128)S(1)}, u32[]{:S(2)}, u32[]{:S(2)}) collective-permute-start(f32[72,512]{1,0:T(8,128)S(1)} %core_sum.1.here), channel_id=1, source_target_pairs={{0,1},{1,0},{2,3},{3,2},{4,5},{5,4},{6,7},{7,6},{8,9},{9,8},{10,11... | collective-permute-start | bytes 442376 | tf_op jit(solution)/shard_map/ppermute | solution.py:430
  57.9 8.5 %collective-permute-start.23 = (f32[64,512]{1,0:T(8,128)S(1)}, f32[64,512]{1,0:T(8,128)S(1)}, u32[]{:S(2)}, u32[]{:S(2)}) collective-permute-start(f32[64,512]{1,0:T(8,128)S(1)} %get-tuple-element.39), channel_id=1, source_target_pairs={{0,8},{1,13},{2,10},{3,15},{4,12},{5,9},{6,14},{7,11},{8,0},{9,5},... | collective-permute-start | bytes 393224 | tf_op jit(solution)/shard_map/ppermute | solution.py:448
  58.2 9.8 %collective-permute-start.22 = (f32[64,512]{1,0:T(8,128)S(1)}, f32[64,512]{1,0:T(8,128)S(1)}, u32[]{:S(2)}, u32[]{:S(2)}) collective-permute-start(f32[64,512]{1,0:T(8,128)S(1)} %get-tuple-element.39), channel_id=1, source_target_pairs={{0,2},{1,7},{2,0},{3,5},{4,6},{5,3},{6,4},{7,1},{8,10},{9,15},{10,... | collective-permute-start | bytes 393224 | tf_op jit(solution)/shard_map/ppermute | solution.py:448
  59.0 8.2 %collective-permute-start.21 = (f32[64,512]{1,0:T(8,128)S(1)}, f32[64,512]{1,0:T(8,128)S(1)}, u32[]{:S(2)}, u32[]{:S(2)}) collective-permute-start(f32[64,512]{1,0:T(8,128)S(1)} %get-tuple-element.39), channel_id=1, source_target_pairs={{1,5},{3,7},{5,1},{7,3},{9,13},{11,15},{13,9},{15,11},{17,21},{19,... | collective-permute-start | bytes 393224 | tf_op jit(solution)/shard_map/ppermute | solution.py:448
  66.4 5.0 %collective-permute-start.24 = (f32[64,512]{1,0:T(8,128)S(1)}, f32[64,512]{1,0:T(8,128)S(1)}, u32[]{:S(2)}, u32[]{:S(2)}) collective-permute-start(f32[64,512]{1,0:T(8,128)S(1)} %collective-permute-done.23), channel_id=1, source_target_pairs={{0,2},{1,3},{2,0},{3,1},{4,6},{5,7},{6,4},{7,5},{8,10},{9,11},{10,... | collective-permute-start | bytes 393224 | tf_op jit(solution)/shard_map/ppermute | solution.py:448
  67.2 7.9 %copy-start.2 = (bf16[1,448,4096]{2,1,0:T(8,128)(2,1)S(1)}, bf16[1,448,4096]{2,1,0:T(8,128)(2,1)}, u32[]{:S(2)}) copy-start(bf16[1,448,4096]{2,1,0:T(8,128)(2,1)} %param.7) | copy-start | bytes 11010052
  71.4 3.8 %collective-permute-start.25 = (f32[4,64,512]{2,1,0:T(8,128)S(1)}, f32[4,64,512]{2,1,0:T(8,128)S(1)}, u32[]{:S(2)}, u32[]{:S(2)}) collective-permute-start(f32[4,64,512]{2,1,0:T(8,128)S(1)} %pad_maximum_fusion.mine), channel_id=1, source_target_pairs={{0,1},{1,0},{2,3},{3,2},{4,5},{5,4},{6,7},{7,6},{8,9},{9,8},{10,11... | collective-permute-start | bytes 1572872 | tf_op jit(solution)/shard_map/ppermute | solution.py:430

commit v3 on v2

v3 whole, which is shorter than its diff:
```python
import functools

import jax
import jax.numpy as jnp
import numpy as np
from jax import lax
from jax.experimental import pallas as pl
from jax.experimental.pallas import tpu as pltpu
from jax.sharding import PartitionSpec as P

F32 = jnp.float32
BF16 = jnp.bfloat16
HIGHEST = lax.Precision.HIGHEST
VMEM_LIMIT = 32 * 1024 * 1024
STEPS = 4


def split3(value):
    high = value.astype(BF16)
    rest = value - high.astype(F32)
    middle = rest.astype(BF16)
    low = (rest - middle.astype(F32)).astype(BF16)
    return high, middle, low


def split2(value):
    high = value.astype(BF16)
    return high, (value - high.astype(F32)).astype(BF16)


def fold3(stacked):
    rank = stacked.shape[0] // 3
    return stacked[:rank] + stacked[rank : 2 * rank] + stacked[2 * rank :]


def nn(a, b):
    return lax.dot_general(a, b, (((1,), (0,)), ((), ())), preferred_element_type=F32)


def nt(a, b):
    return lax.dot_general(a, b, (((1,), (1,)), ((), ())), preferred_element_type=F32)


def params(semantics=None, limit=VMEM_LIMIT):
    return pltpu.CompilerParams(vmem_limit_bytes=limit, dimension_semantics=semantics)


def cost(microseconds):
    return pl.CostEstimate(flops=int(microseconds * 1.15e9), bytes_accessed=0, transcendentals=0)


def whole(shape):
    return pl.BlockSpec(shape, lambda *_: (0,) * len(shape))


def halves_kernel(shard, first, second):
    size = first.shape[0]
    first[...] = shard[:size, :]
    second[...] = shard[size:, :]


def halves_of(shard):
    half = jax.ShapeDtypeStruct((shard.shape[0] // 2, shard.shape[1]), BF16)
    return pl.pallas_call(
        halves_kernel,
        in_specs=[pl.BlockSpec(memory_space=pltpu.VMEM)],
        out_specs=[pl.BlockSpec(memory_space=pltpu.VMEM)] * 2,
        out_shape=[half, half],
        compiler_params=params(),
        cost_estimate=cost(4.0),
        name="halves",
    )(shard)


def residue_kernel(right, feedback, terms, left_t):
    cols = right.shape[1] // STEPS
    total = None
    for step in range(STEPS):
        span = slice(step * cols, (step + 1) * cols)
        stacked = jnp.concatenate(split3(right[:, span]), axis=0)
        terms[:, span] = stacked
        part = nt(stacked, feedback[:, span])
        total = part if total is None else total + part
    left_t[...] = fold3(total)


def residue_left(right, feedback):
    rank, width = right.shape
    rows = feedback.shape[0]
    return pl.pallas_call(
        residue_kernel,
        in_specs=[pl.BlockSpec(memory_space=pltpu.VMEM)] * 2,
        out_specs=[pl.BlockSpec(memory_space=pltpu.VMEM)] * 2,
        out_shape=[
            jax.ShapeDtypeStruct((3 * rank, width), BF16),
            jax.ShapeDtypeStruct((rank, rows), F32),
        ],
        compiler_params=params(),
        cost_estimate=cost(2.2),
        name="residue_left",
    )(right, feedback)


def early_kernel(places, *refs):
    pieces, (terms, residue_t, hidden_t, tokens, hidden, left_t) = refs[:-6], refs[-6:]
    here = lax.axis_index("tp")
    size = pieces[0].shape[0]
    for index in range(len(pieces) + 2):
        rows = pl.ds(pl.multiple_of(places[here, index] * size, size), size)
        if index < len(pieces):
            tokens[rows, :] = pieces[index][...]
        else:
            tokens[rows, :] = jnp.zeros((size, tokens.shape[1]), BF16)
    projected = fold3(nt(terms[...], tokens[...]))
    stacked = jnp.concatenate(split3(projected), axis=0)
    left_t[...] = residue_t[...] + fold3(nt(stacked, hidden_t[...]))
    hidden[...] = hidden_t[...].T


def early_left(places, pieces, terms, residue_t, hidden_t):
    rows, count = hidden_t.shape
    width = terms.shape[1]
    operands = [*pieces, terms, residue_t, hidden_t]
    return pl.pallas_call(
        early_kernel,
        in_specs=[pl.BlockSpec(memory_space=pltpu.SMEM)]
        + [pl.BlockSpec(memory_space=pltpu.VMEM)] * len(operands),
        out_specs=[pl.BlockSpec(memory_space=pltpu.VMEM)] * 3,
        out_shape=[
            jax.ShapeDtypeStruct((count, width), BF16),
            jax.ShapeDtypeStruct((count, rows), BF16),
            jax.ShapeDtypeStruct(residue_t.shape, F32),
        ],
        compiler_params=params(),
        cost_estimate=cost(2.0),
        name="early_left",
    )(places, *operands)


def late_kernel(places, first, second, terms, hidden, early_t, _, tokens, left_t):
    here = lax.axis_index("tp")
    size = first.shape[0]
    count = places.shape[1]
    seen = []
    for index, piece in enumerate((first, second)):
        rows = pl.ds(pl.multiple_of(places[here, count - 2 + index] * size, size), size)
        tokens[rows, :] = piece[...]
        seen.append(hidden[rows, :])
    projected = fold3(nt(terms[...], jnp.concatenate([first[...], second[...]], axis=0)))
    stacked = jnp.concatenate(split3(projected), axis=0)
    left_t[...] = early_t[...] + fold3(nn(stacked, jnp.concatenate(seen, axis=0)))


def late_left(places, pieces, terms, hidden, early_t, tokens):
    operands = [*pieces, terms, hidden, early_t, tokens]
    return pl.pallas_call(
        late_kernel,
        in_specs=[pl.BlockSpec(memory_space=pltpu.SMEM)]
        + [pl.BlockSpec(memory_space=pltpu.VMEM)] * len(operands),
        out_specs=[pl.BlockSpec(memory_space=pltpu.VMEM)] * 2,
        out_shape=[
            jax.ShapeDtypeStruct(tokens.shape, BF16),
            jax.ShapeDtypeStruct(early_t.shape, F32),
        ],
        input_output_aliases={len(operands): 0},
        compiler_params=params(),
        cost_estimate=cost(1.0),
        name="late_left",
    )(places, *operands)


def core_of(place):
    return (place >> 1) & 1


def index_of(place):
    return (place >> 2) * 2 + (place & 1)


def place_of(core, index):
    return (index >> 1) * 4 + core * 2 + (index & 1)


def columns_of(place, cols):
    shard = lax.axis_index("tp") ^ place
    return pl.ds(pl.multiple_of(shard * cols, cols), cols)


def give_kernel(here_l, other_l, hidden_t, feedback, tokens, give, left_sum, lhs, rhs):
    left_t = here_l[...] + other_l[...]
    left_sum[...] = left_t
    lhs[...] = jnp.concatenate(split3(left_t), axis=0)
    seen_t = fold3(nn(lhs[...], hidden_t[...]))
    rhs[...] = jnp.concatenate(split3(seen_t), axis=0)
    other = 1 - lax.axis_index("dp")
    for index in range(give.shape[0]):
        span = columns_of(place_of(other, index), give.shape[2])
        give[index] = fold3(nn(lhs[...], feedback[:, span]) + nn(rhs[...], tokens[:, span]))


def given_terms(here_l, other_l, hidden_t, feedback, tokens, chips):
    rank, rows = here_l.shape
    count, width = tokens.shape
    return pl.pallas_call(
        give_kernel,
        in_specs=[pl.BlockSpec(memory_space=pltpu.VMEM)] * 5,
        out_specs=[pl.BlockSpec(memory_space=pltpu.VMEM)] * 4,
        out_shape=[
            jax.ShapeDtypeStruct((chips // 2, rank, width // chips), F32),
            jax.ShapeDtypeStruct((rank, rows), F32),
            jax.ShapeDtypeStruct((3 * rank, rows), BF16),
            jax.ShapeDtypeStruct((3 * rank, count), BF16),
        ],
        compiler_params=params(),
        cost_estimate=cost(1.8),
        name="given_terms",
    )(here_l, other_l, hidden_t, feedback, tokens)


def keep_kernel(left_sum, lhs, rhs, feedback, tokens, keep, gram):
    core = lax.axis_index("dp")
    for index in range(keep.shape[0]):
        span = columns_of(place_of(core, index), keep.shape[2])
        keep[index] = fold3(nn(lhs[...], feedback[:, span]) + nn(rhs[...], tokens[:, span]))
    left_t = left_sum[...]
    gram[...] = lax.dot_general(
        left_t, left_t, (((1,), (1,)), ((), ())), precision=HIGHEST, preferred_element_type=F32
    )


def kept_terms(left_sum, lhs, rhs, feedback, tokens, chips):
    rank = left_sum.shape[0]
    return pl.pallas_call(
        keep_kernel,
        in_specs=[pl.BlockSpec(memory_space=pltpu.VMEM)] * 5,
        out_specs=[pl.BlockSpec(memory_space=pltpu.VMEM)] * 2,
        out_shape=[
            jax.ShapeDtypeStruct((chips // 2, rank, tokens.shape[1] // chips), F32),
            jax.ShapeDtypeStruct((rank, rank), F32),
        ],
        compiler_params=params(),
        cost_estimate=cost(1.8),
        name="kept_terms",
    )(left_sum, lhs, rhs, feedback, tokens)


def merged_kernel(hidden_t, feedback, tokens, merged):
    cols = tokens.shape[1] // STEPS
    for step in range(STEPS):
        span = slice(step * cols, (step + 1) * cols)
        merged[:, span] = nn(hidden_t[...], tokens[:, span]) + feedback[:, span].astype(F32)


def merged_sum(hidden_t, feedback, tokens):
    return pl.pallas_call(
        merged_kernel,
        in_specs=[pl.BlockSpec(memory_space=pltpu.VMEM)] * 3,
        out_specs=pl.BlockSpec(memory_space=pltpu.VMEM),
        out_shape=jax.ShapeDtypeStruct(feedback.shape, F32),
        compiler_params=params(),
        cost_estimate=cost(2.0),
        name="merged",
    )(hidden_t, feedback, tokens)


def message_kernel(keep, got, gram, *messages):
    rank, cols = keep.shape[1:]
    blocks = cols // rank
    rows = rank // blocks
    for index, message in enumerate(messages):
        message[:rank, :] = keep[index] + got[index]
        for block in range(blocks):
            message[rank:, block * rank : (block + 1) * rank] = gram[block * rows : (block + 1) * rows, :]


def messages_for(keep, got, gram):
    places, rank, cols = keep.shape
    rows = rank + rank // (cols // rank)
    return pl.pallas_call(
        message_kernel,
        in_specs=[pl.BlockSpec(memory_space=pltpu.VMEM)] * 3,
        out_specs=[pl.BlockSpec(memory_space=pltpu.VMEM)] * places,
        out_shape=[jax.ShapeDtypeStruct((rows, cols), F32)] * places,
        compiler_params=params(),
        cost_estimate=cost(0.3),
        name="messages",
    )(keep, got, gram)


def core_sum_kernel(own, second, *refs):
    messages, total = refs[:-1], refs[-1]
    first = jnp.where(lax.axis_index("dp") == 0, own[...], second[...])
    parts = [first + messages[0][...]] + [message[...] for message in messages[1:]]
    while len(parts) > 1:
        parts = [a + b for a, b in zip(parts[::2], parts[1::2])]
    total[...] = parts[0]


def core_sum(own, first, second, across):
    operands = [own, first, second, *across]
    return pl.pallas_call(
        core_sum_kernel,
        in_specs=[pl.BlockSpec(memory_space=pltpu.VMEM)] * len(operands),
        out_specs=pl.BlockSpec(memory_space=pltpu.VMEM),
        out_shape=jax.ShapeDtypeStruct(own.shape, F32),
        compiler_params=params(),
        cost_estimate=cost(0.3),
        name="core_sum",
    )(*operands)


def chip_sum_kernel(here, other, share, gram):
    total = here[...] + other[...]
    rank, cols = share.shape
    blocks = cols // rank
    rows = rank // blocks
    share[...] = total[:rank]
    for block in range(blocks):
        gram[block * rows : (block + 1) * rows, :] = total[rank:, block * rank : (block + 1) * rank]


def chip_sum(here, other, rank):
    return pl.pallas_call(
        chip_sum_kernel,
        in_specs=[pl.BlockSpec(memory_space=pltpu.VMEM)] * 2,
        out_specs=[pl.BlockSpec(memory_space=pltpu.VMEM)] * 2,
        out_shape=[
            jax.ShapeDtypeStruct((rank, here.shape[1]), F32),
            jax.ShapeDtypeStruct((rank, rank), F32),
        ],
        compiler_params=params(),
        cost_estimate=cost(0.3),
        name="chip_sum",
    )(here, other)


def inverse_kernel(gram, inverse):
    rank = gram.shape[0]
    row = lax.broadcasted_iota(jnp.int32, (rank, 2 * rank), 0)
    lane = lax.broadcasted_iota(jnp.int32, (rank, 2 * rank), 1)
    eye = (lane[:, rank:] == row[:, rank:] + rank).astype(F32)
    table = jnp.concatenate([gram[...], eye], axis=1)
    scale = jnp.zeros((rank, 1), F32)
    for pivot in range(rank):
        line = table[pivot : pivot + 1, :]
        column = table[:, pivot : pivot + 1]
        top = line[:, pivot : pivot + 1]
        scale = jnp.where(row[:, :1] == pivot, lax.rsqrt(top), scale)
        if pivot + 1 < rank:
            factor = jnp.where(row[:, :1] > pivot, column / top, 0.0)
            table = table - factor * line
    inverse[...] = table[:, rank:] * scale


def cholesky_inverse(gram):
    return pl.pallas_call(
        inverse_kernel,
        in_specs=[pl.BlockSpec(memory_space=pltpu.VMEM)],
        out_specs=pl.BlockSpec(memory_space=pltpu.VMEM),
        out_shape=jax.ShapeDtypeStruct(gram.shape, F32),
        compiler_params=params(),
        cost_estimate=cost(5.0),
        name="cholesky_inverse",
    )(gram)


def spread(target, rows, value):
    rank = value.shape[1]
    high, low = split2(value)
    for place, term in enumerate((high, high, low, low)):
        target[rows, place * rank : (place + 1) * rank] = term


def operand_kernel(replicas, inverse, left_sum, lhs):
    rank, rows = left_sum.shape
    orth_t = jnp.dot(inverse[...], left_sum[...], precision=HIGHEST, preferred_element_type=F32)
    share = inverse[...] * (1.0 / replicas)
    weight_t = lax.dot_general(
        share, orth_t, (((0,), (0,)), ((), ())), precision=HIGHEST, preferred_element_type=F32
    )
    spread(lhs, slice(0, rows), -weight_t.T)
    spread(lhs, slice(rows, rows + rank), share)


def last_operand(inverse, left_sum, replicas):
    rank, rows = left_sum.shape
    return pl.pallas_call(
        functools.partial(operand_kernel, replicas),
        in_specs=[pl.BlockSpec(memory_space=pltpu.VMEM)] * 2,
        out_specs=pl.BlockSpec(memory_space=pltpu.VMEM),
        out_shape=jax.ShapeDtypeStruct((rows + rank, 4 * rank), BF16),
        compiler_params=params(),
        cost_estimate=cost(1.5),
        name="last_operand",
    )(inverse, left_sum)


def final_kernel(mine, theirs, lhs, merged, out, factor, rhs, out_here, factor_here, sems):
    chip, core = lax.axis_index("tp"), lax.axis_index("dp")
    rows = merged.shape[0]
    rank, cols = mine.shape[1:]
    group = 2 * mine.shape[0] // STEPS
    copies = []
    for step in range(STEPS):
        for part in range(group):
            place = (group * step + part) ^ chip
            index = index_of(place)
            high, low = split2(jnp.where(core_of(place) == core, mine[index], theirs[index]))
            span = slice(part * cols, (part + 1) * cols)
            for order, term in enumerate((high, low, high, low)):
                rhs[step % 2, order * rank : (order + 1) * rank, span] = term
        span = slice(step * group * cols, (step + 1) * group * cols)
        product = nn(lhs[...], rhs[step % 2])
        factor_here[:, span] = product[rows:]
        out_here[:, span] = (merged[:, span] + product[:rows]).astype(BF16)
        for index, (source, target) in enumerate(((out_here, out), (factor_here, factor))):
            copies.append(pltpu.make_async_copy(source.at[:, span], target.at[:, span], sems.at[step, index]))
            copies[-1].start()
    for copy in copies:
        copy.wait()


def finish(mine, theirs, lhs, merged):
    rank = mine.shape[1]
    rows, width = merged.shape
    return pl.pallas_call(
        final_kernel,
        in_specs=[pl.BlockSpec(memory_space=pltpu.VMEM)] * 4,
        out_specs=[pl.BlockSpec(memory_space=pl.ANY)] * 2,
        out_shape=[
            jax.ShapeDtypeStruct((rows, width), BF16),
            jax.ShapeDtypeStruct((rank, width), F32),
        ],
        scratch_shapes=[
            pltpu.VMEM((2, lhs.shape[1], width // STEPS), BF16),
            pltpu.VMEM((rows, width), BF16),
            pltpu.VMEM((rank, width), F32),
            pltpu.SemaphoreType.DMA((STEPS, 2)),
        ],
        compiler_params=params(),
        cost_estimate=cost(3.0),
        name="finish",
    )(mine, theirs, lhs, merged)


def ring_order(chips):
    if chips == 8:
        return [0, 1, 3, 5, 7, 6, 4, 2]
    return list(range(chips))


def ring_gather(shard, chips, beside):
    order = ring_order(chips)
    position = {chip: place for place, chip in enumerate(order)}
    right = [(order[i], order[(i + 1) % chips]) for i in range(chips)]
    left = [(b, a) for a, b in right]
    halves = halves_of(shard)
    pieces = list(halves)
    origin = [(0, 0), (0, 1)]
    going = {(way, half): halves[half] for way in (1, -1) for half in (0, 1)}
    far = chips // 2
    for hop in range(1, far + 1):
        for way, pairs in ((1, right), (-1, left)):
            for half in (0, 1):
                if hop == far and (half == 0) != (way == 1):
                    continue
                going[way, half] = lax.ppermute(going[way, half], "tp", pairs)
                if hop == 1 and (way, half) == (-1, 0):
                    going[way, half], beside = lax.optimization_barrier((going[way, half], beside))
                pieces.append(going[way, half])
                origin.append((-way * hop, half))
    places = np.zeros((chips, len(pieces)), np.int32)
    for chip in range(chips):
        for index, (shift, half) in enumerate(origin):
            places[chip, index] = 2 * order[(position[chip] + shift) % chips] + half
    return pieces, places, beside


def swap(value):
    return lax.ppermute(value, "dp", [(0, 1), (1, 0)])


def local(grad_out, hidden, feedback, right_factor):
    shard, residue = grad_out[0], feedback[0]
    hidden_t = hidden[0].T
    chips, replicas = lax.axis_size("tp"), lax.axis_size("dp")
    rank = right_factor.shape[0]

    half = chips // 2

    def exchange(value, index, place=None):
        pairs = []
        for chip in range(chips):
            for core in range(2):
                to = (index >> 1) * 4 + core * 2 + (index & 1) if place is None else place
                if to:
                    pairs.append((2 * chip + core, 2 * (chip ^ to) + core))
        return lax.ppermute(value, ("tp", "dp"), pairs)

    pieces, places, (terms, residue_t) = ring_gather(shard, chips, residue_left(right_factor, residue))
    places = jnp.asarray(places)
    tokens, hidden_rows, left_t = early_left(places, pieces[:-2], terms, residue_t, hidden_t)
    tokens, left_t = late_left(places, pieces[-2:], terms, hidden_rows, left_t, tokens)
    give, left_sum, lhs, rhs = given_terms(left_t, swap(left_t), hidden_t, residue, tokens, chips)
    got = swap(give)
    keep, gram = kept_terms(left_sum, lhs, rhs, residue, tokens, chips)

    messages = messages_for(keep, got, gram)
    passed = [exchange(messages[index + 1], index + 1, 1) for index in range(2, half, 2)]
    across = [messages[2 * i + 2] + value for i, value in enumerate(passed)]
    across = [exchange(value, 2 * i + 2) for i, value in enumerate(across)]
    merged = merged_sum(hidden_t, residue, tokens)
    own, beside, passed, merged = lax.optimization_barrier((messages[0], messages[1], passed, merged))
    beside = exchange(beside, 1), exchange(own, 0)
    partial = core_sum(own, beside[1], beside[0], across)
    share, gram_matrix = chip_sum(partial, swap(partial), rank)

    across = [exchange(share, index) for index in range(2, half, 2)]
    beside = exchange(share, 1), exchange(share, 0)
    inverse = cholesky_inverse(gram_matrix)
    across[0], inverse = lax.optimization_barrier((across[0], inverse))
    passed = [exchange(value, 2 * i + 3, 1) for i, value in enumerate(across)]
    lhs = last_operand(inverse, left_sum, replicas)
    first = jnp.where(lax.axis_index("dp") == 0, share, beside[1])
    mine = jnp.stack([first, beside[0]] + [value for pair in zip(across, passed) for value in pair])
    mine, lhs = lax.optimization_barrier((mine, lhs))
    new_feedback, new_factor = finish(mine, swap(mine), lhs, merged)
    return new_feedback[None], new_factor


def solution(mesh):
    return jax.shard_map(
        local,
        mesh=mesh,
        in_specs=(
            P(("runs", "dp"), "tp", None),
            P(("runs", "dp"), None, "tp"),
            P(("runs", "dp"), "tp", None),
            P(),
        ),
        out_specs=(P(("runs", "dp"), "tp", None), P("runs", None)),
        check_vma=False,
    )
```

time: 79.9 us -> 72.3 us (0.905)
  waiting for transfers between devices: 30.6 us -> 23 us
  starting transfers between devices: 26 us -> 27.8 us
  Pallas kernels: 17.9 us -> 16.7 us
    ppermute x8, waiting for transfers between devices: 15.8 us -> 9.52 us  [exchange(): return lax.ppermute(value, ('tp', 'dp'), pairs)]
    ppermute x8, starting transfers between devices: 8.15 us -> 10.2 us  [exchange(): return lax.ppermute(value, ('tp', 'dp'), pairs)]
    ppermute x4, waiting for transfers between devices: 5.98 us -> 4.74 us  [swap(): return lax.ppermute(value, 'dp', [(0, 1), (1, 0)])]
    slice x1 -> x0, local copies, waits for them, and re-layouts: 0.99 us -> none  [ring_gather(): halves = [shard[:size], shard[size:]]]
    pallas_call x1, Pallas kernels: 2.13 us -> 1.18 us  [residue_left(): pl.pallas_call(residue_kernel, in_specs=[pl.BlockSpec(memory_space=pltpu....]
    unnamed x12 -> x16, local copies, waits for them, and re-layouts: 3.28 us -> 3.86 us
    pallas_call x3 -> x7, Pallas kernels: 9.17 us -> 8.9 us  [the longest x1 2.67 us: finish(): pl.pallas_call(final_kernel, in_specs=[pl.BlockSpec(memory_space=pltpu.VM...]
  transfers between devices with their start and end apart: 26 -> 26, of which waited for: 15 -> 18; matrix products, arithmetic and copies ran while one was open for 0% -> 0% of each run, Pallas kernels for 11% -> 16%
where the time goes in v3:
time: 72.3 us; the launch traced here: 72.2 us
  starting transfers between devices  27.8 us (38%)
  waiting for transfers between devices  23 us (32%)
  Pallas kernels  16.7 us (23%)
  local copies, waits for them, and re-layouts  3.86 us (5%)
  between operations  0.79 us (1%)
    ppermute x14, starting transfers between devices, ring_gather(): going[way, half] = lax.ppermute(going[way, half], 'tp', pairs)  14.8 us
    ppermute x8, starting transfers between devices, exchange(): return lax.ppermute(value, ('tp', 'dp'), pairs)  10.2 us
    ppermute x8, waiting for transfers between devices, exchange(): return lax.ppermute(value, ('tp', 'dp'), pairs)  9.52 us
    ppermute x14, waiting for transfers between devices, ring_gather(): going[way, half] = lax.ppermute(going[way, half], 'tp', pairs)  8.73 us
    pallas_call x1, Pallas kernels, cholesky_inverse(): pl.pallas_call(inverse_kernel, in_specs=[pl.BlockSpec(memory_space=pltpu....  5.61 us
    ppermute x4, waiting for transfers between devices, swap(): return lax.ppermute(value, 'dp', [(0, 1), (1, 0)])  4.74 us
    unnamed x16, local copies, waits for them, and re-layouts  3.86 us
    ppermute x4, starting transfers between devices, swap(): return lax.ppermute(value, 'dp', [(0, 1), (1, 0)])  2.8 us
  transfers between devices with their start and end apart: 26, of which 18 were waited for; matrix products, arithmetic and copies ran while one was open for 0% of the time, Pallas kernels for 16%

profile of v3, /device:TPU:0, one launch (start us, length us, event | category | flops | bytes accessed | tf_op | source)
XLA Modules:
  0.0 72.2 jit_solution(15398477182318915872)
XLA Ops:
  0.6 0.9 %copy-done.5 = bf16[1,32,4096]{2,1,0:T(8,128)(2,1)S(1)} copy-done((bf16[1,32,4096]{2,1,0:T(8,128)(2,1)S(1)}, bf16[1,32,4096]{2,1,0:T(8,128)(2,1)}, u32[]{:S(2)}) %copy-start.5) | copy-done | bytes 262168
  1.6 3.1 %collective-permute-start.8 = (bf16[16,4096]{1,0:T(8,128)(2,1)S(1)}, bf16[16,4096]{1,0:T(8,128)(2,1)S(1)}, u32[]{:S(2)}, u32[]{:S(2)}) collective-permute-start(bf16[16,4096]{1,0:T(8,128)(2,1)S(1)} %get-tuple-element.35.refs_0_), channel_id=1, source_target_pairs={{2,0},{6,2},{10,6},{14,10},{12,14},{8,12},{4,8},{0,4},{3,1},{7,3},... | collective-permute-start | bytes 393224 | tf_op jit(solution)/shard_map/ppermute | solution.py:467
  4.7 2.0 %collective-permute-start.9 = (bf16[16,4096]{1,0:T(8,128)(2,1)S(1)}, bf16[16,4096]{1,0:T(8,128)(2,1)S(1)}, u32[]{:S(2)}, u32[]{:S(2)}) collective-permute-start(bf16[16,4096]{1,0:T(8,128)(2,1)S(1)} %get-tuple-element.36.refs_1_), channel_id=1, source_target_pairs={{0,2},{2,6},{6,10},{10,14},{14,12},{12,8},{8,4},{4,0},{1,3},{3,7},... | collective-permute-start | bytes 393224 | tf_op jit(solution)/shard_map/ppermute | solution.py:467
  6.7 0.1 collective-permute-start.4
  6.8 1.2 %residue_left.1 = (bf16[192,4096]{1,0:T(8,128)(2,1)S(1)}, f32[64,448]{1,0:T(8,128)S(1)}) custom-call(f32[64,4096]{1,0:T(8,128)S(1)} %copy-done.4, bf16[448,4096]{1,0:T(8,128)(2,1)S(1)} %bitcast.13), custom_call_target="tpu_custom_call" | custom-call | flops 2529999872 | tf_op jit(solution)/shard_map/residue_left/pallas_call | solution.py:90
  7.9 0.6 collective-permute-done.8.refs_4_
  8.6 2.5 %collective-permute-done.refs_2_ = bf16[16,4096]{1,0:T(8,128)(2,1)S(1)} collective-permute-done((bf16[16,4096]{1,0:T(8,128)(2,1)S(1)}, bf16[16,4096]{1,0:T(8,128)(2,1)S(1)}, u32[]{:S(2)}, u32[]{:S(2)}) %collective-permute-start) | collective-permute-done | bytes 131104 | tf_op jit(solution)/shard_map/ppermute | solution.py:467
  11.1 0.5 collective-permute-done.4.refs_5_
  11.6 1.5 %collective-permute-start.5 = (bf16[16,4096]{1,0:T(8,128)(2,1)S(1)}, bf16[16,4096]{1,0:T(8,128)(2,1)S(1)}, u32[]{:S(2)}, u32[]{:S(2)}) collective-permute-start(bf16[16,4096]{1,0:T(8,128)(2,1)S(1)} %collective-permute-done.4.refs_5_), channel_id=1, source_target_pairs={{2,0},{6,2},{10,6},{14,10},{12,14},{8,12},{4,8},{0,4},{3,1},{7,3},... | collective-permute-start | bytes 393224 | tf_op jit(solution)/shard_map/ppermute | solution.py:467
  13.1 0.7 collective-permute-done.9.refs_3_
  13.9 2.0 %collective-permute-start.11 = (bf16[16,4096]{1,0:T(8,128)(2,1)S(1)}, bf16[16,4096]{1,0:T(8,128)(2,1)S(1)}, u32[]{:S(2)}, u32[]{:S(2)}) collective-permute-start(bf16[16,4096]{1,0:T(8,128)(2,1)S(1)} %collective-permute-done.8.refs_4_), channel_id=1, source_target_pairs={{2,0},{6,2},{10,6},{14,10},{12,14},{8,12},{4,8},{0,4},{3,1},{7,3},... | collective-permute-start | bytes 393224 | tf_op jit(solution)/shard_map/ppermute | solution.py:467
  15.9 1.2 %collective-permute-done.1.refs_6_ = bf16[16,4096]{1,0:T(8,128)(2,1)S(1)} collective-permute-done((bf16[16,4096]{1,0:T(8,128)(2,1)S(1)}, bf16[16,4096]{1,0:T(8,128)(2,1)S(1)}, u32[]{:S(2)}, u32[]{:S(2)}) %collective-permute-start.1) | collective-permute-done | bytes 131104 | tf_op jit(solution)/shard_map/ppermute | solution.py:467
  17.1 0.3 collective-permute-start.2
  17.4 1.7 %collective-permute-start.6 = (bf16[16,4096]{1,0:T(8,128)(2,1)S(1)}, bf16[16,4096]{1,0:T(8,128)(2,1)S(1)}, u32[]{:S(2)}, u32[]{:S(2)}) collective-permute-start(bf16[16,4096]{1,0:T(8,128)(2,1)S(1)} %collective-permute-done.5.refs_9_), channel_id=1, source_target_pairs={{2,0},{6,2},{10,6},{14,10},{12,14},{8,12},{4,8},{0,4},{3,1},{7,3},... | collective-permute-start | bytes 393224 | tf_op jit(solution)/shard_map/ppermute | solution.py:467
  19.1 1.1 %collective-permute-done.10.refs_7_ = bf16[16,4096]{1,0:T(8,128)(2,1)S(1)} collective-permute-done((bf16[16,4096]{1,0:T(8,128)(2,1)S(1)}, bf16[16,4096]{1,0:T(8,128)(2,1)S(1)}, u32[]{:S(2)}, u32[]{:S(2)}) %collective-permute-start.10) | collective-permute-done | bytes 131104 | tf_op jit(solution)/shard_map/ppermute | solution.py:467
  20.2 2.0 %collective-permute-start.13 = (bf16[16,4096]{1,0:T(8,128)(2,1)S(1)}, bf16[16,4096]{1,0:T(8,128)(2,1)S(1)}, u32[]{:S(2)}, u32[]{:S(2)}) collective-permute-start(bf16[16,4096]{1,0:T(8,128)(2,1)S(1)} %collective-permute-done.11.refs_8_), channel_id=1, source_target_pairs={{2,0},{6,2},{10,6},{14,10},{12,14},{8,12},{4,8},{0,4},{3,1},{7,3},... | collective-permute-start | bytes 393224 | tf_op jit(solution)/shard_map/ppermute | solution.py:467
  22.2 0.9 %collective-permute-done.2.refs_10_ = bf16[16,4096]{1,0:T(8,128)(2,1)S(1)} collective-permute-done((bf16[16,4096]{1,0:T(8,128)(2,1)S(1)}, bf16[16,4096]{1,0:T(8,128)(2,1)S(1)}, u32[]{:S(2)}, u32[]{:S(2)}) %collective-permute-start.2) | collective-permute-done | bytes 131104 | tf_op jit(solution)/shard_map/ppermute | solution.py:467
  23.2 1.9 %collective-permute-start.7 = (bf16[16,4096]{1,0:T(8,128)(2,1)S(1)}, bf16[16,4096]{1,0:T(8,128)(2,1)S(1)}, u32[]{:S(2)}, u32[]{:S(2)}) collective-permute-start(bf16[16,4096]{1,0:T(8,128)(2,1)S(1)} %collective-permute-done.6.refs_13_), channel_id=1, source_target_pairs={{2,0},{6,2},{10,6},{14,10},{12,14},{8,12},{4,8},{0,4},{3,1},{7,3},... | collective-permute-start | bytes 393224 | tf_op jit(solution)/shard_map/ppermute | solution.py:467
  25.1 0.1 collective-permute-done.12.refs_11_
  25.3 1.9 %early_left.1 = (bf16[256,4096]{1,0:T(8,128)(2,1)S(1)}, bf16[256,448]{1,0:T(8,128)(2,1)S(1)}, f32[64,448]{1,0:T(8,128)S(1)}) custom-call(s32[8,16]{1,0:T(8,128)S(1)} %copy-done.3, bf16[16,4096]{1,0:T(8,128)(2,1)S(1)} %get-tuple-element.35.refs_0_, bf16[16,4096]{1,0:T(8,128)(2,1)S(1)} %get-tuple-element.36.refs_1_, ...), custom_call_target="tpu_custom_call" | custom-call | flops 2300000000 | tf_op jit(solution)/shard_map/early_left/pallas_call | solution.py:124
  27.1 1.0 %collective-permute-done.3.first = bf16[16,4096]{1,0:T(8,128)(2,1)S(1)} collective-permute-done((bf16[16,4096]{1,0:T(8,128)(2,1)S(1)}, bf16[16,4096]{1,0:T(8,128)(2,1)S(1)}, u32[]{:S(2)}, u32[]{:S(2)}) %collective-permute-start.3) | collective-permute-done | bytes 131104 | tf_op jit(solution)/shard_map/ppermute | solution.py:467
  28.2 1.4 %late_left.1 = (bf16[256,4096]{1,0:T(8,128)(2,1)S(1)}, f32[64,448]{1,0:T(8,128)S(1)}) custom-call(s32[8,16]{1,0:T(8,128)S(1)} %copy-done.3, bf16[16,4096]{1,0:T(8,128)(2,1)S(1)} %collective-permute-done.3.first, bf16[16,4096]{1,0:T(8,128)(2,1)S(1)} %collective-permute-done.7.second, ...), custom_call_target="tpu_custom_call", output_to_operand_aliasing={{0}: (6, {})} | custom-call | flops 1150000000 | tf_op jit(solution)/shard_map/late_left/pallas_call | solution.py:156
  29.7 1.3 %collective-permute-done.14.other_l = f32[64,448]{1,0:T(8,128)S(1)} collective-permute-done((f32[64,448]{1,0:T(8,128)S(1)}, f32[64,448]{1,0:T(8,128)S(1)}, u32[]{:S(2)}, u32[]{:S(2)}) %collective-permute-start.14) | collective-permute-done | bytes 114720 | tf_op jit(solution)/shard_map/ppermute | solution.py:480
  31.0 1.0 %given_terms.1 = (f32[4,64,512]{2,1,0:T(8,128)S(1)}, f32[64,448]{1,0:T(8,128)S(1)}, bf16[192,448]{1,0:T(8,128)(2,1)S(1)}, bf16[192,256]{1,0:T(8,128)(2,1)S(1)}) custom-call(f32[64,448]{1,0:T(8,128)S(1)} %get-tuple-element.45.here_l, f32[64,448]{1,0:T(8,128)S(1)} %collective-permute-done.14.other_l, bf16[448,256]{1,0:T(8,128)(2,1)S(1)} %bitcast.18, ...), custom_call_target="tpu_custom_call" | custom-call | flops 2070000000 | tf_op jit(solution)/shard_map/given_terms/pallas_call | solution.py:204
  32.0 0.2 collective-permute-start.15
  32.2 0.9 %kept_terms.1 = (f32[4,64,512]{2,1,0:T(8,128)S(1)}, f32[64,64]{1,0:T(8,128)S(1)}) custom-call(f32[64,448]{1,0:T(8,128)S(1)} %get-tuple-element.47.left_sum, bf16[192,448]{1,0:T(8,128)(2,1)S(1)} %get-tuple-element.48.lhs, bf16[192,256]{1,0:T(8,128)(2,1)S(1)} %get-tuple-element.49.rhs, bf16[448,4096]{1,0:T(8,128)(2,1)S(1)} %bitcast.15, ...), custom_call_target="tpu_custom_call" | custom-call | flops 2070000000 | tf_op jit(solution)/shard_map/kept_terms/pallas_call | solution.py:233
  33.1 0.9 %collective-permute-done.15.got = f32[4,64,512]{2,1,0:T(8,128)S(1)} collective-permute-done((f32[4,64,512]{2,1,0:T(8,128)S(1)}, f32[4,64,512]{2,1,0:T(8,128)S(1)}, u32[]{:S(2)}, u32[]{:S(2)}) %collective-permute-start.15) | collective-permute-done | bytes 524320 | tf_op jit(solution)/shard_map/ppermute | solution.py:480
  34.0 1.9 %collective-permute-start.16 = (f32[72,512]{1,0:T(8,128)S(1)}, f32[72,512]{1,0:T(8,128)S(1)}, u32[]{:S(2)}, u32[]{:S(2)}) collective-permute-start(f32[72,512]{1,0:T(8,128)S(1)} %get-tuple-element.55), channel_id=1, source_target_pairs={{0,2},{1,3},{2,0},{3,1},{4,6},{5,7},{6,4},{7,5},{8,10},{9,11},{10,... | collective-permute-start | bytes 442376 | tf_op jit(solution)/shard_map/ppermute | solution.py:498
  35.9 1.1 %merged.1 = f32[448,4096]{1,0:T(8,128)S(1)} custom-call(bf16[448,256]{1,0:T(8,128)(2,1)S(1)} %bitcast.19, bf16[448,4096]{1,0:T(8,128)(2,1)S(1)} %bitcast.16, bf16[256,4096]{1,0:T(8,128)(2,1)S(1)} %get-tuple-element.46.tokens), custom_call_target="tpu_custom_call" | custom-call | flops 2300000000 | tf_op jit(solution)/shard_map/merged/pallas_call | solution.py:255
  37.0 2.9 %copy-done = f32[448,4096]{1,0:T(8,128)} copy-done((f32[448,4096]{1,0:T(8,128)}, f32[448,4096]{1,0:T(8,128)S(1)}, u32[]{:S(2)}) %copy-start) | copy-done | bytes 7340056
  39.9 0.1 collective-permute-done.16
  40.1 3.0 %collective-permute-start.19 = (f32[72,512]{1,0:T(8,128)S(1)}, f32[72,512]{1,0:T(8,128)S(1)}, u32[]{:S(2)}, u32[]{:S(2)}) collective-permute-start(f32[72,512]{1,0:T(8,128)S(1)} %add.3), channel_id=1, source_target_pairs={{0,8},{1,13},{2,10},{3,15},{4,12},{5,9},{6,14},{7,11},{8,0},{9,5},... | collective-permute-start | bytes 442376 | tf_op jit(solution)/shard_map/ppermute | solution.py:498
  43.0 1.4 %collective-permute-start.18 = (f32[72,512]{1,0:T(8,128)S(1)}, f32[72,512]{1,0:T(8,128)S(1)}, u32[]{:S(2)}, u32[]{:S(2)}) collective-permute-start(f32[72,512]{1,0:T(8,128)S(1)} %get-tuple-element.57), channel_id=1, source_target_pairs={{0,2},{1,7},{2,0},{3,5},{4,6},{5,3},{6,4},{7,1},{8,10},{9,15},{10,... | collective-permute-start | bytes 442376 | tf_op jit(solution)/shard_map/ppermute | solution.py:498
  44.5 0.7 collective-permute-start.17
  45.2 4.8 %collective-permute-done.19.refs_1_ = f32[72,512]{1,0:T(8,128)S(1)} collective-permute-done((f32[72,512]{1,0:T(8,128)S(1)}, f32[72,512]{1,0:T(8,128)S(1)}, u32[]{:S(2)}, u32[]{:S(2)}) %collective-permute-start.19) | collective-permute-done | bytes 147488 | tf_op jit(solution)/shard_map/ppermute | solution.py:498
  50.0 1.3 %collective-permute-start.20 = (f32[72,512]{1,0:T(8,128)S(1)}, f32[72,512]{1,0:T(8,128)S(1)}, u32[]{:S(2)}, u32[]{:S(2)}) collective-permute-start(f32[72,512]{1,0:T(8,128)S(1)} %core_sum.1.here), channel_id=1, source_target_pairs={{0,1},{1,0},{2,3},{3,2},{4,5},{5,4},{6,7},{7,6},{8,9},{9,8},{10,11... | collective-permute-start | bytes 442376 | tf_op jit(solution)/shard_map/ppermute | solution.py:480
  51.2 1.0 %collective-permute-done.20.other = f32[72,512]{1,0:T(8,128)S(1)} collective-permute-done((f32[72,512]{1,0:T(8,128)S(1)}, f32[72,512]{1,0:T(8,128)S(1)}, u32[]{:S(2)}, u32[]{:S(2)}) %collective-permute-start.20) | collective-permute-done | bytes 147488 | tf_op jit(solution)/shard_map/ppermute | solution.py:480
  52.3 0.4 collective-permute-start.23
  52.7 1.0 %collective-permute-start.22 = (f32[64,512]{1,0:T(8,128)S(1)}, f32[64,512]{1,0:T(8,128)S(1)}, u32[]{:S(2)}, u32[]{:S(2)}) collective-permute-start(f32[64,512]{1,0:T(8,128)S(1)} %get-tuple-element.59), channel_id=1, source_target_pairs={{0,2},{1,7},{2,0},{3,5},{4,6},{5,3},{6,4},{7,1},{8,10},{9,15},{10,... | collective-permute-start | bytes 393224 | tf_op jit(solution)/shard_map/ppermute | solution.py:498
  53.7 0.7 collective-permute-start.21
  54.4 5.6 %cholesky_inverse.1.inverse = f32[64,64]{1,0:T(8,128)S(1)} custom-call(f32[64,64]{1,0:T(8,128)S(1)} %get-tuple-element.60.gram), custom_call_target="tpu_custom_call" | custom-call | flops 5750000128 | tf_op jit(solution)/shard_map/cholesky_inverse/pallas_call | solution.py:356
  60.0 1.7 %collective-permute-done.23 = f32[64,512]{1,0:T(8,128)S(1)} collective-permute-done((f32[64,512]{1,0:T(8,128)S(1)}, f32[64,512]{1,0:T(8,128)S(1)}, u32[]{:S(2)}, u32[]{:S(2)}) %collective-permute-start.23) | collective-permute-done | bytes 131104 | tf_op jit(solution)/shard_map/ppermute | solution.py:498
  61.7 1.3 %collective-permute-start.24 = (f32[64,512]{1,0:T(8,128)S(1)}, f32[64,512]{1,0:T(8,128)S(1)}, u32[]{:S(2)}, u32[]{:S(2)}) collective-permute-start(f32[64,512]{1,0:T(8,128)S(1)} %collective-permute-done.23), channel_id=1, source_target_pairs={{0,2},{1,3},{2,0},{3,1},{4,6},{5,7},{6,4},{7,5},{8,10},{9,11},{10,... | collective-permute-start | bytes 393224 | tf_op jit(solution)/shard_map/ppermute | solution.py:498
  63.0 0.8 %last_operand.1.lhs = bf16[512,256]{1,0:T(8,128)(2,1)S(1)} custom-call(f32[64,64]{1,0:T(8,128)S(1)} %cholesky_inverse.1.inverse, f32[64,448]{1,0:T(8,128)S(1)} %get-tuple-element.47.left_sum), custom_call_target="tpu_custom_call" | custom-call | flops 1724999936 | tf_op jit(solution)/shard_map/last_operand/pallas_call | solution.py:387
  63.7 2.9 %collective-permute-done.24 = f32[64,512]{1,0:T(8,128)S(1)} collective-permute-done((f32[64,512]{1,0:T(8,128)S(1)}, f32[64,512]{1,0:T(8,128)S(1)}, u32[]{:S(2)}, u32[]{:S(2)}) %collective-permute-start.24) | collective-permute-done | bytes 131104 | tf_op jit(solution)/shard_map/ppermute | solution.py:498
  66.7 1.3 %collective-permute-start.25 = (f32[4,64,512]{2,1,0:T(8,128)S(1)}, f32[4,64,512]{2,1,0:T(8,128)S(1)}, u32[]{:S(2)}, u32[]{:S(2)}) collective-permute-start(f32[4,64,512]{2,1,0:T(8,128)S(1)} %pad_maximum_fusion.mine), channel_id=1, source_target_pairs={{0,1},{1,0},{2,3},{3,2},{4,5},{5,4},{6,7},{7,6},{8,9},{9,8},{10,11... | collective-permute-start | bytes 1572872 | tf_op jit(solution)/shard_map/ppermute | solution.py:480
  68.0 1.5 %collective-permute-done.25.theirs = f32[4,64,512]{2,1,0:T(8,128)S(1)} collective-permute-done((f32[4,64,512]{2,1,0:T(8,128)S(1)}, f32[4,64,512]{2,1,0:T(8,128)S(1)}, u32[]{:S(2)}, u32[]{:S(2)}) %collective-permute-start.25) | collective-permute-done | bytes 524320 | tf_op jit(solution)/shard_map/ppermute | solution.py:480
  69.5 2.7 %finish.1 = (bf16[448,4096]{1,0:T(8,128)(2,1)}, f32[64,4096]{1,0:T(8,128)}) custom-call(f32[4,64,512]{2,1,0:T(8,128)S(1)} %pad_maximum_fusion.mine, f32[4,64,512]{2,1,0:T(8,128)S(1)} %collective-permute-done.25.theirs, bf16[512,256]{1,0:T(8,128)(2,1)S(1)} %last_operand.1.lhs, f32[448,4096]{1,0:T(8,128)S(1)} %bitcast.12), custom_call_target="tpu_custom_call" | custom-call | flops 3449999872 | tf_op jit(solution)/shard_map/finish/pallas_call | solution.py:426
  (37 shorter events, 0.6 us)
Async XLA Ops:
  0.6 1.0 %copy-start.5 = (bf16[1,32,4096]{2,1,0:T(8,128)(2,1)S(1)}, bf16[1,32,4096]{2,1,0:T(8,128)(2,1)}, u32[]{:S(2)}) copy-start(bf16[1,32,4096]{2,1,0:T(8,128)(2,1)} %param.5) | copy-start | bytes 786436
  1.6 5.2 %copy-start.1 = (bf16[1,448,4096]{2,1,0:T(8,128)(2,1)S(1)}, bf16[1,448,4096]{2,1,0:T(8,128)(2,1)}, u32[]{:S(2)}) copy-start(bf16[1,448,4096]{2,1,0:T(8,128)(2,1)} %param.7) | copy-start | bytes 11010052
  1.6 5.2 %copy-start.4 = (f32[64,4096]{1,0:T(8,128)S(1)}, f32[64,4096]{1,0:T(8,128)}, u32[]{:S(2)}) copy-start(f32[64,4096]{1,0:T(8,128)} %right.1) | copy-start | bytes 3145732
  1.6 7.0 %collective-permute-start.8 = (bf16[16,4096]{1,0:T(8,128)(2,1)S(1)}, bf16[16,4096]{1,0:T(8,128)(2,1)S(1)}, u32[]{:S(2)}, u32[]{:S(2)}) collective-permute-start(bf16[16,4096]{1,0:T(8,128)(2,1)S(1)} %get-tuple-element.35.refs_0_), channel_id=1, source_target_pairs={{2,0},{6,2},{10,6},{14,10},{12,14},{8,12},{4,8},{0,4},{3,1},{7,3},... | collective-permute-start | bytes 393224 | tf_op jit(solution)/shard_map/ppermute | solution.py:467
  4.7 6.4 %collective-permute-start = (bf16[16,4096]{1,0:T(8,128)(2,1)S(1)}, bf16[16,4096]{1,0:T(8,128)(2,1)S(1)}, u32[]{:S(2)}, u32[]{:S(2)}) collective-permute-start(bf16[16,4096]{1,0:T(8,128)(2,1)S(1)} %get-tuple-element.35.refs_0_), channel_id=1, source_target_pairs={{0,2},{2,6},{6,10},{10,14},{14,12},{12,8},{8,4},{4,0},{1,3},{3,7},... | collective-permute-start | bytes 393224 | tf_op jit(solution)/shard_map/ppermute | solution.py:467
  4.7 9.2 %collective-permute-start.9 = (bf16[16,4096]{1,0:T(8,128)(2,1)S(1)}, bf16[16,4096]{1,0:T(8,128)(2,1)S(1)}, u32[]{:S(2)}, u32[]{:S(2)}) collective-permute-start(bf16[16,4096]{1,0:T(8,128)(2,1)S(1)} %get-tuple-element.36.refs_1_), channel_id=1, source_target_pairs={{0,2},{2,6},{6,10},{10,14},{14,12},{12,8},{8,4},{4,0},{1,3},{3,7},... | collective-permute-start | bytes 393224 | tf_op jit(solution)/shard_map/ppermute | solution.py:467
  6.7 5.0 %collective-permute-start.4 = (bf16[16,4096]{1,0:T(8,128)(2,1)S(1)}, bf16[16,4096]{1,0:T(8,128)(2,1)S(1)}, u32[]{:S(2)}, u32[]{:S(2)}) collective-permute-start(bf16[16,4096]{1,0:T(8,128)(2,1)S(1)} %get-tuple-element.36.refs_1_), channel_id=1, source_target_pairs={{2,0},{6,2},{10,6},{14,10},{12,14},{8,12},{4,8},{0,4},{3,1},{7,3},... | collective-permute-start | bytes 393224 | tf_op jit(solution)/shard_map/ppermute | solution.py:467
  6.7 18.5 %copy-start.2 = (bf16[1,256,448]{1,2,0:T(8,128)(2,1)S(1)}, bf16[1,256,448]{1,2,0:T(8,128)(2,1)}, u32[]{:S(2)}) copy-start(bf16[1,256,448]{1,2,0:T(8,128)(2,1)} %param.6) | copy-start | bytes 688132
  6.8 18.5 %copy-start.3 = (s32[8,16]{1,0:T(8,128)S(1)}, s32[8,16]{1,0:T(8,128)}, u32[]{:S(2)}) copy-start(s32[8,16]{1,0:T(8,128)} %constant.8.clone.places) | copy-start | bytes 1540
  11.1 6.0 %collective-permute-start.1 = (bf16[16,4096]{1,0:T(8,128)(2,1)S(1)}, bf16[16,4096]{1,0:T(8,128)(2,1)S(1)}, u32[]{:S(2)}, u32[]{:S(2)}) collective-permute-start(bf16[16,4096]{1,0:T(8,128)(2,1)S(1)} %collective-permute-done.refs_2_), channel_id=1, source_target_pairs={{0,2},{2,6},{6,10},{10,14},{14,12},{12,8},{8,4},{4,0},{1,3},{3,7},... | collective-permute-start | bytes 393224 | tf_op jit(solution)/shard_map/ppermute | solution.py:467
  11.6 5.8 %collective-permute-start.5 = (bf16[16,4096]{1,0:T(8,128)(2,1)S(1)}, bf16[16,4096]{1,0:T(8,128)(2,1)S(1)}, u32[]{:S(2)}, u32[]{:S(2)}) collective-permute-start(bf16[16,4096]{1,0:T(8,128)(2,1)S(1)} %collective-permute-done.4.refs_5_), channel_id=1, source_target_pairs={{2,0},{6,2},{10,6},{14,10},{12,14},{8,12},{4,8},{0,4},{3,1},{7,3},... | collective-permute-start | bytes 393224 | tf_op jit(solution)/shard_map/ppermute | solution.py:467
  13.9 6.4 %collective-permute-start.10 = (bf16[16,4096]{1,0:T(8,128)(2,1)S(1)}, bf16[16,4096]{1,0:T(8,128)(2,1)S(1)}, u32[]{:S(2)}, u32[]{:S(2)}) collective-permute-start(bf16[16,4096]{1,0:T(8,128)(2,1)S(1)} %collective-permute-done.9.refs_3_), channel_id=1, source_target_pairs={{0,2},{2,6},{6,10},{10,14},{14,12},{12,8},{8,4},{4,0},{1,3},{3,7},... | collective-permute-start | bytes 393224 | tf_op jit(solution)/shard_map/ppermute | solution.py:467
  13.9 6.4 %collective-permute-start.11 = (bf16[16,4096]{1,0:T(8,128)(2,1)S(1)}, bf16[16,4096]{1,0:T(8,128)(2,1)S(1)}, u32[]{:S(2)}, u32[]{:S(2)}) collective-permute-start(bf16[16,4096]{1,0:T(8,128)(2,1)S(1)} %collective-permute-done.8.refs_4_), channel_id=1, source_target_pairs={{2,0},{6,2},{10,6},{14,10},{12,14},{8,12},{4,8},{0,4},{3,1},{7,3},... | collective-permute-start | bytes 393224 | tf_op jit(solution)/shard_map/ppermute | solution.py:467
  17.1 6.0 %collective-permute-start.2 = (bf16[16,4096]{1,0:T(8,128)(2,1)S(1)}, bf16[16,4096]{1,0:T(8,128)(2,1)S(1)}, u32[]{:S(2)}, u32[]{:S(2)}) collective-permute-start(bf16[16,4096]{1,0:T(8,128)(2,1)S(1)} %collective-permute-done.1.refs_6_), channel_id=1, source_target_pairs={{0,2},{2,6},{6,10},{10,14},{14,12},{12,8},{8,4},{4,0},{1,3},{3,7},... | collective-permute-start | bytes 393224 | tf_op jit(solution)/shard_map/ppermute | solution.py:467
  17.4 5.8 %collective-permute-start.6 = (bf16[16,4096]{1,0:T(8,128)(2,1)S(1)}, bf16[16,4096]{1,0:T(8,128)(2,1)S(1)}, u32[]{:S(2)}, u32[]{:S(2)}) collective-permute-start(bf16[16,4096]{1,0:T(8,128)(2,1)S(1)} %collective-permute-done.5.refs_9_), channel_id=1, source_target_pairs={{2,0},{6,2},{10,6},{14,10},{12,14},{8,12},{4,8},{0,4},{3,1},{7,3},... | collective-permute-start | bytes 393224 | tf_op jit(solution)/shard_map/ppermute | solution.py:467
  20.2 5.0 %collective-permute-start.12 = (bf16[16,4096]{1,0:T(8,128)(2,1)S(1)}, bf16[16,4096]{1,0:T(8,128)(2,1)S(1)}, u32[]{:S(2)}, u32[]{:S(2)}) collective-permute-start(bf16[16,4096]{1,0:T(8,128)(2,1)S(1)} %collective-permute-done.10.refs_7_), channel_id=1, source_target_pairs={{0,2},{2,6},{6,10},{10,14},{14,12},{12,8},{8,4},{4,0},{1,3},{3,7},... | collective-permute-start | bytes 393224 | tf_op jit(solution)/shard_map/ppermute | solution.py:467
  20.2 5.0 %collective-permute-start.13 = (bf16[16,4096]{1,0:T(8,128)(2,1)S(1)}, bf16[16,4096]{1,0:T(8,128)(2,1)S(1)}, u32[]{:S(2)}, u32[]{:S(2)}) collective-permute-start(bf16[16,4096]{1,0:T(8,128)(2,1)S(1)} %collective-permute-done.11.refs_8_), channel_id=1, source_target_pairs={{2,0},{6,2},{10,6},{14,10},{12,14},{8,12},{4,8},{0,4},{3,1},{7,3},... | collective-permute-start | bytes 393224 | tf_op jit(solution)/shard_map/ppermute | solution.py:467
  23.1 5.0 %collective-permute-start.3 = (bf16[16,4096]{1,0:T(8,128)(2,1)S(1)}, bf16[16,4096]{1,0:T(8,128)(2,1)S(1)}, u32[]{:S(2)}, u32[]{:S(2)}) collective-permute-start(bf16[16,4096]{1,0:T(8,128)(2,1)S(1)} %collective-permute-done.2.refs_10_), channel_id=1, source_target_pairs={{0,2},{2,6},{6,10},{10,14},{14,12},{12,8},{8,4},{4,0},{1,3},{3,7},... | collective-permute-start | bytes 393224 | tf_op jit(solution)/shard_map/ppermute | solution.py:467
  23.2 5.0 %collective-permute-start.7 = (bf16[16,4096]{1,0:T(8,128)(2,1)S(1)}, bf16[16,4096]{1,0:T(8,128)(2,1)S(1)}, u32[]{:S(2)}, u32[]{:S(2)}) collective-permute-start(bf16[16,4096]{1,0:T(8,128)(2,1)S(1)} %collective-permute-done.6.refs_13_), channel_id=1, source_target_pairs={{2,0},{6,2},{10,6},{14,10},{12,14},{8,12},{4,8},{0,4},{3,1},{7,3},... | collective-permute-start | bytes 393224 | tf_op jit(solution)/shard_map/ppermute | solution.py:467
  29.6 1.4 %collective-permute-start.14 = (f32[64,448]{1,0:T(8,128)S(1)}, f32[64,448]{1,0:T(8,128)S(1)}, u32[]{:S(2)}, u32[]{:S(2)}) collective-permute-start(f32[64,448]{1,0:T(8,128)S(1)} %get-tuple-element.45.here_l), channel_id=1, source_target_pairs={{0,1},{1,0},{2,3},{3,2},{4,5},{5,4},{6,7},{7,6},{8,9},{9,8},{10,11... | collective-permute-start | bytes 344072 | tf_op jit(solution)/shard_map/ppermute | solution.py:480
  32.0 2.0 %collective-permute-start.15 = (f32[4,64,512]{2,1,0:T(8,128)S(1)}, f32[4,64,512]{2,1,0:T(8,128)S(1)}, u32[]{:S(2)}, u32[]{:S(2)}) collective-permute-start(f32[4,64,512]{2,1,0:T(8,128)S(1)} %get-tuple-element.51), channel_id=1, source_target_pairs={{0,1},{1,0},{2,3},{3,2},{4,5},{5,4},{6,7},{7,6},{8,9},{9,8},{10,11... | collective-permute-start | bytes 1572872 | tf_op jit(solution)/shard_map/ppermute | solution.py:480
  34.0 6.0 %collective-permute-start.16 = (f32[72,512]{1,0:T(8,128)S(1)}, f32[72,512]{1,0:T(8,128)S(1)}, u32[]{:S(2)}, u32[]{:S(2)}) collective-permute-start(f32[72,512]{1,0:T(8,128)S(1)} %get-tuple-element.55), channel_id=1, source_target_pairs={{0,2},{1,3},{2,0},{3,1},{4,6},{5,7},{6,4},{7,5},{8,10},{9,11},{10,... | collective-permute-start | bytes 442376 | tf_op jit(solution)/shard_map/ppermute | solution.py:498
  37.0 2.9 %copy-start = (f32[448,4096]{1,0:T(8,128)}, f32[448,4096]{1,0:T(8,128)S(1)}, u32[]{:S(2)}) copy-start(f32[448,4096]{1,0:T(8,128)S(1)} %merged.1) | copy-start | bytes 22020100
  40.1 9.8 %collective-permute-start.19 = (f32[72,512]{1,0:T(8,128)S(1)}, f32[72,512]{1,0:T(8,128)S(1)}, u32[]{:S(2)}, u32[]{:S(2)}) collective-permute-start(f32[72,512]{1,0:T(8,128)S(1)} %add.3), channel_id=1, source_target_pairs={{0,8},{1,13},{2,10},{3,15},{4,12},{5,9},{6,14},{7,11},{8,0},{9,5},... | collective-permute-start | bytes 442376 | tf_op jit(solution)/shard_map/ppermute | solution.py:498
  43.0 6.9 %collective-permute-start.18 = (f32[72,512]{1,0:T(8,128)S(1)}, f32[72,512]{1,0:T(8,128)S(1)}, u32[]{:S(2)}, u32[]{:S(2)}) collective-permute-start(f32[72,512]{1,0:T(8,128)S(1)} %get-tuple-element.57), channel_id=1, source_target_pairs={{0,2},{1,7},{2,0},{3,5},{4,6},{5,3},{6,4},{7,1},{8,10},{9,15},{10,... | collective-permute-start | bytes 442376 | tf_op jit(solution)/shard_map/ppermute | solution.py:498
  44.5 5.4 %collective-permute-start.17 = (f32[72,512]{1,0:T(8,128)S(1)}, f32[72,512]{1,0:T(8,128)S(1)}, u32[]{:S(2)}, u32[]{:S(2)}) collective-permute-start(f32[72,512]{1,0:T(8,128)S(1)} %get-tuple-element.56.own), channel_id=1, source_target_pairs={{1,5},{3,7},{5,1},{7,3},{9,13},{11,15},{13,9},{15,11},{17,21},{19,... | collective-permute-start | bytes 442376 | tf_op jit(solution)/shard_map/ppermute | solution.py:498
  50.0 2.3 %collective-permute-start.20 = (f32[72,512]{1,0:T(8,128)S(1)}, f32[72,512]{1,0:T(8,128)S(1)}, u32[]{:S(2)}, u32[]{:S(2)}) collective-permute-start(f32[72,512]{1,0:T(8,128)S(1)} %core_sum.1.here), channel_id=1, source_target_pairs={{0,1},{1,0},{2,3},{3,2},{4,5},{5,4},{6,7},{7,6},{8,9},{9,8},{10,11... | collective-permute-start | bytes 442376 | tf_op jit(solution)/shard_map/ppermute | solution.py:480
  52.2 17.3 %slice-start = ((s8[7340032]{0:T(1024)(128)(4,1)}), s8[4194304]{0:T(1024)(128)(4,1)S(1)}, s32[]{:S(2)}) async-start(s8[7340032]{0:T(1024)(128)(4,1)} %bitcast.11), calls=%async_computation | async-start | bytes 8388608
  52.3 9.4 %collective-permute-start.23 = (f32[64,512]{1,0:T(8,128)S(1)}, f32[64,512]{1,0:T(8,128)S(1)}, u32[]{:S(2)}, u32[]{:S(2)}) collective-permute-start(f32[64,512]{1,0:T(8,128)S(1)} %get-tuple-element.59), channel_id=1, source_target_pairs={{0,8},{1,13},{2,10},{3,15},{4,12},{5,9},{6,14},{7,11},{8,0},{9,5},... | collective-permute-start | bytes 393224 | tf_op jit(solution)/shard_map/ppermute | solution.py:498
  52.7 11.0 %collective-permute-start.22 = (f32[64,512]{1,0:T(8,128)S(1)}, f32[64,512]{1,0:T(8,128)S(1)}, u32[]{:S(2)}, u32[]{:S(2)}) collective-permute-start(f32[64,512]{1,0:T(8,128)S(1)} %get-tuple-element.59), channel_id=1, source_target_pairs={{0,2},{1,7},{2,0},{3,5},{4,6},{5,3},{6,4},{7,1},{8,10},{9,15},{10,... | collective-permute-start | bytes 393224 | tf_op jit(solution)/shard_map/ppermute | solution.py:498
  53.7 9.2 %collective-permute-start.21 = (f32[64,512]{1,0:T(8,128)S(1)}, f32[64,512]{1,0:T(8,128)S(1)}, u32[]{:S(2)}, u32[]{:S(2)}) collective-permute-start(f32[64,512]{1,0:T(8,128)S(1)} %get-tuple-element.59), channel_id=1, source_target_pairs={{1,5},{3,7},{5,1},{7,3},{9,13},{11,15},{13,9},{15,11},{17,21},{19,... | collective-permute-start | bytes 393224 | tf_op jit(solution)/shard_map/ppermute | solution.py:498
  54.4 15.1 %slice-start.1 = ((s8[7340032]{0:T(1024)(128)(4,1)}), s8[3145728]{0:T(1024)(128)(4,1)S(1)}, s32[]{:S(2)}) async-start(s8[7340032]{0:T(1024)(128)(4,1)} %bitcast.11), calls=%async_computation.1 | async-start | bytes 6291456
  61.7 5.0 %collective-permute-start.24 = (f32[64,512]{1,0:T(8,128)S(1)}, f32[64,512]{1,0:T(8,128)S(1)}, u32[]{:S(2)}, u32[]{:S(2)}) collective-permute-start(f32[64,512]{1,0:T(8,128)S(1)} %collective-permute-done.23), channel_id=1, source_target_pairs={{0,2},{1,3},{2,0},{3,1},{4,6},{5,7},{6,4},{7,5},{8,10},{9,11},{10,... | collective-permute-start | bytes 393224 | tf_op jit(solution)/shard_map/ppermute | solution.py:498
  66.7 2.8 %collective-permute-start.25 = (f32[4,64,512]{2,1,0:T(8,128)S(1)}, f32[4,64,512]{2,1,0:T(8,128)S(1)}, u32[]{:S(2)}, u32[]{:S(2)}) collective-permute-start(f32[4,64,512]{2,1,0:T(8,128)S(1)} %pad_maximum_fusion.mine), channel_id=1, source_target_pairs={{0,1},{1,0},{2,3},{3,2},{4,5},{5,4},{6,7},{7,6},{8,9},{9,8},{10,11... | collective-permute-start | bytes 1572872 | tf_op jit(solution)/shard_map/ppermute | solution.py:480

commit v4 on v3

--- a/solution.py
+++ b/solution.py
@@ -11,8 +11,10 @@
 F32 = jnp.float32
 BF16 = jnp.bfloat16
 HIGHEST = lax.Precision.HIGHEST
-VMEM_LIMIT = 32 * 1024 * 1024
+VMEM_LIMIT = 24 * 1024 * 1024
 STEPS = 4
+SMALL = 0.05
+PIVOTS = 8
 
 
 def split3(value):
@@ -186,7 +188,12 @@
     return pl.ds(pl.multiple_of(shard * cols, cols), cols)
 
 
-def give_kernel(here_l, other_l, hidden_t, feedback, tokens, give, left_sum, lhs, rhs):
+def block_sum(lhs, rhs, feedback, tokens, core, index, cols):
+    span = columns_of(place_of(core, index), cols)
+    return fold3(nn(lhs[...], feedback[:, span]) + nn(rhs[...], tokens[:, span]))
+
+
+def give_far_kernel(here_l, other_l, hidden_t, feedback, tokens, give, left_sum, lhs, rhs):
     left_t = here_l[...] + other_l[...]
     left_sum[...] = left_t
     lhs[...] = jnp.concatenate(split3(left_t), axis=0)
@@ -194,54 +201,72 @@
     rhs[...] = jnp.concatenate(split3(seen_t), axis=0)
     other = 1 - lax.axis_index("dp")
     for index in range(give.shape[0]):
-        span = columns_of(place_of(other, index), give.shape[2])
-        give[index] = fold3(nn(lhs[...], feedback[:, span]) + nn(rhs[...], tokens[:, span]))
-
-
-def given_terms(here_l, other_l, hidden_t, feedback, tokens, chips):
+        give[index] = block_sum(lhs, rhs, feedback, tokens, other, index + 2, give.shape[2])
+
+
+def given_far(here_l, other_l, hidden_t, feedback, tokens, chips):
     rank, rows = here_l.shape
     count, width = tokens.shape
     return pl.pallas_call(
-        give_kernel,
+        give_far_kernel,
         in_specs=[pl.BlockSpec(memory_space=pltpu.VMEM)] * 5,
         out_specs=[pl.BlockSpec(memory_space=pltpu.VMEM)] * 4,
         out_shape=[
-            jax.ShapeDtypeStruct((chips // 2, rank, width // chips), F32),
+            jax.ShapeDtypeStruct((chips // 2 - 2, rank, width // chips), F32),
             jax.ShapeDtypeStruct((rank, rows), F32),
             jax.ShapeDtypeStruct((3 * rank, rows), BF16),
             jax.ShapeDtypeStruct((3 * rank, count), BF16),
         ],
         compiler_params=params(),
-        cost_estimate=cost(1.8),
-        name="given_terms",
+        cost_estimate=cost(SMALL),
+        name="given_far",
     )(here_l, other_l, hidden_t, feedback, tokens)
 
 
-def keep_kernel(left_sum, lhs, rhs, feedback, tokens, keep, gram):
+def keep_far_kernel(left_sum, lhs, rhs, feedback, tokens, keep, gram):
     core = lax.axis_index("dp")
     for index in range(keep.shape[0]):
-        span = columns_of(place_of(core, index), keep.shape[2])
-        keep[index] = fold3(nn(lhs[...], feedback[:, span]) + nn(rhs[...], tokens[:, span]))
+        keep[index] = block_sum(lhs, rhs, feedback, tokens, core, index + 2, keep.shape[2])
     left_t = left_sum[...]
     gram[...] = lax.dot_general(
         left_t, left_t, (((1,), (1,)), ((), ())), precision=HIGHEST, preferred_element_type=F32
     )
 
 
-def kept_terms(left_sum, lhs, rhs, feedback, tokens, chips):
+def kept_far(left_sum, lhs, rhs, feedback, tokens, chips):
     rank = left_sum.shape[0]
     return pl.pallas_call(
-        keep_kernel,
+        keep_far_kernel,
         in_specs=[pl.BlockSpec(memory_space=pltpu.VMEM)] * 5,
         out_specs=[pl.BlockSpec(memory_space=pltpu.VMEM)] * 2,
         out_shape=[
-            jax.ShapeDtypeStruct((chips // 2, rank, tokens.shape[1] // chips), F32),
+            jax.ShapeDtypeStruct((chips // 2 - 2, rank, tokens.shape[1] // chips), F32),
             jax.ShapeDtypeStruct((rank, rank), F32),
         ],
         compiler_params=params(),
-        cost_estimate=cost(1.8),
-        name="kept_terms",
+        cost_estimate=cost(SMALL),
+        name="kept_far",
     )(left_sum, lhs, rhs, feedback, tokens)
+
+
+def near_kernel(lhs, rhs, feedback, tokens, give, keep):
+    core = lax.axis_index("dp")
+    for target, owner in ((give, 1 - core), (keep, core)):
+        for index in range(2):
+            target[index] = block_sum(lhs, rhs, feedback, tokens, owner, index, target.shape[2])
+
+
+def near_terms(lhs, rhs, feedback, tokens, chips):
+    block = jax.ShapeDtypeStruct((2, lhs.shape[0] // 3, tokens.shape[1] // chips), F32)
+    return pl.pallas_call(
+        near_kernel,
+        in_specs=[pl.BlockSpec(memory_space=pltpu.VMEM)] * 4,
+        out_specs=[pl.BlockSpec(memory_space=pltpu.VMEM)] * 2,
+        out_shape=[block, block],
+        compiler_params=params(),
+        cost_estimate=cost(SMALL),
+        name="near_terms",
+    )(lhs, rhs, feedback, tokens)
 
 
 def merged_kernel(hidden_t, feedback, tokens, merged):
@@ -258,7 +283,7 @@
         out_specs=pl.BlockSpec(memory_space=pltpu.VMEM),
         out_shape=jax.ShapeDtypeStruct(feedback.shape, F32),
         compiler_params=params(),
-        cost_estimate=cost(2.0),
+        cost_estimate=cost(SMALL),
         name="merged",
     )(hidden_t, feedback, tokens)
 
@@ -282,9 +307,46 @@
         out_specs=[pl.BlockSpec(memory_space=pltpu.VMEM)] * places,
         out_shape=[jax.ShapeDtypeStruct((rows, cols), F32)] * places,
         compiler_params=params(),
-        cost_estimate=cost(0.3),
+        cost_estimate=cost(SMALL),
         name="messages",
     )(keep, got, gram)
+
+
+def add_kernel(a, b, total):
+    total[...] = a[...] + b[...]
+
+
+def added(a, b):
+    return pl.pallas_call(
+        add_kernel,
+        in_specs=[pl.BlockSpec(memory_space=pltpu.VMEM)] * 2,
+        out_specs=pl.BlockSpec(memory_space=pltpu.VMEM),
+        out_shape=jax.ShapeDtypeStruct(a.shape, a.dtype),
+        compiler_params=params(),
+        cost_estimate=cost(SMALL),
+        name="added",
+    )(a, b)
+
+
+def join_kernel(share, second, first, *refs):
+    across, mine = refs[:-1], refs[-1]
+    mine[0] = jnp.where(lax.axis_index("dp") == 0, share[...], second[...])
+    mine[1] = first[...]
+    for index, value in enumerate(across):
+        mine[index + 2] = value[...]
+
+
+def joined(share, second, first, across):
+    operands = [share, second, first, *across]
+    return pl.pallas_call(
+        join_kernel,
+        in_specs=[pl.BlockSpec(memory_space=pltpu.VMEM)] * len(operands),
+        out_specs=pl.BlockSpec(memory_space=pltpu.VMEM),
+        out_shape=jax.ShapeDtypeStruct((len(operands) - 1, *share.shape), F32),
+        compiler_params=params(),
+        cost_estimate=cost(SMALL),
+        name="joined",
+    )(*operands)
 
 
 def core_sum_kernel(own, second, *refs):
@@ -304,7 +366,7 @@
         out_specs=pl.BlockSpec(memory_space=pltpu.VMEM),
         out_shape=jax.ShapeDtypeStruct(own.shape, F32),
         compiler_params=params(),
-        cost_estimate=cost(0.3),
+        cost_estimate=cost(SMALL),
         name="core_sum",
     )(*operands)
 
@@ -329,7 +391,7 @@
             jax.ShapeDtypeStruct((rank, rank), F32),
         ],
         compiler_params=params(),
-        cost_estimate=cost(0.3),
+        cost_estimate=cost(SMALL),
         name="chip_sum",
     )(here, other)
 
@@ -340,16 +402,26 @@
     lane = lax.broadcasted_iota(jnp.int32, (rank, 2 * rank), 1)
     eye = (lane[:, rank:] == row[:, rank:] + rank).astype(F32)
     table = jnp.concatenate([gram[...], eye], axis=1)
-    scale = jnp.zeros((rank, 1), F32)
-    for pivot in range(rank):
-        line = table[pivot : pivot + 1, :]
-        column = table[:, pivot : pivot + 1]
-        top = line[:, pivot : pivot + 1]
-        scale = jnp.where(row[:, :1] == pivot, lax.rsqrt(top), scale)
-        if pivot + 1 < rank:
-            factor = jnp.where(row[:, :1] > pivot, column / top, 0.0)
-            table = table - factor * line
-    inverse[...] = table[:, rank:] * scale
+    done = []
+    for start in range(0, rank, PIVOTS):
+        below = row[start:]
+        each = range(PIVOTS)
+        lines = [table[k : k + 1, :] for k in each]
+        columns = [jnp.broadcast_to(table[:, start + k : start + k + 1], table.shape) for k in each]
+        change = None
+        for k in each:
+            top = columns[k][k : k + 1, :]
+            reciprocal = 1.0 / top
+            factor = jnp.where(below > start + k, columns[k] * reciprocal, 0.0)
+            for m in range(k + 1, PIVOTS):
+                entry = columns[m][k : k + 1, :]
+                lines[m] = lines[m] - (entry * reciprocal) * lines[k]
+                columns[m] = columns[m] - factor * entry
+            done.append(lines[k] * lax.rsqrt(top))
+            part = factor * lines[k]
+            change = part if change is None else change + part
+        table = (table - change)[PIVOTS:]
+    inverse[...] = jnp.concatenate(done, axis=0)[:, rank:]
 
 
 def cholesky_inverse(gram):
@@ -359,7 +431,7 @@
         out_specs=pl.BlockSpec(memory_space=pltpu.VMEM),
         out_shape=jax.ShapeDtypeStruct(gram.shape, F32),
         compiler_params=params(),
-        cost_estimate=cost(5.0),
+        cost_estimate=cost(SMALL),
         name="cholesky_inverse",
     )(gram)
 
@@ -390,57 +462,57 @@
         out_specs=pl.BlockSpec(memory_space=pltpu.VMEM),
         out_shape=jax.ShapeDtypeStruct((rows + rank, 4 * rank), BF16),
         compiler_params=params(),
-        cost_estimate=cost(1.5),
+        cost_estimate=cost(SMALL),
         name="last_operand",
     )(inverse, left_sum)
 
 
-def final_kernel(mine, theirs, lhs, merged, out, factor, rhs, out_here, factor_here, sems):
-    chip, core = lax.axis_index("tp"), lax.axis_index("dp")
+def final_kernel(side, shares, lhs, merged, *refs):
+    out, factor, rhs, out_here, factor_here, sems = refs[-6:]
+    owner = lax.axis_index("dp") ^ side
     rows = merged.shape[0]
-    rank, cols = mine.shape[1:]
-    group = 2 * mine.shape[0] // STEPS
+    count, rank, cols = shares.shape
     copies = []
-    for step in range(STEPS):
-        for part in range(group):
-            place = (group * step + part) ^ chip
-            index = index_of(place)
-            high, low = split2(jnp.where(core_of(place) == core, mine[index], theirs[index]))
-            span = slice(part * cols, (part + 1) * cols)
-            for order, term in enumerate((high, low, high, low)):
-                rhs[step % 2, order * rank : (order + 1) * rank, span] = term
-        span = slice(step * group * cols, (step + 1) * group * cols)
-        product = nn(lhs[...], rhs[step % 2])
-        factor_here[:, span] = product[rows:]
-        out_here[:, span] = (merged[:, span] + product[:rows]).astype(BF16)
-        for index, (source, target) in enumerate(((out_here, out), (factor_here, factor))):
-            copies.append(pltpu.make_async_copy(source.at[:, span], target.at[:, span], sems.at[step, index]))
+    for index in range(count):
+        span = columns_of(place_of(owner, index), cols)
+        high, low = split2(shares[index])
+        for place, term in enumerate((high, low, high, low)):
+            rhs[index % 2, place * rank : (place + 1) * rank, :] = term
+        product = nn(lhs[...], rhs[index % 2])
+        factor_here[index] = product[rows:]
+        out_here[index] = (merged[:, span] + product[:rows]).astype(BF16)
+        for order, (source, target) in enumerate(((out_here, out), (factor_here, factor))):
+            copies.append(
+                pltpu.make_async_copy(source.at[index], target.at[:, span], sems.at[index, order])
+            )
             copies[-1].start()
     for copy in copies:
         copy.wait()
 
 
-def finish(mine, theirs, lhs, merged):
-    rank = mine.shape[1]
+def finish(side, shares, lhs, merged, begun=()):
+    count, rank, cols = shares.shape
     rows, width = merged.shape
     return pl.pallas_call(
-        final_kernel,
-        in_specs=[pl.BlockSpec(memory_space=pltpu.VMEM)] * 4,
+        functools.partial(final_kernel, side),
+        in_specs=[pl.BlockSpec(memory_space=pltpu.VMEM)] * 3
+        + [pl.BlockSpec(memory_space=pl.ANY)] * len(begun),
         out_specs=[pl.BlockSpec(memory_space=pl.ANY)] * 2,
         out_shape=[
             jax.ShapeDtypeStruct((rows, width), BF16),
             jax.ShapeDtypeStruct((rank, width), F32),
         ],
+        input_output_aliases={3 + index: index for index in range(len(begun))},
         scratch_shapes=[
-            pltpu.VMEM((2, lhs.shape[1], width // STEPS), BF16),
-            pltpu.VMEM((rows, width), BF16),
-            pltpu.VMEM((rank, width), F32),
-            pltpu.SemaphoreType.DMA((STEPS, 2)),
-        ],
-        compiler_params=params(),
-        cost_estimate=cost(3.0),
+            pltpu.VMEM((2, lhs.shape[1], cols), BF16),
+            pltpu.VMEM((count, rows, cols), BF16),
+            pltpu.VMEM((count, rank, cols), F32),
+            pltpu.SemaphoreType.DMA((count, 2)),
+        ],
+        compiler_params=params(),
+        cost_estimate=cost(1.5),
         name="finish",
-    )(mine, theirs, lhs, merged)
+    )(shares, lhs, merged, *begun)
 
 
 def ring_order(chips):
@@ -457,18 +529,16 @@
     halves = halves_of(shard)
     pieces = list(halves)
     origin = [(0, 0), (0, 1)]
-    going = {(way, half): halves[half] for way in (1, -1) for half in (0, 1)}
     far = chips // 2
+    *later, beside = lax.optimization_barrier((*halves, beside))
+    going = {(1, 0): halves[0], (-1, 1): halves[1], (1, 1): later[1], (-1, 0): later[0]}
     for hop in range(1, far + 1):
-        for way, pairs in ((1, right), (-1, left)):
-            for half in (0, 1):
-                if hop == far and (half == 0) != (way == 1):
-                    continue
-                going[way, half] = lax.ppermute(going[way, half], "tp", pairs)
-                if hop == 1 and (way, half) == (-1, 0):
-                    going[way, half], beside = lax.optimization_barrier((going[way, half], beside))
-                pieces.append(going[way, half])
-                origin.append((-way * hop, half))
+        for way, half in ((1, 0), (-1, 1), (1, 1), (-1, 0)):
+            if hop == far and (half == 0) != (way == 1):
+                continue
+            going[way, half] = lax.ppermute(going[way, half], "tp", right if way == 1 else left)
+            pieces.append(going[way, half])
+            origin.append((-way * hop, half))
     places = np.zeros((chips, len(pieces)), np.int32)
     for chip in range(chips):
         for index, (shift, half) in enumerate(origin):
@@ -501,30 +571,34 @@
     places = jnp.asarray(places)
     tokens, hidden_rows, left_t = early_left(places, pieces[:-2], terms, residue_t, hidden_t)
     tokens, left_t = late_left(places, pieces[-2:], terms, hidden_rows, left_t, tokens)
-    give, left_sum, lhs, rhs = given_terms(left_t, swap(left_t), hidden_t, residue, tokens, chips)
+    give, left_sum, lhs, rhs = given_far(left_t, swap(left_t), hidden_t, residue, tokens, chips)
     got = swap(give)
-    keep, gram = kept_terms(left_sum, lhs, rhs, residue, tokens, chips)
-
-    messages = messages_for(keep, got, gram)
+    keep, gram = kept_far(left_sum, lhs, rhs, residue, tokens, chips)
+    far = messages_for(keep, got, gram)
+    give, keep = near_terms(lhs, rhs, residue, tokens, chips)
+    messages = [*messages_for(keep, swap(give), gram), *far]
+
     passed = [exchange(messages[index + 1], index + 1, 1) for index in range(2, half, 2)]
-    across = [messages[2 * i + 2] + value for i, value in enumerate(passed)]
-    across = [exchange(value, 2 * i + 2) for i, value in enumerate(across)]
+    second = exchange(messages[0], 0)
+    across = [exchange(added(messages[2 * i + 2], value), 2 * i + 2) for i, value in enumerate(passed)]
+    tokens, _ = lax.optimization_barrier((tokens, messages[1]))
     merged = merged_sum(hidden_t, residue, tokens)
-    own, beside, passed, merged = lax.optimization_barrier((messages[0], messages[1], passed, merged))
-    beside = exchange(beside, 1), exchange(own, 0)
-    partial = core_sum(own, beside[1], beside[0], across)
+    beside, passed = lax.optimization_barrier((messages[1], passed))
+    first = exchange(beside, 1)
+    second, merged = lax.optimization_barrier((second, merged))
+    partial = core_sum(messages[0], second, first, across)
     share, gram_matrix = chip_sum(partial, swap(partial), rank)
 
     across = [exchange(share, index) for index in range(2, half, 2)]
-    beside = exchange(share, 1), exchange(share, 0)
-    inverse = cholesky_inverse(gram_matrix)
-    across[0], inverse = lax.optimization_barrier((across[0], inverse))
+    first, second = exchange(share, 1), exchange(share, 0)
     passed = [exchange(value, 2 * i + 3, 1) for i, value in enumerate(across)]
-    lhs = last_operand(inverse, left_sum, replicas)
-    first = jnp.where(lax.axis_index("dp") == 0, share, beside[1])
-    mine = jnp.stack([first, beside[0]] + [value for pair in zip(across, passed) for value in pair])
-    mine, lhs = lax.optimization_barrier((mine, lhs))
-    new_feedback, new_factor = finish(mine, swap(mine), lhs, merged)
+    gram_matrix, first, second, across[0] = lax.optimization_barrier((gram_matrix, first, second, across[0]))
+    lhs = last_operand(cholesky_inverse(gram_matrix), left_sum, replicas)
+    passed, lhs = lax.optimization_barrier((passed, lhs))
+    mine = joined(share, second, first, [value for pair in zip(across, passed) for value in pair])
+    theirs = swap(mine)
+    begun = finish(0, mine, lhs, merged)
+    new_feedback, new_factor = finish(1, theirs, lhs, merged, begun)
     return new_feedback[None], new_factor
 
 

time: 72.3 us -> 69.6 us (0.963)
  local copies, waits for them, and re-layouts: 3.86 us -> 0.96 us
  Pallas kernels: 16.7 us -> 14 us
  waiting for transfers between devices: 23 us -> 24.8 us
  starting transfers between devices: 27.8 us -> 28.8 us
    ppermute x8, waiting for transfers between devices: 9.52 us -> 14.2 us  [exchange(): return lax.ppermute(value, ('tp', 'dp'), pairs)]
    pallas_call x1, Pallas kernels: 5.61 us -> 1.77 us  [cholesky_inverse(): pl.pallas_call(inverse_kernel, in_specs=[pl.BlockSpec(memory_space=pltpu....]
    unnamed x16 -> x10, local copies, waits for them, and re-layouts: 3.86 us -> 0.96 us
    ppermute x4 -> x5, waiting for transfers between devices: 4.74 us -> 2.7 us  [swap(): return lax.ppermute(value, 'dp', [(0, 1), (1, 0)])]
    ppermute x14, starting transfers between devices: 14.8 us -> 16 us  [ring_gather(): lax.ppermute(going[way, half], 'tp', right if way == 1 else left)]
    pallas_call x3 -> x7, Pallas kernels: 4.52 us -> 5.59 us  [the longest x2 3.5 us: finish(): pl.pallas_call(functools.partial(final_kernel, side), in_specs=[pl.BlockS...]
    ppermute x4 -> x5, starting transfers between devices: 2.8 us -> 1.76 us  [swap(): return lax.ppermute(value, 'dp', [(0, 1), (1, 0)])]
    ppermute x8, starting transfers between devices: 10.2 us -> 11.1 us  [exchange(): return lax.ppermute(value, ('tp', 'dp'), pairs)]
  transfers between devices with their start and end apart: 26 -> 27, of which waited for: 18 -> 13; matrix products, arithmetic and copies ran while one was open for 0% -> 0% of each run, Pallas kernels for 16% -> 14%
where the time goes in v4:
time: 69.6 us; the launch traced here: 69.4 us
  starting transfers between devices  28.8 us (41%)
  waiting for transfers between devices  24.8 us (36%)
  Pallas kernels  14 us (20%)
  local copies, waits for them, and re-layouts  0.96 us (1%)
  between operations  0.81 us (1%)
    ppermute x14, starting transfers between devices, ring_gather(): lax.ppermute(going[way, half], 'tp', right if way == 1 else left)  16 us
    ppermute x8, waiting for transfers between devices, exchange(): return lax.ppermute(value, ('tp', 'dp'), pairs)  14.2 us
    ppermute x8, starting transfers between devices, exchange(): return lax.ppermute(value, ('tp', 'dp'), pairs)  11.1 us
    ppermute x14, waiting for transfers between devices, ring_gather(): lax.ppermute(going[way, half], 'tp', right if way == 1 else left)  7.92 us
    pallas_call x2, Pallas kernels, finish(): pl.pallas_call(functools.partial(final_kernel, side), in_specs=[pl.BlockS...  3.5 us
    ppermute x5, waiting for transfers between devices, swap(): return lax.ppermute(value, 'dp', [(0, 1), (1, 0)])  2.7 us
    pallas_call x1, Pallas kernels, early_left(): pl.pallas_call(early_kernel, in_specs=[pl.BlockSpec(memory_space=pltpu.SM...  1.84 us
    pallas_call x1, Pallas kernels, cholesky_inverse(): pl.pallas_call(inverse_kernel, in_specs=[pl.BlockSpec(memory_space=pltpu....  1.77 us
  transfers between devices with their start and end apart: 27, of which 13 were waited for; matrix products, arithmetic and copies ran while one was open for 0% of the time, Pallas kernels for 14%

profile of v4, /device:TPU:0, one launch (start us, length us, event | category | flops | bytes accessed | tf_op | source)
XLA Modules:
  0.0 69.4 jit_solution(16122788754805598033)
XLA Ops:
  0.6 0.9 %copy-done.4 = bf16[1,32,4096]{2,1,0:T(8,128)(2,1)S(1)} copy-done((bf16[1,32,4096]{2,1,0:T(8,128)(2,1)S(1)}, bf16[1,32,4096]{2,1,0:T(8,128)(2,1)}, u32[]{:S(2)}) %copy-start.4) | copy-done | bytes 262168
  1.6 3.0 %collective-permute-start = (bf16[16,4096]{1,0:T(8,128)(2,1)S(1)}, bf16[16,4096]{1,0:T(8,128)(2,1)S(1)}, u32[]{:S(2)}, u32[]{:S(2)}) collective-permute-start(bf16[16,4096]{1,0:T(8,128)(2,1)S(1)} %get-tuple-element.49.refs_0_), channel_id=1, source_target_pairs={{0,2},{2,6},{6,10},{10,14},{14,12},{12,8},{8,4},{4,0},{1,3},{3,7},... | collective-permute-start | bytes 393224 | tf_op jit(solution)/shard_map/ppermute | solution.py:539
  4.6 0.1 collective-permute-start.4
  4.8 1.2 %residue_left.1 = (bf16[192,4096]{1,0:T(8,128)(2,1)S(1)}, f32[64,448]{1,0:T(8,128)S(1)}) custom-call(f32[64,4096]{1,0:T(8,128)S(1)} %copy-done.3, bf16[448,4096]{1,0:T(8,128)(2,1)S(1)} %bitcast.6), custom_call_target="tpu_custom_call" | custom-call | flops 2529999872 | tf_op jit(solution)/shard_map/residue_left/pallas_call | solution.py:92
  6.0 2.2 %collective-permute-start.8 = (bf16[16,4096]{1,0:T(8,128)(2,1)S(1)}, bf16[16,4096]{1,0:T(8,128)(2,1)S(1)}, u32[]{:S(2)}, u32[]{:S(2)}) collective-permute-start(bf16[16,4096]{1,0:T(8,128)(2,1)S(1)} %get-tuple-element.48.refs_1_), channel_id=1, source_target_pairs={{0,2},{2,6},{6,10},{10,14},{14,12},{12,8},{8,4},{4,0},{1,3},{3,7},... | collective-permute-start | bytes 393224 | tf_op jit(solution)/shard_map/ppermute | solution.py:539
  8.1 0.1 collective-permute-start.9
  8.2 1.9 %collective-permute-start.1 = (bf16[16,4096]{1,0:T(8,128)(2,1)S(1)}, bf16[16,4096]{1,0:T(8,128)(2,1)S(1)}, u32[]{:S(2)}, u32[]{:S(2)}) collective-permute-start(bf16[16,4096]{1,0:T(8,128)(2,1)S(1)} %collective-permute-done.refs_2_), channel_id=1, source_target_pairs={{0,2},{2,6},{6,10},{10,14},{14,12},{12,8},{8,4},{4,0},{1,3},{3,7},... | collective-permute-start | bytes 393224 | tf_op jit(solution)/shard_map/ppermute | solution.py:539
  10.2 0.1 collective-permute-start.5
  10.3 2.2 %collective-permute-done.8.refs_4_ = bf16[16,4096]{1,0:T(8,128)(2,1)S(1)} collective-permute-done((bf16[16,4096]{1,0:T(8,128)(2,1)S(1)}, bf16[16,4096]{1,0:T(8,128)(2,1)S(1)}, u32[]{:S(2)}, u32[]{:S(2)}) %collective-permute-start.8) | collective-permute-done | bytes 131104 | tf_op jit(solution)/shard_map/ppermute | solution.py:539
  12.5 2.0 %collective-permute-start.10 = (bf16[16,4096]{1,0:T(8,128)(2,1)S(1)}, bf16[16,4096]{1,0:T(8,128)(2,1)S(1)}, u32[]{:S(2)}, u32[]{:S(2)}) collective-permute-start(bf16[16,4096]{1,0:T(8,128)(2,1)S(1)} %collective-permute-done.8.refs_4_), channel_id=1, source_target_pairs={{0,2},{2,6},{6,10},{10,14},{14,12},{12,8},{8,4},{4,0},{1,3},{3,7},... | collective-permute-start | bytes 393224 | tf_op jit(solution)/shard_map/ppermute | solution.py:539
  14.6 0.7 collective-permute-done.1.refs_6_
  15.3 2.0 %collective-permute-start.2 = (bf16[16,4096]{1,0:T(8,128)(2,1)S(1)}, bf16[16,4096]{1,0:T(8,128)(2,1)S(1)}, u32[]{:S(2)}, u32[]{:S(2)}) collective-permute-start(bf16[16,4096]{1,0:T(8,128)(2,1)S(1)} %collective-permute-done.1.refs_6_), channel_id=1, source_target_pairs={{0,2},{2,6},{6,10},{10,14},{14,12},{12,8},{8,4},{4,0},{1,3},{3,7},... | collective-permute-start | bytes 393224 | tf_op jit(solution)/shard_map/ppermute | solution.py:539
  17.4 1.3 %collective-permute-done.10.refs_8_ = bf16[16,4096]{1,0:T(8,128)(2,1)S(1)} collective-permute-done((bf16[16,4096]{1,0:T(8,128)(2,1)S(1)}, bf16[16,4096]{1,0:T(8,128)(2,1)S(1)}, u32[]{:S(2)}, u32[]{:S(2)}) %collective-permute-start.10) | collective-permute-done | bytes 131104 | tf_op jit(solution)/shard_map/ppermute | solution.py:539
  18.7 2.1 %collective-permute-start.12 = (bf16[16,4096]{1,0:T(8,128)(2,1)S(1)}, bf16[16,4096]{1,0:T(8,128)(2,1)S(1)}, u32[]{:S(2)}, u32[]{:S(2)}) collective-permute-start(bf16[16,4096]{1,0:T(8,128)(2,1)S(1)} %collective-permute-done.10.refs_8_), channel_id=1, source_target_pairs={{0,2},{2,6},{6,10},{10,14},{14,12},{12,8},{8,4},{4,0},{1,3},{3,7},... | collective-permute-start | bytes 393224 | tf_op jit(solution)/shard_map/ppermute | solution.py:539
  20.7 0.3 collective-permute-start.13
  21.0 0.8 %collective-permute-done.2.refs_10_ = bf16[16,4096]{1,0:T(8,128)(2,1)S(1)} collective-permute-done((bf16[16,4096]{1,0:T(8,128)(2,1)S(1)}, bf16[16,4096]{1,0:T(8,128)(2,1)S(1)}, u32[]{:S(2)}, u32[]{:S(2)}) %collective-permute-start.2) | collective-permute-done | bytes 131104 | tf_op jit(solution)/shard_map/ppermute | solution.py:539
  21.8 1.9 %collective-permute-start.3 = (bf16[16,4096]{1,0:T(8,128)(2,1)S(1)}, bf16[16,4096]{1,0:T(8,128)(2,1)S(1)}, u32[]{:S(2)}, u32[]{:S(2)}) collective-permute-start(bf16[16,4096]{1,0:T(8,128)(2,1)S(1)} %collective-permute-done.2.refs_10_), channel_id=1, source_target_pairs={{0,2},{2,6},{6,10},{10,14},{14,12},{12,8},{8,4},{4,0},{1,3},{3,7},... | collective-permute-start | bytes 393224 | tf_op jit(solution)/shard_map/ppermute | solution.py:539
  23.6 0.2 collective-permute-start.7
  23.8 0.7 %collective-permute-done.12.refs_12_ = bf16[16,4096]{1,0:T(8,128)(2,1)S(1)} collective-permute-done((bf16[16,4096]{1,0:T(8,128)(2,1)S(1)}, bf16[16,4096]{1,0:T(8,128)(2,1)S(1)}, u32[]{:S(2)}, u32[]{:S(2)}) %collective-permute-start.12) | collective-permute-done | bytes 131104 | tf_op jit(solution)/shard_map/ppermute | solution.py:539
  24.5 1.3 %collective-permute-done.13.refs_13_ = bf16[16,4096]{1,0:T(8,128)(2,1)S(1)} collective-permute-done((bf16[16,4096]{1,0:T(8,128)(2,1)S(1)}, bf16[16,4096]{1,0:T(8,128)(2,1)S(1)}, u32[]{:S(2)}, u32[]{:S(2)}) %collective-permute-start.13) | collective-permute-done | bytes 131104 | tf_op jit(solution)/shard_map/ppermute | solution.py:539
  25.9 1.8 %early_left.1 = (bf16[256,4096]{1,0:T(8,128)(2,1)S(1)}, bf16[256,448]{1,0:T(8,128)(2,1)S(1)}, f32[64,448]{1,0:T(8,128)S(1)}) custom-call(s32[8,16]{1,0:T(8,128)S(1)} %copy-done.2, bf16[16,4096]{1,0:T(8,128)(2,1)S(1)} %get-tuple-element.49.refs_0_, bf16[16,4096]{1,0:T(8,128)(2,1)S(1)} %get-tuple-element.48.refs_1_, ...), custom_call_target="tpu_custom_call" | custom-call | flops 2300000000 | tf_op jit(solution)/shard_map/early_left/pallas_call | solution.py:126
  27.7 0.9 %collective-permute-done.7.second = bf16[16,4096]{1,0:T(8,128)(2,1)S(1)} collective-permute-done((bf16[16,4096]{1,0:T(8,128)(2,1)S(1)}, bf16[16,4096]{1,0:T(8,128)(2,1)S(1)}, u32[]{:S(2)}, u32[]{:S(2)}) %collective-permute-start.7) | collective-permute-done | bytes 131104 | tf_op jit(solution)/shard_map/ppermute | solution.py:539
  28.6 1.4 %late_left.1 = (bf16[256,4096]{1,0:T(8,128)(2,1)S(1)}, f32[64,448]{1,0:T(8,128)S(1)}) custom-call(s32[8,16]{1,0:T(8,128)S(1)} %copy-done.2, bf16[16,4096]{1,0:T(8,128)(2,1)S(1)} %collective-permute-done.3.first, bf16[16,4096]{1,0:T(8,128)(2,1)S(1)} %collective-permute-done.7.second, ...), custom_call_target="tpu_custom_call", output_to_operand_aliasing={{0}: (6, {})} | custom-call | flops 1150000000 | tf_op jit(solution)/shard_map/late_left/pallas_call | solution.py:158
  30.1 1.3 %collective-permute-done.14.other_l = f32[64,448]{1,0:T(8,128)S(1)} collective-permute-done((f32[64,448]{1,0:T(8,128)S(1)}, f32[64,448]{1,0:T(8,128)S(1)}, u32[]{:S(2)}, u32[]{:S(2)}) %collective-permute-start.14) | collective-permute-done | bytes 114720 | tf_op jit(solution)/shard_map/ppermute | solution.py:550
  31.4 0.7 given_far.1
  32.1 0.2 collective-permute-start.17
  32.3 0.8 %near_terms.1 = (f32[2,64,512]{2,1,0:T(8,128)S(1)}, f32[2,64,512]{2,1,0:T(8,128)S(1)}) custom-call(bf16[192,448]{1,0:T(8,128)(2,1)S(1)} %get-tuple-element.56.lhs, bf16[192,256]{1,0:T(8,128)(2,1)S(1)} %get-tuple-element.57.rhs, bf16[448,4096]{1,0:T(8,128)(2,1)S(1)} %bitcast.8, bf16[256,4096]{1,0:T(8,128)(2,1)S(1)} %get-tuple-element.64.tokens), custom_call_target="tpu_custom_call" | custom-call | flops 57500000 | tf_op jit(solution)/shard_map/near_terms/pallas_call | solution.py:261
  33.1 0.4 collective-permute-start.15
  33.5 0.6 kept_far.1
  34.2 1.6 %collective-permute-start.18 = (f32[72,512]{1,0:T(8,128)S(1)}, f32[72,512]{1,0:T(8,128)S(1)}, u32[]{:S(2)}, u32[]{:S(2)}) collective-permute-start(f32[72,512]{1,0:T(8,128)S(1)} %get-tuple-element.68), channel_id=1, source_target_pairs={{0,2},{1,3},{2,0},{3,1},{4,6},{5,7},{6,4},{7,5},{8,10},{9,11},{10,... | collective-permute-start | bytes 442376 | tf_op jit(solution)/shard_map/ppermute | solution.py:568
  35.9 0.7 collective-permute-start.16
  36.6 3.6 %collective-permute-done.18.b = f32[72,512]{1,0:T(8,128)S(1)} collective-permute-done((f32[72,512]{1,0:T(8,128)S(1)}, f32[72,512]{1,0:T(8,128)S(1)}, u32[]{:S(2)}, u32[]{:S(2)}) %collective-permute-start.18) | collective-permute-done | bytes 147488 | tf_op jit(solution)/shard_map/ppermute | solution.py:568
  40.2 2.5 %collective-permute-start.20 = (f32[72,512]{1,0:T(8,128)S(1)}, f32[72,512]{1,0:T(8,128)S(1)}, u32[]{:S(2)}, u32[]{:S(2)}) collective-permute-start(f32[72,512]{1,0:T(8,128)S(1)} %added.1), channel_id=1, source_target_pairs={{0,8},{1,13},{2,10},{3,15},{4,12},{5,9},{6,14},{7,11},{8,0},{9,5},... | collective-permute-start | bytes 442376 | tf_op jit(solution)/shard_map/ppermute | solution.py:568
  42.7 1.7 %collective-permute-start.19 = (f32[72,512]{1,0:T(8,128)S(1)}, f32[72,512]{1,0:T(8,128)S(1)}, u32[]{:S(2)}, u32[]{:S(2)}) collective-permute-start(f32[72,512]{1,0:T(8,128)S(1)} %get-tuple-element.69), channel_id=1, source_target_pairs={{0,2},{1,7},{2,0},{3,5},{4,6},{5,3},{6,4},{7,1},{8,10},{9,15},{10,... | collective-permute-start | bytes 442376 | tf_op jit(solution)/shard_map/ppermute | solution.py:568
  44.4 1.1 %merged.1 = f32[448,4096]{1,0:T(8,128)S(1)} custom-call(bf16[448,256]{1,0:T(8,128)(2,1)S(1)} %bitcast.13, bf16[448,4096]{1,0:T(8,128)(2,1)S(1)} %bitcast.10, bf16[256,4096]{1,0:T(8,128)(2,1)S(1)} %get-tuple-element.64.tokens), custom_call_target="tpu_custom_call" | custom-call | flops 57500000 | tf_op jit(solution)/shard_map/merged/pallas_call | solution.py:280
  45.6 4.1 %collective-permute-done.20.refs_1_ = f32[72,512]{1,0:T(8,128)S(1)} collective-permute-done((f32[72,512]{1,0:T(8,128)S(1)}, f32[72,512]{1,0:T(8,128)S(1)}, u32[]{:S(2)}, u32[]{:S(2)}) %collective-permute-start.20) | collective-permute-done | bytes 147488 | tf_op jit(solution)/shard_map/ppermute | solution.py:568
  49.8 1.4 %collective-permute-done.21.other = f32[72,512]{1,0:T(8,128)S(1)} collective-permute-done((f32[72,512]{1,0:T(8,128)S(1)}, f32[72,512]{1,0:T(8,128)S(1)}, u32[]{:S(2)}, u32[]{:S(2)}) %collective-permute-start.21) | collective-permute-done | bytes 147488 | tf_op jit(solution)/shard_map/ppermute | solution.py:550
  51.2 0.7 %collective-permute-start.24 = (f32[64,512]{1,0:T(8,128)S(1)}, f32[64,512]{1,0:T(8,128)S(1)}, u32[]{:S(2)}, u32[]{:S(2)}) collective-permute-start(f32[64,512]{1,0:T(8,128)S(1)} %get-tuple-element.71.share), channel_id=1, source_target_pairs={{0,8},{1,13},{2,10},{3,15},{4,12},{5,9},{6,14},{7,11},{8,0},{9,5},... | collective-permute-start | bytes 393224 | tf_op jit(solution)/shard_map/ppermute | solution.py:568
  51.9 0.7 collective-permute-start.23
  52.6 1.7 %collective-permute-start.22 = (f32[64,512]{1,0:T(8,128)S(1)}, f32[64,512]{1,0:T(8,128)S(1)}, u32[]{:S(2)}, u32[]{:S(2)}) collective-permute-start(f32[64,512]{1,0:T(8,128)S(1)} %get-tuple-element.71.share), channel_id=1, source_target_pairs={{0,2},{1,7},{2,0},{3,5},{4,6},{5,3},{6,4},{7,1},{8,10},{9,15},{10,... | collective-permute-start | bytes 393224 | tf_op jit(solution)/shard_map/ppermute | solution.py:568
  54.3 5.3 %collective-permute-done.24.refs_0_ = f32[64,512]{1,0:T(8,128)S(1)} collective-permute-done((f32[64,512]{1,0:T(8,128)S(1)}, f32[64,512]{1,0:T(8,128)S(1)}, u32[]{:S(2)}, u32[]{:S(2)}) %collective-permute-start.24) | collective-permute-done | bytes 131104 | tf_op jit(solution)/shard_map/ppermute | solution.py:568
  59.6 1.5 %collective-permute-start.25 = (f32[64,512]{1,0:T(8,128)S(1)}, f32[64,512]{1,0:T(8,128)S(1)}, u32[]{:S(2)}, u32[]{:S(2)}) collective-permute-start(f32[64,512]{1,0:T(8,128)S(1)} %collective-permute-done.24.refs_0_), channel_id=1, source_target_pairs={{0,2},{1,3},{2,0},{3,1},{4,6},{5,7},{6,4},{7,5},{8,10},{9,11},{10,... | collective-permute-start | bytes 393224 | tf_op jit(solution)/shard_map/ppermute | solution.py:568
  61.1 1.8 %cholesky_inverse.1.inverse = f32[64,64]{1,0:T(8,128)S(1)} custom-call(f32[64,64]{1,0:T(8,128)S(1)} %get-tuple-element.76.gram), custom_call_target="tpu_custom_call" | custom-call | flops 57500000 | tf_op jit(solution)/shard_map/cholesky_inverse/pallas_call | solution.py:428
  62.9 0.8 %last_operand.1.lhs = bf16[512,256]{1,0:T(8,128)(2,1)S(1)} custom-call(f32[64,64]{1,0:T(8,128)S(1)} %cholesky_inverse.1.inverse, f32[64,448]{1,0:T(8,128)S(1)} %get-tuple-element.60.left_sum), custom_call_target="tpu_custom_call" | custom-call | flops 57500000 | tf_op jit(solution)/shard_map/last_operand/pallas_call | solution.py:459
  63.7 1.2 %collective-permute-done.25.refs_1_ = f32[64,512]{1,0:T(8,128)S(1)} collective-permute-done((f32[64,512]{1,0:T(8,128)S(1)}, f32[64,512]{1,0:T(8,128)S(1)}, u32[]{:S(2)}, u32[]{:S(2)}) %collective-permute-start.25) | collective-permute-done | bytes 131104 | tf_op jit(solution)/shard_map/ppermute | solution.py:568
  64.9 1.0 %collective-permute-start.26 = (f32[4,64,512]{2,1,0:T(8,128)S(1)}, f32[4,64,512]{2,1,0:T(8,128)S(1)}, u32[]{:S(2)}, u32[]{:S(2)}) collective-permute-start(f32[4,64,512]{2,1,0:T(8,128)S(1)} %joined.1.shares), channel_id=1, source_target_pairs={{0,1},{1,0},{2,3},{3,2},{4,5},{5,4},{6,7},{7,6},{8,9},{9,8},{10,11... | collective-permute-start | bytes 1572872 | tf_op jit(solution)/shard_map/ppermute | solution.py:550
  65.9 1.7 %finish.2 = (bf16[448,4096]{1,0:T(8,128)(2,1)}, f32[64,4096]{1,0:T(8,128)}) custom-call(f32[4,64,512]{2,1,0:T(8,128)S(1)} %joined.1.shares, bf16[512,256]{1,0:T(8,128)(2,1)S(1)} %last_operand.1.lhs, f32[448,4096]{1,0:T(8,128)S(1)} %merged.1), custom_call_target="tpu_custom_call" | custom-call | flops 1724999936 | tf_op jit(solution)/shard_map/finish/pallas_call | solution.py:496
  67.6 1.8 %finish.3 = (bf16[448,4096]{1,0:T(8,128)(2,1)}, f32[64,4096]{1,0:T(8,128)}) custom-call(f32[4,64,512]{2,1,0:T(8,128)S(1)} %collective-permute-done.26.shares, bf16[512,256]{1,0:T(8,128)(2,1)S(1)} %last_operand.1.lhs, f32[448,4096]{1,0:T(8,128)S(1)} %merged.1, ...), custom_call_target="tpu_custom_call", output_to_operand_aliasing={{0}: (3, {}), {1}: (4, {})} | custom-call | flops 1724999936 | tf_op jit(solution)/shard_map/finish/pallas_call | solution.py:496
  (34 shorter events, 0.7 us)
Async XLA Ops:
  0.6 1.0 %copy-start.4 = (bf16[1,32,4096]{2,1,0:T(8,128)(2,1)S(1)}, bf16[1,32,4096]{2,1,0:T(8,128)(2,1)}, u32[]{:S(2)}) copy-start(bf16[1,32,4096]{2,1,0:T(8,128)(2,1)} %param.5) | copy-start | bytes 786436
  1.6 3.2 %copy-start = (bf16[1,448,4096]{2,1,0:T(8,128)(2,1)S(1)}, bf16[1,448,4096]{2,1,0:T(8,128)(2,1)}, u32[]{:S(2)}) copy-start(bf16[1,448,4096]{2,1,0:T(8,128)(2,1)} %param.7) | copy-start | bytes 11010052
  1.6 3.2 %copy-start.3 = (f32[64,4096]{1,0:T(8,128)S(1)}, f32[64,4096]{1,0:T(8,128)}, u32[]{:S(2)}) copy-start(f32[64,4096]{1,0:T(8,128)} %right.1) | copy-start | bytes 3145732
  1.6 6.6 %collective-permute-start = (bf16[16,4096]{1,0:T(8,128)(2,1)S(1)}, bf16[16,4096]{1,0:T(8,128)(2,1)S(1)}, u32[]{:S(2)}, u32[]{:S(2)}) collective-permute-start(bf16[16,4096]{1,0:T(8,128)(2,1)S(1)} %get-tuple-element.49.refs_0_), channel_id=1, source_target_pairs={{0,2},{2,6},{6,10},{10,14},{14,12},{12,8},{8,4},{4,0},{1,3},{3,7},... | collective-permute-start | bytes 393224 | tf_op jit(solution)/shard_map/ppermute | solution.py:539
  4.6 5.5 %collective-permute-start.4 = (bf16[16,4096]{1,0:T(8,128)(2,1)S(1)}, bf16[16,4096]{1,0:T(8,128)(2,1)S(1)}, u32[]{:S(2)}, u32[]{:S(2)}) collective-permute-start(bf16[16,4096]{1,0:T(8,128)(2,1)S(1)} %get-tuple-element.48.refs_1_), channel_id=1, source_target_pairs={{2,0},{6,2},{10,6},{14,10},{12,14},{8,12},{4,8},{0,4},{3,1},{7,3},... | collective-permute-start | bytes 393224 | tf_op jit(solution)/shard_map/ppermute | solution.py:539
  4.8 21.1 %copy-start.1 = (bf16[1,256,448]{1,2,0:T(8,128)(2,1)S(1)}, bf16[1,256,448]{1,2,0:T(8,128)(2,1)}, u32[]{:S(2)}) copy-start(bf16[1,256,448]{1,2,0:T(8,128)(2,1)} %param.6) | copy-start | bytes 688132
  4.8 21.1 %copy-start.2 = (s32[8,16]{1,0:T(8,128)S(1)}, s32[8,16]{1,0:T(8,128)}, u32[]{:S(2)}) copy-start(s32[8,16]{1,0:T(8,128)} %constant.2.clone.places) | copy-start | bytes 1540
  6.0 6.5 %collective-permute-start.8 = (bf16[16,4096]{1,0:T(8,128)(2,1)S(1)}, bf16[16,4096]{1,0:T(8,128)(2,1)S(1)}, u32[]{:S(2)}, u32[]{:S(2)}) collective-permute-start(bf16[16,4096]{1,0:T(8,128)(2,1)S(1)} %get-tuple-element.48.refs_1_), channel_id=1, source_target_pairs={{0,2},{2,6},{6,10},{10,14},{14,12},{12,8},{8,4},{4,0},{1,3},{3,7},... | collective-permute-start | bytes 393224 | tf_op jit(solution)/shard_map/ppermute | solution.py:539
  8.1 6.4 %collective-permute-start.9 = (bf16[16,4096]{1,0:T(8,128)(2,1)S(1)}, bf16[16,4096]{1,0:T(8,128)(2,1)S(1)}, u32[]{:S(2)}, u32[]{:S(2)}) collective-permute-start(bf16[16,4096]{1,0:T(8,128)(2,1)S(1)} %get-tuple-element.49.refs_0_), channel_id=1, source_target_pairs={{2,0},{6,2},{10,6},{14,10},{12,14},{8,12},{4,8},{0,4},{3,1},{7,3},... | collective-permute-start | bytes 393224 | tf_op jit(solution)/shard_map/ppermute | solution.py:539
  8.2 7.1 %collective-permute-start.1 = (bf16[16,4096]{1,0:T(8,128)(2,1)S(1)}, bf16[16,4096]{1,0:T(8,128)(2,1)S(1)}, u32[]{:S(2)}, u32[]{:S(2)}) collective-permute-start(bf16[16,4096]{1,0:T(8,128)(2,1)S(1)} %collective-permute-done.refs_2_), channel_id=1, source_target_pairs={{0,2},{2,6},{6,10},{10,14},{14,12},{12,8},{8,4},{4,0},{1,3},{3,7},... | collective-permute-start | bytes 393224 | tf_op jit(solution)/shard_map/ppermute | solution.py:539
  10.2 7.2 %collective-permute-start.5 = (bf16[16,4096]{1,0:T(8,128)(2,1)S(1)}, bf16[16,4096]{1,0:T(8,128)(2,1)S(1)}, u32[]{:S(2)}, u32[]{:S(2)}) collective-permute-start(bf16[16,4096]{1,0:T(8,128)(2,1)S(1)} %collective-permute-done.4.refs_3_), channel_id=1, source_target_pairs={{2,0},{6,2},{10,6},{14,10},{12,14},{8,12},{4,8},{0,4},{3,1},{7,3},... | collective-permute-start | bytes 393224 | tf_op jit(solution)/shard_map/ppermute | solution.py:539
  12.5 6.2 %collective-permute-start.10 = (bf16[16,4096]{1,0:T(8,128)(2,1)S(1)}, bf16[16,4096]{1,0:T(8,128)(2,1)S(1)}, u32[]{:S(2)}, u32[]{:S(2)}) collective-permute-start(bf16[16,4096]{1,0:T(8,128)(2,1)S(1)} %collective-permute-done.8.refs_4_), channel_id=1, source_target_pairs={{0,2},{2,6},{6,10},{10,14},{14,12},{12,8},{8,4},{4,0},{1,3},{3,7},... | collective-permute-start | bytes 393224 | tf_op jit(solution)/shard_map/ppermute | solution.py:539
  14.5 6.2 %collective-permute-start.11 = (bf16[16,4096]{1,0:T(8,128)(2,1)S(1)}, bf16[16,4096]{1,0:T(8,128)(2,1)S(1)}, u32[]{:S(2)}, u32[]{:S(2)}) collective-permute-start(bf16[16,4096]{1,0:T(8,128)(2,1)S(1)} %collective-permute-done.9.refs_5_), channel_id=1, source_target_pairs={{2,0},{6,2},{10,6},{14,10},{12,14},{8,12},{4,8},{0,4},{3,1},{7,3},... | collective-permute-start | bytes 393224 | tf_op jit(solution)/shard_map/ppermute | solution.py:539
  15.3 6.5 %collective-permute-start.2 = (bf16[16,4096]{1,0:T(8,128)(2,1)S(1)}, bf16[16,4096]{1,0:T(8,128)(2,1)S(1)}, u32[]{:S(2)}, u32[]{:S(2)}) collective-permute-start(bf16[16,4096]{1,0:T(8,128)(2,1)S(1)} %collective-permute-done.1.refs_6_), channel_id=1, source_target_pairs={{0,2},{2,6},{6,10},{10,14},{14,12},{12,8},{8,4},{4,0},{1,3},{3,7},... | collective-permute-start | bytes 393224 | tf_op jit(solution)/shard_map/ppermute | solution.py:539
  17.3 6.3 %collective-permute-start.6 = (bf16[16,4096]{1,0:T(8,128)(2,1)S(1)}, bf16[16,4096]{1,0:T(8,128)(2,1)S(1)}, u32[]{:S(2)}, u32[]{:S(2)}) collective-permute-start(bf16[16,4096]{1,0:T(8,128)(2,1)S(1)} %collective-permute-done.5.refs_7_), channel_id=1, source_target_pairs={{2,0},{6,2},{10,6},{14,10},{12,14},{8,12},{4,8},{0,4},{3,1},{7,3},... | collective-permute-start | bytes 393224 | tf_op jit(solution)/shard_map/ppermute | solution.py:539
  18.7 5.9 %collective-permute-start.12 = (bf16[16,4096]{1,0:T(8,128)(2,1)S(1)}, bf16[16,4096]{1,0:T(8,128)(2,1)S(1)}, u32[]{:S(2)}, u32[]{:S(2)}) collective-permute-start(bf16[16,4096]{1,0:T(8,128)(2,1)S(1)} %collective-permute-done.10.refs_8_), channel_id=1, source_target_pairs={{0,2},{2,6},{6,10},{10,14},{14,12},{12,8},{8,4},{4,0},{1,3},{3,7},... | collective-permute-start | bytes 393224 | tf_op jit(solution)/shard_map/ppermute | solution.py:539
  20.7 5.2 %collective-permute-start.13 = (bf16[16,4096]{1,0:T(8,128)(2,1)S(1)}, bf16[16,4096]{1,0:T(8,128)(2,1)S(1)}, u32[]{:S(2)}, u32[]{:S(2)}) collective-permute-start(bf16[16,4096]{1,0:T(8,128)(2,1)S(1)} %collective-permute-done.11.refs_9_), channel_id=1, source_target_pairs={{2,0},{6,2},{10,6},{14,10},{12,14},{8,12},{4,8},{0,4},{3,1},{7,3},... | collective-permute-start | bytes 393224 | tf_op jit(solution)/shard_map/ppermute | solution.py:539
  21.8 5.9 %collective-permute-start.3 = (bf16[16,4096]{1,0:T(8,128)(2,1)S(1)}, bf16[16,4096]{1,0:T(8,128)(2,1)S(1)}, u32[]{:S(2)}, u32[]{:S(2)}) collective-permute-start(bf16[16,4096]{1,0:T(8,128)(2,1)S(1)} %collective-permute-done.2.refs_10_), channel_id=1, source_target_pairs={{0,2},{2,6},{6,10},{10,14},{14,12},{12,8},{8,4},{4,0},{1,3},{3,7},... | collective-permute-start | bytes 393224 | tf_op jit(solution)/shard_map/ppermute | solution.py:539
  23.6 5.0 %collective-permute-start.7 = (bf16[16,4096]{1,0:T(8,128)(2,1)S(1)}, bf16[16,4096]{1,0:T(8,128)(2,1)S(1)}, u32[]{:S(2)}, u32[]{:S(2)}) collective-permute-start(bf16[16,4096]{1,0:T(8,128)(2,1)S(1)} %collective-permute-done.6.refs_11_), channel_id=1, source_target_pairs={{2,0},{6,2},{10,6},{14,10},{12,14},{8,12},{4,8},{0,4},{3,1},{7,3},... | collective-permute-start | bytes 393224 | tf_op jit(solution)/shard_map/ppermute | solution.py:539
  30.0 1.4 %collective-permute-start.14 = (f32[64,448]{1,0:T(8,128)S(1)}, f32[64,448]{1,0:T(8,128)S(1)}, u32[]{:S(2)}, u32[]{:S(2)}) collective-permute-start(f32[64,448]{1,0:T(8,128)S(1)} %get-tuple-element.54.here_l), channel_id=1, source_target_pairs={{0,1},{1,0},{2,3},{3,2},{4,5},{5,4},{6,7},{7,6},{8,9},{9,8},{10,11... | collective-permute-start | bytes 344072 | tf_op jit(solution)/shard_map/ppermute | solution.py:550
  32.1 2.0 %collective-permute-start.17 = (f32[2,64,512]{2,1,0:T(8,128)S(1)}, f32[2,64,512]{2,1,0:T(8,128)S(1)}, u32[]{:S(2)}, u32[]{:S(2)}) collective-permute-start(f32[2,64,512]{2,1,0:T(8,128)S(1)} %get-tuple-element.67), channel_id=1, source_target_pairs={{0,1},{1,0},{2,3},{3,2},{4,5},{5,4},{6,7},{7,6},{8,9},{9,8},{10,11... | collective-permute-start | bytes 786440 | tf_op jit(solution)/shard_map/ppermute | solution.py:550
  33.1 2.7 %collective-permute-start.15 = (f32[2,64,512]{2,1,0:T(8,128)S(1)}, f32[2,64,512]{2,1,0:T(8,128)S(1)}, u32[]{:S(2)}, u32[]{:S(2)}) collective-permute-start(f32[2,64,512]{2,1,0:T(8,128)S(1)} %get-tuple-element.59), channel_id=1, source_target_pairs={{0,1},{1,0},{2,3},{3,2},{4,5},{5,4},{6,7},{7,6},{8,9},{9,8},{10,11... | collective-permute-start | bytes 786440 | tf_op jit(solution)/shard_map/ppermute | solution.py:550
  34.2 5.9 %collective-permute-start.18 = (f32[72,512]{1,0:T(8,128)S(1)}, f32[72,512]{1,0:T(8,128)S(1)}, u32[]{:S(2)}, u32[]{:S(2)}) collective-permute-start(f32[72,512]{1,0:T(8,128)S(1)} %get-tuple-element.68), channel_id=1, source_target_pairs={{0,2},{1,3},{2,0},{3,1},{4,6},{5,7},{6,4},{7,5},{8,10},{9,11},{10,... | collective-permute-start | bytes 442376 | tf_op jit(solution)/shard_map/ppermute | solution.py:568
  35.9 9.6 %collective-permute-start.16 = (f32[72,512]{1,0:T(8,128)S(1)}, f32[72,512]{1,0:T(8,128)S(1)}, u32[]{:S(2)}, u32[]{:S(2)}) collective-permute-start(f32[72,512]{1,0:T(8,128)S(1)} %get-tuple-element.62.own), channel_id=1, source_target_pairs={{1,5},{3,7},{5,1},{7,3},{9,13},{11,15},{13,9},{15,11},{17,21},{19,... | collective-permute-start | bytes 442376 | tf_op jit(solution)/shard_map/ppermute | solution.py:568
  40.2 9.5 %collective-permute-start.20 = (f32[72,512]{1,0:T(8,128)S(1)}, f32[72,512]{1,0:T(8,128)S(1)}, u32[]{:S(2)}, u32[]{:S(2)}) collective-permute-start(f32[72,512]{1,0:T(8,128)S(1)} %added.1), channel_id=1, source_target_pairs={{0,8},{1,13},{2,10},{3,15},{4,12},{5,9},{6,14},{7,11},{8,0},{9,5},... | collective-permute-start | bytes 442376 | tf_op jit(solution)/shard_map/ppermute | solution.py:568
  42.7 7.0 %collective-permute-start.19 = (f32[72,512]{1,0:T(8,128)S(1)}, f32[72,512]{1,0:T(8,128)S(1)}, u32[]{:S(2)}, u32[]{:S(2)}) collective-permute-start(f32[72,512]{1,0:T(8,128)S(1)} %get-tuple-element.69), channel_id=1, source_target_pairs={{0,2},{1,7},{2,0},{3,5},{4,6},{5,3},{6,4},{7,1},{8,10},{9,15},{10,... | collective-permute-start | bytes 442376 | tf_op jit(solution)/shard_map/ppermute | solution.py:568
  49.7 1.4 %collective-permute-start.21 = (f32[72,512]{1,0:T(8,128)S(1)}, f32[72,512]{1,0:T(8,128)S(1)}, u32[]{:S(2)}, u32[]{:S(2)}) collective-permute-start(f32[72,512]{1,0:T(8,128)S(1)} %core_sum.1.here), channel_id=1, source_target_pairs={{0,1},{1,0},{2,3},{3,2},{4,5},{5,4},{6,7},{7,6},{8,9},{9,8},{10,11... | collective-permute-start | bytes 442376 | tf_op jit(solution)/shard_map/ppermute | solution.py:550
  51.2 8.4 %collective-permute-start.24 = (f32[64,512]{1,0:T(8,128)S(1)}, f32[64,512]{1,0:T(8,128)S(1)}, u32[]{:S(2)}, u32[]{:S(2)}) collective-permute-start(f32[64,512]{1,0:T(8,128)S(1)} %get-tuple-element.71.share), channel_id=1, source_target_pairs={{0,8},{1,13},{2,10},{3,15},{4,12},{5,9},{6,14},{7,11},{8,0},{9,5},... | collective-permute-start | bytes 393224 | tf_op jit(solution)/shard_map/ppermute | solution.py:568
  51.9 9.2 %collective-permute-start.23 = (f32[64,512]{1,0:T(8,128)S(1)}, f32[64,512]{1,0:T(8,128)S(1)}, u32[]{:S(2)}, u32[]{:S(2)}) collective-permute-start(f32[64,512]{1,0:T(8,128)S(1)} %get-tuple-element.71.share), channel_id=1, source_target_pairs={{1,5},{3,7},{5,1},{7,3},{9,13},{11,15},{13,9},{15,11},{17,21},{19,... | collective-permute-start | bytes 393224 | tf_op jit(solution)/shard_map/ppermute | solution.py:568
  52.6 8.5 %collective-permute-start.22 = (f32[64,512]{1,0:T(8,128)S(1)}, f32[64,512]{1,0:T(8,128)S(1)}, u32[]{:S(2)}, u32[]{:S(2)}) collective-permute-start(f32[64,512]{1,0:T(8,128)S(1)} %get-tuple-element.71.share), channel_id=1, source_target_pairs={{0,2},{1,7},{2,0},{3,5},{4,6},{5,3},{6,4},{7,1},{8,10},{9,15},{10,... | collective-permute-start | bytes 393224 | tf_op jit(solution)/shard_map/ppermute | solution.py:568
  59.6 5.2 %collective-permute-start.25 = (f32[64,512]{1,0:T(8,128)S(1)}, f32[64,512]{1,0:T(8,128)S(1)}, u32[]{:S(2)}, u32[]{:S(2)}) collective-permute-start(f32[64,512]{1,0:T(8,128)S(1)} %collective-permute-done.24.refs_0_), channel_id=1, source_target_pairs={{0,2},{1,3},{2,0},{3,1},{4,6},{5,7},{6,4},{7,5},{8,10},{9,11},{10,... | collective-permute-start | bytes 393224 | tf_op jit(solution)/shard_map/ppermute | solution.py:568
  64.9 2.7 %collective-permute-start.26 = (f32[4,64,512]{2,1,0:T(8,128)S(1)}, f32[4,64,512]{2,1,0:T(8,128)S(1)}, u32[]{:S(2)}, u32[]{:S(2)}) collective-permute-start(f32[4,64,512]{2,1,0:T(8,128)S(1)} %joined.1.shares), channel_id=1, source_target_pairs={{0,1},{1,0},{2,3},{3,2},{4,5},{5,4},{6,7},{7,6},{8,9},{9,8},{10,11... | collective-permute-start | bytes 1572872 | tf_op jit(solution)/shard_map/ppermute | solution.py:550

commit v5 on v4

--- a/solution.py
+++ b/solution.py
@@ -17,22 +17,14 @@
 PIVOTS = 8
 
 
-def split3(value):
-    high = value.astype(BF16)
-    rest = value - high.astype(F32)
-    middle = rest.astype(BF16)
-    low = (rest - middle.astype(F32)).astype(BF16)
-    return high, middle, low
-
-
 def split2(value):
     high = value.astype(BF16)
     return high, (value - high.astype(F32)).astype(BF16)
 
 
-def fold3(stacked):
-    rank = stacked.shape[0] // 3
-    return stacked[:rank] + stacked[rank : 2 * rank] + stacked[2 * rank :]
+def fold2(stacked):
+    rank = stacked.shape[0] // 2
+    return stacked[:rank] + stacked[rank:]
 
 
 def nn(a, b):
@@ -79,11 +71,11 @@
     total = None
     for step in range(STEPS):
         span = slice(step * cols, (step + 1) * cols)
-        stacked = jnp.concatenate(split3(right[:, span]), axis=0)
+        stacked = jnp.concatenate(split2(right[:, span]), axis=0)
         terms[:, span] = stacked
         part = nt(stacked, feedback[:, span])
         total = part if total is None else total + part
-    left_t[...] = fold3(total)
+    left_t[...] = fold2(total)
 
 
 def residue_left(right, feedback):
@@ -94,7 +86,7 @@
         in_specs=[pl.BlockSpec(memory_space=pltpu.VMEM)] * 2,
         out_specs=[pl.BlockSpec(memory_space=pltpu.VMEM)] * 2,
         out_shape=[
-            jax.ShapeDtypeStruct((3 * rank, width), BF16),
+            jax.ShapeDtypeStruct((2 * rank, width), BF16),
             jax.ShapeDtypeStruct((rank, rows), F32),
         ],
         compiler_params=params(),
@@ -105,7 +97,7 @@
 
 def early_kernel(places, *refs):
     pieces, (terms, residue_t, hidden_t, tokens, hidden, left_t) = refs[:-6], refs[-6:]
-    here = lax.axis_index("tp")
+    here = 2 * lax.axis_index("tp") + lax.axis_index("dp")
     size = pieces[0].shape[0]
     for index in range(len(pieces) + 2):
         rows = pl.ds(pl.multiple_of(places[here, index] * size, size), size)
@@ -113,9 +105,9 @@
             tokens[rows, :] = pieces[index][...]
         else:
             tokens[rows, :] = jnp.zeros((size, tokens.shape[1]), BF16)
-    projected = fold3(nt(terms[...], tokens[...]))
-    stacked = jnp.concatenate(split3(projected), axis=0)
-    left_t[...] = residue_t[...] + fold3(nt(stacked, hidden_t[...]))
+    projected = fold2(nt(terms[...], tokens[...]))
+    stacked = jnp.concatenate(split2(projected), axis=0)
+    left_t[...] = residue_t[...] + fold2(nt(stacked, hidden_t[...]))
     hidden[...] = hidden_t[...].T
 
 
@@ -140,7 +132,7 @@
 
 
 def late_kernel(places, first, second, terms, hidden, early_t, _, tokens, left_t):
-    here = lax.axis_index("tp")
+    here = 2 * lax.axis_index("tp") + lax.axis_index("dp")
     size = first.shape[0]
     count = places.shape[1]
     seen = []
@@ -148,9 +140,9 @@
         rows = pl.ds(pl.multiple_of(places[here, count - 2 + index] * size, size), size)
         tokens[rows, :] = piece[...]
         seen.append(hidden[rows, :])
-    projected = fold3(nt(terms[...], jnp.concatenate([first[...], second[...]], axis=0)))
-    stacked = jnp.concatenate(split3(projected), axis=0)
-    left_t[...] = early_t[...] + fold3(nn(stacked, jnp.concatenate(seen, axis=0)))
+    projected = fold2(nt(terms[...], jnp.concatenate([first[...], second[...]], axis=0)))
+    stacked = jnp.concatenate(split2(projected), axis=0)
+    left_t[...] = early_t[...] + fold2(nn(stacked, jnp.concatenate(seen, axis=0)))
 
 
 def late_left(places, pieces, terms, hidden, early_t, tokens):
@@ -190,15 +182,15 @@
 
 def block_sum(lhs, rhs, feedback, tokens, core, index, cols):
     span = columns_of(place_of(core, index), cols)
-    return fold3(nn(lhs[...], feedback[:, span]) + nn(rhs[...], tokens[:, span]))
+    return fold2(nn(lhs[...], feedback[:, span]) + nn(rhs[...], tokens[:, span]))
 
 
 def give_far_kernel(here_l, other_l, hidden_t, feedback, tokens, give, left_sum, lhs, rhs):
     left_t = here_l[...] + other_l[...]
     left_sum[...] = left_t
-    lhs[...] = jnp.concatenate(split3(left_t), axis=0)
-    seen_t = fold3(nn(lhs[...], hidden_t[...]))
-    rhs[...] = jnp.concatenate(split3(seen_t), axis=0)
+    lhs[...] = jnp.concatenate(split2(left_t), axis=0)
+    seen_t = fold2(nn(lhs[...], hidden_t[...]))
+    rhs[...] = jnp.concatenate(split2(seen_t), axis=0)
     other = 1 - lax.axis_index("dp")
     for index in range(give.shape[0]):
         give[index] = block_sum(lhs, rhs, feedback, tokens, other, index + 2, give.shape[2])
@@ -214,8 +206,8 @@
         out_shape=[
             jax.ShapeDtypeStruct((chips // 2 - 2, rank, width // chips), F32),
             jax.ShapeDtypeStruct((rank, rows), F32),
-            jax.ShapeDtypeStruct((3 * rank, rows), BF16),
-            jax.ShapeDtypeStruct((3 * rank, count), BF16),
+            jax.ShapeDtypeStruct((2 * rank, rows), BF16),
+            jax.ShapeDtypeStruct((2 * rank, count), BF16),
         ],
         compiler_params=params(),
         cost_estimate=cost(SMALL),
@@ -257,7 +249,7 @@
 
 
 def near_terms(lhs, rhs, feedback, tokens, chips):
-    block = jax.ShapeDtypeStruct((2, lhs.shape[0] // 3, tokens.shape[1] // chips), F32)
+    block = jax.ShapeDtypeStruct((2, lhs.shape[0] // 2, tokens.shape[1] // chips), F32)
     return pl.pallas_call(
         near_kernel,
         in_specs=[pl.BlockSpec(memory_space=pltpu.VMEM)] * 4,
@@ -431,7 +423,7 @@
         out_specs=pl.BlockSpec(memory_space=pltpu.VMEM),
         out_shape=jax.ShapeDtypeStruct(gram.shape, F32),
         compiler_params=params(),
-        cost_estimate=cost(SMALL),
+        cost_estimate=cost(5.0),
         name="cholesky_inverse",
     )(gram)
 
@@ -467,34 +459,35 @@
     )(inverse, left_sum)
 
 
-def final_kernel(side, shares, lhs, merged, *refs):
+def final_kernel(indices, side, shares, lhs, merged, *refs):
     out, factor, rhs, out_here, factor_here, sems = refs[-6:]
     owner = lax.axis_index("dp") ^ side
     rows = merged.shape[0]
-    count, rank, cols = shares.shape
+    rank, cols = shares.shape[1:]
     copies = []
-    for index in range(count):
+    for block, index in enumerate(indices):
         span = columns_of(place_of(owner, index), cols)
-        high, low = split2(shares[index])
+        high, low = split2(shares[block])
         for place, term in enumerate((high, low, high, low)):
-            rhs[index % 2, place * rank : (place + 1) * rank, :] = term
-        product = nn(lhs[...], rhs[index % 2])
-        factor_here[index] = product[rows:]
-        out_here[index] = (merged[:, span] + product[:rows]).astype(BF16)
-        for order, (source, target) in enumerate(((out_here, out), (factor_here, factor))):
+            rhs[block % 2, place * rank : (place + 1) * rank, :] = term
+        product = nn(lhs[...], rhs[block % 2])
+        factor_here[block] = product[rows:]
+        out_here[block] = (merged[:, span] + product[:rows]).astype(BF16)
+        for number, (source, target) in enumerate(((out_here, out), (factor_here, factor))):
             copies.append(
-                pltpu.make_async_copy(source.at[index], target.at[:, span], sems.at[index, order])
+                pltpu.make_async_copy(source.at[block], target.at[:, span], sems.at[block, number])
             )
             copies[-1].start()
     for copy in copies:
         copy.wait()
 
 
-def finish(side, shares, lhs, merged, begun=()):
-    count, rank, cols = shares.shape
+def finish(indices, shares, side, lhs, merged, begun=()):
+    rank, cols = shares.shape[1:]
     rows, width = merged.shape
-    return pl.pallas_call(
-        functools.partial(final_kernel, side),
+    blocks = len(indices)
+    return pl.pallas_call(
+        functools.partial(final_kernel, indices, side),
         in_specs=[pl.BlockSpec(memory_space=pltpu.VMEM)] * 3
         + [pl.BlockSpec(memory_space=pl.ANY)] * len(begun),
         out_specs=[pl.BlockSpec(memory_space=pl.ANY)] * 2,
@@ -505,12 +498,12 @@
         input_output_aliases={3 + index: index for index in range(len(begun))},
         scratch_shapes=[
             pltpu.VMEM((2, lhs.shape[1], cols), BF16),
-            pltpu.VMEM((count, rows, cols), BF16),
-            pltpu.VMEM((count, rank, cols), F32),
-            pltpu.SemaphoreType.DMA((count, 2)),
-        ],
-        compiler_params=params(),
-        cost_estimate=cost(1.5),
+            pltpu.VMEM((blocks, rows, cols), BF16),
+            pltpu.VMEM((blocks, rank, cols), F32),
+            pltpu.SemaphoreType.DMA((blocks, 2)),
+        ],
+        compiler_params=params(),
+        cost_estimate=cost(SMALL),
         name="finish",
     )(shares, lhs, merged, *begun)
 
@@ -524,8 +517,15 @@
 def ring_gather(shard, chips, beside):
     order = ring_order(chips)
     position = {chip: place for place, chip in enumerate(order)}
-    right = [(order[i], order[(i + 1) % chips]) for i in range(chips)]
-    left = [(b, a) for a, b in right]
+
+    def pairs(way):
+        steps = ((0, way), (1, -way))
+        return [
+            (2 * order[i] + core, 2 * order[(i + step) % chips] + core)
+            for i in range(chips)
+            for core, step in steps
+        ]
+
     halves = halves_of(shard)
     pieces = list(halves)
     origin = [(0, 0), (0, 1)]
@@ -536,13 +536,15 @@
         for way, half in ((1, 0), (-1, 1), (1, 1), (-1, 0)):
             if hop == far and (half == 0) != (way == 1):
                 continue
-            going[way, half] = lax.ppermute(going[way, half], "tp", right if way == 1 else left)
+            going[way, half] = lax.ppermute(going[way, half], ("tp", "dp"), pairs(way))
             pieces.append(going[way, half])
             origin.append((-way * hop, half))
-    places = np.zeros((chips, len(pieces)), np.int32)
+    places = np.zeros((2 * chips, len(pieces)), np.int32)
     for chip in range(chips):
-        for index, (shift, half) in enumerate(origin):
-            places[chip, index] = 2 * order[(position[chip] + shift) % chips] + half
+        for core, sign in ((0, 1), (1, -1)):
+            for index, (shift, half) in enumerate(origin):
+                source = order[(position[chip] + sign * shift) % chips]
+                places[2 * chip + core, index] = 2 * source + half
     return pieces, places, beside
 
 
@@ -592,13 +594,18 @@
     across = [exchange(share, index) for index in range(2, half, 2)]
     first, second = exchange(share, 1), exchange(share, 0)
     passed = [exchange(value, 2 * i + 3, 1) for i, value in enumerate(across)]
-    gram_matrix, first, second, across[0] = lax.optimization_barrier((gram_matrix, first, second, across[0]))
-    lhs = last_operand(cholesky_inverse(gram_matrix), left_sum, replicas)
-    passed, lhs = lax.optimization_barrier((passed, lhs))
-    mine = joined(share, second, first, [value for pair in zip(across, passed) for value in pair])
-    theirs = swap(mine)
-    begun = finish(0, mine, lhs, merged)
-    new_feedback, new_factor = finish(1, theirs, lhs, merged, begun)
+    passed = [exchange(value, 2 * i + 3, 1) for i, value in enumerate(across)]
+    inverse = cholesky_inverse(gram_matrix)
+    inverse, first, second, across[0] = lax.optimization_barrier((inverse, first, second, across[0]))
+    lhs = last_operand(inverse, left_sum, replicas)
+    mine = joined(share, second, first, across)
+    begun = finish([0, 1, *range(2, half, 2)], mine, 0, lhs, merged)
+    passed, begun = lax.optimization_barrier((passed, begun))
+    rest = passed[0][None] if len(passed) == 1 else jnp.stack(passed)
+    theirs = swap(jnp.concatenate([mine, rest]))
+    begun = finish([*range(3, half, 2)], rest, 0, lhs, merged, begun)
+    order = [0, 1, *range(2, half, 2), *range(3, half, 2)]
+    new_feedback, new_factor = finish(order, theirs, 1, lhs, merged, begun)
     return new_feedback[None], new_factor
 
 

time: 69.6 us -> 68.7 us (0.987)
  waiting for transfers between devices: 24.8 us -> 22.7 us
  starting transfers between devices: 28.8 us -> 29.7 us
    ppermute x14, waiting for transfers between devices: 7.92 us -> 6.55 us  [ring_gather(): going[way, half] = lax.ppermute(going[way, half], ('tp', 'dp'), pairs(way))]
    ppermute x8, waiting for transfers between devices: 14.2 us -> 12.9 us  [exchange(): return lax.ppermute(value, ('tp', 'dp'), pairs)]
    ppermute x14, starting transfers between devices: 16 us -> 17.1 us  [ring_gather(): going[way, half] = lax.ppermute(going[way, half], ('tp', 'dp'), pairs(way))]
    pallas_call x2 -> x3, Pallas kernels: 3.5 us -> 4.39 us  [finish(): pl.pallas_call(functools.partial(final_kernel, indices, side), in_specs=[...]
  transfers between devices with their start and end apart: 27 -> 27, of which waited for: 13 -> 15; matrix products, arithmetic and copies ran while one was open for 0% -> 0% of each run, Pallas kernels for 14% -> 16%
where the time goes in v5:
time: 68.7 us; the launch traced here: 68.6 us
  starting transfers between devices  29.7 us (43%)
  waiting for transfers between devices  22.7 us (33%)
  Pallas kernels  14.4 us (21%)
  local copies, waits for them, and re-layouts  0.96 us (1%)
  between operations  0.83 us (1%)
    ppermute x14, starting transfers between devices, ring_gather(): going[way, half] = lax.ppermute(going[way, half], ('tp', 'dp'), pairs(way))  17.1 us
    ppermute x8, waiting for transfers between devices, exchange(): return lax.ppermute(value, ('tp', 'dp'), pairs)  12.9 us
    ppermute x8, starting transfers between devices, exchange(): return lax.ppermute(value, ('tp', 'dp'), pairs)  11.4 us
    ppermute x14, waiting for transfers between devices, ring_gather(): going[way, half] = lax.ppermute(going[way, half], ('tp', 'dp'), pairs(way))  6.55 us
    pallas_call x3, Pallas kernels, finish(): pl.pallas_call(functools.partial(final_kernel, indices, side), in_specs=[...  4.39 us
    ppermute x5, waiting for transfers between devices, swap(): return lax.ppermute(value, 'dp', [(0, 1), (1, 0)])  3.23 us
    pallas_call x1, Pallas kernels, early_left(): pl.pallas_call(early_kernel, in_specs=[pl.BlockSpec(memory_space=pltpu.SM...  1.87 us
    pallas_call x1, Pallas kernels, cholesky_inverse(): pl.pallas_call(inverse_kernel, in_specs=[pl.BlockSpec(memory_space=pltpu....  1.77 us
  transfers between devices with their start and end apart: 27, of which 15 were waited for; matrix products, arithmetic and copies ran while one was open for 0% of the time, Pallas kernels for 16%

profile of v5, /device:TPU:0, one launch (start us, length us, event | category | flops | bytes accessed | tf_op | source)
XLA Modules:
  0.0 68.6 jit_solution(7454352873985610978)
XLA Ops:
  0.6 0.9 %copy-done.3 = bf16[1,32,4096]{2,1,0:T(8,128)(2,1)S(1)} copy-done((bf16[1,32,4096]{2,1,0:T(8,128)(2,1)S(1)}, bf16[1,32,4096]{2,1,0:T(8,128)(2,1)}, u32[]{:S(2)}) %copy-start.3) | copy-done | bytes 262168
  1.6 3.0 %collective-permute-start = (bf16[16,4096]{1,0:T(8,128)(2,1)S(1)}, bf16[16,4096]{1,0:T(8,128)(2,1)S(1)}, u32[]{:S(2)}, u32[]{:S(2)}) collective-permute-start(bf16[16,4096]{1,0:T(8,128)(2,1)S(1)} %get-tuple-element.52.refs_0_), channel_id=1, source_target_pairs={{0,2},{1,5},{2,6},{3,1},{6,10},{7,3},{10,14},{11,7},{14,12},{15,11... | collective-permute-start | bytes 393224 | tf_op jit(solution)/shard_map/ppermute | solution.py:539
  4.8 1.2 %residue_left.1 = (bf16[128,4096]{1,0:T(8,128)(2,1)S(1)}, f32[64,448]{1,0:T(8,128)S(1)}) custom-call(f32[64,4096]{1,0:T(8,128)S(1)} %copy-done.2, bf16[448,4096]{1,0:T(8,128)(2,1)S(1)} %bitcast.7), custom_call_target="tpu_custom_call" | custom-call | flops 2529999872 | tf_op jit(solution)/shard_map/residue_left/pallas_call | solution.py:84
  6.0 2.2 %collective-permute-start.8 = (bf16[16,4096]{1,0:T(8,128)(2,1)S(1)}, bf16[16,4096]{1,0:T(8,128)(2,1)S(1)}, u32[]{:S(2)}, u32[]{:S(2)}) collective-permute-start(bf16[16,4096]{1,0:T(8,128)(2,1)S(1)} %get-tuple-element.51.refs_1_), channel_id=1, source_target_pairs={{0,2},{1,5},{2,6},{3,1},{6,10},{7,3},{10,14},{11,7},{14,12},{15,11... | collective-permute-start | bytes 393224 | tf_op jit(solution)/shard_map/ppermute | solution.py:539
  8.5 1.7 %collective-permute-start.1 = (bf16[16,4096]{1,0:T(8,128)(2,1)S(1)}, bf16[16,4096]{1,0:T(8,128)(2,1)S(1)}, u32[]{:S(2)}, u32[]{:S(2)}) collective-permute-start(bf16[16,4096]{1,0:T(8,128)(2,1)S(1)} %collective-permute-done.refs_2_), channel_id=1, source_target_pairs={{0,2},{1,5},{2,6},{3,1},{6,10},{7,3},{10,14},{11,7},{14,12},{15,11... | collective-permute-start | bytes 393224 | tf_op jit(solution)/shard_map/ppermute | solution.py:539
  10.2 0.2 collective-permute-done.4.refs_3_
  10.4 0.5 collective-permute-start.5
  10.9 1.2 %collective-permute-done.8.refs_4_ = bf16[16,4096]{1,0:T(8,128)(2,1)S(1)} collective-permute-done((bf16[16,4096]{1,0:T(8,128)(2,1)S(1)}, bf16[16,4096]{1,0:T(8,128)(2,1)S(1)}, u32[]{:S(2)}, u32[]{:S(2)}) %collective-permute-start.8) | collective-permute-done | bytes 131104 | tf_op jit(solution)/shard_map/ppermute | solution.py:539
  12.1 2.5 %collective-permute-start.10 = (bf16[16,4096]{1,0:T(8,128)(2,1)S(1)}, bf16[16,4096]{1,0:T(8,128)(2,1)S(1)}, u32[]{:S(2)}, u32[]{:S(2)}) collective-permute-start(bf16[16,4096]{1,0:T(8,128)(2,1)S(1)} %collective-permute-done.8.refs_4_), channel_id=1, source_target_pairs={{0,2},{1,5},{2,6},{3,1},{6,10},{7,3},{10,14},{11,7},{14,12},{15,11... | collective-permute-start | bytes 393224 | tf_op jit(solution)/shard_map/ppermute | solution.py:539
  14.7 0.6 collective-permute-done.1.refs_6_
  15.3 1.5 %collective-permute-start.2 = (bf16[16,4096]{1,0:T(8,128)(2,1)S(1)}, bf16[16,4096]{1,0:T(8,128)(2,1)S(1)}, u32[]{:S(2)}, u32[]{:S(2)}) collective-permute-start(bf16[16,4096]{1,0:T(8,128)(2,1)S(1)} %collective-permute-done.1.refs_6_), channel_id=1, source_target_pairs={{0,2},{1,5},{2,6},{3,1},{6,10},{7,3},{10,14},{11,7},{14,12},{15,11... | collective-permute-start | bytes 393224 | tf_op jit(solution)/shard_map/ppermute | solution.py:539
  16.8 0.6 collective-permute-start.6
  17.5 0.9 %collective-permute-done.10.refs_8_ = bf16[16,4096]{1,0:T(8,128)(2,1)S(1)} collective-permute-done((bf16[16,4096]{1,0:T(8,128)(2,1)S(1)}, bf16[16,4096]{1,0:T(8,128)(2,1)S(1)}, u32[]{:S(2)}, u32[]{:S(2)}) %collective-permute-start.10) | collective-permute-done | bytes 131104 | tf_op jit(solution)/shard_map/ppermute | solution.py:539
  18.4 2.2 %collective-permute-start.12 = (bf16[16,4096]{1,0:T(8,128)(2,1)S(1)}, bf16[16,4096]{1,0:T(8,128)(2,1)S(1)}, u32[]{:S(2)}, u32[]{:S(2)}) collective-permute-start(bf16[16,4096]{1,0:T(8,128)(2,1)S(1)} %collective-permute-done.10.refs_8_), channel_id=1, source_target_pairs={{0,2},{1,5},{2,6},{3,1},{6,10},{7,3},{10,14},{11,7},{14,12},{15,11... | collective-permute-start | bytes 393224 | tf_op jit(solution)/shard_map/ppermute | solution.py:539
  20.8 0.7 %collective-permute-done.2.refs_10_ = bf16[16,4096]{1,0:T(8,128)(2,1)S(1)} collective-permute-done((bf16[16,4096]{1,0:T(8,128)(2,1)S(1)}, bf16[16,4096]{1,0:T(8,128)(2,1)S(1)}, u32[]{:S(2)}, u32[]{:S(2)}) %collective-permute-start.2) | collective-permute-done | bytes 131104 | tf_op jit(solution)/shard_map/ppermute | solution.py:539
  21.5 1.9 %collective-permute-start.3 = (bf16[16,4096]{1,0:T(8,128)(2,1)S(1)}, bf16[16,4096]{1,0:T(8,128)(2,1)S(1)}, u32[]{:S(2)}, u32[]{:S(2)}) collective-permute-start(bf16[16,4096]{1,0:T(8,128)(2,1)S(1)} %collective-permute-done.2.refs_10_), channel_id=1, source_target_pairs={{0,2},{1,5},{2,6},{3,1},{6,10},{7,3},{10,14},{11,7},{14,12},{15,11... | collective-permute-start | bytes 393224 | tf_op jit(solution)/shard_map/ppermute | solution.py:539
  23.5 0.4 collective-permute-start.7
  23.8 0.6 collective-permute-done.12.refs_12_
  24.4 1.2 %collective-permute-done.13.refs_13_ = bf16[16,4096]{1,0:T(8,128)(2,1)S(1)} collective-permute-done((bf16[16,4096]{1,0:T(8,128)(2,1)S(1)}, bf16[16,4096]{1,0:T(8,128)(2,1)S(1)}, u32[]{:S(2)}, u32[]{:S(2)}) %collective-permute-start.13) | collective-permute-done | bytes 131104 | tf_op jit(solution)/shard_map/ppermute | solution.py:539
  25.6 1.9 %early_left.1 = (bf16[256,4096]{1,0:T(8,128)(2,1)S(1)}, bf16[256,448]{1,0:T(8,128)(2,1)S(1)}, f32[64,448]{1,0:T(8,128)S(1)}) custom-call(s32[16,16]{1,0:T(8,128)S(1)} %copy-done.4, bf16[16,4096]{1,0:T(8,128)(2,1)S(1)} %get-tuple-element.52.refs_0_, bf16[16,4096]{1,0:T(8,128)(2,1)S(1)} %get-tuple-element.51.refs_1_, ...), custom_call_target="tpu_custom_call" | custom-call | flops 2300000000 | tf_op jit(solution)/shard_map/early_left/pallas_call | solution.py:118
  27.5 0.9 %collective-permute-done.7.second = bf16[16,4096]{1,0:T(8,128)(2,1)S(1)} collective-permute-done((bf16[16,4096]{1,0:T(8,128)(2,1)S(1)}, bf16[16,4096]{1,0:T(8,128)(2,1)S(1)}, u32[]{:S(2)}, u32[]{:S(2)}) %collective-permute-start.7) | collective-permute-done | bytes 131104 | tf_op jit(solution)/shard_map/ppermute | solution.py:539
  28.4 1.3 %late_left.1 = (bf16[256,4096]{1,0:T(8,128)(2,1)S(1)}, f32[64,448]{1,0:T(8,128)S(1)}) custom-call(s32[16,16]{1,0:T(8,128)S(1)} %copy-done.4, bf16[16,4096]{1,0:T(8,128)(2,1)S(1)} %collective-permute-done.3.first, bf16[16,4096]{1,0:T(8,128)(2,1)S(1)} %collective-permute-done.7.second, ...), custom_call_target="tpu_custom_call", output_to_operand_aliasing={{0}: (6, {})} | custom-call | flops 1150000000 | tf_op jit(solution)/shard_map/late_left/pallas_call | solution.py:150
  29.8 1.3 %collective-permute-done.14.other_l = f32[64,448]{1,0:T(8,128)S(1)} collective-permute-done((f32[64,448]{1,0:T(8,128)S(1)}, f32[64,448]{1,0:T(8,128)S(1)}, u32[]{:S(2)}, u32[]{:S(2)}) %collective-permute-start.14) | collective-permute-done | bytes 114720 | tf_op jit(solution)/shard_map/ppermute | solution.py:552
  31.1 0.5 given_far.1
  31.7 0.2 collective-permute-start.17
  31.9 0.6 near_terms.1
  32.5 0.4 collective-permute-start.15
  32.9 0.5 kept_far.1
  33.5 1.8 %collective-permute-start.18 = (f32[72,512]{1,0:T(8,128)S(1)}, f32[72,512]{1,0:T(8,128)S(1)}, u32[]{:S(2)}, u32[]{:S(2)}) collective-permute-start(f32[72,512]{1,0:T(8,128)S(1)} %get-tuple-element.71), channel_id=1, source_target_pairs={{0,2},{1,3},{2,0},{3,1},{4,6},{5,7},{6,4},{7,5},{8,10},{9,11},{10,... | collective-permute-start | bytes 442376 | tf_op jit(solution)/shard_map/ppermute | solution.py:570
  35.4 0.7 collective-permute-start.16
  36.0 3.4 %collective-permute-done.18.b = f32[72,512]{1,0:T(8,128)S(1)} collective-permute-done((f32[72,512]{1,0:T(8,128)S(1)}, f32[72,512]{1,0:T(8,128)S(1)}, u32[]{:S(2)}, u32[]{:S(2)}) %collective-permute-start.18) | collective-permute-done | bytes 147488 | tf_op jit(solution)/shard_map/ppermute | solution.py:570
  39.5 2.7 %collective-permute-start.20 = (f32[72,512]{1,0:T(8,128)S(1)}, f32[72,512]{1,0:T(8,128)S(1)}, u32[]{:S(2)}, u32[]{:S(2)}) collective-permute-start(f32[72,512]{1,0:T(8,128)S(1)} %added.1), channel_id=1, source_target_pairs={{0,8},{1,13},{2,10},{3,15},{4,12},{5,9},{6,14},{7,11},{8,0},{9,5},... | collective-permute-start | bytes 442376 | tf_op jit(solution)/shard_map/ppermute | solution.py:570
  42.1 1.7 %collective-permute-start.19 = (f32[72,512]{1,0:T(8,128)S(1)}, f32[72,512]{1,0:T(8,128)S(1)}, u32[]{:S(2)}, u32[]{:S(2)}) collective-permute-start(f32[72,512]{1,0:T(8,128)S(1)} %get-tuple-element.72), channel_id=1, source_target_pairs={{0,2},{1,7},{2,0},{3,5},{4,6},{5,3},{6,4},{7,1},{8,10},{9,15},{10,... | collective-permute-start | bytes 442376 | tf_op jit(solution)/shard_map/ppermute | solution.py:570
  43.9 1.1 %merged.1 = f32[448,4096]{1,0:T(8,128)S(1)} custom-call(bf16[448,256]{1,0:T(8,128)(2,1)S(1)} %bitcast.14, bf16[448,4096]{1,0:T(8,128)(2,1)S(1)} %bitcast.11, bf16[256,4096]{1,0:T(8,128)(2,1)S(1)} %get-tuple-element.67.tokens), custom_call_target="tpu_custom_call" | custom-call | flops 57500000 | tf_op jit(solution)/shard_map/merged/pallas_call | solution.py:272
  45.0 4.1 %collective-permute-done.20.refs_1_ = f32[72,512]{1,0:T(8,128)S(1)} collective-permute-done((f32[72,512]{1,0:T(8,128)S(1)}, f32[72,512]{1,0:T(8,128)S(1)}, u32[]{:S(2)}, u32[]{:S(2)}) %collective-permute-start.20) | collective-permute-done | bytes 147488 | tf_op jit(solution)/shard_map/ppermute | solution.py:570
  49.2 1.4 %collective-permute-done.21.other = f32[72,512]{1,0:T(8,128)S(1)} collective-permute-done((f32[72,512]{1,0:T(8,128)S(1)}, f32[72,512]{1,0:T(8,128)S(1)}, u32[]{:S(2)}, u32[]{:S(2)}) %collective-permute-start.21) | collective-permute-done | bytes 147488 | tf_op jit(solution)/shard_map/ppermute | solution.py:552
  50.7 0.7 %collective-permute-start.24 = (f32[64,512]{1,0:T(8,128)S(1)}, f32[64,512]{1,0:T(8,128)S(1)}, u32[]{:S(2)}, u32[]{:S(2)}) collective-permute-start(f32[64,512]{1,0:T(8,128)S(1)} %get-tuple-element.74.share), channel_id=1, source_target_pairs={{0,8},{1,13},{2,10},{3,15},{4,12},{5,9},{6,14},{7,11},{8,0},{9,5},... | collective-permute-start | bytes 393224 | tf_op jit(solution)/shard_map/ppermute | solution.py:570
  51.4 0.7 collective-permute-start.23
  52.1 1.7 %collective-permute-start.22 = (f32[64,512]{1,0:T(8,128)S(1)}, f32[64,512]{1,0:T(8,128)S(1)}, u32[]{:S(2)}, u32[]{:S(2)}) collective-permute-start(f32[64,512]{1,0:T(8,128)S(1)} %get-tuple-element.74.share), channel_id=1, source_target_pairs={{0,2},{1,7},{2,0},{3,5},{4,6},{5,3},{6,4},{7,1},{8,10},{9,15},{10,... | collective-permute-start | bytes 393224 | tf_op jit(solution)/shard_map/ppermute | solution.py:570
  53.8 5.4 %collective-permute-done.24.refs_0_ = f32[64,512]{1,0:T(8,128)S(1)} collective-permute-done((f32[64,512]{1,0:T(8,128)S(1)}, f32[64,512]{1,0:T(8,128)S(1)}, u32[]{:S(2)}, u32[]{:S(2)}) %collective-permute-start.24) | collective-permute-done | bytes 131104 | tf_op jit(solution)/shard_map/ppermute | solution.py:570
  59.1 1.5 %collective-permute-start.25 = (f32[64,512]{1,0:T(8,128)S(1)}, f32[64,512]{1,0:T(8,128)S(1)}, u32[]{:S(2)}, u32[]{:S(2)}) collective-permute-start(f32[64,512]{1,0:T(8,128)S(1)} %collective-permute-done.24.refs_0_), channel_id=1, source_target_pairs={{0,2},{1,3},{2,0},{3,1},{4,6},{5,7},{6,4},{7,5},{8,10},{9,11},{10,... | collective-permute-start | bytes 393224 | tf_op jit(solution)/shard_map/ppermute | solution.py:570
  60.6 1.8 %cholesky_inverse.1.inverse = f32[64,64]{1,0:T(8,128)S(1)} custom-call(f32[64,64]{1,0:T(8,128)S(1)} %get-tuple-element.75.gram), custom_call_target="tpu_custom_call" | custom-call | flops 5750000128 | tf_op jit(solution)/shard_map/cholesky_inverse/pallas_call | solution.py:420
  62.4 0.8 %last_operand.1.lhs = bf16[512,256]{1,0:T(8,128)(2,1)S(1)} custom-call(f32[64,64]{1,0:T(8,128)S(1)} %cholesky_inverse.1.inverse, f32[64,448]{1,0:T(8,128)S(1)} %get-tuple-element.63.left_sum), custom_call_target="tpu_custom_call" | custom-call | flops 57500000 | tf_op jit(solution)/shard_map/last_operand/pallas_call | solution.py:451
  63.2 1.5 %finish.3 = (bf16[448,4096]{1,0:T(8,128)(2,1)}, f32[64,4096]{1,0:T(8,128)}) custom-call(f32[3,64,512]{2,1,0:T(8,128)S(1)} %joined.1.shares, bf16[512,256]{1,0:T(8,128)(2,1)S(1)} %last_operand.1.lhs, f32[448,4096]{1,0:T(8,128)S(1)} %merged.1), custom_call_target="tpu_custom_call" | custom-call | flops 57500000 | tf_op jit(solution)/shard_map/finish/pallas_call | solution.py:489
  64.8 0.3 collective-permute-start.26
  65.2 1.1 %finish.4 = (bf16[448,4096]{1,0:T(8,128)(2,1)}, f32[64,4096]{1,0:T(8,128)}) custom-call(f32[1,64,512]{2,1,0:T(8,128)S(1)} %bitcast.16, bf16[512,256]{1,0:T(8,128)(2,1)S(1)} %last_operand.1.lhs, f32[448,4096]{1,0:T(8,128)S(1)} %merged.1, bf16[448,4096]{1,0:T(8,128)(2,1)} %get-tuple-element.84.refs_0_, ...), custom_call_target="tpu_custom_call", output_to_operand_aliasing={{0}: (3, {}), {1}: (4, {})} | custom-call | flops 57500000 | tf_op jit(solution)/shard_map/finish/pallas_call | solution.py:489
  66.3 0.5 collective-permute-done.26.shares
  66.8 1.7 %finish.5 = (bf16[448,4096]{1,0:T(8,128)(2,1)}, f32[64,4096]{1,0:T(8,128)}) custom-call(f32[4,64,512]{2,1,0:T(8,128)S(1)} %collective-permute-done.26.shares, bf16[512,256]{1,0:T(8,128)(2,1)S(1)} %last_operand.1.lhs, f32[448,4096]{1,0:T(8,128)S(1)} %merged.1, ...), custom_call_target="tpu_custom_call", output_to_operand_aliasing={{0}: (3, {}), {1}: (4, {})} | custom-call | flops 57500000 | tf_op jit(solution)/shard_map/finish/pallas_call | solution.py:489
  (36 shorter events, 1.3 us)
Async XLA Ops:
  0.6 1.0 %copy-start.3 = (bf16[1,32,4096]{2,1,0:T(8,128)(2,1)S(1)}, bf16[1,32,4096]{2,1,0:T(8,128)(2,1)}, u32[]{:S(2)}) copy-start(bf16[1,32,4096]{2,1,0:T(8,128)(2,1)} %param.5) | copy-start | bytes 786436
  1.6 3.2 %copy-start = (bf16[1,448,4096]{2,1,0:T(8,128)(2,1)S(1)}, bf16[1,448,4096]{2,1,0:T(8,128)(2,1)}, u32[]{:S(2)}) copy-start(bf16[1,448,4096]{2,1,0:T(8,128)(2,1)} %param.7) | copy-start | bytes 11010052
  1.6 3.2 %copy-start.2 = (f32[64,4096]{1,0:T(8,128)S(1)}, f32[64,4096]{1,0:T(8,128)}, u32[]{:S(2)}) copy-start(f32[64,4096]{1,0:T(8,128)} %right.1) | copy-start | bytes 3145732
  1.6 6.9 %collective-permute-start = (bf16[16,4096]{1,0:T(8,128)(2,1)S(1)}, bf16[16,4096]{1,0:T(8,128)(2,1)S(1)}, u32[]{:S(2)}, u32[]{:S(2)}) collective-permute-start(bf16[16,4096]{1,0:T(8,128)(2,1)S(1)} %get-tuple-element.52.refs_0_), channel_id=1, source_target_pairs={{0,2},{1,5},{2,6},{3,1},{6,10},{7,3},{10,14},{11,7},{14,12},{15,11... | collective-permute-start | bytes 393224 | tf_op jit(solution)/shard_map/ppermute | solution.py:539
  4.6 5.8 %collective-permute-start.4 = (bf16[16,4096]{1,0:T(8,128)(2,1)S(1)}, bf16[16,4096]{1,0:T(8,128)(2,1)S(1)}, u32[]{:S(2)}, u32[]{:S(2)}) collective-permute-start(bf16[16,4096]{1,0:T(8,128)(2,1)S(1)} %get-tuple-element.51.refs_1_), channel_id=1, source_target_pairs={{0,4},{1,3},{2,0},{3,7},{6,2},{7,11},{10,6},{11,15},{14,10},{15,13... | collective-permute-start | bytes 393224 | tf_op jit(solution)/shard_map/ppermute | solution.py:539
  4.8 20.9 %copy-start.1 = (bf16[1,256,448]{1,2,0:T(8,128)(2,1)S(1)}, bf16[1,256,448]{1,2,0:T(8,128)(2,1)}, u32[]{:S(2)}) copy-start(bf16[1,256,448]{1,2,0:T(8,128)(2,1)} %param.6) | copy-start | bytes 688132
  4.8 20.9 %copy-start.4 = (s32[16,16]{1,0:T(8,128)S(1)}, s32[16,16]{1,0:T(8,128)}, u32[]{:S(2)}) copy-start(s32[16,16]{1,0:T(8,128)} %constant.2.clone.places) | copy-start | bytes 3076
  6.0 6.1 %collective-permute-start.8 = (bf16[16,4096]{1,0:T(8,128)(2,1)S(1)}, bf16[16,4096]{1,0:T(8,128)(2,1)S(1)}, u32[]{:S(2)}, u32[]{:S(2)}) collective-permute-start(bf16[16,4096]{1,0:T(8,128)(2,1)S(1)} %get-tuple-element.51.refs_1_), channel_id=1, source_target_pairs={{0,2},{1,5},{2,6},{3,1},{6,10},{7,3},{10,14},{11,7},{14,12},{15,11... | collective-permute-start | bytes 393224 | tf_op jit(solution)/shard_map/ppermute | solution.py:539
  8.2 6.4 %collective-permute-start.9 = (bf16[16,4096]{1,0:T(8,128)(2,1)S(1)}, bf16[16,4096]{1,0:T(8,128)(2,1)S(1)}, u32[]{:S(2)}, u32[]{:S(2)}) collective-permute-start(bf16[16,4096]{1,0:T(8,128)(2,1)S(1)} %get-tuple-element.52.refs_0_), channel_id=1, source_target_pairs={{0,4},{1,3},{2,0},{3,7},{6,2},{7,11},{10,6},{11,15},{14,10},{15,13... | collective-permute-start | bytes 393224 | tf_op jit(solution)/shard_map/ppermute | solution.py:539
  8.5 6.8 %collective-permute-start.1 = (bf16[16,4096]{1,0:T(8,128)(2,1)S(1)}, bf16[16,4096]{1,0:T(8,128)(2,1)S(1)}, u32[]{:S(2)}, u32[]{:S(2)}) collective-permute-start(bf16[16,4096]{1,0:T(8,128)(2,1)S(1)} %collective-permute-done.refs_2_), channel_id=1, source_target_pairs={{0,2},{1,5},{2,6},{3,1},{6,10},{7,3},{10,14},{11,7},{14,12},{15,11... | collective-permute-start | bytes 393224 | tf_op jit(solution)/shard_map/ppermute | solution.py:539
  10.4 6.4 %collective-permute-start.5 = (bf16[16,4096]{1,0:T(8,128)(2,1)S(1)}, bf16[16,4096]{1,0:T(8,128)(2,1)S(1)}, u32[]{:S(2)}, u32[]{:S(2)}) collective-permute-start(bf16[16,4096]{1,0:T(8,128)(2,1)S(1)} %collective-permute-done.4.refs_3_), channel_id=1, source_target_pairs={{0,4},{1,3},{2,0},{3,7},{6,2},{7,11},{10,6},{11,15},{14,10},{15,13... | collective-permute-start | bytes 393224 | tf_op jit(solution)/shard_map/ppermute | solution.py:539
  12.1 6.4 %collective-permute-start.10 = (bf16[16,4096]{1,0:T(8,128)(2,1)S(1)}, bf16[16,4096]{1,0:T(8,128)(2,1)S(1)}, u32[]{:S(2)}, u32[]{:S(2)}) collective-permute-start(bf16[16,4096]{1,0:T(8,128)(2,1)S(1)} %collective-permute-done.8.refs_4_), channel_id=1, source_target_pairs={{0,2},{1,5},{2,6},{3,1},{6,10},{7,3},{10,14},{11,7},{14,12},{15,11... | collective-permute-start | bytes 393224 | tf_op jit(solution)/shard_map/ppermute | solution.py:539
  14.5 6.1 %collective-permute-start.11 = (bf16[16,4096]{1,0:T(8,128)(2,1)S(1)}, bf16[16,4096]{1,0:T(8,128)(2,1)S(1)}, u32[]{:S(2)}, u32[]{:S(2)}) collective-permute-start(bf16[16,4096]{1,0:T(8,128)(2,1)S(1)} %collective-permute-done.9.refs_5_), channel_id=1, source_target_pairs={{0,4},{1,3},{2,0},{3,7},{6,2},{7,11},{10,6},{11,15},{14,10},{15,13... | collective-permute-start | bytes 393224 | tf_op jit(solution)/shard_map/ppermute | solution.py:539
  15.3 6.2 %collective-permute-start.2 = (bf16[16,4096]{1,0:T(8,128)(2,1)S(1)}, bf16[16,4096]{1,0:T(8,128)(2,1)S(1)}, u32[]{:S(2)}, u32[]{:S(2)}) collective-permute-start(bf16[16,4096]{1,0:T(8,128)(2,1)S(1)} %collective-permute-done.1.refs_6_), channel_id=1, source_target_pairs={{0,2},{1,5},{2,6},{3,1},{6,10},{7,3},{10,14},{11,7},{14,12},{15,11... | collective-permute-start | bytes 393224 | tf_op jit(solution)/shard_map/ppermute | solution.py:539
  16.8 6.6 %collective-permute-start.6 = (bf16[16,4096]{1,0:T(8,128)(2,1)S(1)}, bf16[16,4096]{1,0:T(8,128)(2,1)S(1)}, u32[]{:S(2)}, u32[]{:S(2)}) collective-permute-start(bf16[16,4096]{1,0:T(8,128)(2,1)S(1)} %collective-permute-done.5.refs_7_), channel_id=1, source_target_pairs={{0,4},{1,3},{2,0},{3,7},{6,2},{7,11},{10,6},{11,15},{14,10},{15,13... | collective-permute-start | bytes 393224 | tf_op jit(solution)/shard_map/ppermute | solution.py:539
  18.4 6.0 %collective-permute-start.12 = (bf16[16,4096]{1,0:T(8,128)(2,1)S(1)}, bf16[16,4096]{1,0:T(8,128)(2,1)S(1)}, u32[]{:S(2)}, u32[]{:S(2)}) collective-permute-start(bf16[16,4096]{1,0:T(8,128)(2,1)S(1)} %collective-permute-done.10.refs_8_), channel_id=1, source_target_pairs={{0,2},{1,5},{2,6},{3,1},{6,10},{7,3},{10,14},{11,7},{14,12},{15,11... | collective-permute-start | bytes 393224 | tf_op jit(solution)/shard_map/ppermute | solution.py:539
  20.7 5.0 %collective-permute-start.13 = (bf16[16,4096]{1,0:T(8,128)(2,1)S(1)}, bf16[16,4096]{1,0:T(8,128)(2,1)S(1)}, u32[]{:S(2)}, u32[]{:S(2)}) collective-permute-start(bf16[16,4096]{1,0:T(8,128)(2,1)S(1)} %collective-permute-done.11.refs_9_), channel_id=1, source_target_pairs={{0,4},{1,3},{2,0},{3,7},{6,2},{7,11},{10,6},{11,15},{14,10},{15,13... | collective-permute-start | bytes 393224 | tf_op jit(solution)/shard_map/ppermute | solution.py:539
  21.5 6.0 %collective-permute-start.3 = (bf16[16,4096]{1,0:T(8,128)(2,1)S(1)}, bf16[16,4096]{1,0:T(8,128)(2,1)S(1)}, u32[]{:S(2)}, u32[]{:S(2)}) collective-permute-start(bf16[16,4096]{1,0:T(8,128)(2,1)S(1)} %collective-permute-done.2.refs_10_), channel_id=1, source_target_pairs={{0,2},{1,5},{2,6},{3,1},{6,10},{7,3},{10,14},{11,7},{14,12},{15,11... | collective-permute-start | bytes 393224 | tf_op jit(solution)/shard_map/ppermute | solution.py:539
  23.5 5.0 %collective-permute-start.7 = (bf16[16,4096]{1,0:T(8,128)(2,1)S(1)}, bf16[16,4096]{1,0:T(8,128)(2,1)S(1)}, u32[]{:S(2)}, u32[]{:S(2)}) collective-permute-start(bf16[16,4096]{1,0:T(8,128)(2,1)S(1)} %collective-permute-done.6.refs_11_), channel_id=1, source_target_pairs={{0,4},{1,3},{2,0},{3,7},{6,2},{7,11},{10,6},{11,15},{14,10},{15,13... | collective-permute-start | bytes 393224 | tf_op jit(solution)/shard_map/ppermute | solution.py:539
  29.7 1.4 %collective-permute-start.14 = (f32[64,448]{1,0:T(8,128)S(1)}, f32[64,448]{1,0:T(8,128)S(1)}, u32[]{:S(2)}, u32[]{:S(2)}) collective-permute-start(f32[64,448]{1,0:T(8,128)S(1)} %get-tuple-element.57.here_l), channel_id=1, source_target_pairs={{0,1},{1,0},{2,3},{3,2},{4,5},{5,4},{6,7},{7,6},{8,9},{9,8},{10,11... | collective-permute-start | bytes 344072 | tf_op jit(solution)/shard_map/ppermute | solution.py:552
  31.7 1.7 %collective-permute-start.17 = (f32[2,64,512]{2,1,0:T(8,128)S(1)}, f32[2,64,512]{2,1,0:T(8,128)S(1)}, u32[]{:S(2)}, u32[]{:S(2)}) collective-permute-start(f32[2,64,512]{2,1,0:T(8,128)S(1)} %get-tuple-element.70), channel_id=1, source_target_pairs={{0,1},{1,0},{2,3},{3,2},{4,5},{5,4},{6,7},{7,6},{8,9},{9,8},{10,11... | collective-permute-start | bytes 786440 | tf_op jit(solution)/shard_map/ppermute | solution.py:552
  32.5 2.8 %collective-permute-start.15 = (f32[2,64,512]{2,1,0:T(8,128)S(1)}, f32[2,64,512]{2,1,0:T(8,128)S(1)}, u32[]{:S(2)}, u32[]{:S(2)}) collective-permute-start(f32[2,64,512]{2,1,0:T(8,128)S(1)} %get-tuple-element.62), channel_id=1, source_target_pairs={{0,1},{1,0},{2,3},{3,2},{4,5},{5,4},{6,7},{7,6},{8,9},{9,8},{10,11... | collective-permute-start | bytes 786440 | tf_op jit(solution)/shard_map/ppermute | solution.py:552
  33.5 6.0 %collective-permute-start.18 = (f32[72,512]{1,0:T(8,128)S(1)}, f32[72,512]{1,0:T(8,128)S(1)}, u32[]{:S(2)}, u32[]{:S(2)}) collective-permute-start(f32[72,512]{1,0:T(8,128)S(1)} %get-tuple-element.71), channel_id=1, source_target_pairs={{0,2},{1,3},{2,0},{3,1},{4,6},{5,7},{6,4},{7,5},{8,10},{9,11},{10,... | collective-permute-start | bytes 442376 | tf_op jit(solution)/shard_map/ppermute | solution.py:570
  35.4 9.7 %collective-permute-start.16 = (f32[72,512]{1,0:T(8,128)S(1)}, f32[72,512]{1,0:T(8,128)S(1)}, u32[]{:S(2)}, u32[]{:S(2)}) collective-permute-start(f32[72,512]{1,0:T(8,128)S(1)} %get-tuple-element.65.own), channel_id=1, source_target_pairs={{1,5},{3,7},{5,1},{7,3},{9,13},{11,15},{13,9},{15,11},{17,21},{19,... | collective-permute-start | bytes 442376 | tf_op jit(solution)/shard_map/ppermute | solution.py:570
  39.5 9.6 %collective-permute-start.20 = (f32[72,512]{1,0:T(8,128)S(1)}, f32[72,512]{1,0:T(8,128)S(1)}, u32[]{:S(2)}, u32[]{:S(2)}) collective-permute-start(f32[72,512]{1,0:T(8,128)S(1)} %added.1), channel_id=1, source_target_pairs={{0,8},{1,13},{2,10},{3,15},{4,12},{5,9},{6,14},{7,11},{8,0},{9,5},... | collective-permute-start | bytes 442376 | tf_op jit(solution)/shard_map/ppermute | solution.py:570
  42.1 7.0 %collective-permute-start.19 = (f32[72,512]{1,0:T(8,128)S(1)}, f32[72,512]{1,0:T(8,128)S(1)}, u32[]{:S(2)}, u32[]{:S(2)}) collective-permute-start(f32[72,512]{1,0:T(8,128)S(1)} %get-tuple-element.72), channel_id=1, source_target_pairs={{0,2},{1,7},{2,0},{3,5},{4,6},{5,3},{6,4},{7,1},{8,10},{9,15},{10,... | collective-permute-start | bytes 442376 | tf_op jit(solution)/shard_map/ppermute | solution.py:570
  49.2 1.4 %collective-permute-start.21 = (f32[72,512]{1,0:T(8,128)S(1)}, f32[72,512]{1,0:T(8,128)S(1)}, u32[]{:S(2)}, u32[]{:S(2)}) collective-permute-start(f32[72,512]{1,0:T(8,128)S(1)} %core_sum.1.here), channel_id=1, source_target_pairs={{0,1},{1,0},{2,3},{3,2},{4,5},{5,4},{6,7},{7,6},{8,9},{9,8},{10,11... | collective-permute-start | bytes 442376 | tf_op jit(solution)/shard_map/ppermute | solution.py:552
  50.7 8.5 %collective-permute-start.24 = (f32[64,512]{1,0:T(8,128)S(1)}, f32[64,512]{1,0:T(8,128)S(1)}, u32[]{:S(2)}, u32[]{:S(2)}) collective-permute-start(f32[64,512]{1,0:T(8,128)S(1)} %get-tuple-element.74.share), channel_id=1, source_target_pairs={{0,8},{1,13},{2,10},{3,15},{4,12},{5,9},{6,14},{7,11},{8,0},{9,5},... | collective-permute-start | bytes 393224 | tf_op jit(solution)/shard_map/ppermute | solution.py:570
  51.4 11.0 %collective-permute-start.23 = (f32[64,512]{1,0:T(8,128)S(1)}, f32[64,512]{1,0:T(8,128)S(1)}, u32[]{:S(2)}, u32[]{:S(2)}) collective-permute-start(f32[64,512]{1,0:T(8,128)S(1)} %get-tuple-element.74.share), channel_id=1, source_target_pairs={{1,5},{3,7},{5,1},{7,3},{9,13},{11,15},{13,9},{15,11},{17,21},{19,... | collective-permute-start | bytes 393224 | tf_op jit(solution)/shard_map/ppermute | solution.py:570
  52.1 10.3 %collective-permute-start.22 = (f32[64,512]{1,0:T(8,128)S(1)}, f32[64,512]{1,0:T(8,128)S(1)}, u32[]{:S(2)}, u32[]{:S(2)}) collective-permute-start(f32[64,512]{1,0:T(8,128)S(1)} %get-tuple-element.74.share), channel_id=1, source_target_pairs={{0,2},{1,7},{2,0},{3,5},{4,6},{5,3},{6,4},{7,1},{8,10},{9,15},{10,... | collective-permute-start | bytes 393224 | tf_op jit(solution)/shard_map/ppermute | solution.py:570
  59.1 5.6 %collective-permute-start.25 = (f32[64,512]{1,0:T(8,128)S(1)}, f32[64,512]{1,0:T(8,128)S(1)}, u32[]{:S(2)}, u32[]{:S(2)}) collective-permute-start(f32[64,512]{1,0:T(8,128)S(1)} %collective-permute-done.24.refs_0_), channel_id=1, source_target_pairs={{0,2},{1,3},{2,0},{3,1},{4,6},{5,7},{6,4},{7,5},{8,10},{9,11},{10,... | collective-permute-start | bytes 393224 | tf_op jit(solution)/shard_map/ppermute | solution.py:570
  64.8 2.0 %collective-permute-start.26 = (f32[4,64,512]{2,1,0:T(8,128)S(1)}, f32[4,64,512]{2,1,0:T(8,128)S(1)}, u32[]{:S(2)}, u32[]{:S(2)}) collective-permute-start(f32[4,64,512]{2,1,0:T(8,128)S(1)} %pad_maximum_fusion), channel_id=1, source_target_pairs={{0,1},{1,0},{2,3},{3,2},{4,5},{5,4},{6,7},{7,6},{8,9},{9,8},{10,11... | collective-permute-start | bytes 1572872 | tf_op jit(solution)/shard_map/ppermute | solution.py:552

commit v6 on v5

--- a/solution.py
+++ b/solution.py
@@ -280,78 +280,98 @@
     )(hidden_t, feedback, tokens)
 
 
-def message_kernel(keep, got, gram, *messages):
+def put_message(message, value, gram):
+    rank = gram.shape[0]
+    blocks = value.shape[1] // rank
+    rows = rank // blocks
+    message[:rank, :] = value
+    for block in range(blocks):
+        message[rank:, block * rank : (block + 1) * rank] = gram[block * rows : (block + 1) * rows, :]
+
+
+def begin_kernel(keep, got, gram, *messages):
+    core = lax.axis_index("dp")
+    for pair, message in enumerate(messages):
+        index = 2 * pair + core
+        put_message(message, keep[index] + got[index], gram)
+
+
+def begin_messages(keep, got, gram):
     rank, cols = keep.shape[1:]
-    blocks = cols // rank
-    rows = rank // blocks
-    for index, message in enumerate(messages):
-        message[:rank, :] = keep[index] + got[index]
-        for block in range(blocks):
-            message[rank:, block * rank : (block + 1) * rank] = gram[block * rows : (block + 1) * rows, :]
-
-
-def messages_for(keep, got, gram):
-    places, rank, cols = keep.shape
+    pairs = keep.shape[0] // 2
     rows = rank + rank // (cols // rank)
     return pl.pallas_call(
-        message_kernel,
+        begin_kernel,
         in_specs=[pl.BlockSpec(memory_space=pltpu.VMEM)] * 3,
-        out_specs=[pl.BlockSpec(memory_space=pltpu.VMEM)] * places,
-        out_shape=[jax.ShapeDtypeStruct((rows, cols), F32)] * places,
-        compiler_params=params(),
-        cost_estimate=cost(SMALL),
-        name="messages",
+        out_specs=[pl.BlockSpec(memory_space=pltpu.VMEM)] * pairs,
+        out_shape=[jax.ShapeDtypeStruct((rows, cols), F32)] * pairs,
+        compiler_params=params(),
+        cost_estimate=cost(SMALL),
+        name="begin_messages",
     )(keep, got, gram)
 
 
-def add_kernel(a, b, total):
-    total[...] = a[...] + b[...]
-
-
-def added(a, b):
-    return pl.pallas_call(
-        add_kernel,
+def rest_kernel(keep_far, got_far, keep, got, gram, own, beside, *messages):
+    first = lax.axis_index("dp") == 0
+    put_message(own, keep[0] + got[0], gram)
+    put_message(beside, keep[1] + got[1], gram)
+    for pair in range(len(messages) // 2):
+        direct = keep_far[2 * pair + 1] + got_far[2 * pair + 1]
+        crossing = keep_far[2 * pair] + got_far[2 * pair]
+        if pair == 0:
+            direct = jnp.where(first, direct, keep[0] + got[0])
+            crossing = jnp.where(first, keep[1] + got[1], crossing)
+        put_message(messages[2 * pair], direct, gram)
+        put_message(messages[2 * pair + 1], crossing, gram)
+
+
+def rest_messages(keep_far, got_far, keep, got, gram):
+    rank, cols = keep.shape[1:]
+    count = 2 + keep_far.shape[0]
+    rows = rank + rank // (cols // rank)
+    own, beside, *messages = pl.pallas_call(
+        rest_kernel,
+        in_specs=[pl.BlockSpec(memory_space=pltpu.VMEM)] * 5,
+        out_specs=[pl.BlockSpec(memory_space=pltpu.VMEM)] * count,
+        out_shape=[jax.ShapeDtypeStruct((rows, cols), F32)] * count,
+        compiler_params=params(),
+        cost_estimate=cost(SMALL),
+        name="rest_messages",
+    )(keep_far, got_far, keep, got, gram)
+    return own, beside, messages[::2], messages[1::2]
+
+
+def cross_kernel(message, passed, total):
+    total[...] = message[...] + jnp.where(lax.axis_index("dp") == 0, 0.0, passed[...])
+
+
+def crossing(message, passed):
+    return pl.pallas_call(
+        cross_kernel,
         in_specs=[pl.BlockSpec(memory_space=pltpu.VMEM)] * 2,
         out_specs=pl.BlockSpec(memory_space=pltpu.VMEM),
-        out_shape=jax.ShapeDtypeStruct(a.shape, a.dtype),
-        compiler_params=params(),
-        cost_estimate=cost(SMALL),
-        name="added",
-    )(a, b)
-
-
-def join_kernel(share, second, first, *refs):
-    across, mine = refs[:-1], refs[-1]
-    mine[0] = jnp.where(lax.axis_index("dp") == 0, share[...], second[...])
-    mine[1] = first[...]
-    for index, value in enumerate(across):
-        mine[index + 2] = value[...]
-
-
-def joined(share, second, first, across):
-    operands = [share, second, first, *across]
-    return pl.pallas_call(
-        join_kernel,
-        in_specs=[pl.BlockSpec(memory_space=pltpu.VMEM)] * len(operands),
-        out_specs=pl.BlockSpec(memory_space=pltpu.VMEM),
-        out_shape=jax.ShapeDtypeStruct((len(operands) - 1, *share.shape), F32),
-        compiler_params=params(),
-        cost_estimate=cost(SMALL),
-        name="joined",
-    )(*operands)
-
-
-def core_sum_kernel(own, second, *refs):
+        out_shape=jax.ShapeDtypeStruct(message.shape, F32),
+        compiler_params=params(),
+        cost_estimate=cost(SMALL),
+        name="crossing",
+    )(message, passed)
+
+
+def core_sum_kernel(own, third, *refs):
     messages, total = refs[:-1], refs[-1]
-    first = jnp.where(lax.axis_index("dp") == 0, own[...], second[...])
-    parts = [first + messages[0][...]] + [message[...] for message in messages[1:]]
+    pairs = len(messages) // 3
+    begun, direct, crossed = messages[:pairs], messages[pairs : 2 * pairs], messages[2 * pairs :]
+    first = lax.axis_index("dp") == 0
+    parts = [jnp.where(first, own[...] + crossed[0][...], direct[0][...] + third[...])]
+    for pair in range(pairs):
+        parts.append(jnp.where(first, begun[pair][...] + direct[pair][...], crossed[pair][...]))
     while len(parts) > 1:
         parts = [a + b for a, b in zip(parts[::2], parts[1::2])]
     total[...] = parts[0]
 
 
-def core_sum(own, first, second, across):
-    operands = [own, first, second, *across]
+def core_sum(own, third, begun, direct, crossed):
+    operands = [own, third, *begun, *direct, *crossed]
     return pl.pallas_call(
         core_sum_kernel,
         in_specs=[pl.BlockSpec(memory_space=pltpu.VMEM)] * len(operands),
@@ -360,6 +380,46 @@
         compiler_params=params(),
         cost_estimate=cost(SMALL),
         name="core_sum",
+    )(*operands)
+
+
+def choose_kernel(here, there, chosen):
+    chosen[...] = jnp.where(lax.axis_index("dp") == 0, here[...], there[...])
+
+
+def by_core(here, there):
+    return pl.pallas_call(
+        choose_kernel,
+        in_specs=[pl.BlockSpec(memory_space=pltpu.VMEM)] * 2,
+        out_specs=pl.BlockSpec(memory_space=pltpu.VMEM),
+        out_shape=jax.ShapeDtypeStruct(here.shape, F32),
+        compiler_params=params(),
+        cost_estimate=cost(SMALL),
+        name="by_core",
+    )(here, there)
+
+
+def join_kernel(share, third, *refs):
+    shares, mine = refs[:-1], refs[-1]
+    pairs = len(shares) // 2
+    begun, direct = shares[:pairs], shares[pairs:]
+    first = lax.axis_index("dp") == 0
+    mine[0] = jnp.where(first, share[...], direct[0][...])
+    mine[1] = jnp.where(first, begun[0][...], third[...])
+    for pair in range(pairs):
+        mine[pair + 2] = jnp.where(first, direct[pair][...], begun[pair][...])
+
+
+def joined(share, third, begun, direct):
+    operands = [share, third, *begun, *direct]
+    return pl.pallas_call(
+        join_kernel,
+        in_specs=[pl.BlockSpec(memory_space=pltpu.VMEM)] * len(operands),
+        out_specs=pl.BlockSpec(memory_space=pltpu.VMEM),
+        out_shape=jax.ShapeDtypeStruct((len(begun) + 2, *share.shape), F32),
+        compiler_params=params(),
+        cost_estimate=cost(SMALL),
+        name="joined",
     )(*operands)
 
 
@@ -558,15 +618,12 @@
     chips, replicas = lax.axis_size("tp"), lax.axis_size("dp")
     rank = right_factor.shape[0]
 
-    half = chips // 2
-
-    def exchange(value, index, place=None):
+    def send(value, first, second):
         pairs = []
         for chip in range(chips):
-            for core in range(2):
-                to = (index >> 1) * 4 + core * 2 + (index & 1) if place is None else place
-                if to:
-                    pairs.append((2 * chip + core, 2 * (chip ^ to) + core))
+            for core, place in enumerate((first, second)):
+                if place:
+                    pairs.append((2 * chip + core, 2 * (chip ^ place) + core))
         return lax.ppermute(value, ("tp", "dp"), pairs)
 
     pieces, places, (terms, residue_t) = ring_gather(shard, chips, residue_left(right_factor, residue))
@@ -576,29 +633,31 @@
     give, left_sum, lhs, rhs = given_far(left_t, swap(left_t), hidden_t, residue, tokens, chips)
     got = swap(give)
     keep, gram = kept_far(left_sum, lhs, rhs, residue, tokens, chips)
-    far = messages_for(keep, got, gram)
-    give, keep = near_terms(lhs, rhs, residue, tokens, chips)
-    messages = [*messages_for(keep, swap(give), gram), *far]
-
-    passed = [exchange(messages[index + 1], index + 1, 1) for index in range(2, half, 2)]
-    second = exchange(messages[0], 0)
-    across = [exchange(added(messages[2 * i + 2], value), 2 * i + 2) for i, value in enumerate(passed)]
-    tokens, _ = lax.optimization_barrier((tokens, messages[1]))
+    begin = begin_messages(keep, got, gram)
+    give, keep_near = near_terms(lhs, rhs, residue, tokens, chips)
+    own, beside, direct, cross = rest_messages(keep, got, keep_near, swap(give), gram)
+
+    evens = range(4, chips, 4)
+    begun = [send(value, place, 1) for value, place in zip(begin, evens)]
+    direct = [send(value, place + 1, 2 * (place == 4)) for value, place in zip(direct, evens)]
+    third = send(beside, 0, 3)
+    cross = [crossing(value, passed) for value, passed in zip(cross, begun)]
+    crossed = [send(value, int(place == 4), place + 2) for value, place in zip(cross, evens)]
+    tokens, _ = lax.optimization_barrier((tokens, beside))
     merged = merged_sum(hidden_t, residue, tokens)
-    beside, passed = lax.optimization_barrier((messages[1], passed))
-    first = exchange(beside, 1)
-    second, merged = lax.optimization_barrier((second, merged))
-    partial = core_sum(messages[0], second, first, across)
+    third, merged = lax.optimization_barrier((third, merged))
+    partial = core_sum(own, third, begun, direct, crossed)
     share, gram_matrix = chip_sum(partial, swap(partial), rank)
 
-    across = [exchange(share, index) for index in range(2, half, 2)]
-    first, second = exchange(share, 1), exchange(share, 0)
-    passed = [exchange(value, 2 * i + 3, 1) for i, value in enumerate(across)]
-    passed = [exchange(value, 2 * i + 3, 1) for i, value in enumerate(across)]
+    begun = [send(share, int(place == 4), place + 2) for place in evens]
+    direct = [send(share, place, 2 * (place == 4)) for place in evens]
+    third = send(share, 0, 3)
+    passed = [send(by_core(share, value), place + 1, 1) for value, place in zip(begun, evens)]
     inverse = cholesky_inverse(gram_matrix)
-    inverse, first, second, across[0] = lax.optimization_barrier((inverse, first, second, across[0]))
+    inverse, third, begun, direct = lax.optimization_barrier((inverse, third, begun, direct))
     lhs = last_operand(inverse, left_sum, replicas)
-    mine = joined(share, second, first, across)
+    mine = joined(share, third, begun, direct)
+    half = chips // 2
     begun = finish([0, 1, *range(2, half, 2)], mine, 0, lhs, merged)
     passed, begun = lax.optimization_barrier((passed, begun))
     rest = passed[0][None] if len(passed) == 1 else jnp.stack(passed)

time: 68.7 us -> 67.4 us (0.981)
  waiting for transfers between devices: 22.7 us -> 18.2 us
  starting transfers between devices: 29.7 us -> 32.8 us
    ppermute x8, waiting for transfers between devices: 12.9 us -> 8.48 us  [send(): return lax.ppermute(value, ('tp', 'dp'), pairs)]
    ppermute x8, starting transfers between devices: 11.4 us -> 13.3 us  [send(): return lax.ppermute(value, ('tp', 'dp'), pairs)]
    ppermute x5, starting transfers between devices: 1.1 us -> 2.42 us  [swap(): return lax.ppermute(value, 'dp', [(0, 1), (1, 0)])]
  transfers between devices with their start and end apart: 27 -> 27, of which waited for: 15 -> 17; matrix products, arithmetic and copies ran while one was open for 0% -> 0% of each run, Pallas kernels for 16% -> 16%
where the time goes in v6:
time: 67.4 us; the launch traced here: 67.2 us
  starting transfers between devices  32.8 us (49%)
  waiting for transfers between devices  18.2 us (27%)
  Pallas kernels  14.4 us (21%)
  local copies, waits for them, and re-layouts  0.96 us (1%)
  between operations  0.83 us (1%)
    ppermute x14, starting transfers between devices, ring_gather(): going[way, half] = lax.ppermute(going[way, half], ('tp', 'dp'), pairs(way))  17.1 us
    ppermute x8, starting transfers between devices, send(): return lax.ppermute(value, ('tp', 'dp'), pairs)  13.3 us
    ppermute x8, waiting for transfers between devices, send(): return lax.ppermute(value, ('tp', 'dp'), pairs)  8.48 us
    ppermute x14, waiting for transfers between devices, ring_gather(): going[way, half] = lax.ppermute(going[way, half], ('tp', 'dp'), pairs(way))  6.55 us
    pallas_call x3, Pallas kernels, finish(): pl.pallas_call(functools.partial(final_kernel, indices, side), in_specs=[...  4.39 us
    ppermute x5, waiting for transfers between devices, swap(): return lax.ppermute(value, 'dp', [(0, 1), (1, 0)])  3.12 us
    ppermute x5, starting transfers between devices, swap(): return lax.ppermute(value, 'dp', [(0, 1), (1, 0)])  2.42 us
    pallas_call x1, Pallas kernels, early_left(): pl.pallas_call(early_kernel, in_specs=[pl.BlockSpec(memory_space=pltpu.SM...  1.87 us
  transfers between devices with their start and end apart: 27, of which 17 were waited for; matrix products, arithmetic and copies ran while one was open for 0% of the time, Pallas kernels for 16%

profile of v6, /device:TPU:0, one launch (start us, length us, event | category | flops | bytes accessed | tf_op | source)
XLA Modules:
  0.0 67.2 jit_solution(7907741885184693484)
XLA Ops:
  0.6 0.9 %copy-done.3 = bf16[1,32,4096]{2,1,0:T(8,128)(2,1)S(1)} copy-done((bf16[1,32,4096]{2,1,0:T(8,128)(2,1)S(1)}, bf16[1,32,4096]{2,1,0:T(8,128)(2,1)}, u32[]{:S(2)}) %copy-start.3) | copy-done | bytes 262168
  1.6 3.0 %collective-permute-start = (bf16[16,4096]{1,0:T(8,128)(2,1)S(1)}, bf16[16,4096]{1,0:T(8,128)(2,1)S(1)}, u32[]{:S(2)}, u32[]{:S(2)}) collective-permute-start(bf16[16,4096]{1,0:T(8,128)(2,1)S(1)} %get-tuple-element.51.refs_0_), channel_id=1, source_target_pairs={{0,2},{1,5},{2,6},{3,1},{6,10},{7,3},{10,14},{11,7},{14,12},{15,11... | collective-permute-start | bytes 393224 | tf_op jit(solution)/shard_map/ppermute | solution.py:599
  4.8 1.2 %residue_left.1 = (bf16[128,4096]{1,0:T(8,128)(2,1)S(1)}, f32[64,448]{1,0:T(8,128)S(1)}) custom-call(f32[64,4096]{1,0:T(8,128)S(1)} %copy-done.2, bf16[448,4096]{1,0:T(8,128)(2,1)S(1)} %bitcast.7), custom_call_target="tpu_custom_call" | custom-call | flops 2529999872 | tf_op jit(solution)/shard_map/residue_left/pallas_call | solution.py:84
  6.0 2.2 %collective-permute-start.8 = (bf16[16,4096]{1,0:T(8,128)(2,1)S(1)}, bf16[16,4096]{1,0:T(8,128)(2,1)S(1)}, u32[]{:S(2)}, u32[]{:S(2)}) collective-permute-start(bf16[16,4096]{1,0:T(8,128)(2,1)S(1)} %get-tuple-element.50.refs_1_), channel_id=1, source_target_pairs={{0,2},{1,5},{2,6},{3,1},{6,10},{7,3},{10,14},{11,7},{14,12},{15,11... | collective-permute-start | bytes 393224 | tf_op jit(solution)/shard_map/ppermute | solution.py:599
  8.5 1.7 %collective-permute-start.1 = (bf16[16,4096]{1,0:T(8,128)(2,1)S(1)}, bf16[16,4096]{1,0:T(8,128)(2,1)S(1)}, u32[]{:S(2)}, u32[]{:S(2)}) collective-permute-start(bf16[16,4096]{1,0:T(8,128)(2,1)S(1)} %collective-permute-done.refs_2_), channel_id=1, source_target_pairs={{0,2},{1,5},{2,6},{3,1},{6,10},{7,3},{10,14},{11,7},{14,12},{15,11... | collective-permute-start | bytes 393224 | tf_op jit(solution)/shard_map/ppermute | solution.py:599
  10.4 0.5 collective-permute-start.5
  10.9 1.2 %collective-permute-done.8.refs_4_ = bf16[16,4096]{1,0:T(8,128)(2,1)S(1)} collective-permute-done((bf16[16,4096]{1,0:T(8,128)(2,1)S(1)}, bf16[16,4096]{1,0:T(8,128)(2,1)S(1)}, u32[]{:S(2)}, u32[]{:S(2)}) %collective-permute-start.8) | collective-permute-done | bytes 131104 | tf_op jit(solution)/shard_map/ppermute | solution.py:599
  12.1 2.5 %collective-permute-start.10 = (bf16[16,4096]{1,0:T(8,128)(2,1)S(1)}, bf16[16,4096]{1,0:T(8,128)(2,1)S(1)}, u32[]{:S(2)}, u32[]{:S(2)}) collective-permute-start(bf16[16,4096]{1,0:T(8,128)(2,1)S(1)} %collective-permute-done.8.refs_4_), channel_id=1, source_target_pairs={{0,2},{1,5},{2,6},{3,1},{6,10},{7,3},{10,14},{11,7},{14,12},{15,11... | collective-permute-start | bytes 393224 | tf_op jit(solution)/shard_map/ppermute | solution.py:599
  14.7 0.6 collective-permute-done.1.refs_6_
  15.3 1.5 %collective-permute-start.2 = (bf16[16,4096]{1,0:T(8,128)(2,1)S(1)}, bf16[16,4096]{1,0:T(8,128)(2,1)S(1)}, u32[]{:S(2)}, u32[]{:S(2)}) collective-permute-start(bf16[16,4096]{1,0:T(8,128)(2,1)S(1)} %collective-permute-done.1.refs_6_), channel_id=1, source_target_pairs={{0,2},{1,5},{2,6},{3,1},{6,10},{7,3},{10,14},{11,7},{14,12},{15,11... | collective-permute-start | bytes 393224 | tf_op jit(solution)/shard_map/ppermute | solution.py:599
  16.8 0.6 collective-permute-start.6
  17.5 0.9 %collective-permute-done.10.refs_8_ = bf16[16,4096]{1,0:T(8,128)(2,1)S(1)} collective-permute-done((bf16[16,4096]{1,0:T(8,128)(2,1)S(1)}, bf16[16,4096]{1,0:T(8,128)(2,1)S(1)}, u32[]{:S(2)}, u32[]{:S(2)}) %collective-permute-start.10) | collective-permute-done | bytes 131104 | tf_op jit(solution)/shard_map/ppermute | solution.py:599
  18.4 2.2 %collective-permute-start.12 = (bf16[16,4096]{1,0:T(8,128)(2,1)S(1)}, bf16[16,4096]{1,0:T(8,128)(2,1)S(1)}, u32[]{:S(2)}, u32[]{:S(2)}) collective-permute-start(bf16[16,4096]{1,0:T(8,128)(2,1)S(1)} %collective-permute-done.10.refs_8_), channel_id=1, source_target_pairs={{0,2},{1,5},{2,6},{3,1},{6,10},{7,3},{10,14},{11,7},{14,12},{15,11... | collective-permute-start | bytes 393224 | tf_op jit(solution)/shard_map/ppermute | solution.py:599
  20.8 0.7 %collective-permute-done.2.refs_10_ = bf16[16,4096]{1,0:T(8,128)(2,1)S(1)} collective-permute-done((bf16[16,4096]{1,0:T(8,128)(2,1)S(1)}, bf16[16,4096]{1,0:T(8,128)(2,1)S(1)}, u32[]{:S(2)}, u32[]{:S(2)}) %collective-permute-start.2) | collective-permute-done | bytes 131104 | tf_op jit(solution)/shard_map/ppermute | solution.py:599
  21.5 1.9 %collective-permute-start.3 = (bf16[16,4096]{1,0:T(8,128)(2,1)S(1)}, bf16[16,4096]{1,0:T(8,128)(2,1)S(1)}, u32[]{:S(2)}, u32[]{:S(2)}) collective-permute-start(bf16[16,4096]{1,0:T(8,128)(2,1)S(1)} %collective-permute-done.2.refs_10_), channel_id=1, source_target_pairs={{0,2},{1,5},{2,6},{3,1},{6,10},{7,3},{10,14},{11,7},{14,12},{15,11... | collective-permute-start | bytes 393224 | tf_op jit(solution)/shard_map/ppermute | solution.py:599
  23.5 0.4 collective-permute-start.7
  23.8 0.6 collective-permute-done.12.refs_12_
  24.4 1.2 %collective-permute-done.13.refs_13_ = bf16[16,4096]{1,0:T(8,128)(2,1)S(1)} collective-permute-done((bf16[16,4096]{1,0:T(8,128)(2,1)S(1)}, bf16[16,4096]{1,0:T(8,128)(2,1)S(1)}, u32[]{:S(2)}, u32[]{:S(2)}) %collective-permute-start.13) | collective-permute-done | bytes 131104 | tf_op jit(solution)/shard_map/ppermute | solution.py:599
  25.6 1.9 %early_left.1 = (bf16[256,4096]{1,0:T(8,128)(2,1)S(1)}, bf16[256,448]{1,0:T(8,128)(2,1)S(1)}, f32[64,448]{1,0:T(8,128)S(1)}) custom-call(s32[16,16]{1,0:T(8,128)S(1)} %copy-done.4, bf16[16,4096]{1,0:T(8,128)(2,1)S(1)} %get-tuple-element.51.refs_0_, bf16[16,4096]{1,0:T(8,128)(2,1)S(1)} %get-tuple-element.50.refs_1_, ...), custom_call_target="tpu_custom_call" | custom-call | flops 2300000000 | tf_op jit(solution)/shard_map/early_left/pallas_call | solution.py:118
  27.5 0.9 %collective-permute-done.7.second = bf16[16,4096]{1,0:T(8,128)(2,1)S(1)} collective-permute-done((bf16[16,4096]{1,0:T(8,128)(2,1)S(1)}, bf16[16,4096]{1,0:T(8,128)(2,1)S(1)}, u32[]{:S(2)}, u32[]{:S(2)}) %collective-permute-start.7) | collective-permute-done | bytes 131104 | tf_op jit(solution)/shard_map/ppermute | solution.py:599
  28.4 1.3 %late_left.1 = (bf16[256,4096]{1,0:T(8,128)(2,1)S(1)}, f32[64,448]{1,0:T(8,128)S(1)}) custom-call(s32[16,16]{1,0:T(8,128)S(1)} %copy-done.4, bf16[16,4096]{1,0:T(8,128)(2,1)S(1)} %collective-permute-done.3.first, bf16[16,4096]{1,0:T(8,128)(2,1)S(1)} %collective-permute-done.7.second, ...), custom_call_target="tpu_custom_call", output_to_operand_aliasing={{0}: (6, {})} | custom-call | flops 1150000000 | tf_op jit(solution)/shard_map/late_left/pallas_call | solution.py:150
  29.8 1.3 %collective-permute-done.14.other_l = f32[64,448]{1,0:T(8,128)S(1)} collective-permute-done((f32[64,448]{1,0:T(8,128)S(1)}, f32[64,448]{1,0:T(8,128)S(1)}, u32[]{:S(2)}, u32[]{:S(2)}) %collective-permute-start.14) | collective-permute-done | bytes 114720 | tf_op jit(solution)/shard_map/ppermute | solution.py:612
  31.1 0.5 given_far.1
  31.9 0.6 near_terms.1
  32.5 0.4 collective-permute-start.16
  32.9 0.5 kept_far.1
  33.5 1.8 %collective-permute-start.18 = (f32[72,512]{1,0:T(8,128)S(1)}, f32[72,512]{1,0:T(8,128)S(1)}, u32[]{:S(2)}, u32[]{:S(2)}) collective-permute-start(f32[72,512]{1,0:T(8,128)S(1)} %begin_messages.1), channel_id=1, source_target_pairs={{0,8},{1,3},{2,10},{3,1},{4,12},{5,7},{6,14},{7,5},{8,0},{9,11},{1... | collective-permute-start | bytes 442376 | tf_op jit(solution)/shard_map/ppermute | solution.py:627
  35.4 2.6 %collective-permute-start.19 = (f32[72,512]{1,0:T(8,128)S(1)}, f32[72,512]{1,0:T(8,128)S(1)}, u32[]{:S(2)}, u32[]{:S(2)}) collective-permute-start(f32[72,512]{1,0:T(8,128)S(1)} %get-tuple-element.70), channel_id=1, source_target_pairs={{0,10},{1,5},{2,8},{3,7},{4,14},{5,1},{6,12},{7,3},{8,2},{9,13},{1... | collective-permute-start | bytes 442376 | tf_op jit(solution)/shard_map/ppermute | solution.py:627
  38.0 0.7 collective-permute-start.17
  38.7 2.3 %collective-permute-done.18.passed.refs_0_ = f32[72,512]{1,0:T(8,128)S(1)} collective-permute-done((f32[72,512]{1,0:T(8,128)S(1)}, f32[72,512]{1,0:T(8,128)S(1)}, u32[]{:S(2)}, u32[]{:S(2)}) %collective-permute-start.18) | collective-permute-done | bytes 147488 | tf_op jit(solution)/shard_map/ppermute | solution.py:627
  41.1 1.2 %collective-permute-start.20 = (f32[72,512]{1,0:T(8,128)S(1)}, f32[72,512]{1,0:T(8,128)S(1)}, u32[]{:S(2)}, u32[]{:S(2)}) collective-permute-start(f32[72,512]{1,0:T(8,128)S(1)} %crossing.1), channel_id=1, source_target_pairs={{0,2},{1,13},{2,0},{3,15},{4,6},{5,9},{6,4},{7,11},{8,10},{9,5},{1... | collective-permute-start | bytes 442376 | tf_op jit(solution)/shard_map/ppermute | solution.py:627
  42.3 1.1 %merged.1 = f32[448,4096]{1,0:T(8,128)S(1)} custom-call(bf16[448,256]{1,0:T(8,128)(2,1)S(1)} %bitcast.14, bf16[448,4096]{1,0:T(8,128)(2,1)S(1)} %bitcast.11, bf16[256,4096]{1,0:T(8,128)(2,1)S(1)} %get-tuple-element.68.tokens), custom_call_target="tpu_custom_call" | custom-call | flops 57500000 | tf_op jit(solution)/shard_map/merged/pallas_call | solution.py:272
  43.4 2.7 %collective-permute-done.19.refs_1_ = f32[72,512]{1,0:T(8,128)S(1)} collective-permute-done((f32[72,512]{1,0:T(8,128)S(1)}, f32[72,512]{1,0:T(8,128)S(1)}, u32[]{:S(2)}, u32[]{:S(2)}) %collective-permute-start.19) | collective-permute-done | bytes 147488 | tf_op jit(solution)/shard_map/ppermute | solution.py:627
  46.2 0.5 collective-permute-done.20.refs_2_
  46.8 1.4 %collective-permute-done.21.other = f32[72,512]{1,0:T(8,128)S(1)} collective-permute-done((f32[72,512]{1,0:T(8,128)S(1)}, f32[72,512]{1,0:T(8,128)S(1)}, u32[]{:S(2)}, u32[]{:S(2)}) %collective-permute-start.21) | collective-permute-done | bytes 147488 | tf_op jit(solution)/shard_map/ppermute | solution.py:612
  48.2 2.9 %collective-permute-start.23 = (f32[64,512]{1,0:T(8,128)S(1)}, f32[64,512]{1,0:T(8,128)S(1)}, u32[]{:S(2)}, u32[]{:S(2)}) collective-permute-start(f32[64,512]{1,0:T(8,128)S(1)} %get-tuple-element.72.share.here), channel_id=1, source_target_pairs={{0,2},{1,13},{2,0},{3,15},{4,6},{5,9},{6,4},{7,11},{8,10},{9,5},{1... | collective-permute-start | bytes 393224 | tf_op jit(solution)/shard_map/ppermute | solution.py:627
  51.1 1.0 %collective-permute-start.24 = (f32[64,512]{1,0:T(8,128)S(1)}, f32[64,512]{1,0:T(8,128)S(1)}, u32[]{:S(2)}, u32[]{:S(2)}) collective-permute-start(f32[64,512]{1,0:T(8,128)S(1)} %get-tuple-element.72.share.here), channel_id=1, source_target_pairs={{0,8},{1,5},{2,10},{3,7},{4,12},{5,1},{6,14},{7,3},{8,0},{9,13},{1... | collective-permute-start | bytes 393224 | tf_op jit(solution)/shard_map/ppermute | solution.py:627
  52.0 0.7 collective-permute-start.22
  52.7 1.3 %collective-permute-done.23.refs_0_.there = f32[64,512]{1,0:T(8,128)S(1)} collective-permute-done((f32[64,512]{1,0:T(8,128)S(1)}, f32[64,512]{1,0:T(8,128)S(1)}, u32[]{:S(2)}, u32[]{:S(2)}) %collective-permute-start.23) | collective-permute-done | bytes 131104 | tf_op jit(solution)/shard_map/ppermute | solution.py:627
  54.0 2.5 %collective-permute-start.25 = (f32[64,512]{1,0:T(8,128)S(1)}, f32[64,512]{1,0:T(8,128)S(1)}, u32[]{:S(2)}, u32[]{:S(2)}) collective-permute-start(f32[64,512]{1,0:T(8,128)S(1)} %by_core.1), channel_id=1, source_target_pairs={{0,10},{1,3},{2,8},{3,1},{4,14},{5,7},{6,12},{7,5},{8,2},{9,11},{1... | collective-permute-start | bytes 393224 | tf_op jit(solution)/shard_map/ppermute | solution.py:627
  56.5 1.8 %cholesky_inverse.1.inverse = f32[64,64]{1,0:T(8,128)S(1)} custom-call(f32[64,64]{1,0:T(8,128)S(1)} %get-tuple-element.73.gram), custom_call_target="tpu_custom_call" | custom-call | flops 5750000128 | tf_op jit(solution)/shard_map/cholesky_inverse/pallas_call | solution.py:480
  58.3 0.8 %last_operand.1.lhs = bf16[512,256]{1,0:T(8,128)(2,1)S(1)} custom-call(f32[64,64]{1,0:T(8,128)S(1)} %cholesky_inverse.1.inverse, f32[64,448]{1,0:T(8,128)S(1)} %get-tuple-element.58.left_sum), custom_call_target="tpu_custom_call" | custom-call | flops 57500000 | tf_op jit(solution)/shard_map/last_operand/pallas_call | solution.py:511
  59.1 1.5 %finish.3 = (bf16[448,4096]{1,0:T(8,128)(2,1)}, f32[64,4096]{1,0:T(8,128)}) custom-call(f32[3,64,512]{2,1,0:T(8,128)S(1)} %joined.1.shares, bf16[512,256]{1,0:T(8,128)(2,1)S(1)} %last_operand.1.lhs, f32[448,4096]{1,0:T(8,128)S(1)} %merged.1), custom_call_target="tpu_custom_call" | custom-call | flops 57500000 | tf_op jit(solution)/shard_map/finish/pallas_call | solution.py:549
  60.7 1.6 %collective-permute-done.25 = f32[64,512]{1,0:T(8,128)S(1)} collective-permute-done((f32[64,512]{1,0:T(8,128)S(1)}, f32[64,512]{1,0:T(8,128)S(1)}, u32[]{:S(2)}, u32[]{:S(2)}) %collective-permute-start.25) | collective-permute-done | bytes 131104 | tf_op jit(solution)/shard_map/ppermute | solution.py:627
  62.3 1.6 %collective-permute-start.26 = (f32[4,64,512]{2,1,0:T(8,128)S(1)}, f32[4,64,512]{2,1,0:T(8,128)S(1)}, u32[]{:S(2)}, u32[]{:S(2)}) collective-permute-start(f32[4,64,512]{2,1,0:T(8,128)S(1)} %pad_maximum_fusion), channel_id=1, source_target_pairs={{0,1},{1,0},{2,3},{3,2},{4,5},{5,4},{6,7},{7,6},{8,9},{9,8},{10,11... | collective-permute-start | bytes 1572872 | tf_op jit(solution)/shard_map/ppermute | solution.py:612
  63.9 1.1 %finish.4 = (bf16[448,4096]{1,0:T(8,128)(2,1)}, f32[64,4096]{1,0:T(8,128)}) custom-call(f32[1,64,512]{2,1,0:T(8,128)S(1)} %bitcast.16, bf16[512,256]{1,0:T(8,128)(2,1)S(1)} %last_operand.1.lhs, f32[448,4096]{1,0:T(8,128)S(1)} %merged.1, bf16[448,4096]{1,0:T(8,128)(2,1)} %get-tuple-element.82.refs_0_, ...), custom_call_target="tpu_custom_call", output_to_operand_aliasing={{0}: (3, {}), {1}: (4, {})} | custom-call | flops 57500000 | tf_op jit(solution)/shard_map/finish/pallas_call | solution.py:549
  65.1 0.4 collective-permute-done.26.shares
  65.5 1.7 %finish.5 = (bf16[448,4096]{1,0:T(8,128)(2,1)}, f32[64,4096]{1,0:T(8,128)}) custom-call(f32[4,64,512]{2,1,0:T(8,128)S(1)} %collective-permute-done.26.shares, bf16[512,256]{1,0:T(8,128)(2,1)S(1)} %last_operand.1.lhs, f32[448,4096]{1,0:T(8,128)S(1)} %merged.1, ...), custom_call_target="tpu_custom_call", output_to_operand_aliasing={{0}: (3, {}), {1}: (4, {})} | custom-call | flops 57500000 | tf_op jit(solution)/shard_map/finish/pallas_call | solution.py:549
  (37 shorter events, 1.8 us)
Async XLA Ops:
  0.6 1.0 %copy-start.3 = (bf16[1,32,4096]{2,1,0:T(8,128)(2,1)S(1)}, bf16[1,32,4096]{2,1,0:T(8,128)(2,1)}, u32[]{:S(2)}) copy-start(bf16[1,32,4096]{2,1,0:T(8,128)(2,1)} %param.5) | copy-start | bytes 786436
  1.6 3.2 %copy-start = (bf16[1,448,4096]{2,1,0:T(8,128)(2,1)S(1)}, bf16[1,448,4096]{2,1,0:T(8,128)(2,1)}, u32[]{:S(2)}) copy-start(bf16[1,448,4096]{2,1,0:T(8,128)(2,1)} %param.7) | copy-start | bytes 11010052
  1.6 3.2 %copy-start.2 = (f32[64,4096]{1,0:T(8,128)S(1)}, f32[64,4096]{1,0:T(8,128)}, u32[]{:S(2)}) copy-start(f32[64,4096]{1,0:T(8,128)} %right.1) | copy-start | bytes 3145732
  1.6 6.9 %collective-permute-start = (bf16[16,4096]{1,0:T(8,128)(2,1)S(1)}, bf16[16,4096]{1,0:T(8,128)(2,1)S(1)}, u32[]{:S(2)}, u32[]{:S(2)}) collective-permute-start(bf16[16,4096]{1,0:T(8,128)(2,1)S(1)} %get-tuple-element.51.refs_0_), channel_id=1, source_target_pairs={{0,2},{1,5},{2,6},{3,1},{6,10},{7,3},{10,14},{11,7},{14,12},{15,11... | collective-permute-start | bytes 393224 | tf_op jit(solution)/shard_map/ppermute | solution.py:599
  4.6 5.8 %collective-permute-start.4 = (bf16[16,4096]{1,0:T(8,128)(2,1)S(1)}, bf16[16,4096]{1,0:T(8,128)(2,1)S(1)}, u32[]{:S(2)}, u32[]{:S(2)}) collective-permute-start(bf16[16,4096]{1,0:T(8,128)(2,1)S(1)} %get-tuple-element.50.refs_1_), channel_id=1, source_target_pairs={{0,4},{1,3},{2,0},{3,7},{6,2},{7,11},{10,6},{11,15},{14,10},{15,13... | collective-permute-start | bytes 393224 | tf_op jit(solution)/shard_map/ppermute | solution.py:599
  4.8 20.9 %copy-start.1 = (bf16[1,256,448]{1,2,0:T(8,128)(2,1)S(1)}, bf16[1,256,448]{1,2,0:T(8,128)(2,1)}, u32[]{:S(2)}) copy-start(bf16[1,256,448]{1,2,0:T(8,128)(2,1)} %param.6) | copy-start | bytes 688132
  4.8 20.9 %copy-start.4 = (s32[16,16]{1,0:T(8,128)S(1)}, s32[16,16]{1,0:T(8,128)}, u32[]{:S(2)}) copy-start(s32[16,16]{1,0:T(8,128)} %constant.2.clone.places) | copy-start | bytes 3076
  6.0 6.1 %collective-permute-start.8 = (bf16[16,4096]{1,0:T(8,128)(2,1)S(1)}, bf16[16,4096]{1,0:T(8,128)(2,1)S(1)}, u32[]{:S(2)}, u32[]{:S(2)}) collective-permute-start(bf16[16,4096]{1,0:T(8,128)(2,1)S(1)} %get-tuple-element.50.refs_1_), channel_id=1, source_target_pairs={{0,2},{1,5},{2,6},{3,1},{6,10},{7,3},{10,14},{11,7},{14,12},{15,11... | collective-permute-start | bytes 393224 | tf_op jit(solution)/shard_map/ppermute | solution.py:599
  8.2 6.4 %collective-permute-start.9 = (bf16[16,4096]{1,0:T(8,128)(2,1)S(1)}, bf16[16,4096]{1,0:T(8,128)(2,1)S(1)}, u32[]{:S(2)}, u32[]{:S(2)}) collective-permute-start(bf16[16,4096]{1,0:T(8,128)(2,1)S(1)} %get-tuple-element.51.refs_0_), channel_id=1, source_target_pairs={{0,4},{1,3},{2,0},{3,7},{6,2},{7,11},{10,6},{11,15},{14,10},{15,13... | collective-permute-start | bytes 393224 | tf_op jit(solution)/shard_map/ppermute | solution.py:599
  8.5 6.8 %collective-permute-start.1 = (bf16[16,4096]{1,0:T(8,128)(2,1)S(1)}, bf16[16,4096]{1,0:T(8,128)(2,1)S(1)}, u32[]{:S(2)}, u32[]{:S(2)}) collective-permute-start(bf16[16,4096]{1,0:T(8,128)(2,1)S(1)} %collective-permute-done.refs_2_), channel_id=1, source_target_pairs={{0,2},{1,5},{2,6},{3,1},{6,10},{7,3},{10,14},{11,7},{14,12},{15,11... | collective-permute-start | bytes 393224 | tf_op jit(solution)/shard_map/ppermute | solution.py:599
  10.4 6.4 %collective-permute-start.5 = (bf16[16,4096]{1,0:T(8,128)(2,1)S(1)}, bf16[16,4096]{1,0:T(8,128)(2,1)S(1)}, u32[]{:S(2)}, u32[]{:S(2)}) collective-permute-start(bf16[16,4096]{1,0:T(8,128)(2,1)S(1)} %collective-permute-done.4.refs_3_), channel_id=1, source_target_pairs={{0,4},{1,3},{2,0},{3,7},{6,2},{7,11},{10,6},{11,15},{14,10},{15,13... | collective-permute-start | bytes 393224 | tf_op jit(solution)/shard_map/ppermute | solution.py:599
  12.1 6.4 %collective-permute-start.10 = (bf16[16,4096]{1,0:T(8,128)(2,1)S(1)}, bf16[16,4096]{1,0:T(8,128)(2,1)S(1)}, u32[]{:S(2)}, u32[]{:S(2)}) collective-permute-start(bf16[16,4096]{1,0:T(8,128)(2,1)S(1)} %collective-permute-done.8.refs_4_), channel_id=1, source_target_pairs={{0,2},{1,5},{2,6},{3,1},{6,10},{7,3},{10,14},{11,7},{14,12},{15,11... | collective-permute-start | bytes 393224 | tf_op jit(solution)/shard_map/ppermute | solution.py:599
  14.5 6.1 %collective-permute-start.11 = (bf16[16,4096]{1,0:T(8,128)(2,1)S(1)}, bf16[16,4096]{1,0:T(8,128)(2,1)S(1)}, u32[]{:S(2)}, u32[]{:S(2)}) collective-permute-start(bf16[16,4096]{1,0:T(8,128)(2,1)S(1)} %collective-permute-done.9.refs_5_), channel_id=1, source_target_pairs={{0,4},{1,3},{2,0},{3,7},{6,2},{7,11},{10,6},{11,15},{14,10},{15,13... | collective-permute-start | bytes 393224 | tf_op jit(solution)/shard_map/ppermute | solution.py:599
  15.3 6.2 %collective-permute-start.2 = (bf16[16,4096]{1,0:T(8,128)(2,1)S(1)}, bf16[16,4096]{1,0:T(8,128)(2,1)S(1)}, u32[]{:S(2)}, u32[]{:S(2)}) collective-permute-start(bf16[16,4096]{1,0:T(8,128)(2,1)S(1)} %collective-permute-done.1.refs_6_), channel_id=1, source_target_pairs={{0,2},{1,5},{2,6},{3,1},{6,10},{7,3},{10,14},{11,7},{14,12},{15,11... | collective-permute-start | bytes 393224 | tf_op jit(solution)/shard_map/ppermute | solution.py:599
  16.8 6.6 %collective-permute-start.6 = (bf16[16,4096]{1,0:T(8,128)(2,1)S(1)}, bf16[16,4096]{1,0:T(8,128)(2,1)S(1)}, u32[]{:S(2)}, u32[]{:S(2)}) collective-permute-start(bf16[16,4096]{1,0:T(8,128)(2,1)S(1)} %collective-permute-done.5.refs_7_), channel_id=1, source_target_pairs={{0,4},{1,3},{2,0},{3,7},{6,2},{7,11},{10,6},{11,15},{14,10},{15,13... | collective-permute-start | bytes 393224 | tf_op jit(solution)/shard_map/ppermute | solution.py:599
  18.4 6.0 %collective-permute-start.12 = (bf16[16,4096]{1,0:T(8,128)(2,1)S(1)}, bf16[16,4096]{1,0:T(8,128)(2,1)S(1)}, u32[]{:S(2)}, u32[]{:S(2)}) collective-permute-start(bf16[16,4096]{1,0:T(8,128)(2,1)S(1)} %collective-permute-done.10.refs_8_), channel_id=1, source_target_pairs={{0,2},{1,5},{2,6},{3,1},{6,10},{7,3},{10,14},{11,7},{14,12},{15,11... | collective-permute-start | bytes 393224 | tf_op jit(solution)/shard_map/ppermute | solution.py:599
  20.7 5.0 %collective-permute-start.13 = (bf16[16,4096]{1,0:T(8,128)(2,1)S(1)}, bf16[16,4096]{1,0:T(8,128)(2,1)S(1)}, u32[]{:S(2)}, u32[]{:S(2)}) collective-permute-start(bf16[16,4096]{1,0:T(8,128)(2,1)S(1)} %collective-permute-done.11.refs_9_), channel_id=1, source_target_pairs={{0,4},{1,3},{2,0},{3,7},{6,2},{7,11},{10,6},{11,15},{14,10},{15,13... | collective-permute-start | bytes 393224 | tf_op jit(solution)/shard_map/ppermute | solution.py:599
  21.5 6.0 %collective-permute-start.3 = (bf16[16,4096]{1,0:T(8,128)(2,1)S(1)}, bf16[16,4096]{1,0:T(8,128)(2,1)S(1)}, u32[]{:S(2)}, u32[]{:S(2)}) collective-permute-start(bf16[16,4096]{1,0:T(8,128)(2,1)S(1)} %collective-permute-done.2.refs_10_), channel_id=1, source_target_pairs={{0,2},{1,5},{2,6},{3,1},{6,10},{7,3},{10,14},{11,7},{14,12},{15,11... | collective-permute-start | bytes 393224 | tf_op jit(solution)/shard_map/ppermute | solution.py:599
  23.5 5.0 %collective-permute-start.7 = (bf16[16,4096]{1,0:T(8,128)(2,1)S(1)}, bf16[16,4096]{1,0:T(8,128)(2,1)S(1)}, u32[]{:S(2)}, u32[]{:S(2)}) collective-permute-start(bf16[16,4096]{1,0:T(8,128)(2,1)S(1)} %collective-permute-done.6.refs_11_), channel_id=1, source_target_pairs={{0,4},{1,3},{2,0},{3,7},{6,2},{7,11},{10,6},{11,15},{14,10},{15,13... | collective-permute-start | bytes 393224 | tf_op jit(solution)/shard_map/ppermute | solution.py:599
  29.7 1.4 %collective-permute-start.14 = (f32[64,448]{1,0:T(8,128)S(1)}, f32[64,448]{1,0:T(8,128)S(1)}, u32[]{:S(2)}, u32[]{:S(2)}) collective-permute-start(f32[64,448]{1,0:T(8,128)S(1)} %get-tuple-element.56.here_l), channel_id=1, source_target_pairs={{0,1},{1,0},{2,3},{3,2},{4,5},{5,4},{6,7},{7,6},{8,9},{9,8},{10,11... | collective-permute-start | bytes 344072 | tf_op jit(solution)/shard_map/ppermute | solution.py:612
  31.7 1.7 %collective-permute-start.15 = (f32[2,64,512]{2,1,0:T(8,128)S(1)}, f32[2,64,512]{2,1,0:T(8,128)S(1)}, u32[]{:S(2)}, u32[]{:S(2)}) collective-permute-start(f32[2,64,512]{2,1,0:T(8,128)S(1)} %get-tuple-element.62), channel_id=1, source_target_pairs={{0,1},{1,0},{2,3},{3,2},{4,5},{5,4},{6,7},{7,6},{8,9},{9,8},{10,11... | collective-permute-start | bytes 786440 | tf_op jit(solution)/shard_map/ppermute | solution.py:612
  32.5 2.8 %collective-permute-start.16 = (f32[2,64,512]{2,1,0:T(8,128)S(1)}, f32[2,64,512]{2,1,0:T(8,128)S(1)}, u32[]{:S(2)}, u32[]{:S(2)}) collective-permute-start(f32[2,64,512]{2,1,0:T(8,128)S(1)} %get-tuple-element.64), channel_id=1, source_target_pairs={{0,1},{1,0},{2,3},{3,2},{4,5},{5,4},{6,7},{7,6},{8,9},{9,8},{10,11... | collective-permute-start | bytes 786440 | tf_op jit(solution)/shard_map/ppermute | solution.py:612
  33.5 7.5 %collective-permute-start.18 = (f32[72,512]{1,0:T(8,128)S(1)}, f32[72,512]{1,0:T(8,128)S(1)}, u32[]{:S(2)}, u32[]{:S(2)}) collective-permute-start(f32[72,512]{1,0:T(8,128)S(1)} %begin_messages.1), channel_id=1, source_target_pairs={{0,8},{1,3},{2,10},{3,1},{4,12},{5,7},{6,14},{7,5},{8,0},{9,11},{1... | collective-permute-start | bytes 442376 | tf_op jit(solution)/shard_map/ppermute | solution.py:627
  35.4 10.8 %collective-permute-start.19 = (f32[72,512]{1,0:T(8,128)S(1)}, f32[72,512]{1,0:T(8,128)S(1)}, u32[]{:S(2)}, u32[]{:S(2)}) collective-permute-start(f32[72,512]{1,0:T(8,128)S(1)} %get-tuple-element.70), channel_id=1, source_target_pairs={{0,10},{1,5},{2,8},{3,7},{4,14},{5,1},{6,12},{7,3},{8,2},{9,13},{1... | collective-permute-start | bytes 442376 | tf_op jit(solution)/shard_map/ppermute | solution.py:627
  38.0 5.4 %collective-permute-start.17 = (f32[72,512]{1,0:T(8,128)S(1)}, f32[72,512]{1,0:T(8,128)S(1)}, u32[]{:S(2)}, u32[]{:S(2)}) collective-permute-start(f32[72,512]{1,0:T(8,128)S(1)} %get-tuple-element.67), channel_id=1, source_target_pairs={{1,7},{3,5},{5,3},{7,1},{9,15},{11,13},{13,11},{15,9},{17,23},{19,... | collective-permute-start | bytes 442376 | tf_op jit(solution)/shard_map/ppermute | solution.py:627
  41.1 5.6 %collective-permute-start.20 = (f32[72,512]{1,0:T(8,128)S(1)}, f32[72,512]{1,0:T(8,128)S(1)}, u32[]{:S(2)}, u32[]{:S(2)}) collective-permute-start(f32[72,512]{1,0:T(8,128)S(1)} %crossing.1), channel_id=1, source_target_pairs={{0,2},{1,13},{2,0},{3,15},{4,6},{5,9},{6,4},{7,11},{8,10},{9,5},{1... | collective-permute-start | bytes 442376 | tf_op jit(solution)/shard_map/ppermute | solution.py:627
  46.7 1.4 %collective-permute-start.21 = (f32[72,512]{1,0:T(8,128)S(1)}, f32[72,512]{1,0:T(8,128)S(1)}, u32[]{:S(2)}, u32[]{:S(2)}) collective-permute-start(f32[72,512]{1,0:T(8,128)S(1)} %core_sum.1.here), channel_id=1, source_target_pairs={{0,1},{1,0},{2,3},{3,2},{4,5},{5,4},{6,7},{7,6},{8,9},{9,8},{10,11... | collective-permute-start | bytes 442376 | tf_op jit(solution)/shard_map/ppermute | solution.py:612
  48.2 5.8 %collective-permute-start.23 = (f32[64,512]{1,0:T(8,128)S(1)}, f32[64,512]{1,0:T(8,128)S(1)}, u32[]{:S(2)}, u32[]{:S(2)}) collective-permute-start(f32[64,512]{1,0:T(8,128)S(1)} %get-tuple-element.72.share.here), channel_id=1, source_target_pairs={{0,2},{1,13},{2,0},{3,15},{4,6},{5,9},{6,4},{7,11},{8,10},{9,5},{1... | collective-permute-start | bytes 393224 | tf_op jit(solution)/shard_map/ppermute | solution.py:627
  51.1 7.2 %collective-permute-start.24 = (f32[64,512]{1,0:T(8,128)S(1)}, f32[64,512]{1,0:T(8,128)S(1)}, u32[]{:S(2)}, u32[]{:S(2)}) collective-permute-start(f32[64,512]{1,0:T(8,128)S(1)} %get-tuple-element.72.share.here), channel_id=1, source_target_pairs={{0,8},{1,5},{2,10},{3,7},{4,12},{5,1},{6,14},{7,3},{8,0},{9,13},{1... | collective-permute-start | bytes 393224 | tf_op jit(solution)/shard_map/ppermute | solution.py:627
  52.0 6.3 %collective-permute-start.22 = (f32[64,512]{1,0:T(8,128)S(1)}, f32[64,512]{1,0:T(8,128)S(1)}, u32[]{:S(2)}, u32[]{:S(2)}) collective-permute-start(f32[64,512]{1,0:T(8,128)S(1)} %get-tuple-element.72.share.here), channel_id=1, source_target_pairs={{1,7},{3,5},{5,3},{7,1},{9,15},{11,13},{13,11},{15,9},{17,23},{19,... | collective-permute-start | bytes 393224 | tf_op jit(solution)/shard_map/ppermute | solution.py:627
  54.0 8.2 %collective-permute-start.25 = (f32[64,512]{1,0:T(8,128)S(1)}, f32[64,512]{1,0:T(8,128)S(1)}, u32[]{:S(2)}, u32[]{:S(2)}) collective-permute-start(f32[64,512]{1,0:T(8,128)S(1)} %by_core.1), channel_id=1, source_target_pairs={{0,10},{1,3},{2,8},{3,1},{4,14},{5,7},{6,12},{7,5},{8,2},{9,11},{1... | collective-permute-start | bytes 393224 | tf_op jit(solution)/shard_map/ppermute | solution.py:627
  62.3 3.2 %collective-permute-start.26 = (f32[4,64,512]{2,1,0:T(8,128)S(1)}, f32[4,64,512]{2,1,0:T(8,128)S(1)}, u32[]{:S(2)}, u32[]{:S(2)}) collective-permute-start(f32[4,64,512]{2,1,0:T(8,128)S(1)} %pad_maximum_fusion), channel_id=1, source_target_pairs={{0,1},{1,0},{2,3},{3,2},{4,5},{5,4},{6,7},{7,6},{8,9},{9,8},{10,11... | collective-permute-start | bytes 1572872 | tf_op jit(solution)/shard_map/ppermute | solution.py:612

commit v7 on v6

--- a/solution.py
+++ b/solution.py
@@ -654,7 +654,7 @@
     third = send(share, 0, 3)
     passed = [send(by_core(share, value), place + 1, 1) for value, place in zip(begun, evens)]
     inverse = cholesky_inverse(gram_matrix)
-    inverse, third, begun, direct = lax.optimization_barrier((inverse, third, begun, direct))
+    inverse, begun, direct = lax.optimization_barrier((inverse, begun, direct))
     lhs = last_operand(inverse, left_sum, replicas)
     mine = joined(share, third, begun, direct)
     half = chips // 2

time: 67.4 us -> 66.6 us (0.988)
  starting transfers between devices: 32.8 us -> 32 us
    ppermute x5, starting transfers between devices: 2.42 us -> 1.64 us  [swap(): return lax.ppermute(value, 'dp', [(0, 1), (1, 0)])]
where the time goes in v7:
time: 66.6 us; the launch traced here: 66.4 us
  starting transfers between devices  32 us (48%)
  waiting for transfers between devices  18.2 us (27%)
  Pallas kernels  14.4 us (22%)
  local copies, waits for them, and re-layouts  0.96 us (1%)
  between operations  0.83 us (1%)
    ppermute x14, starting transfers between devices, ring_gather(): going[way, half] = lax.ppermute(going[way, half], ('tp', 'dp'), pairs(way))  17.1 us
    ppermute x8, starting transfers between devices, send(): return lax.ppermute(value, ('tp', 'dp'), pairs)  13.3 us
    ppermute x8, waiting for transfers between devices, send(): return lax.ppermute(value, ('tp', 'dp'), pairs)  8.49 us
    ppermute x14, waiting for transfers between devices, ring_gather(): going[way, half] = lax.ppermute(going[way, half], ('tp', 'dp'), pairs(way))  6.55 us
    pallas_call x3, Pallas kernels, finish(): pl.pallas_call(functools.partial(final_kernel, indices, side), in_specs=[...  4.39 us
    ppermute x5, waiting for transfers between devices, swap(): return lax.ppermute(value, 'dp', [(0, 1), (1, 0)])  3.12 us
    pallas_call x1, Pallas kernels, early_left(): pl.pallas_call(early_kernel, in_specs=[pl.BlockSpec(memory_space=pltpu.SM...  1.87 us
    pallas_call x1, Pallas kernels, cholesky_inverse(): pl.pallas_call(inverse_kernel, in_specs=[pl.BlockSpec(memory_space=pltpu....  1.77 us
  transfers between devices with their start and end apart: 27, of which 17 were waited for; matrix products, arithmetic and copies ran while one was open for 0% of the time, Pallas kernels for 16%

profile of v7, /device:TPU:0, one launch (start us, length us, event | category | flops | bytes accessed | tf_op | source)
XLA Modules:
  0.0 66.4 jit_solution(1111574350724995024)
XLA Ops:
  0.6 0.9 %copy-done.3 = bf16[1,32,4096]{2,1,0:T(8,128)(2,1)S(1)} copy-done((bf16[1,32,4096]{2,1,0:T(8,128)(2,1)S(1)}, bf16[1,32,4096]{2,1,0:T(8,128)(2,1)}, u32[]{:S(2)}) %copy-start.3) | copy-done | bytes 262168
  1.6 3.0 %collective-permute-start = (bf16[16,4096]{1,0:T(8,128)(2,1)S(1)}, bf16[16,4096]{1,0:T(8,128)(2,1)S(1)}, u32[]{:S(2)}, u32[]{:S(2)}) collective-permute-start(bf16[16,4096]{1,0:T(8,128)(2,1)S(1)} %get-tuple-element.50.refs_0_), channel_id=1, source_target_pairs={{0,2},{1,5},{2,6},{3,1},{6,10},{7,3},{10,14},{11,7},{14,12},{15,11... | collective-permute-start | bytes 393224 | tf_op jit(solution)/shard_map/ppermute | solution.py:599
  4.8 1.2 %residue_left.1 = (bf16[128,4096]{1,0:T(8,128)(2,1)S(1)}, f32[64,448]{1,0:T(8,128)S(1)}) custom-call(f32[64,4096]{1,0:T(8,128)S(1)} %copy-done.2, bf16[448,4096]{1,0:T(8,128)(2,1)S(1)} %bitcast.7), custom_call_target="tpu_custom_call" | custom-call | flops 2529999872 | tf_op jit(solution)/shard_map/residue_left/pallas_call | solution.py:84
  6.0 2.2 %collective-permute-start.8 = (bf16[16,4096]{1,0:T(8,128)(2,1)S(1)}, bf16[16,4096]{1,0:T(8,128)(2,1)S(1)}, u32[]{:S(2)}, u32[]{:S(2)}) collective-permute-start(bf16[16,4096]{1,0:T(8,128)(2,1)S(1)} %get-tuple-element.49.refs_1_), channel_id=1, source_target_pairs={{0,2},{1,5},{2,6},{3,1},{6,10},{7,3},{10,14},{11,7},{14,12},{15,11... | collective-permute-start | bytes 393224 | tf_op jit(solution)/shard_map/ppermute | solution.py:599
  8.5 1.7 %collective-permute-start.1 = (bf16[16,4096]{1,0:T(8,128)(2,1)S(1)}, bf16[16,4096]{1,0:T(8,128)(2,1)S(1)}, u32[]{:S(2)}, u32[]{:S(2)}) collective-permute-start(bf16[16,4096]{1,0:T(8,128)(2,1)S(1)} %collective-permute-done.refs_2_), channel_id=1, source_target_pairs={{0,2},{1,5},{2,6},{3,1},{6,10},{7,3},{10,14},{11,7},{14,12},{15,11... | collective-permute-start | bytes 393224 | tf_op jit(solution)/shard_map/ppermute | solution.py:599
  10.4 0.5 collective-permute-start.5
  10.9 1.2 %collective-permute-done.8.refs_4_ = bf16[16,4096]{1,0:T(8,128)(2,1)S(1)} collective-permute-done((bf16[16,4096]{1,0:T(8,128)(2,1)S(1)}, bf16[16,4096]{1,0:T(8,128)(2,1)S(1)}, u32[]{:S(2)}, u32[]{:S(2)}) %collective-permute-start.8) | collective-permute-done | bytes 131104 | tf_op jit(solution)/shard_map/ppermute | solution.py:599
  12.1 2.5 %collective-permute-start.10 = (bf16[16,4096]{1,0:T(8,128)(2,1)S(1)}, bf16[16,4096]{1,0:T(8,128)(2,1)S(1)}, u32[]{:S(2)}, u32[]{:S(2)}) collective-permute-start(bf16[16,4096]{1,0:T(8,128)(2,1)S(1)} %collective-permute-done.8.refs_4_), channel_id=1, source_target_pairs={{0,2},{1,5},{2,6},{3,1},{6,10},{7,3},{10,14},{11,7},{14,12},{15,11... | collective-permute-start | bytes 393224 | tf_op jit(solution)/shard_map/ppermute | solution.py:599
  14.7 0.6 collective-permute-done.1.refs_6_
  15.3 1.5 %collective-permute-start.2 = (bf16[16,4096]{1,0:T(8,128)(2,1)S(1)}, bf16[16,4096]{1,0:T(8,128)(2,1)S(1)}, u32[]{:S(2)}, u32[]{:S(2)}) collective-permute-start(bf16[16,4096]{1,0:T(8,128)(2,1)S(1)} %collective-permute-done.1.refs_6_), channel_id=1, source_target_pairs={{0,2},{1,5},{2,6},{3,1},{6,10},{7,3},{10,14},{11,7},{14,12},{15,11... | collective-permute-start | bytes 393224 | tf_op jit(solution)/shard_map/ppermute | solution.py:599
  16.8 0.6 collective-permute-start.6
  17.5 0.9 %collective-permute-done.10.refs_8_ = bf16[16,4096]{1,0:T(8,128)(2,1)S(1)} collective-permute-done((bf16[16,4096]{1,0:T(8,128)(2,1)S(1)}, bf16[16,4096]{1,0:T(8,128)(2,1)S(1)}, u32[]{:S(2)}, u32[]{:S(2)}) %collective-permute-start.10) | collective-permute-done | bytes 131104 | tf_op jit(solution)/shard_map/ppermute | solution.py:599
  18.4 2.2 %collective-permute-start.12 = (bf16[16,4096]{1,0:T(8,128)(2,1)S(1)}, bf16[16,4096]{1,0:T(8,128)(2,1)S(1)}, u32[]{:S(2)}, u32[]{:S(2)}) collective-permute-start(bf16[16,4096]{1,0:T(8,128)(2,1)S(1)} %collective-permute-done.10.refs_8_), channel_id=1, source_target_pairs={{0,2},{1,5},{2,6},{3,1},{6,10},{7,3},{10,14},{11,7},{14,12},{15,11... | collective-permute-start | bytes 393224 | tf_op jit(solution)/shard_map/ppermute | solution.py:599
  20.8 0.7 %collective-permute-done.2.refs_10_ = bf16[16,4096]{1,0:T(8,128)(2,1)S(1)} collective-permute-done((bf16[16,4096]{1,0:T(8,128)(2,1)S(1)}, bf16[16,4096]{1,0:T(8,128)(2,1)S(1)}, u32[]{:S(2)}, u32[]{:S(2)}) %collective-permute-start.2) | collective-permute-done | bytes 131104 | tf_op jit(solution)/shard_map/ppermute | solution.py:599
  21.5 1.9 %collective-permute-start.3 = (bf16[16,4096]{1,0:T(8,128)(2,1)S(1)}, bf16[16,4096]{1,0:T(8,128)(2,1)S(1)}, u32[]{:S(2)}, u32[]{:S(2)}) collective-permute-start(bf16[16,4096]{1,0:T(8,128)(2,1)S(1)} %collective-permute-done.2.refs_10_), channel_id=1, source_target_pairs={{0,2},{1,5},{2,6},{3,1},{6,10},{7,3},{10,14},{11,7},{14,12},{15,11... | collective-permute-start | bytes 393224 | tf_op jit(solution)/shard_map/ppermute | solution.py:599
  23.5 0.4 collective-permute-start.7
  23.8 0.6 collective-permute-done.12.refs_12_
  24.4 1.2 %collective-permute-done.13.refs_13_ = bf16[16,4096]{1,0:T(8,128)(2,1)S(1)} collective-permute-done((bf16[16,4096]{1,0:T(8,128)(2,1)S(1)}, bf16[16,4096]{1,0:T(8,128)(2,1)S(1)}, u32[]{:S(2)}, u32[]{:S(2)}) %collective-permute-start.13) | collective-permute-done | bytes 131104 | tf_op jit(solution)/shard_map/ppermute | solution.py:599
  25.6 1.9 %early_left.1 = (bf16[256,4096]{1,0:T(8,128)(2,1)S(1)}, bf16[256,448]{1,0:T(8,128)(2,1)S(1)}, f32[64,448]{1,0:T(8,128)S(1)}) custom-call(s32[16,16]{1,0:T(8,128)S(1)} %copy-done.4, bf16[16,4096]{1,0:T(8,128)(2,1)S(1)} %get-tuple-element.50.refs_0_, bf16[16,4096]{1,0:T(8,128)(2,1)S(1)} %get-tuple-element.49.refs_1_, ...), custom_call_target="tpu_custom_call" | custom-call | flops 2300000000 | tf_op jit(solution)/shard_map/early_left/pallas_call | solution.py:118
  27.5 0.9 %collective-permute-done.7.second = bf16[16,4096]{1,0:T(8,128)(2,1)S(1)} collective-permute-done((bf16[16,4096]{1,0:T(8,128)(2,1)S(1)}, bf16[16,4096]{1,0:T(8,128)(2,1)S(1)}, u32[]{:S(2)}, u32[]{:S(2)}) %collective-permute-start.7) | collective-permute-done | bytes 131104 | tf_op jit(solution)/shard_map/ppermute | solution.py:599
  28.4 1.3 %late_left.1 = (bf16[256,4096]{1,0:T(8,128)(2,1)S(1)}, f32[64,448]{1,0:T(8,128)S(1)}) custom-call(s32[16,16]{1,0:T(8,128)S(1)} %copy-done.4, bf16[16,4096]{1,0:T(8,128)(2,1)S(1)} %collective-permute-done.3.first, bf16[16,4096]{1,0:T(8,128)(2,1)S(1)} %collective-permute-done.7.second, ...), custom_call_target="tpu_custom_call", output_to_operand_aliasing={{0}: (6, {})} | custom-call | flops 1150000000 | tf_op jit(solution)/shard_map/late_left/pallas_call | solution.py:150
  29.8 1.3 %collective-permute-done.14.other_l = f32[64,448]{1,0:T(8,128)S(1)} collective-permute-done((f32[64,448]{1,0:T(8,128)S(1)}, f32[64,448]{1,0:T(8,128)S(1)}, u32[]{:S(2)}, u32[]{:S(2)}) %collective-permute-start.14) | collective-permute-done | bytes 114720 | tf_op jit(solution)/shard_map/ppermute | solution.py:612
  31.1 0.5 given_far.1
  31.9 0.6 near_terms.1
  32.5 0.4 collective-permute-start.16
  32.9 0.5 kept_far.1
  33.5 1.8 %collective-permute-start.18 = (f32[72,512]{1,0:T(8,128)S(1)}, f32[72,512]{1,0:T(8,128)S(1)}, u32[]{:S(2)}, u32[]{:S(2)}) collective-permute-start(f32[72,512]{1,0:T(8,128)S(1)} %begin_messages.1), channel_id=1, source_target_pairs={{0,8},{1,3},{2,10},{3,1},{4,12},{5,7},{6,14},{7,5},{8,0},{9,11},{1... | collective-permute-start | bytes 442376 | tf_op jit(solution)/shard_map/ppermute | solution.py:627
  35.4 2.6 %collective-permute-start.19 = (f32[72,512]{1,0:T(8,128)S(1)}, f32[72,512]{1,0:T(8,128)S(1)}, u32[]{:S(2)}, u32[]{:S(2)}) collective-permute-start(f32[72,512]{1,0:T(8,128)S(1)} %get-tuple-element.69), channel_id=1, source_target_pairs={{0,10},{1,5},{2,8},{3,7},{4,14},{5,1},{6,12},{7,3},{8,2},{9,13},{1... | collective-permute-start | bytes 442376 | tf_op jit(solution)/shard_map/ppermute | solution.py:627
  38.0 0.7 collective-permute-start.17
  38.7 2.3 %collective-permute-done.18.passed.refs_0_ = f32[72,512]{1,0:T(8,128)S(1)} collective-permute-done((f32[72,512]{1,0:T(8,128)S(1)}, f32[72,512]{1,0:T(8,128)S(1)}, u32[]{:S(2)}, u32[]{:S(2)}) %collective-permute-start.18) | collective-permute-done | bytes 147488 | tf_op jit(solution)/shard_map/ppermute | solution.py:627
  41.1 1.2 %collective-permute-start.20 = (f32[72,512]{1,0:T(8,128)S(1)}, f32[72,512]{1,0:T(8,128)S(1)}, u32[]{:S(2)}, u32[]{:S(2)}) collective-permute-start(f32[72,512]{1,0:T(8,128)S(1)} %crossing.1), channel_id=1, source_target_pairs={{0,2},{1,13},{2,0},{3,15},{4,6},{5,9},{6,4},{7,11},{8,10},{9,5},{1... | collective-permute-start | bytes 442376 | tf_op jit(solution)/shard_map/ppermute | solution.py:627
  42.3 1.1 %merged.1 = f32[448,4096]{1,0:T(8,128)S(1)} custom-call(bf16[448,256]{1,0:T(8,128)(2,1)S(1)} %bitcast.14, bf16[448,4096]{1,0:T(8,128)(2,1)S(1)} %bitcast.11, bf16[256,4096]{1,0:T(8,128)(2,1)S(1)} %get-tuple-element.67.tokens), custom_call_target="tpu_custom_call" | custom-call | flops 57500000 | tf_op jit(solution)/shard_map/merged/pallas_call | solution.py:272
  43.4 2.7 %collective-permute-done.19.refs_1_ = f32[72,512]{1,0:T(8,128)S(1)} collective-permute-done((f32[72,512]{1,0:T(8,128)S(1)}, f32[72,512]{1,0:T(8,128)S(1)}, u32[]{:S(2)}, u32[]{:S(2)}) %collective-permute-start.19) | collective-permute-done | bytes 147488 | tf_op jit(solution)/shard_map/ppermute | solution.py:627
  46.2 0.5 collective-permute-done.20.refs_2_
  46.8 1.4 %collective-permute-done.21.other = f32[72,512]{1,0:T(8,128)S(1)} collective-permute-done((f32[72,512]{1,0:T(8,128)S(1)}, f32[72,512]{1,0:T(8,128)S(1)}, u32[]{:S(2)}, u32[]{:S(2)}) %collective-permute-start.21) | collective-permute-done | bytes 147488 | tf_op jit(solution)/shard_map/ppermute | solution.py:612
  48.2 2.9 %collective-permute-start.23 = (f32[64,512]{1,0:T(8,128)S(1)}, f32[64,512]{1,0:T(8,128)S(1)}, u32[]{:S(2)}, u32[]{:S(2)}) collective-permute-start(f32[64,512]{1,0:T(8,128)S(1)} %get-tuple-element.71.share.here), channel_id=1, source_target_pairs={{0,2},{1,13},{2,0},{3,15},{4,6},{5,9},{6,4},{7,11},{8,10},{9,5},{1... | collective-permute-start | bytes 393224 | tf_op jit(solution)/shard_map/ppermute | solution.py:627
  51.1 1.0 %collective-permute-start.24 = (f32[64,512]{1,0:T(8,128)S(1)}, f32[64,512]{1,0:T(8,128)S(1)}, u32[]{:S(2)}, u32[]{:S(2)}) collective-permute-start(f32[64,512]{1,0:T(8,128)S(1)} %get-tuple-element.71.share.here), channel_id=1, source_target_pairs={{0,8},{1,5},{2,10},{3,7},{4,12},{5,1},{6,14},{7,3},{8,0},{9,13},{1... | collective-permute-start | bytes 393224 | tf_op jit(solution)/shard_map/ppermute | solution.py:627
  52.0 0.7 collective-permute-start.22
  52.7 1.3 %collective-permute-done.23.refs_0_.there = f32[64,512]{1,0:T(8,128)S(1)} collective-permute-done((f32[64,512]{1,0:T(8,128)S(1)}, f32[64,512]{1,0:T(8,128)S(1)}, u32[]{:S(2)}, u32[]{:S(2)}) %collective-permute-start.23) | collective-permute-done | bytes 131104 | tf_op jit(solution)/shard_map/ppermute | solution.py:627
  54.0 2.5 %collective-permute-start.25 = (f32[64,512]{1,0:T(8,128)S(1)}, f32[64,512]{1,0:T(8,128)S(1)}, u32[]{:S(2)}, u32[]{:S(2)}) collective-permute-start(f32[64,512]{1,0:T(8,128)S(1)} %by_core.1), channel_id=1, source_target_pairs={{0,10},{1,3},{2,8},{3,1},{4,14},{5,7},{6,12},{7,5},{8,2},{9,11},{1... | collective-permute-start | bytes 393224 | tf_op jit(solution)/shard_map/ppermute | solution.py:627
  56.5 1.8 %cholesky_inverse.1.inverse = f32[64,64]{1,0:T(8,128)S(1)} custom-call(f32[64,64]{1,0:T(8,128)S(1)} %get-tuple-element.72.gram), custom_call_target="tpu_custom_call" | custom-call | flops 5750000128 | tf_op jit(solution)/shard_map/cholesky_inverse/pallas_call | solution.py:480
  58.3 0.8 %last_operand.1.lhs = bf16[512,256]{1,0:T(8,128)(2,1)S(1)} custom-call(f32[64,64]{1,0:T(8,128)S(1)} %cholesky_inverse.1.inverse, f32[64,448]{1,0:T(8,128)S(1)} %get-tuple-element.57.left_sum), custom_call_target="tpu_custom_call" | custom-call | flops 57500000 | tf_op jit(solution)/shard_map/last_operand/pallas_call | solution.py:511
  59.1 1.5 %finish.3 = (bf16[448,4096]{1,0:T(8,128)(2,1)}, f32[64,4096]{1,0:T(8,128)}) custom-call(f32[3,64,512]{2,1,0:T(8,128)S(1)} %joined.1.shares, bf16[512,256]{1,0:T(8,128)(2,1)S(1)} %last_operand.1.lhs, f32[448,4096]{1,0:T(8,128)S(1)} %merged.1), custom_call_target="tpu_custom_call" | custom-call | flops 57500000 | tf_op jit(solution)/shard_map/finish/pallas_call | solution.py:549
  60.7 1.6 %collective-permute-done.25 = f32[64,512]{1,0:T(8,128)S(1)} collective-permute-done((f32[64,512]{1,0:T(8,128)S(1)}, f32[64,512]{1,0:T(8,128)S(1)}, u32[]{:S(2)}, u32[]{:S(2)}) %collective-permute-start.25) | collective-permute-done | bytes 131104 | tf_op jit(solution)/shard_map/ppermute | solution.py:627
  62.3 0.8 %collective-permute-start.26 = (f32[4,64,512]{2,1,0:T(8,128)S(1)}, f32[4,64,512]{2,1,0:T(8,128)S(1)}, u32[]{:S(2)}, u32[]{:S(2)}) collective-permute-start(f32[4,64,512]{2,1,0:T(8,128)S(1)} %pad_maximum_fusion), channel_id=1, source_target_pairs={{0,1},{1,0},{2,3},{3,2},{4,5},{5,4},{6,7},{7,6},{8,9},{9,8},{10,11... | collective-permute-start | bytes 1572872 | tf_op jit(solution)/shard_map/ppermute | solution.py:612
  63.2 1.1 %finish.4 = (bf16[448,4096]{1,0:T(8,128)(2,1)}, f32[64,4096]{1,0:T(8,128)}) custom-call(f32[1,64,512]{2,1,0:T(8,128)S(1)} %bitcast.16, bf16[512,256]{1,0:T(8,128)(2,1)S(1)} %last_operand.1.lhs, f32[448,4096]{1,0:T(8,128)S(1)} %merged.1, bf16[448,4096]{1,0:T(8,128)(2,1)} %get-tuple-element.80.refs_0_, ...), custom_call_target="tpu_custom_call", output_to_operand_aliasing={{0}: (3, {}), {1}: (4, {})} | custom-call | flops 57500000 | tf_op jit(solution)/shard_map/finish/pallas_call | solution.py:549
  64.3 0.4 collective-permute-done.26.shares
  64.7 1.7 %finish.5 = (bf16[448,4096]{1,0:T(8,128)(2,1)}, f32[64,4096]{1,0:T(8,128)}) custom-call(f32[4,64,512]{2,1,0:T(8,128)S(1)} %collective-permute-done.26.shares, bf16[512,256]{1,0:T(8,128)(2,1)S(1)} %last_operand.1.lhs, f32[448,4096]{1,0:T(8,128)S(1)} %merged.1, ...), custom_call_target="tpu_custom_call", output_to_operand_aliasing={{0}: (3, {}), {1}: (4, {})} | custom-call | flops 57500000 | tf_op jit(solution)/shard_map/finish/pallas_call | solution.py:549
  (37 shorter events, 1.8 us)
Async XLA Ops:
  0.6 1.0 %copy-start.3 = (bf16[1,32,4096]{2,1,0:T(8,128)(2,1)S(1)}, bf16[1,32,4096]{2,1,0:T(8,128)(2,1)}, u32[]{:S(2)}) copy-start(bf16[1,32,4096]{2,1,0:T(8,128)(2,1)} %param.5) | copy-start | bytes 786436
  1.6 3.2 %copy-start = (bf16[1,448,4096]{2,1,0:T(8,128)(2,1)S(1)}, bf16[1,448,4096]{2,1,0:T(8,128)(2,1)}, u32[]{:S(2)}) copy-start(bf16[1,448,4096]{2,1,0:T(8,128)(2,1)} %param.7) | copy-start | bytes 11010052
  1.6 3.2 %copy-start.2 = (f32[64,4096]{1,0:T(8,128)S(1)}, f32[64,4096]{1,0:T(8,128)}, u32[]{:S(2)}) copy-start(f32[64,4096]{1,0:T(8,128)} %right.1) | copy-start | bytes 3145732
  1.6 6.9 %collective-permute-start = (bf16[16,4096]{1,0:T(8,128)(2,1)S(1)}, bf16[16,4096]{1,0:T(8,128)(2,1)S(1)}, u32[]{:S(2)}, u32[]{:S(2)}) collective-permute-start(bf16[16,4096]{1,0:T(8,128)(2,1)S(1)} %get-tuple-element.50.refs_0_), channel_id=1, source_target_pairs={{0,2},{1,5},{2,6},{3,1},{6,10},{7,3},{10,14},{11,7},{14,12},{15,11... | collective-permute-start | bytes 393224 | tf_op jit(solution)/shard_map/ppermute | solution.py:599
  4.6 5.8 %collective-permute-start.4 = (bf16[16,4096]{1,0:T(8,128)(2,1)S(1)}, bf16[16,4096]{1,0:T(8,128)(2,1)S(1)}, u32[]{:S(2)}, u32[]{:S(2)}) collective-permute-start(bf16[16,4096]{1,0:T(8,128)(2,1)S(1)} %get-tuple-element.49.refs_1_), channel_id=1, source_target_pairs={{0,4},{1,3},{2,0},{3,7},{6,2},{7,11},{10,6},{11,15},{14,10},{15,13... | collective-permute-start | bytes 393224 | tf_op jit(solution)/shard_map/ppermute | solution.py:599
  4.8 20.9 %copy-start.1 = (bf16[1,256,448]{1,2,0:T(8,128)(2,1)S(1)}, bf16[1,256,448]{1,2,0:T(8,128)(2,1)}, u32[]{:S(2)}) copy-start(bf16[1,256,448]{1,2,0:T(8,128)(2,1)} %param.6) | copy-start | bytes 688132
  4.8 20.9 %copy-start.4 = (s32[16,16]{1,0:T(8,128)S(1)}, s32[16,16]{1,0:T(8,128)}, u32[]{:S(2)}) copy-start(s32[16,16]{1,0:T(8,128)} %constant.2.clone.places) | copy-start | bytes 3076
  6.0 6.1 %collective-permute-start.8 = (bf16[16,4096]{1,0:T(8,128)(2,1)S(1)}, bf16[16,4096]{1,0:T(8,128)(2,1)S(1)}, u32[]{:S(2)}, u32[]{:S(2)}) collective-permute-start(bf16[16,4096]{1,0:T(8,128)(2,1)S(1)} %get-tuple-element.49.refs_1_), channel_id=1, source_target_pairs={{0,2},{1,5},{2,6},{3,1},{6,10},{7,3},{10,14},{11,7},{14,12},{15,11... | collective-permute-start | bytes 393224 | tf_op jit(solution)/shard_map/ppermute | solution.py:599
  8.2 6.4 %collective-permute-start.9 = (bf16[16,4096]{1,0:T(8,128)(2,1)S(1)}, bf16[16,4096]{1,0:T(8,128)(2,1)S(1)}, u32[]{:S(2)}, u32[]{:S(2)}) collective-permute-start(bf16[16,4096]{1,0:T(8,128)(2,1)S(1)} %get-tuple-element.50.refs_0_), channel_id=1, source_target_pairs={{0,4},{1,3},{2,0},{3,7},{6,2},{7,11},{10,6},{11,15},{14,10},{15,13... | collective-permute-start | bytes 393224 | tf_op jit(solution)/shard_map/ppermute | solution.py:599
  8.5 6.8 %collective-permute-start.1 = (bf16[16,4096]{1,0:T(8,128)(2,1)S(1)}, bf16[16,4096]{1,0:T(8,128)(2,1)S(1)}, u32[]{:S(2)}, u32[]{:S(2)}) collective-permute-start(bf16[16,4096]{1,0:T(8,128)(2,1)S(1)} %collective-permute-done.refs_2_), channel_id=1, source_target_pairs={{0,2},{1,5},{2,6},{3,1},{6,10},{7,3},{10,14},{11,7},{14,12},{15,11... | collective-permute-start | bytes 393224 | tf_op jit(solution)/shard_map/ppermute | solution.py:599
  10.4 6.4 %collective-permute-start.5 = (bf16[16,4096]{1,0:T(8,128)(2,1)S(1)}, bf16[16,4096]{1,0:T(8,128)(2,1)S(1)}, u32[]{:S(2)}, u32[]{:S(2)}) collective-permute-start(bf16[16,4096]{1,0:T(8,128)(2,1)S(1)} %collective-permute-done.4.refs_3_), channel_id=1, source_target_pairs={{0,4},{1,3},{2,0},{3,7},{6,2},{7,11},{10,6},{11,15},{14,10},{15,13... | collective-permute-start | bytes 393224 | tf_op jit(solution)/shard_map/ppermute | solution.py:599
  12.1 6.4 %collective-permute-start.10 = (bf16[16,4096]{1,0:T(8,128)(2,1)S(1)}, bf16[16,4096]{1,0:T(8,128)(2,1)S(1)}, u32[]{:S(2)}, u32[]{:S(2)}) collective-permute-start(bf16[16,4096]{1,0:T(8,128)(2,1)S(1)} %collective-permute-done.8.refs_4_), channel_id=1, source_target_pairs={{0,2},{1,5},{2,6},{3,1},{6,10},{7,3},{10,14},{11,7},{14,12},{15,11... | collective-permute-start | bytes 393224 | tf_op jit(solution)/shard_map/ppermute | solution.py:599
  14.5 6.1 %collective-permute-start.11 = (bf16[16,4096]{1,0:T(8,128)(2,1)S(1)}, bf16[16,4096]{1,0:T(8,128)(2,1)S(1)}, u32[]{:S(2)}, u32[]{:S(2)}) collective-permute-start(bf16[16,4096]{1,0:T(8,128)(2,1)S(1)} %collective-permute-done.9.refs_5_), channel_id=1, source_target_pairs={{0,4},{1,3},{2,0},{3,7},{6,2},{7,11},{10,6},{11,15},{14,10},{15,13... | collective-permute-start | bytes 393224 | tf_op jit(solution)/shard_map/ppermute | solution.py:599
  15.3 6.2 %collective-permute-start.2 = (bf16[16,4096]{1,0:T(8,128)(2,1)S(1)}, bf16[16,4096]{1,0:T(8,128)(2,1)S(1)}, u32[]{:S(2)}, u32[]{:S(2)}) collective-permute-start(bf16[16,4096]{1,0:T(8,128)(2,1)S(1)} %collective-permute-done.1.refs_6_), channel_id=1, source_target_pairs={{0,2},{1,5},{2,6},{3,1},{6,10},{7,3},{10,14},{11,7},{14,12},{15,11... | collective-permute-start | bytes 393224 | tf_op jit(solution)/shard_map/ppermute | solution.py:599
  16.8 6.6 %collective-permute-start.6 = (bf16[16,4096]{1,0:T(8,128)(2,1)S(1)}, bf16[16,4096]{1,0:T(8,128)(2,1)S(1)}, u32[]{:S(2)}, u32[]{:S(2)}) collective-permute-start(bf16[16,4096]{1,0:T(8,128)(2,1)S(1)} %collective-permute-done.5.refs_7_), channel_id=1, source_target_pairs={{0,4},{1,3},{2,0},{3,7},{6,2},{7,11},{10,6},{11,15},{14,10},{15,13... | collective-permute-start | bytes 393224 | tf_op jit(solution)/shard_map/ppermute | solution.py:599
  18.4 6.0 %collective-permute-start.12 = (bf16[16,4096]{1,0:T(8,128)(2,1)S(1)}, bf16[16,4096]{1,0:T(8,128)(2,1)S(1)}, u32[]{:S(2)}, u32[]{:S(2)}) collective-permute-start(bf16[16,4096]{1,0:T(8,128)(2,1)S(1)} %collective-permute-done.10.refs_8_), channel_id=1, source_target_pairs={{0,2},{1,5},{2,6},{3,1},{6,10},{7,3},{10,14},{11,7},{14,12},{15,11... | collective-permute-start | bytes 393224 | tf_op jit(solution)/shard_map/ppermute | solution.py:599
  20.7 5.0 %collective-permute-start.13 = (bf16[16,4096]{1,0:T(8,128)(2,1)S(1)}, bf16[16,4096]{1,0:T(8,128)(2,1)S(1)}, u32[]{:S(2)}, u32[]{:S(2)}) collective-permute-start(bf16[16,4096]{1,0:T(8,128)(2,1)S(1)} %collective-permute-done.11.refs_9_), channel_id=1, source_target_pairs={{0,4},{1,3},{2,0},{3,7},{6,2},{7,11},{10,6},{11,15},{14,10},{15,13... | collective-permute-start | bytes 393224 | tf_op jit(solution)/shard_map/ppermute | solution.py:599
  21.5 6.0 %collective-permute-start.3 = (bf16[16,4096]{1,0:T(8,128)(2,1)S(1)}, bf16[16,4096]{1,0:T(8,128)(2,1)S(1)}, u32[]{:S(2)}, u32[]{:S(2)}) collective-permute-start(bf16[16,4096]{1,0:T(8,128)(2,1)S(1)} %collective-permute-done.2.refs_10_), channel_id=1, source_target_pairs={{0,2},{1,5},{2,6},{3,1},{6,10},{7,3},{10,14},{11,7},{14,12},{15,11... | collective-permute-start | bytes 393224 | tf_op jit(solution)/shard_map/ppermute | solution.py:599
  23.5 5.0 %collective-permute-start.7 = (bf16[16,4096]{1,0:T(8,128)(2,1)S(1)}, bf16[16,4096]{1,0:T(8,128)(2,1)S(1)}, u32[]{:S(2)}, u32[]{:S(2)}) collective-permute-start(bf16[16,4096]{1,0:T(8,128)(2,1)S(1)} %collective-permute-done.6.refs_11_), channel_id=1, source_target_pairs={{0,4},{1,3},{2,0},{3,7},{6,2},{7,11},{10,6},{11,15},{14,10},{15,13... | collective-permute-start | bytes 393224 | tf_op jit(solution)/shard_map/ppermute | solution.py:599
  29.7 1.4 %collective-permute-start.14 = (f32[64,448]{1,0:T(8,128)S(1)}, f32[64,448]{1,0:T(8,128)S(1)}, u32[]{:S(2)}, u32[]{:S(2)}) collective-permute-start(f32[64,448]{1,0:T(8,128)S(1)} %get-tuple-element.55.here_l), channel_id=1, source_target_pairs={{0,1},{1,0},{2,3},{3,2},{4,5},{5,4},{6,7},{7,6},{8,9},{9,8},{10,11... | collective-permute-start | bytes 344072 | tf_op jit(solution)/shard_map/ppermute | solution.py:612
  31.7 1.7 %collective-permute-start.15 = (f32[2,64,512]{2,1,0:T(8,128)S(1)}, f32[2,64,512]{2,1,0:T(8,128)S(1)}, u32[]{:S(2)}, u32[]{:S(2)}) collective-permute-start(f32[2,64,512]{2,1,0:T(8,128)S(1)} %get-tuple-element.61), channel_id=1, source_target_pairs={{0,1},{1,0},{2,3},{3,2},{4,5},{5,4},{6,7},{7,6},{8,9},{9,8},{10,11... | collective-permute-start | bytes 786440 | tf_op jit(solution)/shard_map/ppermute | solution.py:612
  32.5 2.8 %collective-permute-start.16 = (f32[2,64,512]{2,1,0:T(8,128)S(1)}, f32[2,64,512]{2,1,0:T(8,128)S(1)}, u32[]{:S(2)}, u32[]{:S(2)}) collective-permute-start(f32[2,64,512]{2,1,0:T(8,128)S(1)} %get-tuple-element.63), channel_id=1, source_target_pairs={{0,1},{1,0},{2,3},{3,2},{4,5},{5,4},{6,7},{7,6},{8,9},{9,8},{10,11... | collective-permute-start | bytes 786440 | tf_op jit(solution)/shard_map/ppermute | solution.py:612
  33.5 7.5 %collective-permute-start.18 = (f32[72,512]{1,0:T(8,128)S(1)}, f32[72,512]{1,0:T(8,128)S(1)}, u32[]{:S(2)}, u32[]{:S(2)}) collective-permute-start(f32[72,512]{1,0:T(8,128)S(1)} %begin_messages.1), channel_id=1, source_target_pairs={{0,8},{1,3},{2,10},{3,1},{4,12},{5,7},{6,14},{7,5},{8,0},{9,11},{1... | collective-permute-start | bytes 442376 | tf_op jit(solution)/shard_map/ppermute | solution.py:627
  35.4 10.8 %collective-permute-start.19 = (f32[72,512]{1,0:T(8,128)S(1)}, f32[72,512]{1,0:T(8,128)S(1)}, u32[]{:S(2)}, u32[]{:S(2)}) collective-permute-start(f32[72,512]{1,0:T(8,128)S(1)} %get-tuple-element.69), channel_id=1, source_target_pairs={{0,10},{1,5},{2,8},{3,7},{4,14},{5,1},{6,12},{7,3},{8,2},{9,13},{1... | collective-permute-start | bytes 442376 | tf_op jit(solution)/shard_map/ppermute | solution.py:627
  38.0 5.4 %collective-permute-start.17 = (f32[72,512]{1,0:T(8,128)S(1)}, f32[72,512]{1,0:T(8,128)S(1)}, u32[]{:S(2)}, u32[]{:S(2)}) collective-permute-start(f32[72,512]{1,0:T(8,128)S(1)} %get-tuple-element.66), channel_id=1, source_target_pairs={{1,7},{3,5},{5,3},{7,1},{9,15},{11,13},{13,11},{15,9},{17,23},{19,... | collective-permute-start | bytes 442376 | tf_op jit(solution)/shard_map/ppermute | solution.py:627
  41.1 5.6 %collective-permute-start.20 = (f32[72,512]{1,0:T(8,128)S(1)}, f32[72,512]{1,0:T(8,128)S(1)}, u32[]{:S(2)}, u32[]{:S(2)}) collective-permute-start(f32[72,512]{1,0:T(8,128)S(1)} %crossing.1), channel_id=1, source_target_pairs={{0,2},{1,13},{2,0},{3,15},{4,6},{5,9},{6,4},{7,11},{8,10},{9,5},{1... | collective-permute-start | bytes 442376 | tf_op jit(solution)/shard_map/ppermute | solution.py:627
  46.7 1.4 %collective-permute-start.21 = (f32[72,512]{1,0:T(8,128)S(1)}, f32[72,512]{1,0:T(8,128)S(1)}, u32[]{:S(2)}, u32[]{:S(2)}) collective-permute-start(f32[72,512]{1,0:T(8,128)S(1)} %core_sum.1.here), channel_id=1, source_target_pairs={{0,1},{1,0},{2,3},{3,2},{4,5},{5,4},{6,7},{7,6},{8,9},{9,8},{10,11... | collective-permute-start | bytes 442376 | tf_op jit(solution)/shard_map/ppermute | solution.py:612
  48.2 5.8 %collective-permute-start.23 = (f32[64,512]{1,0:T(8,128)S(1)}, f32[64,512]{1,0:T(8,128)S(1)}, u32[]{:S(2)}, u32[]{:S(2)}) collective-permute-start(f32[64,512]{1,0:T(8,128)S(1)} %get-tuple-element.71.share.here), channel_id=1, source_target_pairs={{0,2},{1,13},{2,0},{3,15},{4,6},{5,9},{6,4},{7,11},{8,10},{9,5},{1... | collective-permute-start | bytes 393224 | tf_op jit(solution)/shard_map/ppermute | solution.py:627
  51.1 7.2 %collective-permute-start.24 = (f32[64,512]{1,0:T(8,128)S(1)}, f32[64,512]{1,0:T(8,128)S(1)}, u32[]{:S(2)}, u32[]{:S(2)}) collective-permute-start(f32[64,512]{1,0:T(8,128)S(1)} %get-tuple-element.71.share.here), channel_id=1, source_target_pairs={{0,8},{1,5},{2,10},{3,7},{4,12},{5,1},{6,14},{7,3},{8,0},{9,13},{1... | collective-permute-start | bytes 393224 | tf_op jit(solution)/shard_map/ppermute | solution.py:627
  52.0 7.1 %collective-permute-start.22 = (f32[64,512]{1,0:T(8,128)S(1)}, f32[64,512]{1,0:T(8,128)S(1)}, u32[]{:S(2)}, u32[]{:S(2)}) collective-permute-start(f32[64,512]{1,0:T(8,128)S(1)} %get-tuple-element.71.share.here), channel_id=1, source_target_pairs={{1,7},{3,5},{5,3},{7,1},{9,15},{11,13},{13,11},{15,9},{17,23},{19,... | collective-permute-start | bytes 393224 | tf_op jit(solution)/shard_map/ppermute | solution.py:627
  54.0 8.2 %collective-permute-start.25 = (f32[64,512]{1,0:T(8,128)S(1)}, f32[64,512]{1,0:T(8,128)S(1)}, u32[]{:S(2)}, u32[]{:S(2)}) collective-permute-start(f32[64,512]{1,0:T(8,128)S(1)} %by_core.1), channel_id=1, source_target_pairs={{0,10},{1,3},{2,8},{3,1},{4,14},{5,7},{6,12},{7,5},{8,2},{9,11},{1... | collective-permute-start | bytes 393224 | tf_op jit(solution)/shard_map/ppermute | solution.py:627
  62.3 2.4 %collective-permute-start.26 = (f32[4,64,512]{2,1,0:T(8,128)S(1)}, f32[4,64,512]{2,1,0:T(8,128)S(1)}, u32[]{:S(2)}, u32[]{:S(2)}) collective-permute-start(f32[4,64,512]{2,1,0:T(8,128)S(1)} %pad_maximum_fusion), channel_id=1, source_target_pairs={{0,1},{1,0},{2,3},{3,2},{4,5},{5,4},{6,7},{7,6},{8,9},{9,8},{10,11... | collective-permute-start | bytes 1572872 | tf_op jit(solution)/shard_map/ppermute | solution.py:612

commit v8 on v7

--- a/solution.py
+++ b/solution.py
@@ -2,7 +2,6 @@
 
 import jax
 import jax.numpy as jnp
-import numpy as np
 from jax import lax
 from jax.experimental import pallas as pl
 from jax.experimental.pallas import tpu as pltpu
@@ -64,6 +63,23 @@
         cost_estimate=cost(4.0),
         name="halves",
     )(shard)
+
+
+def relay_kernel(first, second, first_copy, second_copy):
+    first_copy[...] = first[...]
+    second_copy[...] = second[...]
+
+
+def relayed(halves):
+    return pl.pallas_call(
+        relay_kernel,
+        in_specs=[pl.BlockSpec(memory_space=pltpu.VMEM)] * 2,
+        out_specs=[pl.BlockSpec(memory_space=pltpu.VMEM)] * 2,
+        out_shape=[jax.ShapeDtypeStruct(half.shape, BF16) for half in halves],
+        compiler_params=params(),
+        cost_estimate=cost(2.2),
+        name="relayed",
+    )(*halves)
 
 
 def residue_kernel(right, feedback, terms, left_t):
@@ -95,12 +111,33 @@
     )(right, feedback)
 
 
-def early_kernel(places, *refs):
+def ring_chip(position, chips):
+    if chips != 8:
+        return position
+    up = jnp.where(position == 0, 0, 2 * position - 1)
+    return jnp.where(position < 4, up, jnp.where(position == 4, 7, 2 * (8 - position)))
+
+
+def ring_position(chip, chips):
+    if chips != 8:
+        return chip
+    return jnp.where(chip % 2 == 1, (chip + 1) // 2, jnp.where(chip == 0, 0, 8 - chip // 2))
+
+
+def piece_rows(origin, size):
+    shift, half = origin
+    chips = lax.axis_size("tp")
+    sign = 1 - 2 * lax.axis_index("dp")
+    position = ring_position(lax.axis_index("tp"), chips) + sign * shift + chips
+    source = ring_chip(position % chips, chips)
+    return pl.ds(pl.multiple_of((2 * source + half) * size, size), size)
+
+
+def early_kernel(origins, *refs):
     pieces, (terms, residue_t, hidden_t, tokens, hidden, left_t) = refs[:-6], refs[-6:]
-    here = 2 * lax.axis_index("tp") + lax.axis_index("dp")
     size = pieces[0].shape[0]
-    for index in range(len(pieces) + 2):
-        rows = pl.ds(pl.multiple_of(places[here, index] * size, size), size)
+    for index, origin in enumerate(origins):
+        rows = piece_rows(origin, size)
         if index < len(pieces):
             tokens[rows, :] = pieces[index][...]
         else:
@@ -111,14 +148,13 @@
     hidden[...] = hidden_t[...].T
 
 
-def early_left(places, pieces, terms, residue_t, hidden_t):
+def early_left(origins, pieces, terms, residue_t, hidden_t):
     rows, count = hidden_t.shape
     width = terms.shape[1]
     operands = [*pieces, terms, residue_t, hidden_t]
     return pl.pallas_call(
-        early_kernel,
-        in_specs=[pl.BlockSpec(memory_space=pltpu.SMEM)]
-        + [pl.BlockSpec(memory_space=pltpu.VMEM)] * len(operands),
+        functools.partial(early_kernel, origins),
+        in_specs=[pl.BlockSpec(memory_space=pltpu.VMEM)] * len(operands),
         out_specs=[pl.BlockSpec(memory_space=pltpu.VMEM)] * 3,
         out_shape=[
             jax.ShapeDtypeStruct((count, width), BF16),
@@ -128,16 +164,14 @@
         compiler_params=params(),
         cost_estimate=cost(2.0),
         name="early_left",
-    )(places, *operands)
-
-
-def late_kernel(places, first, second, terms, hidden, early_t, _, tokens, left_t):
-    here = 2 * lax.axis_index("tp") + lax.axis_index("dp")
+    )(*operands)
+
+
+def late_kernel(origins, first, second, terms, hidden, early_t, _, tokens, left_t):
     size = first.shape[0]
-    count = places.shape[1]
     seen = []
-    for index, piece in enumerate((first, second)):
-        rows = pl.ds(pl.multiple_of(places[here, count - 2 + index] * size, size), size)
+    for origin, piece in zip(origins, (first, second)):
+        rows = piece_rows(origin, size)
         tokens[rows, :] = piece[...]
         seen.append(hidden[rows, :])
     projected = fold2(nt(terms[...], jnp.concatenate([first[...], second[...]], axis=0)))
@@ -145,22 +179,21 @@
     left_t[...] = early_t[...] + fold2(nn(stacked, jnp.concatenate(seen, axis=0)))
 
 
-def late_left(places, pieces, terms, hidden, early_t, tokens):
+def late_left(origins, pieces, terms, hidden, early_t, tokens):
     operands = [*pieces, terms, hidden, early_t, tokens]
     return pl.pallas_call(
-        late_kernel,
-        in_specs=[pl.BlockSpec(memory_space=pltpu.SMEM)]
-        + [pl.BlockSpec(memory_space=pltpu.VMEM)] * len(operands),
+        functools.partial(late_kernel, origins),
+        in_specs=[pl.BlockSpec(memory_space=pltpu.VMEM)] * len(operands),
         out_specs=[pl.BlockSpec(memory_space=pltpu.VMEM)] * 2,
         out_shape=[
             jax.ShapeDtypeStruct(tokens.shape, BF16),
             jax.ShapeDtypeStruct(early_t.shape, F32),
         ],
-        input_output_aliases={len(operands): 0},
+        input_output_aliases={len(operands) - 1: 0},
         compiler_params=params(),
         cost_estimate=cost(1.0),
         name="late_left",
-    )(places, *operands)
+    )(*operands)
 
 
 def core_of(place):
@@ -574,9 +607,8 @@
     return list(range(chips))
 
 
-def ring_gather(shard, chips, beside):
+def ring_gather(shard, chips, right_factor):
     order = ring_order(chips)
-    position = {chip: place for place, chip in enumerate(order)}
 
     def pairs(way):
         steps = ((0, way), (1, -way))
@@ -590,7 +622,7 @@
     pieces = list(halves)
     origin = [(0, 0), (0, 1)]
     far = chips // 2
-    *later, beside = lax.optimization_barrier((*halves, beside))
+    later = relayed(halves)
     going = {(1, 0): halves[0], (-1, 1): halves[1], (1, 1): later[1], (-1, 0): later[0]}
     for hop in range(1, far + 1):
         for way, half in ((1, 0), (-1, 1), (1, 1), (-1, 0)):
@@ -599,13 +631,9 @@
             going[way, half] = lax.ppermute(going[way, half], ("tp", "dp"), pairs(way))
             pieces.append(going[way, half])
             origin.append((-way * hop, half))
-    places = np.zeros((2 * chips, len(pieces)), np.int32)
-    for chip in range(chips):
-        for core, sign in ((0, 1), (1, -1)):
-            for index, (shift, half) in enumerate(origin):
-                source = order[(position[chip] + sign * shift) % chips]
-                places[2 * chip + core, index] = 2 * source + half
-    return pieces, places, beside
+        if hop == far - 1:
+            going[1, 0], right_factor = lax.optimization_barrier((going[1, 0], right_factor))
+    return pieces, origin, right_factor
 
 
 def swap(value):
@@ -626,10 +654,10 @@
                     pairs.append((2 * chip + core, 2 * (chip ^ place) + core))
         return lax.ppermute(value, ("tp", "dp"), pairs)
 
-    pieces, places, (terms, residue_t) = ring_gather(shard, chips, residue_left(right_factor, residue))
-    places = jnp.asarray(places)
-    tokens, hidden_rows, left_t = early_left(places, pieces[:-2], terms, residue_t, hidden_t)
-    tokens, left_t = late_left(places, pieces[-2:], terms, hidden_rows, left_t, tokens)
+    pieces, origins, right_factor = ring_gather(shard, chips, right_factor)
+    terms, residue_t = residue_left(right_factor, residue)
+    tokens, hidden_rows, left_t = early_left(origins, pieces[:-2], terms, residue_t, hidden_t)
+    tokens, left_t = late_left(origins[-2:], pieces[-2:], terms, hidden_rows, left_t, tokens)
     give, left_sum, lhs, rhs = given_far(left_t, swap(left_t), hidden_t, residue, tokens, chips)
     got = swap(give)
     keep, gram = kept_far(left_sum, lhs, rhs, residue, tokens, chips)

time: 66.6 us -> 65.2 us (0.979)
  Pallas kernels: 14.4 us -> 13.1 us
  starting transfers between devices: 32 us -> 31.1 us
  waiting for transfers between devices: 18.2 us -> 19 us
    pallas_call x2 -> x3, Pallas kernels: 3.15 us -> 1.86 us  [the longest x1 1.23 us: early_left(): pl.pallas_call(functools.partial(early_kernel, origins), in_specs=[pl.Blo...]
    ppermute x14, waiting for transfers between devices: 6.55 us -> 7.51 us  [ring_gather(): going[way, half] = lax.ppermute(going[way, half], ('tp', 'dp'), pairs(way))]
  transfers between devices with their start and end apart: 27 -> 27, of which waited for: 17 -> 18; matrix products, arithmetic and copies ran while one was open for 0% -> 0% of each run, Pallas kernels for 16% -> 16%
where the time goes in v8:
time: 65.2 us; the launch traced here: 65.1 us
  starting transfers between devices  31.1 us (48%)
  waiting for transfers between devices  19 us (29%)
  Pallas kernels  13.1 us (20%)
  local copies, waits for them, and re-layouts  0.96 us (1%)
  between operations  0.85 us (1%)
    ppermute x14, starting transfers between devices, ring_gather(): going[way, half] = lax.ppermute(going[way, half], ('tp', 'dp'), pairs(way))  16.7 us
    ppermute x8, starting transfers between devices, send(): return lax.ppermute(value, ('tp', 'dp'), pairs)  12.8 us
    ppermute x8, waiting for transfers between devices, send(): return lax.ppermute(value, ('tp', 'dp'), pairs)  8.36 us
    ppermute x14, waiting for transfers between devices, ring_gather(): going[way, half] = lax.ppermute(going[way, half], ('tp', 'dp'), pairs(way))  7.51 us
    pallas_call x3, Pallas kernels, finish(): pl.pallas_call(functools.partial(final_kernel, indices, side), in_specs=[...  4.39 us
    ppermute x5, waiting for transfers between devices, swap(): return lax.ppermute(value, 'dp', [(0, 1), (1, 0)])  3.12 us
    pallas_call x1, Pallas kernels, cholesky_inverse(): pl.pallas_call(inverse_kernel, in_specs=[pl.BlockSpec(memory_space=pltpu....  1.77 us
    ppermute x5, starting transfers between devices, swap(): return lax.ppermute(value, 'dp', [(0, 1), (1, 0)])  1.56 us
  transfers between devices with their start and end apart: 27, of which 18 were waited for; matrix products, arithmetic and copies ran while one was open for 0% of the time, Pallas kernels for 16%

profile of v8, /device:TPU:0, one launch (start us, length us, event | category | flops | bytes accessed | tf_op | source)
XLA Modules:
  0.0 65.1 jit_solution(14157474406763981173)
XLA Ops:
  0.6 0.9 %copy-done.3 = bf16[1,32,4096]{2,1,0:T(8,128)(2,1)S(1)} copy-done((bf16[1,32,4096]{2,1,0:T(8,128)(2,1)S(1)}, bf16[1,32,4096]{2,1,0:T(8,128)(2,1)}, u32[]{:S(2)}) %copy-start.3) | copy-done | bytes 262168
  1.6 3.0 %collective-permute-start = (bf16[16,4096]{1,0:T(8,128)(2,1)S(1)}, bf16[16,4096]{1,0:T(8,128)(2,1)S(1)}, u32[]{:S(2)}, u32[]{:S(2)}) collective-permute-start(bf16[16,4096]{1,0:T(8,128)(2,1)S(1)} %get-tuple-element.44.first.refs_0_), channel_id=1, source_target_pairs={{0,2},{1,5},{2,6},{3,1},{6,10},{7,3},{10,14},{11,7},{14,12},{15,11... | collective-permute-start | bytes 393224 | tf_op jit(solution)/shard_map/ppermute | solution.py:631
  4.8 1.9 %collective-permute-start.8 = (bf16[16,4096]{1,0:T(8,128)(2,1)S(1)}, bf16[16,4096]{1,0:T(8,128)(2,1)S(1)}, u32[]{:S(2)}, u32[]{:S(2)}) collective-permute-start(bf16[16,4096]{1,0:T(8,128)(2,1)S(1)} %get-tuple-element.49), channel_id=1, source_target_pairs={{0,2},{1,5},{2,6},{3,1},{6,10},{7,3},{10,14},{11,7},{14,12},{15,11... | collective-permute-start | bytes 393224 | tf_op jit(solution)/shard_map/ppermute | solution.py:631
  6.9 1.6 %collective-permute-done.refs_2_ = bf16[16,4096]{1,0:T(8,128)(2,1)S(1)} collective-permute-done((bf16[16,4096]{1,0:T(8,128)(2,1)S(1)}, bf16[16,4096]{1,0:T(8,128)(2,1)S(1)}, u32[]{:S(2)}, u32[]{:S(2)}) %collective-permute-start) | collective-permute-done | bytes 131104 | tf_op jit(solution)/shard_map/ppermute | solution.py:631
  8.5 2.5 %collective-permute-start.1 = (bf16[16,4096]{1,0:T(8,128)(2,1)S(1)}, bf16[16,4096]{1,0:T(8,128)(2,1)S(1)}, u32[]{:S(2)}, u32[]{:S(2)}) collective-permute-start(bf16[16,4096]{1,0:T(8,128)(2,1)S(1)} %collective-permute-done.refs_2_), channel_id=1, source_target_pairs={{0,2},{1,5},{2,6},{3,1},{6,10},{7,3},{10,14},{11,7},{14,12},{15,11... | collective-permute-start | bytes 393224 | tf_op jit(solution)/shard_map/ppermute | solution.py:631
  11.3 1.8 %collective-permute-start.10 = (bf16[16,4096]{1,0:T(8,128)(2,1)S(1)}, bf16[16,4096]{1,0:T(8,128)(2,1)S(1)}, u32[]{:S(2)}, u32[]{:S(2)}) collective-permute-start(bf16[16,4096]{1,0:T(8,128)(2,1)S(1)} %collective-permute-done.8.refs_4_), channel_id=1, source_target_pairs={{0,2},{1,5},{2,6},{3,1},{6,10},{7,3},{10,14},{11,7},{14,12},{15,11... | collective-permute-start | bytes 393224 | tf_op jit(solution)/shard_map/ppermute | solution.py:631
  13.0 0.9 %collective-permute-start.11 = (bf16[16,4096]{1,0:T(8,128)(2,1)S(1)}, bf16[16,4096]{1,0:T(8,128)(2,1)S(1)}, u32[]{:S(2)}, u32[]{:S(2)}) collective-permute-start(bf16[16,4096]{1,0:T(8,128)(2,1)S(1)} %collective-permute-done.9.refs_5_), channel_id=1, source_target_pairs={{0,4},{1,3},{2,0},{3,7},{6,2},{7,11},{10,6},{11,15},{14,10},{15,13... | collective-permute-start | bytes 393224 | tf_op jit(solution)/shard_map/ppermute | solution.py:631
  14.0 1.3 %collective-permute-done.1.refs_6_ = bf16[16,4096]{1,0:T(8,128)(2,1)S(1)} collective-permute-done((bf16[16,4096]{1,0:T(8,128)(2,1)S(1)}, bf16[16,4096]{1,0:T(8,128)(2,1)S(1)}, u32[]{:S(2)}, u32[]{:S(2)}) %collective-permute-start.1) | collective-permute-done | bytes 131104 | tf_op jit(solution)/shard_map/ppermute | solution.py:631
  15.2 1.9 %collective-permute-start.2 = (bf16[16,4096]{1,0:T(8,128)(2,1)S(1)}, bf16[16,4096]{1,0:T(8,128)(2,1)S(1)}, u32[]{:S(2)}, u32[]{:S(2)}) collective-permute-start(bf16[16,4096]{1,0:T(8,128)(2,1)S(1)} %collective-permute-done.1.refs_6_), channel_id=1, source_target_pairs={{0,2},{1,5},{2,6},{3,1},{6,10},{7,3},{10,14},{11,7},{14,12},{15,11... | collective-permute-start | bytes 393224 | tf_op jit(solution)/shard_map/ppermute | solution.py:631
  17.3 0.8 %collective-permute-done.10.refs_8_ = bf16[16,4096]{1,0:T(8,128)(2,1)S(1)} collective-permute-done((bf16[16,4096]{1,0:T(8,128)(2,1)S(1)}, bf16[16,4096]{1,0:T(8,128)(2,1)S(1)}, u32[]{:S(2)}, u32[]{:S(2)}) %collective-permute-start.10) | collective-permute-done | bytes 131104 | tf_op jit(solution)/shard_map/ppermute | solution.py:631
  18.1 1.4 %collective-permute-start.12 = (bf16[16,4096]{1,0:T(8,128)(2,1)S(1)}, bf16[16,4096]{1,0:T(8,128)(2,1)S(1)}, u32[]{:S(2)}, u32[]{:S(2)}) collective-permute-start(bf16[16,4096]{1,0:T(8,128)(2,1)S(1)} %collective-permute-done.10.refs_8_), channel_id=1, source_target_pairs={{0,2},{1,5},{2,6},{3,1},{6,10},{7,3},{10,14},{11,7},{14,12},{15,11... | collective-permute-start | bytes 393224 | tf_op jit(solution)/shard_map/ppermute | solution.py:631
  19.5 0.3 collective-permute-done.11.refs_9_
  19.8 0.3 collective-permute-start.13
  20.1 0.8 %collective-permute-done.2.refs_10_ = bf16[16,4096]{1,0:T(8,128)(2,1)S(1)} collective-permute-done((bf16[16,4096]{1,0:T(8,128)(2,1)S(1)}, bf16[16,4096]{1,0:T(8,128)(2,1)S(1)}, u32[]{:S(2)}, u32[]{:S(2)}) %collective-permute-start.2) | collective-permute-done | bytes 131104 | tf_op jit(solution)/shard_map/ppermute | solution.py:631
  20.9 2.5 %collective-permute-start.3 = (bf16[16,4096]{1,0:T(8,128)(2,1)S(1)}, bf16[16,4096]{1,0:T(8,128)(2,1)S(1)}, u32[]{:S(2)}, u32[]{:S(2)}) collective-permute-start(bf16[16,4096]{1,0:T(8,128)(2,1)S(1)} %collective-permute-done.2.refs_10_), channel_id=1, source_target_pairs={{0,2},{1,5},{2,6},{3,1},{6,10},{7,3},{10,14},{11,7},{14,12},{15,11... | collective-permute-start | bytes 393224 | tf_op jit(solution)/shard_map/ppermute | solution.py:631
  23.5 1.2 %residue_left.1 = (bf16[128,4096]{1,0:T(8,128)(2,1)S(1)}, f32[64,448]{1,0:T(8,128)S(1)}) custom-call(f32[64,4096]{1,0:T(8,128)S(1)} %copy-done.2, bf16[448,4096]{1,0:T(8,128)(2,1)S(1)} %bitcast.7), custom_call_target="tpu_custom_call" | custom-call | flops 2529999872 | tf_op jit(solution)/shard_map/residue_left/pallas_call | solution.py:100
  24.8 1.2 %early_left.1 = (bf16[256,4096]{1,0:T(8,128)(2,1)S(1)}, bf16[256,448]{1,0:T(8,128)(2,1)S(1)}, f32[64,448]{1,0:T(8,128)S(1)}) custom-call(bf16[16,4096]{1,0:T(8,128)(2,1)S(1)} %get-tuple-element.44.first.refs_0_, bf16[16,4096]{1,0:T(8,128)(2,1)S(1)} %get-tuple-element.46.second.refs_1_, bf16[16,4096]{1,0:T(8,128)(2,1)S(1)} %collective-permute-done.refs_2_, ...), custom_call_target="tpu_custom_call" | custom-call | flops 2300000000 | tf_op jit(solution)/shard_map/early_left/pallas_call | solution.py:155
  26.0 0.3 collective-permute-done.3.first
  26.3 2.1 %collective-permute-done.7.second = bf16[16,4096]{1,0:T(8,128)(2,1)S(1)} collective-permute-done((bf16[16,4096]{1,0:T(8,128)(2,1)S(1)}, bf16[16,4096]{1,0:T(8,128)(2,1)S(1)}, u32[]{:S(2)}, u32[]{:S(2)}) %collective-permute-start.7) | collective-permute-done | bytes 131104 | tf_op jit(solution)/shard_map/ppermute | solution.py:631
  28.4 0.6 late_left.1
  29.1 1.3 %collective-permute-done.14.other_l = f32[64,448]{1,0:T(8,128)S(1)} collective-permute-done((f32[64,448]{1,0:T(8,128)S(1)}, f32[64,448]{1,0:T(8,128)S(1)}, u32[]{:S(2)}, u32[]{:S(2)}) %collective-permute-start.14) | collective-permute-done | bytes 114720 | tf_op jit(solution)/shard_map/ppermute | solution.py:640
  30.4 0.5 given_far.1
  31.0 0.2 collective-permute-start.15
  31.2 0.6 near_terms.1
  31.8 0.4 collective-permute-start.16
  32.2 0.5 kept_far.1
  32.8 1.1 %collective-permute-start.18 = (f32[72,512]{1,0:T(8,128)S(1)}, f32[72,512]{1,0:T(8,128)S(1)}, u32[]{:S(2)}, u32[]{:S(2)}) collective-permute-start(f32[72,512]{1,0:T(8,128)S(1)} %begin_messages.1), channel_id=1, source_target_pairs={{0,8},{1,3},{2,10},{3,1},{4,12},{5,7},{6,14},{7,5},{8,0},{9,11},{1... | collective-permute-start | bytes 442376 | tf_op jit(solution)/shard_map/ppermute | solution.py:655
  33.9 2.9 %collective-permute-start.19 = (f32[72,512]{1,0:T(8,128)S(1)}, f32[72,512]{1,0:T(8,128)S(1)}, u32[]{:S(2)}, u32[]{:S(2)}) collective-permute-start(f32[72,512]{1,0:T(8,128)S(1)} %get-tuple-element.69), channel_id=1, source_target_pairs={{0,10},{1,5},{2,8},{3,7},{4,14},{5,1},{6,12},{7,3},{8,2},{9,13},{1... | collective-permute-start | bytes 442376 | tf_op jit(solution)/shard_map/ppermute | solution.py:655
  36.8 0.7 %collective-permute-start.17 = (f32[72,512]{1,0:T(8,128)S(1)}, f32[72,512]{1,0:T(8,128)S(1)}, u32[]{:S(2)}, u32[]{:S(2)}) collective-permute-start(f32[72,512]{1,0:T(8,128)S(1)} %get-tuple-element.66), channel_id=1, source_target_pairs={{1,7},{3,5},{5,3},{7,1},{9,15},{11,13},{13,11},{15,9},{17,23},{19,... | collective-permute-start | bytes 442376 | tf_op jit(solution)/shard_map/ppermute | solution.py:655
  37.4 2.4 %collective-permute-done.18.passed.refs_0_ = f32[72,512]{1,0:T(8,128)S(1)} collective-permute-done((f32[72,512]{1,0:T(8,128)S(1)}, f32[72,512]{1,0:T(8,128)S(1)}, u32[]{:S(2)}, u32[]{:S(2)}) %collective-permute-start.18) | collective-permute-done | bytes 147488 | tf_op jit(solution)/shard_map/ppermute | solution.py:655
  39.9 1.1 %collective-permute-start.20 = (f32[72,512]{1,0:T(8,128)S(1)}, f32[72,512]{1,0:T(8,128)S(1)}, u32[]{:S(2)}, u32[]{:S(2)}) collective-permute-start(f32[72,512]{1,0:T(8,128)S(1)} %crossing.1), channel_id=1, source_target_pairs={{0,2},{1,13},{2,0},{3,15},{4,6},{5,9},{6,4},{7,11},{8,10},{9,5},{1... | collective-permute-start | bytes 442376 | tf_op jit(solution)/shard_map/ppermute | solution.py:655
  41.0 1.1 %merged.1 = f32[448,4096]{1,0:T(8,128)S(1)} custom-call(bf16[448,256]{1,0:T(8,128)(2,1)S(1)} %bitcast.14, bf16[448,4096]{1,0:T(8,128)(2,1)S(1)} %bitcast.11, bf16[256,4096]{1,0:T(8,128)(2,1)S(1)} %get-tuple-element.67.tokens), custom_call_target="tpu_custom_call" | custom-call | flops 57500000 | tf_op jit(solution)/shard_map/merged/pallas_call | solution.py:305
  42.2 2.8 %collective-permute-done.19.refs_1_ = f32[72,512]{1,0:T(8,128)S(1)} collective-permute-done((f32[72,512]{1,0:T(8,128)S(1)}, f32[72,512]{1,0:T(8,128)S(1)}, u32[]{:S(2)}, u32[]{:S(2)}) %collective-permute-start.19) | collective-permute-done | bytes 147488 | tf_op jit(solution)/shard_map/ppermute | solution.py:655
  44.9 0.5 collective-permute-done.20.refs_2_
  45.6 1.4 %collective-permute-done.21.other = f32[72,512]{1,0:T(8,128)S(1)} collective-permute-done((f32[72,512]{1,0:T(8,128)S(1)}, f32[72,512]{1,0:T(8,128)S(1)}, u32[]{:S(2)}, u32[]{:S(2)}) %collective-permute-start.21) | collective-permute-done | bytes 147488 | tf_op jit(solution)/shard_map/ppermute | solution.py:640
  47.0 2.6 %collective-permute-start.23 = (f32[64,512]{1,0:T(8,128)S(1)}, f32[64,512]{1,0:T(8,128)S(1)}, u32[]{:S(2)}, u32[]{:S(2)}) collective-permute-start(f32[64,512]{1,0:T(8,128)S(1)} %get-tuple-element.71.share.here), channel_id=1, source_target_pairs={{0,2},{1,13},{2,0},{3,15},{4,6},{5,9},{6,4},{7,11},{8,10},{9,5},{1... | collective-permute-start | bytes 393224 | tf_op jit(solution)/shard_map/ppermute | solution.py:655
  49.7 1.1 %collective-permute-start.24 = (f32[64,512]{1,0:T(8,128)S(1)}, f32[64,512]{1,0:T(8,128)S(1)}, u32[]{:S(2)}, u32[]{:S(2)}) collective-permute-start(f32[64,512]{1,0:T(8,128)S(1)} %get-tuple-element.71.share.here), channel_id=1, source_target_pairs={{0,8},{1,5},{2,10},{3,7},{4,12},{5,1},{6,14},{7,3},{8,0},{9,13},{1... | collective-permute-start | bytes 393224 | tf_op jit(solution)/shard_map/ppermute | solution.py:655
  50.8 0.7 %collective-permute-start.22 = (f32[64,512]{1,0:T(8,128)S(1)}, f32[64,512]{1,0:T(8,128)S(1)}, u32[]{:S(2)}, u32[]{:S(2)}) collective-permute-start(f32[64,512]{1,0:T(8,128)S(1)} %get-tuple-element.71.share.here), channel_id=1, source_target_pairs={{1,7},{3,5},{5,3},{7,1},{9,15},{11,13},{13,11},{15,9},{17,23},{19,... | collective-permute-start | bytes 393224 | tf_op jit(solution)/shard_map/ppermute | solution.py:655
  51.5 1.1 %collective-permute-done.23.refs_0_.there = f32[64,512]{1,0:T(8,128)S(1)} collective-permute-done((f32[64,512]{1,0:T(8,128)S(1)}, f32[64,512]{1,0:T(8,128)S(1)}, u32[]{:S(2)}, u32[]{:S(2)}) %collective-permute-start.23) | collective-permute-done | bytes 131104 | tf_op jit(solution)/shard_map/ppermute | solution.py:655
  52.6 2.7 %collective-permute-start.25 = (f32[64,512]{1,0:T(8,128)S(1)}, f32[64,512]{1,0:T(8,128)S(1)}, u32[]{:S(2)}, u32[]{:S(2)}) collective-permute-start(f32[64,512]{1,0:T(8,128)S(1)} %by_core.1), channel_id=1, source_target_pairs={{0,10},{1,3},{2,8},{3,1},{4,14},{5,7},{6,12},{7,5},{8,2},{9,11},{1... | collective-permute-start | bytes 393224 | tf_op jit(solution)/shard_map/ppermute | solution.py:655
  55.3 1.8 %cholesky_inverse.1.inverse = f32[64,64]{1,0:T(8,128)S(1)} custom-call(f32[64,64]{1,0:T(8,128)S(1)} %get-tuple-element.72.gram), custom_call_target="tpu_custom_call" | custom-call | flops 5750000128 | tf_op jit(solution)/shard_map/cholesky_inverse/pallas_call | solution.py:513
  57.1 0.8 %last_operand.1.lhs = bf16[512,256]{1,0:T(8,128)(2,1)S(1)} custom-call(f32[64,64]{1,0:T(8,128)S(1)} %cholesky_inverse.1.inverse, f32[64,448]{1,0:T(8,128)S(1)} %get-tuple-element.57.left_sum), custom_call_target="tpu_custom_call" | custom-call | flops 57500000 | tf_op jit(solution)/shard_map/last_operand/pallas_call | solution.py:544
  57.9 1.5 %finish.3 = (bf16[448,4096]{1,0:T(8,128)(2,1)}, f32[64,4096]{1,0:T(8,128)}) custom-call(f32[3,64,512]{2,1,0:T(8,128)S(1)} %joined.1.shares, bf16[512,256]{1,0:T(8,128)(2,1)S(1)} %last_operand.1.lhs, f32[448,4096]{1,0:T(8,128)S(1)} %merged.1), custom_call_target="tpu_custom_call" | custom-call | flops 57500000 | tf_op jit(solution)/shard_map/finish/pallas_call | solution.py:582
  59.5 1.5 %collective-permute-done.25 = f32[64,512]{1,0:T(8,128)S(1)} collective-permute-done((f32[64,512]{1,0:T(8,128)S(1)}, f32[64,512]{1,0:T(8,128)S(1)}, u32[]{:S(2)}, u32[]{:S(2)}) %collective-permute-start.25) | collective-permute-done | bytes 131104 | tf_op jit(solution)/shard_map/ppermute | solution.py:655
  61.0 0.8 %collective-permute-start.26 = (f32[4,64,512]{2,1,0:T(8,128)S(1)}, f32[4,64,512]{2,1,0:T(8,128)S(1)}, u32[]{:S(2)}, u32[]{:S(2)}) collective-permute-start(f32[4,64,512]{2,1,0:T(8,128)S(1)} %pad_maximum_fusion), channel_id=1, source_target_pairs={{0,1},{1,0},{2,3},{3,2},{4,5},{5,4},{6,7},{7,6},{8,9},{9,8},{10,11... | collective-permute-start | bytes 1572872 | tf_op jit(solution)/shard_map/ppermute | solution.py:640
  61.8 1.1 %finish.4 = (bf16[448,4096]{1,0:T(8,128)(2,1)}, f32[64,4096]{1,0:T(8,128)}) custom-call(f32[1,64,512]{2,1,0:T(8,128)S(1)} %bitcast.16, bf16[512,256]{1,0:T(8,128)(2,1)S(1)} %last_operand.1.lhs, f32[448,4096]{1,0:T(8,128)S(1)} %merged.1, bf16[448,4096]{1,0:T(8,128)(2,1)} %get-tuple-element.80.refs_0_, ...), custom_call_target="tpu_custom_call", output_to_operand_aliasing={{0}: (3, {}), {1}: (4, {})} | custom-call | flops 57500000 | tf_op jit(solution)/shard_map/finish/pallas_call | solution.py:582
  62.9 0.4 collective-permute-done.26.shares
  63.3 1.7 %finish.5 = (bf16[448,4096]{1,0:T(8,128)(2,1)}, f32[64,4096]{1,0:T(8,128)}) custom-call(f32[4,64,512]{2,1,0:T(8,128)S(1)} %collective-permute-done.26.shares, bf16[512,256]{1,0:T(8,128)(2,1)S(1)} %last_operand.1.lhs, f32[448,4096]{1,0:T(8,128)S(1)} %merged.1, ...), custom_call_target="tpu_custom_call", output_to_operand_aliasing={{0}: (3, {}), {1}: (4, {})} | custom-call | flops 57500000 | tf_op jit(solution)/shard_map/finish/pallas_call | solution.py:582
  (36 shorter events, 1.4 us)
Async XLA Ops:
  0.6 1.0 %copy-start.3 = (bf16[1,32,4096]{2,1,0:T(8,128)(2,1)S(1)}, bf16[1,32,4096]{2,1,0:T(8,128)(2,1)}, u32[]{:S(2)}) copy-start(bf16[1,32,4096]{2,1,0:T(8,128)(2,1)} %param.4) | copy-start | bytes 786436
  1.6 6.9 %collective-permute-start = (bf16[16,4096]{1,0:T(8,128)(2,1)S(1)}, bf16[16,4096]{1,0:T(8,128)(2,1)S(1)}, u32[]{:S(2)}, u32[]{:S(2)}) collective-permute-start(bf16[16,4096]{1,0:T(8,128)(2,1)S(1)} %get-tuple-element.44.first.refs_0_), channel_id=1, source_target_pairs={{0,2},{1,5},{2,6},{3,1},{6,10},{7,3},{10,14},{11,7},{14,12},{15,11... | collective-permute-start | bytes 393224 | tf_op jit(solution)/shard_map/ppermute | solution.py:631
  4.6 18.8 %copy-start = (bf16[1,448,4096]{2,1,0:T(8,128)(2,1)S(1)}, bf16[1,448,4096]{2,1,0:T(8,128)(2,1)}, u32[]{:S(2)}) copy-start(bf16[1,448,4096]{2,1,0:T(8,128)(2,1)} %param.6) | copy-start | bytes 11010052
  4.6 18.8 %copy-start.2 = (f32[64,4096]{1,0:T(8,128)S(1)}, f32[64,4096]{1,0:T(8,128)}, u32[]{:S(2)}) copy-start(f32[64,4096]{1,0:T(8,128)} %right) | copy-start | bytes 3145732
  4.6 6.4 %collective-permute-start.4 = (bf16[16,4096]{1,0:T(8,128)(2,1)S(1)}, bf16[16,4096]{1,0:T(8,128)(2,1)S(1)}, u32[]{:S(2)}, u32[]{:S(2)}) collective-permute-start(bf16[16,4096]{1,0:T(8,128)(2,1)S(1)} %get-tuple-element.46.second.refs_1_), channel_id=1, source_target_pairs={{0,4},{1,3},{2,0},{3,7},{6,2},{7,11},{10,6},{11,15},{14,10},{15,13... | collective-permute-start | bytes 393224 | tf_op jit(solution)/shard_map/ppermute | solution.py:631
  4.8 6.5 %collective-permute-start.8 = (bf16[16,4096]{1,0:T(8,128)(2,1)S(1)}, bf16[16,4096]{1,0:T(8,128)(2,1)S(1)}, u32[]{:S(2)}, u32[]{:S(2)}) collective-permute-start(bf16[16,4096]{1,0:T(8,128)(2,1)S(1)} %get-tuple-element.49), channel_id=1, source_target_pairs={{0,2},{1,5},{2,6},{3,1},{6,10},{7,3},{10,14},{11,7},{14,12},{15,11... | collective-permute-start | bytes 393224 | tf_op jit(solution)/shard_map/ppermute | solution.py:631
  6.7 6.3 %collective-permute-start.9 = (bf16[16,4096]{1,0:T(8,128)(2,1)S(1)}, bf16[16,4096]{1,0:T(8,128)(2,1)S(1)}, u32[]{:S(2)}, u32[]{:S(2)}) collective-permute-start(bf16[16,4096]{1,0:T(8,128)(2,1)S(1)} %get-tuple-element.50), channel_id=1, source_target_pairs={{0,4},{1,3},{2,0},{3,7},{6,2},{7,11},{10,6},{11,15},{14,10},{15,13... | collective-permute-start | bytes 393224 | tf_op jit(solution)/shard_map/ppermute | solution.py:631
  8.5 6.7 %collective-permute-start.1 = (bf16[16,4096]{1,0:T(8,128)(2,1)S(1)}, bf16[16,4096]{1,0:T(8,128)(2,1)S(1)}, u32[]{:S(2)}, u32[]{:S(2)}) collective-permute-start(bf16[16,4096]{1,0:T(8,128)(2,1)S(1)} %collective-permute-done.refs_2_), channel_id=1, source_target_pairs={{0,2},{1,5},{2,6},{3,1},{6,10},{7,3},{10,14},{11,7},{14,12},{15,11... | collective-permute-start | bytes 393224 | tf_op jit(solution)/shard_map/ppermute | solution.py:631
  11.0 6.2 %collective-permute-start.5 = (bf16[16,4096]{1,0:T(8,128)(2,1)S(1)}, bf16[16,4096]{1,0:T(8,128)(2,1)S(1)}, u32[]{:S(2)}, u32[]{:S(2)}) collective-permute-start(bf16[16,4096]{1,0:T(8,128)(2,1)S(1)} %collective-permute-done.4.refs_3_), channel_id=1, source_target_pairs={{0,4},{1,3},{2,0},{3,7},{6,2},{7,11},{10,6},{11,15},{14,10},{15,13... | collective-permute-start | bytes 393224 | tf_op jit(solution)/shard_map/ppermute | solution.py:631
  11.3 6.8 %collective-permute-start.10 = (bf16[16,4096]{1,0:T(8,128)(2,1)S(1)}, bf16[16,4096]{1,0:T(8,128)(2,1)S(1)}, u32[]{:S(2)}, u32[]{:S(2)}) collective-permute-start(bf16[16,4096]{1,0:T(8,128)(2,1)S(1)} %collective-permute-done.8.refs_4_), channel_id=1, source_target_pairs={{0,2},{1,5},{2,6},{3,1},{6,10},{7,3},{10,14},{11,7},{14,12},{15,11... | collective-permute-start | bytes 393224 | tf_op jit(solution)/shard_map/ppermute | solution.py:631
  13.0 6.8 %collective-permute-start.11 = (bf16[16,4096]{1,0:T(8,128)(2,1)S(1)}, bf16[16,4096]{1,0:T(8,128)(2,1)S(1)}, u32[]{:S(2)}, u32[]{:S(2)}) collective-permute-start(bf16[16,4096]{1,0:T(8,128)(2,1)S(1)} %collective-permute-done.9.refs_5_), channel_id=1, source_target_pairs={{0,4},{1,3},{2,0},{3,7},{6,2},{7,11},{10,6},{11,15},{14,10},{15,13... | collective-permute-start | bytes 393224 | tf_op jit(solution)/shard_map/ppermute | solution.py:631
  15.2 5.7 %collective-permute-start.2 = (bf16[16,4096]{1,0:T(8,128)(2,1)S(1)}, bf16[16,4096]{1,0:T(8,128)(2,1)S(1)}, u32[]{:S(2)}, u32[]{:S(2)}) collective-permute-start(bf16[16,4096]{1,0:T(8,128)(2,1)S(1)} %collective-permute-done.1.refs_6_), channel_id=1, source_target_pairs={{0,2},{1,5},{2,6},{3,1},{6,10},{7,3},{10,14},{11,7},{14,12},{15,11... | collective-permute-start | bytes 393224 | tf_op jit(solution)/shard_map/ppermute | solution.py:631
  17.2 6.2 %collective-permute-start.6 = (bf16[16,4096]{1,0:T(8,128)(2,1)S(1)}, bf16[16,4096]{1,0:T(8,128)(2,1)S(1)}, u32[]{:S(2)}, u32[]{:S(2)}) collective-permute-start(bf16[16,4096]{1,0:T(8,128)(2,1)S(1)} %collective-permute-done.5.refs_7_), channel_id=1, source_target_pairs={{0,4},{1,3},{2,0},{3,7},{6,2},{7,11},{10,6},{11,15},{14,10},{15,13... | collective-permute-start | bytes 393224 | tf_op jit(solution)/shard_map/ppermute | solution.py:631
  18.1 6.6 %collective-permute-start.12 = (bf16[16,4096]{1,0:T(8,128)(2,1)S(1)}, bf16[16,4096]{1,0:T(8,128)(2,1)S(1)}, u32[]{:S(2)}, u32[]{:S(2)}) collective-permute-start(bf16[16,4096]{1,0:T(8,128)(2,1)S(1)} %collective-permute-done.10.refs_8_), channel_id=1, source_target_pairs={{0,2},{1,5},{2,6},{3,1},{6,10},{7,3},{10,14},{11,7},{14,12},{15,11... | collective-permute-start | bytes 393224 | tf_op jit(solution)/shard_map/ppermute | solution.py:631
  19.8 5.0 %collective-permute-start.13 = (bf16[16,4096]{1,0:T(8,128)(2,1)S(1)}, bf16[16,4096]{1,0:T(8,128)(2,1)S(1)}, u32[]{:S(2)}, u32[]{:S(2)}) collective-permute-start(bf16[16,4096]{1,0:T(8,128)(2,1)S(1)} %collective-permute-done.11.refs_9_), channel_id=1, source_target_pairs={{0,4},{1,3},{2,0},{3,7},{6,2},{7,11},{10,6},{11,15},{14,10},{15,13... | collective-permute-start | bytes 393224 | tf_op jit(solution)/shard_map/ppermute | solution.py:631
  20.9 5.4 %collective-permute-start.3 = (bf16[16,4096]{1,0:T(8,128)(2,1)S(1)}, bf16[16,4096]{1,0:T(8,128)(2,1)S(1)}, u32[]{:S(2)}, u32[]{:S(2)}) collective-permute-start(bf16[16,4096]{1,0:T(8,128)(2,1)S(1)} %collective-permute-done.2.refs_10_), channel_id=1, source_target_pairs={{0,2},{1,5},{2,6},{3,1},{6,10},{7,3},{10,14},{11,7},{14,12},{15,11... | collective-permute-start | bytes 393224 | tf_op jit(solution)/shard_map/ppermute | solution.py:631
  23.4 5.0 %collective-permute-start.7 = (bf16[16,4096]{1,0:T(8,128)(2,1)S(1)}, bf16[16,4096]{1,0:T(8,128)(2,1)S(1)}, u32[]{:S(2)}, u32[]{:S(2)}) collective-permute-start(bf16[16,4096]{1,0:T(8,128)(2,1)S(1)} %collective-permute-done.6.refs_11_), channel_id=1, source_target_pairs={{0,4},{1,3},{2,0},{3,7},{6,2},{7,11},{10,6},{11,15},{14,10},{15,13... | collective-permute-start | bytes 393224 | tf_op jit(solution)/shard_map/ppermute | solution.py:631
  23.4 1.3 %copy-start.1 = (bf16[1,256,448]{1,2,0:T(8,128)(2,1)S(1)}, bf16[1,256,448]{1,2,0:T(8,128)(2,1)}, u32[]{:S(2)}) copy-start(bf16[1,256,448]{1,2,0:T(8,128)(2,1)} %param.5) | copy-start | bytes 688132
  29.0 1.4 %collective-permute-start.14 = (f32[64,448]{1,0:T(8,128)S(1)}, f32[64,448]{1,0:T(8,128)S(1)}, u32[]{:S(2)}, u32[]{:S(2)}) collective-permute-start(f32[64,448]{1,0:T(8,128)S(1)} %get-tuple-element.55.here_l), channel_id=1, source_target_pairs={{0,1},{1,0},{2,3},{3,2},{4,5},{5,4},{6,7},{7,6},{8,9},{9,8},{10,11... | collective-permute-start | bytes 344072 | tf_op jit(solution)/shard_map/ppermute | solution.py:640
  31.0 1.7 %collective-permute-start.15 = (f32[2,64,512]{2,1,0:T(8,128)S(1)}, f32[2,64,512]{2,1,0:T(8,128)S(1)}, u32[]{:S(2)}, u32[]{:S(2)}) collective-permute-start(f32[2,64,512]{2,1,0:T(8,128)S(1)} %get-tuple-element.61), channel_id=1, source_target_pairs={{0,1},{1,0},{2,3},{3,2},{4,5},{5,4},{6,7},{7,6},{8,9},{9,8},{10,11... | collective-permute-start | bytes 786440 | tf_op jit(solution)/shard_map/ppermute | solution.py:640
  31.8 2.1 %collective-permute-start.16 = (f32[2,64,512]{2,1,0:T(8,128)S(1)}, f32[2,64,512]{2,1,0:T(8,128)S(1)}, u32[]{:S(2)}, u32[]{:S(2)}) collective-permute-start(f32[2,64,512]{2,1,0:T(8,128)S(1)} %get-tuple-element.63), channel_id=1, source_target_pairs={{0,1},{1,0},{2,3},{3,2},{4,5},{5,4},{6,7},{7,6},{8,9},{9,8},{10,11... | collective-permute-start | bytes 786440 | tf_op jit(solution)/shard_map/ppermute | solution.py:640
  32.8 7.1 %collective-permute-start.18 = (f32[72,512]{1,0:T(8,128)S(1)}, f32[72,512]{1,0:T(8,128)S(1)}, u32[]{:S(2)}, u32[]{:S(2)}) collective-permute-start(f32[72,512]{1,0:T(8,128)S(1)} %begin_messages.1), channel_id=1, source_target_pairs={{0,8},{1,3},{2,10},{3,1},{4,12},{5,7},{6,14},{7,5},{8,0},{9,11},{1... | collective-permute-start | bytes 442376 | tf_op jit(solution)/shard_map/ppermute | solution.py:655
  33.9 11.0 %collective-permute-start.19 = (f32[72,512]{1,0:T(8,128)S(1)}, f32[72,512]{1,0:T(8,128)S(1)}, u32[]{:S(2)}, u32[]{:S(2)}) collective-permute-start(f32[72,512]{1,0:T(8,128)S(1)} %get-tuple-element.69), channel_id=1, source_target_pairs={{0,10},{1,5},{2,8},{3,7},{4,14},{5,1},{6,12},{7,3},{8,2},{9,13},{1... | collective-permute-start | bytes 442376 | tf_op jit(solution)/shard_map/ppermute | solution.py:655
  36.8 5.4 %collective-permute-start.17 = (f32[72,512]{1,0:T(8,128)S(1)}, f32[72,512]{1,0:T(8,128)S(1)}, u32[]{:S(2)}, u32[]{:S(2)}) collective-permute-start(f32[72,512]{1,0:T(8,128)S(1)} %get-tuple-element.66), channel_id=1, source_target_pairs={{1,7},{3,5},{5,3},{7,1},{9,15},{11,13},{13,11},{15,9},{17,23},{19,... | collective-permute-start | bytes 442376 | tf_op jit(solution)/shard_map/ppermute | solution.py:655
  39.9 5.6 %collective-permute-start.20 = (f32[72,512]{1,0:T(8,128)S(1)}, f32[72,512]{1,0:T(8,128)S(1)}, u32[]{:S(2)}, u32[]{:S(2)}) collective-permute-start(f32[72,512]{1,0:T(8,128)S(1)} %crossing.1), channel_id=1, source_target_pairs={{0,2},{1,13},{2,0},{3,15},{4,6},{5,9},{6,4},{7,11},{8,10},{9,5},{1... | collective-permute-start | bytes 442376 | tf_op jit(solution)/shard_map/ppermute | solution.py:655
  45.5 1.4 %collective-permute-start.21 = (f32[72,512]{1,0:T(8,128)S(1)}, f32[72,512]{1,0:T(8,128)S(1)}, u32[]{:S(2)}, u32[]{:S(2)}) collective-permute-start(f32[72,512]{1,0:T(8,128)S(1)} %core_sum.1.here), channel_id=1, source_target_pairs={{0,1},{1,0},{2,3},{3,2},{4,5},{5,4},{6,7},{7,6},{8,9},{9,8},{10,11... | collective-permute-start | bytes 442376 | tf_op jit(solution)/shard_map/ppermute | solution.py:640
  47.0 5.6 %collective-permute-start.23 = (f32[64,512]{1,0:T(8,128)S(1)}, f32[64,512]{1,0:T(8,128)S(1)}, u32[]{:S(2)}, u32[]{:S(2)}) collective-permute-start(f32[64,512]{1,0:T(8,128)S(1)} %get-tuple-element.71.share.here), channel_id=1, source_target_pairs={{0,2},{1,13},{2,0},{3,15},{4,6},{5,9},{6,4},{7,11},{8,10},{9,5},{1... | collective-permute-start | bytes 393224 | tf_op jit(solution)/shard_map/ppermute | solution.py:655
  49.7 7.4 %collective-permute-start.24 = (f32[64,512]{1,0:T(8,128)S(1)}, f32[64,512]{1,0:T(8,128)S(1)}, u32[]{:S(2)}, u32[]{:S(2)}) collective-permute-start(f32[64,512]{1,0:T(8,128)S(1)} %get-tuple-element.71.share.here), channel_id=1, source_target_pairs={{0,8},{1,5},{2,10},{3,7},{4,12},{5,1},{6,14},{7,3},{8,0},{9,13},{1... | collective-permute-start | bytes 393224 | tf_op jit(solution)/shard_map/ppermute | solution.py:655
  50.8 7.1 %collective-permute-start.22 = (f32[64,512]{1,0:T(8,128)S(1)}, f32[64,512]{1,0:T(8,128)S(1)}, u32[]{:S(2)}, u32[]{:S(2)}) collective-permute-start(f32[64,512]{1,0:T(8,128)S(1)} %get-tuple-element.71.share.here), channel_id=1, source_target_pairs={{1,7},{3,5},{5,3},{7,1},{9,15},{11,13},{13,11},{15,9},{17,23},{19,... | collective-permute-start | bytes 393224 | tf_op jit(solution)/shard_map/ppermute | solution.py:655
  52.6 8.3 %collective-permute-start.25 = (f32[64,512]{1,0:T(8,128)S(1)}, f32[64,512]{1,0:T(8,128)S(1)}, u32[]{:S(2)}, u32[]{:S(2)}) collective-permute-start(f32[64,512]{1,0:T(8,128)S(1)} %by_core.1), channel_id=1, source_target_pairs={{0,10},{1,3},{2,8},{3,1},{4,14},{5,7},{6,12},{7,5},{8,2},{9,11},{1... | collective-permute-start | bytes 393224 | tf_op jit(solution)/shard_map/ppermute | solution.py:655
  61.0 2.3 %collective-permute-start.26 = (f32[4,64,512]{2,1,0:T(8,128)S(1)}, f32[4,64,512]{2,1,0:T(8,128)S(1)}, u32[]{:S(2)}, u32[]{:S(2)}) collective-permute-start(f32[4,64,512]{2,1,0:T(8,128)S(1)} %pad_maximum_fusion), channel_id=1, source_target_pairs={{0,1},{1,0},{2,3},{3,2},{4,5},{5,4},{6,7},{7,6},{8,9},{9,8},{10,11... | collective-permute-start | bytes 1572872 | tf_op jit(solution)/shard_map/ppermute | solution.py:640

commit v9 on v8

--- a/solution.py
+++ b/solution.py
@@ -558,8 +558,9 @@
     rows = merged.shape[0]
     rank, cols = shares.shape[1:]
     copies = []
-    for block, index in enumerate(indices):
-        span = columns_of(place_of(owner, index), cols)
+    for block, (index, other) in enumerate(indices):
+        place = jnp.where(owner == 0, place_of(0, index), place_of(1, other))
+        span = columns_of(place, cols)
         high, low = split2(shares[block])
         for place, term in enumerate((high, low, high, low)):
             rhs[block % 2, place * rank : (place + 1) * rank, :] = term
@@ -678,21 +679,21 @@
     share, gram_matrix = chip_sum(partial, swap(partial), rank)
 
     begun = [send(share, int(place == 4), place + 2) for place in evens]
-    direct = [send(share, place, 2 * (place == 4)) for place in evens]
+    direct = [send(share, place + 1, 2 * (place == 4)) for place in evens]
     third = send(share, 0, 3)
-    passed = [send(by_core(share, value), place + 1, 1) for value, place in zip(begun, evens)]
+    passed = [send(by_core(share, value), place, 1) for value, place in zip(begun, evens)]
     inverse = cholesky_inverse(gram_matrix)
     inverse, begun, direct = lax.optimization_barrier((inverse, begun, direct))
     lhs = last_operand(inverse, left_sum, replicas)
     mine = joined(share, third, begun, direct)
-    half = chips // 2
-    begun = finish([0, 1, *range(2, half, 2)], mine, 0, lhs, merged)
-    passed, begun = lax.optimization_barrier((passed, begun))
+    early = [(0, 0), (1, 1)] + [(index + 1, index) for index in range(2, chips // 2, 2)]
+    late = [(index, index + 1) for index in range(2, chips // 2, 2)]
+    done = finish(early, mine, 0, lhs, merged)
+    passed, done = lax.optimization_barrier((passed, done))
     rest = passed[0][None] if len(passed) == 1 else jnp.stack(passed)
     theirs = swap(jnp.concatenate([mine, rest]))
-    begun = finish([*range(3, half, 2)], rest, 0, lhs, merged, begun)
-    order = [0, 1, *range(2, half, 2), *range(3, half, 2)]
-    new_feedback, new_factor = finish(order, theirs, 1, lhs, merged, begun)
+    done = finish(late, rest, 0, lhs, merged, done)
+    new_feedback, new_factor = finish(early + late, theirs, 1, lhs, merged, done)
     return new_feedback[None], new_factor
 
 

time: 65.2 us -> 64.3 us (0.986)
  starting transfers between devices: 31.1 us -> 29.8 us
    ppermute x5, starting transfers between devices: 1.56 us -> 0.86 us  [swap(): return lax.ppermute(value, 'dp', [(0, 1), (1, 0)])]
where the time goes in v9:
time: 64.3 us; the launch traced here: 64.1 us
  starting transfers between devices  29.8 us (46%)
  waiting for transfers between devices  19.4 us (30%)
  Pallas kernels  13.1 us (20%)
  local copies, waits for them, and re-layouts  0.96 us (1%)
  between operations  0.86 us (1%)
    ppermute x14, starting transfers between devices, ring_gather(): going[way, half] = lax.ppermute(going[way, half], ('tp', 'dp'), pairs(way))  16.7 us
    ppermute x8, starting transfers between devices, send(): return lax.ppermute(value, ('tp', 'dp'), pairs)  12.2 us
    ppermute x8, waiting for transfers between devices, send(): return lax.ppermute(value, ('tp', 'dp'), pairs)  8.41 us
    ppermute x14, waiting for transfers between devices, ring_gather(): going[way, half] = lax.ppermute(going[way, half], ('tp', 'dp'), pairs(way))  7.51 us
    pallas_call x3, Pallas kernels, finish(): pl.pallas_call(functools.partial(final_kernel, indices, side), in_specs=[...  4.39 us
    ppermute x5, waiting for transfers between devices, swap(): return lax.ppermute(value, 'dp', [(0, 1), (1, 0)])  3.47 us
    pallas_call x1, Pallas kernels, cholesky_inverse(): pl.pallas_call(inverse_kernel, in_specs=[pl.BlockSpec(memory_space=pltpu....  1.77 us
  transfers between devices with their start and end apart: 27, of which 18 were waited for; matrix products, arithmetic and copies ran while one was open for 0% of the time, Pallas kernels for 16%

profile of v9, /device:TPU:0, one launch (start us, length us, event | category | flops | bytes accessed | tf_op | source)
XLA Modules:
  0.0 64.1 jit_solution(3981294874489534483)
XLA Ops:
  0.6 0.9 %copy-done.3 = bf16[1,32,4096]{2,1,0:T(8,128)(2,1)S(1)} copy-done((bf16[1,32,4096]{2,1,0:T(8,128)(2,1)S(1)}, bf16[1,32,4096]{2,1,0:T(8,128)(2,1)}, u32[]{:S(2)}) %copy-start.3) | copy-done | bytes 262168
  1.6 3.0 %collective-permute-start = (bf16[16,4096]{1,0:T(8,128)(2,1)S(1)}, bf16[16,4096]{1,0:T(8,128)(2,1)S(1)}, u32[]{:S(2)}, u32[]{:S(2)}) collective-permute-start(bf16[16,4096]{1,0:T(8,128)(2,1)S(1)} %get-tuple-element.44.first.refs_0_), channel_id=1, source_target_pairs={{0,2},{1,5},{2,6},{3,1},{6,10},{7,3},{10,14},{11,7},{14,12},{15,11... | collective-permute-start | bytes 393224 | tf_op jit(solution)/shard_map/ppermute | solution.py:632
  4.8 1.9 %collective-permute-start.8 = (bf16[16,4096]{1,0:T(8,128)(2,1)S(1)}, bf16[16,4096]{1,0:T(8,128)(2,1)S(1)}, u32[]{:S(2)}, u32[]{:S(2)}) collective-permute-start(bf16[16,4096]{1,0:T(8,128)(2,1)S(1)} %get-tuple-element.49), channel_id=1, source_target_pairs={{0,2},{1,5},{2,6},{3,1},{6,10},{7,3},{10,14},{11,7},{14,12},{15,11... | collective-permute-start | bytes 393224 | tf_op jit(solution)/shard_map/ppermute | solution.py:632
  6.9 1.6 %collective-permute-done.refs_2_ = bf16[16,4096]{1,0:T(8,128)(2,1)S(1)} collective-permute-done((bf16[16,4096]{1,0:T(8,128)(2,1)S(1)}, bf16[16,4096]{1,0:T(8,128)(2,1)S(1)}, u32[]{:S(2)}, u32[]{:S(2)}) %collective-permute-start) | collective-permute-done | bytes 131104 | tf_op jit(solution)/shard_map/ppermute | solution.py:632
  8.5 2.5 %collective-permute-start.1 = (bf16[16,4096]{1,0:T(8,128)(2,1)S(1)}, bf16[16,4096]{1,0:T(8,128)(2,1)S(1)}, u32[]{:S(2)}, u32[]{:S(2)}) collective-permute-start(bf16[16,4096]{1,0:T(8,128)(2,1)S(1)} %collective-permute-done.refs_2_), channel_id=1, source_target_pairs={{0,2},{1,5},{2,6},{3,1},{6,10},{7,3},{10,14},{11,7},{14,12},{15,11... | collective-permute-start | bytes 393224 | tf_op jit(solution)/shard_map/ppermute | solution.py:632
  11.0 0.2 collective-permute-start.5
  11.3 1.8 %collective-permute-start.10 = (bf16[16,4096]{1,0:T(8,128)(2,1)S(1)}, bf16[16,4096]{1,0:T(8,128)(2,1)S(1)}, u32[]{:S(2)}, u32[]{:S(2)}) collective-permute-start(bf16[16,4096]{1,0:T(8,128)(2,1)S(1)} %collective-permute-done.8.refs_4_), channel_id=1, source_target_pairs={{0,2},{1,5},{2,6},{3,1},{6,10},{7,3},{10,14},{11,7},{14,12},{15,11... | collective-permute-start | bytes 393224 | tf_op jit(solution)/shard_map/ppermute | solution.py:632
  13.0 0.9 %collective-permute-start.11 = (bf16[16,4096]{1,0:T(8,128)(2,1)S(1)}, bf16[16,4096]{1,0:T(8,128)(2,1)S(1)}, u32[]{:S(2)}, u32[]{:S(2)}) collective-permute-start(bf16[16,4096]{1,0:T(8,128)(2,1)S(1)} %collective-permute-done.9.refs_5_), channel_id=1, source_target_pairs={{0,4},{1,3},{2,0},{3,7},{6,2},{7,11},{10,6},{11,15},{14,10},{15,13... | collective-permute-start | bytes 393224 | tf_op jit(solution)/shard_map/ppermute | solution.py:632
  14.0 1.3 %collective-permute-done.1.refs_6_ = bf16[16,4096]{1,0:T(8,128)(2,1)S(1)} collective-permute-done((bf16[16,4096]{1,0:T(8,128)(2,1)S(1)}, bf16[16,4096]{1,0:T(8,128)(2,1)S(1)}, u32[]{:S(2)}, u32[]{:S(2)}) %collective-permute-start.1) | collective-permute-done | bytes 131104 | tf_op jit(solution)/shard_map/ppermute | solution.py:632
  15.2 1.9 %collective-permute-start.2 = (bf16[16,4096]{1,0:T(8,128)(2,1)S(1)}, bf16[16,4096]{1,0:T(8,128)(2,1)S(1)}, u32[]{:S(2)}, u32[]{:S(2)}) collective-permute-start(bf16[16,4096]{1,0:T(8,128)(2,1)S(1)} %collective-permute-done.1.refs_6_), channel_id=1, source_target_pairs={{0,2},{1,5},{2,6},{3,1},{6,10},{7,3},{10,14},{11,7},{14,12},{15,11... | collective-permute-start | bytes 393224 | tf_op jit(solution)/shard_map/ppermute | solution.py:632
  17.3 0.8 %collective-permute-done.10.refs_8_ = bf16[16,4096]{1,0:T(8,128)(2,1)S(1)} collective-permute-done((bf16[16,4096]{1,0:T(8,128)(2,1)S(1)}, bf16[16,4096]{1,0:T(8,128)(2,1)S(1)}, u32[]{:S(2)}, u32[]{:S(2)}) %collective-permute-start.10) | collective-permute-done | bytes 131104 | tf_op jit(solution)/shard_map/ppermute | solution.py:632
  18.1 1.4 %collective-permute-start.12 = (bf16[16,4096]{1,0:T(8,128)(2,1)S(1)}, bf16[16,4096]{1,0:T(8,128)(2,1)S(1)}, u32[]{:S(2)}, u32[]{:S(2)}) collective-permute-start(bf16[16,4096]{1,0:T(8,128)(2,1)S(1)} %collective-permute-done.10.refs_8_), channel_id=1, source_target_pairs={{0,2},{1,5},{2,6},{3,1},{6,10},{7,3},{10,14},{11,7},{14,12},{15,11... | collective-permute-start | bytes 393224 | tf_op jit(solution)/shard_map/ppermute | solution.py:632
  19.5 0.3 collective-permute-done.11.refs_9_
  19.8 0.3 collective-permute-start.13
  20.1 0.8 %collective-permute-done.2.refs_10_ = bf16[16,4096]{1,0:T(8,128)(2,1)S(1)} collective-permute-done((bf16[16,4096]{1,0:T(8,128)(2,1)S(1)}, bf16[16,4096]{1,0:T(8,128)(2,1)S(1)}, u32[]{:S(2)}, u32[]{:S(2)}) %collective-permute-start.2) | collective-permute-done | bytes 131104 | tf_op jit(solution)/shard_map/ppermute | solution.py:632
  20.9 2.5 %collective-permute-start.3 = (bf16[16,4096]{1,0:T(8,128)(2,1)S(1)}, bf16[16,4096]{1,0:T(8,128)(2,1)S(1)}, u32[]{:S(2)}, u32[]{:S(2)}) collective-permute-start(bf16[16,4096]{1,0:T(8,128)(2,1)S(1)} %collective-permute-done.2.refs_10_), channel_id=1, source_target_pairs={{0,2},{1,5},{2,6},{3,1},{6,10},{7,3},{10,14},{11,7},{14,12},{15,11... | collective-permute-start | bytes 393224 | tf_op jit(solution)/shard_map/ppermute | solution.py:632
  23.5 1.2 %residue_left.1 = (bf16[128,4096]{1,0:T(8,128)(2,1)S(1)}, f32[64,448]{1,0:T(8,128)S(1)}) custom-call(f32[64,4096]{1,0:T(8,128)S(1)} %copy-done.2, bf16[448,4096]{1,0:T(8,128)(2,1)S(1)} %bitcast.7), custom_call_target="tpu_custom_call" | custom-call | flops 2529999872 | tf_op jit(solution)/shard_map/residue_left/pallas_call | solution.py:100
  24.8 1.2 %early_left.1 = (bf16[256,4096]{1,0:T(8,128)(2,1)S(1)}, bf16[256,448]{1,0:T(8,128)(2,1)S(1)}, f32[64,448]{1,0:T(8,128)S(1)}) custom-call(bf16[16,4096]{1,0:T(8,128)(2,1)S(1)} %get-tuple-element.44.first.refs_0_, bf16[16,4096]{1,0:T(8,128)(2,1)S(1)} %get-tuple-element.46.second.refs_1_, bf16[16,4096]{1,0:T(8,128)(2,1)S(1)} %collective-permute-done.refs_2_, ...), custom_call_target="tpu_custom_call" | custom-call | flops 2300000000 | tf_op jit(solution)/shard_map/early_left/pallas_call | solution.py:155
  26.0 0.3 collective-permute-done.3.first
  26.3 2.1 %collective-permute-done.7.second = bf16[16,4096]{1,0:T(8,128)(2,1)S(1)} collective-permute-done((bf16[16,4096]{1,0:T(8,128)(2,1)S(1)}, bf16[16,4096]{1,0:T(8,128)(2,1)S(1)}, u32[]{:S(2)}, u32[]{:S(2)}) %collective-permute-start.7) | collective-permute-done | bytes 131104 | tf_op jit(solution)/shard_map/ppermute | solution.py:632
  28.4 0.6 late_left.1
  29.1 1.3 %collective-permute-done.14.other_l = f32[64,448]{1,0:T(8,128)S(1)} collective-permute-done((f32[64,448]{1,0:T(8,128)S(1)}, f32[64,448]{1,0:T(8,128)S(1)}, u32[]{:S(2)}, u32[]{:S(2)}) %collective-permute-start.14) | collective-permute-done | bytes 114720 | tf_op jit(solution)/shard_map/ppermute | solution.py:641
  30.4 0.5 given_far.1
  31.0 0.2 collective-permute-start.15
  31.2 0.6 near_terms.1
  31.8 0.4 collective-permute-start.16
  32.2 0.5 kept_far.1
  32.8 1.1 %collective-permute-start.18 = (f32[72,512]{1,0:T(8,128)S(1)}, f32[72,512]{1,0:T(8,128)S(1)}, u32[]{:S(2)}, u32[]{:S(2)}) collective-permute-start(f32[72,512]{1,0:T(8,128)S(1)} %begin_messages.1), channel_id=1, source_target_pairs={{0,8},{1,3},{2,10},{3,1},{4,12},{5,7},{6,14},{7,5},{8,0},{9,11},{1... | collective-permute-start | bytes 442376 | tf_op jit(solution)/shard_map/ppermute | solution.py:656
  33.9 2.9 %collective-permute-start.19 = (f32[72,512]{1,0:T(8,128)S(1)}, f32[72,512]{1,0:T(8,128)S(1)}, u32[]{:S(2)}, u32[]{:S(2)}) collective-permute-start(f32[72,512]{1,0:T(8,128)S(1)} %get-tuple-element.69), channel_id=1, source_target_pairs={{0,10},{1,5},{2,8},{3,7},{4,14},{5,1},{6,12},{7,3},{8,2},{9,13},{1... | collective-permute-start | bytes 442376 | tf_op jit(solution)/shard_map/ppermute | solution.py:656
  36.8 0.7 %collective-permute-start.17 = (f32[72,512]{1,0:T(8,128)S(1)}, f32[72,512]{1,0:T(8,128)S(1)}, u32[]{:S(2)}, u32[]{:S(2)}) collective-permute-start(f32[72,512]{1,0:T(8,128)S(1)} %get-tuple-element.66), channel_id=1, source_target_pairs={{1,7},{3,5},{5,3},{7,1},{9,15},{11,13},{13,11},{15,9},{17,23},{19,... | collective-permute-start | bytes 442376 | tf_op jit(solution)/shard_map/ppermute | solution.py:656
  37.4 2.4 %collective-permute-done.18.passed.refs_0_ = f32[72,512]{1,0:T(8,128)S(1)} collective-permute-done((f32[72,512]{1,0:T(8,128)S(1)}, f32[72,512]{1,0:T(8,128)S(1)}, u32[]{:S(2)}, u32[]{:S(2)}) %collective-permute-start.18) | collective-permute-done | bytes 147488 | tf_op jit(solution)/shard_map/ppermute | solution.py:656
  39.9 1.1 %collective-permute-start.20 = (f32[72,512]{1,0:T(8,128)S(1)}, f32[72,512]{1,0:T(8,128)S(1)}, u32[]{:S(2)}, u32[]{:S(2)}) collective-permute-start(f32[72,512]{1,0:T(8,128)S(1)} %crossing.1), channel_id=1, source_target_pairs={{0,2},{1,13},{2,0},{3,15},{4,6},{5,9},{6,4},{7,11},{8,10},{9,5},{1... | collective-permute-start | bytes 442376 | tf_op jit(solution)/shard_map/ppermute | solution.py:656
  41.0 1.1 %merged.1 = f32[448,4096]{1,0:T(8,128)S(1)} custom-call(bf16[448,256]{1,0:T(8,128)(2,1)S(1)} %bitcast.14, bf16[448,4096]{1,0:T(8,128)(2,1)S(1)} %bitcast.11, bf16[256,4096]{1,0:T(8,128)(2,1)S(1)} %get-tuple-element.67.tokens), custom_call_target="tpu_custom_call" | custom-call | flops 57500000 | tf_op jit(solution)/shard_map/merged/pallas_call | solution.py:305
  42.2 2.8 %collective-permute-done.19.refs_1_ = f32[72,512]{1,0:T(8,128)S(1)} collective-permute-done((f32[72,512]{1,0:T(8,128)S(1)}, f32[72,512]{1,0:T(8,128)S(1)}, u32[]{:S(2)}, u32[]{:S(2)}) %collective-permute-start.19) | collective-permute-done | bytes 147488 | tf_op jit(solution)/shard_map/ppermute | solution.py:656
  44.9 0.5 collective-permute-done.20.refs_2_
  45.6 1.4 %collective-permute-done.21.other = f32[72,512]{1,0:T(8,128)S(1)} collective-permute-done((f32[72,512]{1,0:T(8,128)S(1)}, f32[72,512]{1,0:T(8,128)S(1)}, u32[]{:S(2)}, u32[]{:S(2)}) %collective-permute-start.21) | collective-permute-done | bytes 147488 | tf_op jit(solution)/shard_map/ppermute | solution.py:641
  47.0 2.6 %collective-permute-start.23 = (f32[64,512]{1,0:T(8,128)S(1)}, f32[64,512]{1,0:T(8,128)S(1)}, u32[]{:S(2)}, u32[]{:S(2)}) collective-permute-start(f32[64,512]{1,0:T(8,128)S(1)} %get-tuple-element.71.share.here), channel_id=1, source_target_pairs={{0,2},{1,13},{2,0},{3,15},{4,6},{5,9},{6,4},{7,11},{8,10},{9,5},{1... | collective-permute-start | bytes 393224 | tf_op jit(solution)/shard_map/ppermute | solution.py:656
  49.7 1.3 %collective-permute-start.24 = (f32[64,512]{1,0:T(8,128)S(1)}, f32[64,512]{1,0:T(8,128)S(1)}, u32[]{:S(2)}, u32[]{:S(2)}) collective-permute-start(f32[64,512]{1,0:T(8,128)S(1)} %get-tuple-element.71.share.here), channel_id=1, source_target_pairs={{0,10},{1,5},{2,8},{3,7},{4,14},{5,1},{6,12},{7,3},{8,2},{9,13},{1... | collective-permute-start | bytes 393224 | tf_op jit(solution)/shard_map/ppermute | solution.py:656
  50.9 0.7 %collective-permute-start.22 = (f32[64,512]{1,0:T(8,128)S(1)}, f32[64,512]{1,0:T(8,128)S(1)}, u32[]{:S(2)}, u32[]{:S(2)}) collective-permute-start(f32[64,512]{1,0:T(8,128)S(1)} %get-tuple-element.71.share.here), channel_id=1, source_target_pairs={{1,7},{3,5},{5,3},{7,1},{9,15},{11,13},{13,11},{15,9},{17,23},{19,... | collective-permute-start | bytes 393224 | tf_op jit(solution)/shard_map/ppermute | solution.py:656
  51.6 1.0 %collective-permute-done.23.refs_0_.there = f32[64,512]{1,0:T(8,128)S(1)} collective-permute-done((f32[64,512]{1,0:T(8,128)S(1)}, f32[64,512]{1,0:T(8,128)S(1)}, u32[]{:S(2)}, u32[]{:S(2)}) %collective-permute-start.23) | collective-permute-done | bytes 131104 | tf_op jit(solution)/shard_map/ppermute | solution.py:656
  52.6 1.9 %collective-permute-start.25 = (f32[64,512]{1,0:T(8,128)S(1)}, f32[64,512]{1,0:T(8,128)S(1)}, u32[]{:S(2)}, u32[]{:S(2)}) collective-permute-start(f32[64,512]{1,0:T(8,128)S(1)} %by_core.1), channel_id=1, source_target_pairs={{0,8},{1,3},{2,10},{3,1},{4,12},{5,7},{6,14},{7,5},{8,0},{9,11},{1... | collective-permute-start | bytes 393224 | tf_op jit(solution)/shard_map/ppermute | solution.py:656
  54.5 1.8 %cholesky_inverse.1.inverse = f32[64,64]{1,0:T(8,128)S(1)} custom-call(f32[64,64]{1,0:T(8,128)S(1)} %get-tuple-element.72.gram), custom_call_target="tpu_custom_call" | custom-call | flops 5750000128 | tf_op jit(solution)/shard_map/cholesky_inverse/pallas_call | solution.py:513
  56.3 1.7 %collective-permute-done.24.refs_1_ = f32[64,512]{1,0:T(8,128)S(1)} collective-permute-done((f32[64,512]{1,0:T(8,128)S(1)}, f32[64,512]{1,0:T(8,128)S(1)}, u32[]{:S(2)}, u32[]{:S(2)}) %collective-permute-start.24) | collective-permute-done | bytes 131104 | tf_op jit(solution)/shard_map/ppermute | solution.py:656
  58.0 0.8 %last_operand.1.lhs = bf16[512,256]{1,0:T(8,128)(2,1)S(1)} custom-call(f32[64,64]{1,0:T(8,128)S(1)} %cholesky_inverse.1.inverse, f32[64,448]{1,0:T(8,128)S(1)} %get-tuple-element.57.left_sum), custom_call_target="tpu_custom_call" | custom-call | flops 57500000 | tf_op jit(solution)/shard_map/last_operand/pallas_call | solution.py:544
  58.8 1.5 %finish.3 = (bf16[448,4096]{1,0:T(8,128)(2,1)}, f32[64,4096]{1,0:T(8,128)}) custom-call(f32[3,64,512]{2,1,0:T(8,128)S(1)} %joined.1.shares, bf16[512,256]{1,0:T(8,128)(2,1)S(1)} %last_operand.1.lhs, f32[448,4096]{1,0:T(8,128)S(1)} %merged.1), custom_call_target="tpu_custom_call" | custom-call | flops 57500000 | tf_op jit(solution)/shard_map/finish/pallas_call | solution.py:583
  60.5 1.1 %finish.4 = (bf16[448,4096]{1,0:T(8,128)(2,1)}, f32[64,4096]{1,0:T(8,128)}) custom-call(f32[1,64,512]{2,1,0:T(8,128)S(1)} %bitcast.16, bf16[512,256]{1,0:T(8,128)(2,1)S(1)} %last_operand.1.lhs, f32[448,4096]{1,0:T(8,128)S(1)} %merged.1, bf16[448,4096]{1,0:T(8,128)(2,1)} %get-tuple-element.80.refs_0_, ...), custom_call_target="tpu_custom_call", output_to_operand_aliasing={{0}: (3, {}), {1}: (4, {})} | custom-call | flops 57500000 | tf_op jit(solution)/shard_map/finish/pallas_call | solution.py:583
  61.6 0.8 %collective-permute-done.26.shares = f32[4,64,512]{2,1,0:T(8,128)S(1)} collective-permute-done((f32[4,64,512]{2,1,0:T(8,128)S(1)}, f32[4,64,512]{2,1,0:T(8,128)S(1)}, u32[]{:S(2)}, u32[]{:S(2)}) %collective-permute-start.26) | collective-permute-done | bytes 524320 | tf_op jit(solution)/shard_map/ppermute | solution.py:641
  62.4 1.7 %finish.5 = (bf16[448,4096]{1,0:T(8,128)(2,1)}, f32[64,4096]{1,0:T(8,128)}) custom-call(f32[4,64,512]{2,1,0:T(8,128)S(1)} %collective-permute-done.26.shares, bf16[512,256]{1,0:T(8,128)(2,1)S(1)} %last_operand.1.lhs, f32[448,4096]{1,0:T(8,128)S(1)} %merged.1, ...), custom_call_target="tpu_custom_call", output_to_operand_aliasing={{0}: (3, {}), {1}: (4, {})} | custom-call | flops 57500000 | tf_op jit(solution)/shard_map/finish/pallas_call | solution.py:583
  (36 shorter events, 1.3 us)
Async XLA Ops:
  0.6 1.0 %copy-start.3 = (bf16[1,32,4096]{2,1,0:T(8,128)(2,1)S(1)}, bf16[1,32,4096]{2,1,0:T(8,128)(2,1)}, u32[]{:S(2)}) copy-start(bf16[1,32,4096]{2,1,0:T(8,128)(2,1)} %param.4) | copy-start | bytes 786436
  1.6 6.9 %collective-permute-start = (bf16[16,4096]{1,0:T(8,128)(2,1)S(1)}, bf16[16,4096]{1,0:T(8,128)(2,1)S(1)}, u32[]{:S(2)}, u32[]{:S(2)}) collective-permute-start(bf16[16,4096]{1,0:T(8,128)(2,1)S(1)} %get-tuple-element.44.first.refs_0_), channel_id=1, source_target_pairs={{0,2},{1,5},{2,6},{3,1},{6,10},{7,3},{10,14},{11,7},{14,12},{15,11... | collective-permute-start | bytes 393224 | tf_op jit(solution)/shard_map/ppermute | solution.py:632
  4.6 18.8 %copy-start = (bf16[1,448,4096]{2,1,0:T(8,128)(2,1)S(1)}, bf16[1,448,4096]{2,1,0:T(8,128)(2,1)}, u32[]{:S(2)}) copy-start(bf16[1,448,4096]{2,1,0:T(8,128)(2,1)} %param.6) | copy-start | bytes 11010052
  4.6 18.8 %copy-start.2 = (f32[64,4096]{1,0:T(8,128)S(1)}, f32[64,4096]{1,0:T(8,128)}, u32[]{:S(2)}) copy-start(f32[64,4096]{1,0:T(8,128)} %right) | copy-start | bytes 3145732
  4.6 6.4 %collective-permute-start.4 = (bf16[16,4096]{1,0:T(8,128)(2,1)S(1)}, bf16[16,4096]{1,0:T(8,128)(2,1)S(1)}, u32[]{:S(2)}, u32[]{:S(2)}) collective-permute-start(bf16[16,4096]{1,0:T(8,128)(2,1)S(1)} %get-tuple-element.46.second.refs_1_), channel_id=1, source_target_pairs={{0,4},{1,3},{2,0},{3,7},{6,2},{7,11},{10,6},{11,15},{14,10},{15,13... | collective-permute-start | bytes 393224 | tf_op jit(solution)/shard_map/ppermute | solution.py:632
  4.8 6.5 %collective-permute-start.8 = (bf16[16,4096]{1,0:T(8,128)(2,1)S(1)}, bf16[16,4096]{1,0:T(8,128)(2,1)S(1)}, u32[]{:S(2)}, u32[]{:S(2)}) collective-permute-start(bf16[16,4096]{1,0:T(8,128)(2,1)S(1)} %get-tuple-element.49), channel_id=1, source_target_pairs={{0,2},{1,5},{2,6},{3,1},{6,10},{7,3},{10,14},{11,7},{14,12},{15,11... | collective-permute-start | bytes 393224 | tf_op jit(solution)/shard_map/ppermute | solution.py:632
  6.7 6.3 %collective-permute-start.9 = (bf16[16,4096]{1,0:T(8,128)(2,1)S(1)}, bf16[16,4096]{1,0:T(8,128)(2,1)S(1)}, u32[]{:S(2)}, u32[]{:S(2)}) collective-permute-start(bf16[16,4096]{1,0:T(8,128)(2,1)S(1)} %get-tuple-element.50), channel_id=1, source_target_pairs={{0,4},{1,3},{2,0},{3,7},{6,2},{7,11},{10,6},{11,15},{14,10},{15,13... | collective-permute-start | bytes 393224 | tf_op jit(solution)/shard_map/ppermute | solution.py:632
  8.5 6.7 %collective-permute-start.1 = (bf16[16,4096]{1,0:T(8,128)(2,1)S(1)}, bf16[16,4096]{1,0:T(8,128)(2,1)S(1)}, u32[]{:S(2)}, u32[]{:S(2)}) collective-permute-start(bf16[16,4096]{1,0:T(8,128)(2,1)S(1)} %collective-permute-done.refs_2_), channel_id=1, source_target_pairs={{0,2},{1,5},{2,6},{3,1},{6,10},{7,3},{10,14},{11,7},{14,12},{15,11... | collective-permute-start | bytes 393224 | tf_op jit(solution)/shard_map/ppermute | solution.py:632
  11.0 6.2 %collective-permute-start.5 = (bf16[16,4096]{1,0:T(8,128)(2,1)S(1)}, bf16[16,4096]{1,0:T(8,128)(2,1)S(1)}, u32[]{:S(2)}, u32[]{:S(2)}) collective-permute-start(bf16[16,4096]{1,0:T(8,128)(2,1)S(1)} %collective-permute-done.4.refs_3_), channel_id=1, source_target_pairs={{0,4},{1,3},{2,0},{3,7},{6,2},{7,11},{10,6},{11,15},{14,10},{15,13... | collective-permute-start | bytes 393224 | tf_op jit(solution)/shard_map/ppermute | solution.py:632
  11.3 6.8 %collective-permute-start.10 = (bf16[16,4096]{1,0:T(8,128)(2,1)S(1)}, bf16[16,4096]{1,0:T(8,128)(2,1)S(1)}, u32[]{:S(2)}, u32[]{:S(2)}) collective-permute-start(bf16[16,4096]{1,0:T(8,128)(2,1)S(1)} %collective-permute-done.8.refs_4_), channel_id=1, source_target_pairs={{0,2},{1,5},{2,6},{3,1},{6,10},{7,3},{10,14},{11,7},{14,12},{15,11... | collective-permute-start | bytes 393224 | tf_op jit(solution)/shard_map/ppermute | solution.py:632
  13.0 6.8 %collective-permute-start.11 = (bf16[16,4096]{1,0:T(8,128)(2,1)S(1)}, bf16[16,4096]{1,0:T(8,128)(2,1)S(1)}, u32[]{:S(2)}, u32[]{:S(2)}) collective-permute-start(bf16[16,4096]{1,0:T(8,128)(2,1)S(1)} %collective-permute-done.9.refs_5_), channel_id=1, source_target_pairs={{0,4},{1,3},{2,0},{3,7},{6,2},{7,11},{10,6},{11,15},{14,10},{15,13... | collective-permute-start | bytes 393224 | tf_op jit(solution)/shard_map/ppermute | solution.py:632
  15.2 5.7 %collective-permute-start.2 = (bf16[16,4096]{1,0:T(8,128)(2,1)S(1)}, bf16[16,4096]{1,0:T(8,128)(2,1)S(1)}, u32[]{:S(2)}, u32[]{:S(2)}) collective-permute-start(bf16[16,4096]{1,0:T(8,128)(2,1)S(1)} %collective-permute-done.1.refs_6_), channel_id=1, source_target_pairs={{0,2},{1,5},{2,6},{3,1},{6,10},{7,3},{10,14},{11,7},{14,12},{15,11... | collective-permute-start | bytes 393224 | tf_op jit(solution)/shard_map/ppermute | solution.py:632
  17.2 6.2 %collective-permute-start.6 = (bf16[16,4096]{1,0:T(8,128)(2,1)S(1)}, bf16[16,4096]{1,0:T(8,128)(2,1)S(1)}, u32[]{:S(2)}, u32[]{:S(2)}) collective-permute-start(bf16[16,4096]{1,0:T(8,128)(2,1)S(1)} %collective-permute-done.5.refs_7_), channel_id=1, source_target_pairs={{0,4},{1,3},{2,0},{3,7},{6,2},{7,11},{10,6},{11,15},{14,10},{15,13... | collective-permute-start | bytes 393224 | tf_op jit(solution)/shard_map/ppermute | solution.py:632
  18.1 6.6 %collective-permute-start.12 = (bf16[16,4096]{1,0:T(8,128)(2,1)S(1)}, bf16[16,4096]{1,0:T(8,128)(2,1)S(1)}, u32[]{:S(2)}, u32[]{:S(2)}) collective-permute-start(bf16[16,4096]{1,0:T(8,128)(2,1)S(1)} %collective-permute-done.10.refs_8_), channel_id=1, source_target_pairs={{0,2},{1,5},{2,6},{3,1},{6,10},{7,3},{10,14},{11,7},{14,12},{15,11... | collective-permute-start | bytes 393224 | tf_op jit(solution)/shard_map/ppermute | solution.py:632
  19.8 5.0 %collective-permute-start.13 = (bf16[16,4096]{1,0:T(8,128)(2,1)S(1)}, bf16[16,4096]{1,0:T(8,128)(2,1)S(1)}, u32[]{:S(2)}, u32[]{:S(2)}) collective-permute-start(bf16[16,4096]{1,0:T(8,128)(2,1)S(1)} %collective-permute-done.11.refs_9_), channel_id=1, source_target_pairs={{0,4},{1,3},{2,0},{3,7},{6,2},{7,11},{10,6},{11,15},{14,10},{15,13... | collective-permute-start | bytes 393224 | tf_op jit(solution)/shard_map/ppermute | solution.py:632
  20.9 5.4 %collective-permute-start.3 = (bf16[16,4096]{1,0:T(8,128)(2,1)S(1)}, bf16[16,4096]{1,0:T(8,128)(2,1)S(1)}, u32[]{:S(2)}, u32[]{:S(2)}) collective-permute-start(bf16[16,4096]{1,0:T(8,128)(2,1)S(1)} %collective-permute-done.2.refs_10_), channel_id=1, source_target_pairs={{0,2},{1,5},{2,6},{3,1},{6,10},{7,3},{10,14},{11,7},{14,12},{15,11... | collective-permute-start | bytes 393224 | tf_op jit(solution)/shard_map/ppermute | solution.py:632
  23.4 5.0 %collective-permute-start.7 = (bf16[16,4096]{1,0:T(8,128)(2,1)S(1)}, bf16[16,4096]{1,0:T(8,128)(2,1)S(1)}, u32[]{:S(2)}, u32[]{:S(2)}) collective-permute-start(bf16[16,4096]{1,0:T(8,128)(2,1)S(1)} %collective-permute-done.6.refs_11_), channel_id=1, source_target_pairs={{0,4},{1,3},{2,0},{3,7},{6,2},{7,11},{10,6},{11,15},{14,10},{15,13... | collective-permute-start | bytes 393224 | tf_op jit(solution)/shard_map/ppermute | solution.py:632
  23.4 1.3 %copy-start.1 = (bf16[1,256,448]{1,2,0:T(8,128)(2,1)S(1)}, bf16[1,256,448]{1,2,0:T(8,128)(2,1)}, u32[]{:S(2)}) copy-start(bf16[1,256,448]{1,2,0:T(8,128)(2,1)} %param.5) | copy-start | bytes 688132
  29.0 1.4 %collective-permute-start.14 = (f32[64,448]{1,0:T(8,128)S(1)}, f32[64,448]{1,0:T(8,128)S(1)}, u32[]{:S(2)}, u32[]{:S(2)}) collective-permute-start(f32[64,448]{1,0:T(8,128)S(1)} %get-tuple-element.55.here_l), channel_id=1, source_target_pairs={{0,1},{1,0},{2,3},{3,2},{4,5},{5,4},{6,7},{7,6},{8,9},{9,8},{10,11... | collective-permute-start | bytes 344072 | tf_op jit(solution)/shard_map/ppermute | solution.py:641
  31.0 1.7 %collective-permute-start.15 = (f32[2,64,512]{2,1,0:T(8,128)S(1)}, f32[2,64,512]{2,1,0:T(8,128)S(1)}, u32[]{:S(2)}, u32[]{:S(2)}) collective-permute-start(f32[2,64,512]{2,1,0:T(8,128)S(1)} %get-tuple-element.61), channel_id=1, source_target_pairs={{0,1},{1,0},{2,3},{3,2},{4,5},{5,4},{6,7},{7,6},{8,9},{9,8},{10,11... | collective-permute-start | bytes 786440 | tf_op jit(solution)/shard_map/ppermute | solution.py:641
  31.8 2.1 %collective-permute-start.16 = (f32[2,64,512]{2,1,0:T(8,128)S(1)}, f32[2,64,512]{2,1,0:T(8,128)S(1)}, u32[]{:S(2)}, u32[]{:S(2)}) collective-permute-start(f32[2,64,512]{2,1,0:T(8,128)S(1)} %get-tuple-element.63), channel_id=1, source_target_pairs={{0,1},{1,0},{2,3},{3,2},{4,5},{5,4},{6,7},{7,6},{8,9},{9,8},{10,11... | collective-permute-start | bytes 786440 | tf_op jit(solution)/shard_map/ppermute | solution.py:641
  32.8 7.1 %collective-permute-start.18 = (f32[72,512]{1,0:T(8,128)S(1)}, f32[72,512]{1,0:T(8,128)S(1)}, u32[]{:S(2)}, u32[]{:S(2)}) collective-permute-start(f32[72,512]{1,0:T(8,128)S(1)} %begin_messages.1), channel_id=1, source_target_pairs={{0,8},{1,3},{2,10},{3,1},{4,12},{5,7},{6,14},{7,5},{8,0},{9,11},{1... | collective-permute-start | bytes 442376 | tf_op jit(solution)/shard_map/ppermute | solution.py:656
  33.9 11.0 %collective-permute-start.19 = (f32[72,512]{1,0:T(8,128)S(1)}, f32[72,512]{1,0:T(8,128)S(1)}, u32[]{:S(2)}, u32[]{:S(2)}) collective-permute-start(f32[72,512]{1,0:T(8,128)S(1)} %get-tuple-element.69), channel_id=1, source_target_pairs={{0,10},{1,5},{2,8},{3,7},{4,14},{5,1},{6,12},{7,3},{8,2},{9,13},{1... | collective-permute-start | bytes 442376 | tf_op jit(solution)/shard_map/ppermute | solution.py:656
  36.8 5.4 %collective-permute-start.17 = (f32[72,512]{1,0:T(8,128)S(1)}, f32[72,512]{1,0:T(8,128)S(1)}, u32[]{:S(2)}, u32[]{:S(2)}) collective-permute-start(f32[72,512]{1,0:T(8,128)S(1)} %get-tuple-element.66), channel_id=1, source_target_pairs={{1,7},{3,5},{5,3},{7,1},{9,15},{11,13},{13,11},{15,9},{17,23},{19,... | collective-permute-start | bytes 442376 | tf_op jit(solution)/shard_map/ppermute | solution.py:656
  39.9 5.6 %collective-permute-start.20 = (f32[72,512]{1,0:T(8,128)S(1)}, f32[72,512]{1,0:T(8,128)S(1)}, u32[]{:S(2)}, u32[]{:S(2)}) collective-permute-start(f32[72,512]{1,0:T(8,128)S(1)} %crossing.1), channel_id=1, source_target_pairs={{0,2},{1,13},{2,0},{3,15},{4,6},{5,9},{6,4},{7,11},{8,10},{9,5},{1... | collective-permute-start | bytes 442376 | tf_op jit(solution)/shard_map/ppermute | solution.py:656
  45.5 1.4 %collective-permute-start.21 = (f32[72,512]{1,0:T(8,128)S(1)}, f32[72,512]{1,0:T(8,128)S(1)}, u32[]{:S(2)}, u32[]{:S(2)}) collective-permute-start(f32[72,512]{1,0:T(8,128)S(1)} %core_sum.1.here), channel_id=1, source_target_pairs={{0,1},{1,0},{2,3},{3,2},{4,5},{5,4},{6,7},{7,6},{8,9},{9,8},{10,11... | collective-permute-start | bytes 442376 | tf_op jit(solution)/shard_map/ppermute | solution.py:641
  47.0 5.6 %collective-permute-start.23 = (f32[64,512]{1,0:T(8,128)S(1)}, f32[64,512]{1,0:T(8,128)S(1)}, u32[]{:S(2)}, u32[]{:S(2)}) collective-permute-start(f32[64,512]{1,0:T(8,128)S(1)} %get-tuple-element.71.share.here), channel_id=1, source_target_pairs={{0,2},{1,13},{2,0},{3,15},{4,6},{5,9},{6,4},{7,11},{8,10},{9,5},{1... | collective-permute-start | bytes 393224 | tf_op jit(solution)/shard_map/ppermute | solution.py:656
  49.7 8.3 %collective-permute-start.24 = (f32[64,512]{1,0:T(8,128)S(1)}, f32[64,512]{1,0:T(8,128)S(1)}, u32[]{:S(2)}, u32[]{:S(2)}) collective-permute-start(f32[64,512]{1,0:T(8,128)S(1)} %get-tuple-element.71.share.here), channel_id=1, source_target_pairs={{0,10},{1,5},{2,8},{3,7},{4,14},{5,1},{6,12},{7,3},{8,2},{9,13},{1... | collective-permute-start | bytes 393224 | tf_op jit(solution)/shard_map/ppermute | solution.py:656
  50.9 7.8 %collective-permute-start.22 = (f32[64,512]{1,0:T(8,128)S(1)}, f32[64,512]{1,0:T(8,128)S(1)}, u32[]{:S(2)}, u32[]{:S(2)}) collective-permute-start(f32[64,512]{1,0:T(8,128)S(1)} %get-tuple-element.71.share.here), channel_id=1, source_target_pairs={{1,7},{3,5},{5,3},{7,1},{9,15},{11,13},{13,11},{15,9},{17,23},{19,... | collective-permute-start | bytes 393224 | tf_op jit(solution)/shard_map/ppermute | solution.py:656
  52.6 7.7 %collective-permute-start.25 = (f32[64,512]{1,0:T(8,128)S(1)}, f32[64,512]{1,0:T(8,128)S(1)}, u32[]{:S(2)}, u32[]{:S(2)}) collective-permute-start(f32[64,512]{1,0:T(8,128)S(1)} %by_core.1), channel_id=1, source_target_pairs={{0,8},{1,3},{2,10},{3,1},{4,12},{5,7},{6,14},{7,5},{8,0},{9,11},{1... | collective-permute-start | bytes 393224 | tf_op jit(solution)/shard_map/ppermute | solution.py:656
  60.4 2.0 %collective-permute-start.26 = (f32[4,64,512]{2,1,0:T(8,128)S(1)}, f32[4,64,512]{2,1,0:T(8,128)S(1)}, u32[]{:S(2)}, u32[]{:S(2)}) collective-permute-start(f32[4,64,512]{2,1,0:T(8,128)S(1)} %pad_maximum_fusion), channel_id=1, source_target_pairs={{0,1},{1,0},{2,3},{3,2},{4,5},{5,4},{6,7},{7,6},{8,9},{9,8},{10,11... | collective-permute-start | bytes 1572872 | tf_op jit(solution)/shard_map/ppermute | solution.py:641

commit v10 on v9

--- a/solution.py
+++ b/solution.py
@@ -683,7 +683,7 @@
     third = send(share, 0, 3)
     passed = [send(by_core(share, value), place, 1) for value, place in zip(begun, evens)]
     inverse = cholesky_inverse(gram_matrix)
-    inverse, begun, direct = lax.optimization_barrier((inverse, begun, direct))
+    inverse, begun = lax.optimization_barrier((inverse, begun))
     lhs = last_operand(inverse, left_sum, replicas)
     mine = joined(share, third, begun, direct)
     early = [(0, 0), (1, 1)] + [(index + 1, index) for index in range(2, chips // 2, 2)]

time: 64.3 us -> 63.9 us (level)
  transfers between devices with their start and end apart: 27 -> 27, of which waited for: 18 -> 19; matrix products, arithmetic and copies ran while one was open for 0% -> 0% of each run, Pallas kernels for 16% -> 16%
where the time goes in v10:
time: 63.9 us; the launch traced here: 63.7 us
  starting transfers between devices  30 us (47%)
  waiting for transfers between devices  18.8 us (29%)
  Pallas kernels  13.1 us (21%)
  local copies, waits for them, and re-layouts  0.96 us (2%)
  between operations  0.84 us (1%)
    ppermute x14, starting transfers between devices, ring_gather(): going[way, half] = lax.ppermute(going[way, half], ('tp', 'dp'), pairs(way))  16.7 us
    ppermute x8, starting transfers between devices, send(): return lax.ppermute(value, ('tp', 'dp'), pairs)  12.2 us
    ppermute x8, waiting for transfers between devices, send(): return lax.ppermute(value, ('tp', 'dp'), pairs)  8.01 us
    ppermute x14, waiting for transfers between devices, ring_gather(): going[way, half] = lax.ppermute(going[way, half], ('tp', 'dp'), pairs(way))  7.51 us
    pallas_call x3, Pallas kernels, finish(): pl.pallas_call(functools.partial(final_kernel, indices, side), in_specs=[...  4.39 us
    ppermute x5, waiting for transfers between devices, swap(): return lax.ppermute(value, 'dp', [(0, 1), (1, 0)])  3.23 us
    pallas_call x1, Pallas kernels, cholesky_inverse(): pl.pallas_call(inverse_kernel, in_specs=[pl.BlockSpec(memory_space=pltpu....  1.77 us
  transfers between devices with their start and end apart: 27, of which 19 were waited for; matrix products, arithmetic and copies ran while one was open for 0% of the time, Pallas kernels for 16%

profile of v10, /device:TPU:0, one launch (start us, length us, event | category | flops | bytes accessed | tf_op | source)
XLA Modules:
  0.0 63.7 jit_solution(5844822606399912638)
XLA Ops:
  0.6 0.9 %copy-done.3 = bf16[1,32,4096]{2,1,0:T(8,128)(2,1)S(1)} copy-done((bf16[1,32,4096]{2,1,0:T(8,128)(2,1)S(1)}, bf16[1,32,4096]{2,1,0:T(8,128)(2,1)}, u32[]{:S(2)}) %copy-start.3) | copy-done | bytes 262168
  1.6 3.0 %collective-permute-start = (bf16[16,4096]{1,0:T(8,128)(2,1)S(1)}, bf16[16,4096]{1,0:T(8,128)(2,1)S(1)}, u32[]{:S(2)}, u32[]{:S(2)}) collective-permute-start(bf16[16,4096]{1,0:T(8,128)(2,1)S(1)} %get-tuple-element.43.first.refs_0_), channel_id=1, source_target_pairs={{0,2},{1,5},{2,6},{3,1},{6,10},{7,3},{10,14},{11,7},{14,12},{15,11... | collective-permute-start | bytes 393224 | tf_op jit(solution)/shard_map/ppermute | solution.py:632
  4.8 1.9 %collective-permute-start.8 = (bf16[16,4096]{1,0:T(8,128)(2,1)S(1)}, bf16[16,4096]{1,0:T(8,128)(2,1)S(1)}, u32[]{:S(2)}, u32[]{:S(2)}) collective-permute-start(bf16[16,4096]{1,0:T(8,128)(2,1)S(1)} %get-tuple-element.48), channel_id=1, source_target_pairs={{0,2},{1,5},{2,6},{3,1},{6,10},{7,3},{10,14},{11,7},{14,12},{15,11... | collective-permute-start | bytes 393224 | tf_op jit(solution)/shard_map/ppermute | solution.py:632
  6.9 1.6 %collective-permute-done.refs_2_ = bf16[16,4096]{1,0:T(8,128)(2,1)S(1)} collective-permute-done((bf16[16,4096]{1,0:T(8,128)(2,1)S(1)}, bf16[16,4096]{1,0:T(8,128)(2,1)S(1)}, u32[]{:S(2)}, u32[]{:S(2)}) %collective-permute-start) | collective-permute-done | bytes 131104 | tf_op jit(solution)/shard_map/ppermute | solution.py:632
  8.5 2.5 %collective-permute-start.1 = (bf16[16,4096]{1,0:T(8,128)(2,1)S(1)}, bf16[16,4096]{1,0:T(8,128)(2,1)S(1)}, u32[]{:S(2)}, u32[]{:S(2)}) collective-permute-start(bf16[16,4096]{1,0:T(8,128)(2,1)S(1)} %collective-permute-done.refs_2_), channel_id=1, source_target_pairs={{0,2},{1,5},{2,6},{3,1},{6,10},{7,3},{10,14},{11,7},{14,12},{15,11... | collective-permute-start | bytes 393224 | tf_op jit(solution)/shard_map/ppermute | solution.py:632
  11.3 1.8 %collective-permute-start.10 = (bf16[16,4096]{1,0:T(8,128)(2,1)S(1)}, bf16[16,4096]{1,0:T(8,128)(2,1)S(1)}, u32[]{:S(2)}, u32[]{:S(2)}) collective-permute-start(bf16[16,4096]{1,0:T(8,128)(2,1)S(1)} %collective-permute-done.8.refs_4_), channel_id=1, source_target_pairs={{0,2},{1,5},{2,6},{3,1},{6,10},{7,3},{10,14},{11,7},{14,12},{15,11... | collective-permute-start | bytes 393224 | tf_op jit(solution)/shard_map/ppermute | solution.py:632
  13.0 0.9 %collective-permute-start.11 = (bf16[16,4096]{1,0:T(8,128)(2,1)S(1)}, bf16[16,4096]{1,0:T(8,128)(2,1)S(1)}, u32[]{:S(2)}, u32[]{:S(2)}) collective-permute-start(bf16[16,4096]{1,0:T(8,128)(2,1)S(1)} %collective-permute-done.9.refs_5_), channel_id=1, source_target_pairs={{0,4},{1,3},{2,0},{3,7},{6,2},{7,11},{10,6},{11,15},{14,10},{15,13... | collective-permute-start | bytes 393224 | tf_op jit(solution)/shard_map/ppermute | solution.py:632
  14.0 1.3 %collective-permute-done.1.refs_6_ = bf16[16,4096]{1,0:T(8,128)(2,1)S(1)} collective-permute-done((bf16[16,4096]{1,0:T(8,128)(2,1)S(1)}, bf16[16,4096]{1,0:T(8,128)(2,1)S(1)}, u32[]{:S(2)}, u32[]{:S(2)}) %collective-permute-start.1) | collective-permute-done | bytes 131104 | tf_op jit(solution)/shard_map/ppermute | solution.py:632
  15.2 1.9 %collective-permute-start.2 = (bf16[16,4096]{1,0:T(8,128)(2,1)S(1)}, bf16[16,4096]{1,0:T(8,128)(2,1)S(1)}, u32[]{:S(2)}, u32[]{:S(2)}) collective-permute-start(bf16[16,4096]{1,0:T(8,128)(2,1)S(1)} %collective-permute-done.1.refs_6_), channel_id=1, source_target_pairs={{0,2},{1,5},{2,6},{3,1},{6,10},{7,3},{10,14},{11,7},{14,12},{15,11... | collective-permute-start | bytes 393224 | tf_op jit(solution)/shard_map/ppermute | solution.py:632
  17.3 0.8 %collective-permute-done.10.refs_8_ = bf16[16,4096]{1,0:T(8,128)(2,1)S(1)} collective-permute-done((bf16[16,4096]{1,0:T(8,128)(2,1)S(1)}, bf16[16,4096]{1,0:T(8,128)(2,1)S(1)}, u32[]{:S(2)}, u32[]{:S(2)}) %collective-permute-start.10) | collective-permute-done | bytes 131104 | tf_op jit(solution)/shard_map/ppermute | solution.py:632
  18.1 1.4 %collective-permute-start.12 = (bf16[16,4096]{1,0:T(8,128)(2,1)S(1)}, bf16[16,4096]{1,0:T(8,128)(2,1)S(1)}, u32[]{:S(2)}, u32[]{:S(2)}) collective-permute-start(bf16[16,4096]{1,0:T(8,128)(2,1)S(1)} %collective-permute-done.10.refs_8_), channel_id=1, source_target_pairs={{0,2},{1,5},{2,6},{3,1},{6,10},{7,3},{10,14},{11,7},{14,12},{15,11... | collective-permute-start | bytes 393224 | tf_op jit(solution)/shard_map/ppermute | solution.py:632
  19.5 0.3 collective-permute-done.11.refs_9_
  19.8 0.3 collective-permute-start.13
  20.1 0.8 %collective-permute-done.2.refs_10_ = bf16[16,4096]{1,0:T(8,128)(2,1)S(1)} collective-permute-done((bf16[16,4096]{1,0:T(8,128)(2,1)S(1)}, bf16[16,4096]{1,0:T(8,128)(2,1)S(1)}, u32[]{:S(2)}, u32[]{:S(2)}) %collective-permute-start.2) | collective-permute-done | bytes 131104 | tf_op jit(solution)/shard_map/ppermute | solution.py:632
  20.9 2.5 %collective-permute-start.3 = (bf16[16,4096]{1,0:T(8,128)(2,1)S(1)}, bf16[16,4096]{1,0:T(8,128)(2,1)S(1)}, u32[]{:S(2)}, u32[]{:S(2)}) collective-permute-start(bf16[16,4096]{1,0:T(8,128)(2,1)S(1)} %collective-permute-done.2.refs_10_), channel_id=1, source_target_pairs={{0,2},{1,5},{2,6},{3,1},{6,10},{7,3},{10,14},{11,7},{14,12},{15,11... | collective-permute-start | bytes 393224 | tf_op jit(solution)/shard_map/ppermute | solution.py:632
  23.5 1.2 %residue_left.1 = (bf16[128,4096]{1,0:T(8,128)(2,1)S(1)}, f32[64,448]{1,0:T(8,128)S(1)}) custom-call(f32[64,4096]{1,0:T(8,128)S(1)} %copy-done.2, bf16[448,4096]{1,0:T(8,128)(2,1)S(1)} %bitcast.7), custom_call_target="tpu_custom_call" | custom-call | flops 2529999872 | tf_op jit(solution)/shard_map/residue_left/pallas_call | solution.py:100
  24.8 1.2 %early_left.1 = (bf16[256,4096]{1,0:T(8,128)(2,1)S(1)}, bf16[256,448]{1,0:T(8,128)(2,1)S(1)}, f32[64,448]{1,0:T(8,128)S(1)}) custom-call(bf16[16,4096]{1,0:T(8,128)(2,1)S(1)} %get-tuple-element.43.first.refs_0_, bf16[16,4096]{1,0:T(8,128)(2,1)S(1)} %get-tuple-element.45.second.refs_1_, bf16[16,4096]{1,0:T(8,128)(2,1)S(1)} %collective-permute-done.refs_2_, ...), custom_call_target="tpu_custom_call" | custom-call | flops 2300000000 | tf_op jit(solution)/shard_map/early_left/pallas_call | solution.py:155
  26.0 0.3 collective-permute-done.3.first
  26.3 2.1 %collective-permute-done.7.second = bf16[16,4096]{1,0:T(8,128)(2,1)S(1)} collective-permute-done((bf16[16,4096]{1,0:T(8,128)(2,1)S(1)}, bf16[16,4096]{1,0:T(8,128)(2,1)S(1)}, u32[]{:S(2)}, u32[]{:S(2)}) %collective-permute-start.7) | collective-permute-done | bytes 131104 | tf_op jit(solution)/shard_map/ppermute | solution.py:632
  28.4 0.6 late_left.1
  29.1 1.3 %collective-permute-done.14.other_l = f32[64,448]{1,0:T(8,128)S(1)} collective-permute-done((f32[64,448]{1,0:T(8,128)S(1)}, f32[64,448]{1,0:T(8,128)S(1)}, u32[]{:S(2)}, u32[]{:S(2)}) %collective-permute-start.14) | collective-permute-done | bytes 114720 | tf_op jit(solution)/shard_map/ppermute | solution.py:641
  30.4 0.5 given_far.1
  31.2 0.6 near_terms.1
  31.8 0.4 collective-permute-start.16
  32.2 0.5 kept_far.1
  32.8 1.1 %collective-permute-start.18 = (f32[72,512]{1,0:T(8,128)S(1)}, f32[72,512]{1,0:T(8,128)S(1)}, u32[]{:S(2)}, u32[]{:S(2)}) collective-permute-start(f32[72,512]{1,0:T(8,128)S(1)} %begin_messages.1), channel_id=1, source_target_pairs={{0,8},{1,3},{2,10},{3,1},{4,12},{5,7},{6,14},{7,5},{8,0},{9,11},{1... | collective-permute-start | bytes 442376 | tf_op jit(solution)/shard_map/ppermute | solution.py:656
  33.9 2.9 %collective-permute-start.19 = (f32[72,512]{1,0:T(8,128)S(1)}, f32[72,512]{1,0:T(8,128)S(1)}, u32[]{:S(2)}, u32[]{:S(2)}) collective-permute-start(f32[72,512]{1,0:T(8,128)S(1)} %get-tuple-element.68), channel_id=1, source_target_pairs={{0,10},{1,5},{2,8},{3,7},{4,14},{5,1},{6,12},{7,3},{8,2},{9,13},{1... | collective-permute-start | bytes 442376 | tf_op jit(solution)/shard_map/ppermute | solution.py:656
  36.8 0.7 %collective-permute-start.17 = (f32[72,512]{1,0:T(8,128)S(1)}, f32[72,512]{1,0:T(8,128)S(1)}, u32[]{:S(2)}, u32[]{:S(2)}) collective-permute-start(f32[72,512]{1,0:T(8,128)S(1)} %get-tuple-element.65), channel_id=1, source_target_pairs={{1,7},{3,5},{5,3},{7,1},{9,15},{11,13},{13,11},{15,9},{17,23},{19,... | collective-permute-start | bytes 442376 | tf_op jit(solution)/shard_map/ppermute | solution.py:656
  37.4 2.4 %collective-permute-done.18.passed.refs_0_ = f32[72,512]{1,0:T(8,128)S(1)} collective-permute-done((f32[72,512]{1,0:T(8,128)S(1)}, f32[72,512]{1,0:T(8,128)S(1)}, u32[]{:S(2)}, u32[]{:S(2)}) %collective-permute-start.18) | collective-permute-done | bytes 147488 | tf_op jit(solution)/shard_map/ppermute | solution.py:656
  39.9 1.1 %collective-permute-start.20 = (f32[72,512]{1,0:T(8,128)S(1)}, f32[72,512]{1,0:T(8,128)S(1)}, u32[]{:S(2)}, u32[]{:S(2)}) collective-permute-start(f32[72,512]{1,0:T(8,128)S(1)} %crossing.1), channel_id=1, source_target_pairs={{0,2},{1,13},{2,0},{3,15},{4,6},{5,9},{6,4},{7,11},{8,10},{9,5},{1... | collective-permute-start | bytes 442376 | tf_op jit(solution)/shard_map/ppermute | solution.py:656
  41.0 1.1 %merged.1 = f32[448,4096]{1,0:T(8,128)S(1)} custom-call(bf16[448,256]{1,0:T(8,128)(2,1)S(1)} %bitcast.14, bf16[448,4096]{1,0:T(8,128)(2,1)S(1)} %bitcast.11, bf16[256,4096]{1,0:T(8,128)(2,1)S(1)} %get-tuple-element.66.tokens), custom_call_target="tpu_custom_call" | custom-call | flops 57500000 | tf_op jit(solution)/shard_map/merged/pallas_call | solution.py:305
  42.2 2.8 %collective-permute-done.19.refs_1_ = f32[72,512]{1,0:T(8,128)S(1)} collective-permute-done((f32[72,512]{1,0:T(8,128)S(1)}, f32[72,512]{1,0:T(8,128)S(1)}, u32[]{:S(2)}, u32[]{:S(2)}) %collective-permute-start.19) | collective-permute-done | bytes 147488 | tf_op jit(solution)/shard_map/ppermute | solution.py:656
  44.9 0.5 collective-permute-done.20.refs_2_
  45.6 1.4 %collective-permute-done.21.other = f32[72,512]{1,0:T(8,128)S(1)} collective-permute-done((f32[72,512]{1,0:T(8,128)S(1)}, f32[72,512]{1,0:T(8,128)S(1)}, u32[]{:S(2)}, u32[]{:S(2)}) %collective-permute-start.21) | collective-permute-done | bytes 147488 | tf_op jit(solution)/shard_map/ppermute | solution.py:641
  47.0 2.6 %collective-permute-start.23 = (f32[64,512]{1,0:T(8,128)S(1)}, f32[64,512]{1,0:T(8,128)S(1)}, u32[]{:S(2)}, u32[]{:S(2)}) collective-permute-start(f32[64,512]{1,0:T(8,128)S(1)} %get-tuple-element.70.share.here), channel_id=1, source_target_pairs={{0,2},{1,13},{2,0},{3,15},{4,6},{5,9},{6,4},{7,11},{8,10},{9,5},{1... | collective-permute-start | bytes 393224 | tf_op jit(solution)/shard_map/ppermute | solution.py:656
  49.7 1.3 %collective-permute-start.24 = (f32[64,512]{1,0:T(8,128)S(1)}, f32[64,512]{1,0:T(8,128)S(1)}, u32[]{:S(2)}, u32[]{:S(2)}) collective-permute-start(f32[64,512]{1,0:T(8,128)S(1)} %get-tuple-element.70.share.here), channel_id=1, source_target_pairs={{0,10},{1,5},{2,8},{3,7},{4,14},{5,1},{6,12},{7,3},{8,2},{9,13},{1... | collective-permute-start | bytes 393224 | tf_op jit(solution)/shard_map/ppermute | solution.py:656
  50.9 0.7 %collective-permute-start.22 = (f32[64,512]{1,0:T(8,128)S(1)}, f32[64,512]{1,0:T(8,128)S(1)}, u32[]{:S(2)}, u32[]{:S(2)}) collective-permute-start(f32[64,512]{1,0:T(8,128)S(1)} %get-tuple-element.70.share.here), channel_id=1, source_target_pairs={{1,7},{3,5},{5,3},{7,1},{9,15},{11,13},{13,11},{15,9},{17,23},{19,... | collective-permute-start | bytes 393224 | tf_op jit(solution)/shard_map/ppermute | solution.py:656
  51.6 1.0 %collective-permute-done.23.refs_0_.there = f32[64,512]{1,0:T(8,128)S(1)} collective-permute-done((f32[64,512]{1,0:T(8,128)S(1)}, f32[64,512]{1,0:T(8,128)S(1)}, u32[]{:S(2)}, u32[]{:S(2)}) %collective-permute-start.23) | collective-permute-done | bytes 131104 | tf_op jit(solution)/shard_map/ppermute | solution.py:656
  52.6 1.9 %collective-permute-start.25 = (f32[64,512]{1,0:T(8,128)S(1)}, f32[64,512]{1,0:T(8,128)S(1)}, u32[]{:S(2)}, u32[]{:S(2)}) collective-permute-start(f32[64,512]{1,0:T(8,128)S(1)} %by_core.1), channel_id=1, source_target_pairs={{0,8},{1,3},{2,10},{3,1},{4,12},{5,7},{6,14},{7,5},{8,0},{9,11},{1... | collective-permute-start | bytes 393224 | tf_op jit(solution)/shard_map/ppermute | solution.py:656
  54.5 1.8 %cholesky_inverse.1.inverse = f32[64,64]{1,0:T(8,128)S(1)} custom-call(f32[64,64]{1,0:T(8,128)S(1)} %get-tuple-element.71.gram), custom_call_target="tpu_custom_call" | custom-call | flops 5750000128 | tf_op jit(solution)/shard_map/cholesky_inverse/pallas_call | solution.py:513
  56.3 0.8 %last_operand.1.lhs = bf16[512,256]{1,0:T(8,128)(2,1)S(1)} custom-call(f32[64,64]{1,0:T(8,128)S(1)} %cholesky_inverse.1.inverse, f32[64,448]{1,0:T(8,128)S(1)} %get-tuple-element.56.left_sum), custom_call_target="tpu_custom_call" | custom-call | flops 57500000 | tf_op jit(solution)/shard_map/last_operand/pallas_call | solution.py:544
  57.1 0.9 %collective-permute-done.24.refs_1_ = f32[64,512]{1,0:T(8,128)S(1)} collective-permute-done((f32[64,512]{1,0:T(8,128)S(1)}, f32[64,512]{1,0:T(8,128)S(1)}, u32[]{:S(2)}, u32[]{:S(2)}) %collective-permute-start.24) | collective-permute-done | bytes 131104 | tf_op jit(solution)/shard_map/ppermute | solution.py:656
  58.0 1.5 %finish.3 = (bf16[448,4096]{1,0:T(8,128)(2,1)}, f32[64,4096]{1,0:T(8,128)}) custom-call(f32[3,64,512]{2,1,0:T(8,128)S(1)} %joined.1.shares, bf16[512,256]{1,0:T(8,128)(2,1)S(1)} %last_operand.1.lhs, f32[448,4096]{1,0:T(8,128)S(1)} %merged.1), custom_call_target="tpu_custom_call" | custom-call | flops 57500000 | tf_op jit(solution)/shard_map/finish/pallas_call | solution.py:583
  59.6 0.4 collective-permute-done.25
  60.0 0.3 collective-permute-start.26
  60.3 1.1 %finish.4 = (bf16[448,4096]{1,0:T(8,128)(2,1)}, f32[64,4096]{1,0:T(8,128)}) custom-call(f32[1,64,512]{2,1,0:T(8,128)S(1)} %bitcast.16, bf16[512,256]{1,0:T(8,128)(2,1)S(1)} %last_operand.1.lhs, f32[448,4096]{1,0:T(8,128)S(1)} %merged.1, bf16[448,4096]{1,0:T(8,128)(2,1)} %get-tuple-element.78.refs_0_, ...), custom_call_target="tpu_custom_call", output_to_operand_aliasing={{0}: (3, {}), {1}: (4, {})} | custom-call | flops 57500000 | tf_op jit(solution)/shard_map/finish/pallas_call | solution.py:583
  61.4 0.5 collective-permute-done.26.shares
  62.0 1.7 %finish.5 = (bf16[448,4096]{1,0:T(8,128)(2,1)}, f32[64,4096]{1,0:T(8,128)}) custom-call(f32[4,64,512]{2,1,0:T(8,128)S(1)} %collective-permute-done.26.shares, bf16[512,256]{1,0:T(8,128)(2,1)S(1)} %last_operand.1.lhs, f32[448,4096]{1,0:T(8,128)S(1)} %merged.1, ...), custom_call_target="tpu_custom_call", output_to_operand_aliasing={{0}: (3, {}), {1}: (4, {})} | custom-call | flops 57500000 | tf_op jit(solution)/shard_map/finish/pallas_call | solution.py:583
  (36 shorter events, 1.6 us)
Async XLA Ops:
  0.6 1.0 %copy-start.3 = (bf16[1,32,4096]{2,1,0:T(8,128)(2,1)S(1)}, bf16[1,32,4096]{2,1,0:T(8,128)(2,1)}, u32[]{:S(2)}) copy-start(bf16[1,32,4096]{2,1,0:T(8,128)(2,1)} %param.4) | copy-start | bytes 786436
  1.6 6.9 %collective-permute-start = (bf16[16,4096]{1,0:T(8,128)(2,1)S(1)}, bf16[16,4096]{1,0:T(8,128)(2,1)S(1)}, u32[]{:S(2)}, u32[]{:S(2)}) collective-permute-start(bf16[16,4096]{1,0:T(8,128)(2,1)S(1)} %get-tuple-element.43.first.refs_0_), channel_id=1, source_target_pairs={{0,2},{1,5},{2,6},{3,1},{6,10},{7,3},{10,14},{11,7},{14,12},{15,11... | collective-permute-start | bytes 393224 | tf_op jit(solution)/shard_map/ppermute | solution.py:632
  4.6 18.8 %copy-start = (bf16[1,448,4096]{2,1,0:T(8,128)(2,1)S(1)}, bf16[1,448,4096]{2,1,0:T(8,128)(2,1)}, u32[]{:S(2)}) copy-start(bf16[1,448,4096]{2,1,0:T(8,128)(2,1)} %param.6) | copy-start | bytes 11010052
  4.6 18.8 %copy-start.2 = (f32[64,4096]{1,0:T(8,128)S(1)}, f32[64,4096]{1,0:T(8,128)}, u32[]{:S(2)}) copy-start(f32[64,4096]{1,0:T(8,128)} %right) | copy-start | bytes 3145732
  4.6 6.4 %collective-permute-start.4 = (bf16[16,4096]{1,0:T(8,128)(2,1)S(1)}, bf16[16,4096]{1,0:T(8,128)(2,1)S(1)}, u32[]{:S(2)}, u32[]{:S(2)}) collective-permute-start(bf16[16,4096]{1,0:T(8,128)(2,1)S(1)} %get-tuple-element.45.second.refs_1_), channel_id=1, source_target_pairs={{0,4},{1,3},{2,0},{3,7},{6,2},{7,11},{10,6},{11,15},{14,10},{15,13... | collective-permute-start | bytes 393224 | tf_op jit(solution)/shard_map/ppermute | solution.py:632
  4.8 6.5 %collective-permute-start.8 = (bf16[16,4096]{1,0:T(8,128)(2,1)S(1)}, bf16[16,4096]{1,0:T(8,128)(2,1)S(1)}, u32[]{:S(2)}, u32[]{:S(2)}) collective-permute-start(bf16[16,4096]{1,0:T(8,128)(2,1)S(1)} %get-tuple-element.48), channel_id=1, source_target_pairs={{0,2},{1,5},{2,6},{3,1},{6,10},{7,3},{10,14},{11,7},{14,12},{15,11... | collective-permute-start | bytes 393224 | tf_op jit(solution)/shard_map/ppermute | solution.py:632
  6.7 6.3 %collective-permute-start.9 = (bf16[16,4096]{1,0:T(8,128)(2,1)S(1)}, bf16[16,4096]{1,0:T(8,128)(2,1)S(1)}, u32[]{:S(2)}, u32[]{:S(2)}) collective-permute-start(bf16[16,4096]{1,0:T(8,128)(2,1)S(1)} %get-tuple-element.49), channel_id=1, source_target_pairs={{0,4},{1,3},{2,0},{3,7},{6,2},{7,11},{10,6},{11,15},{14,10},{15,13... | collective-permute-start | bytes 393224 | tf_op jit(solution)/shard_map/ppermute | solution.py:632
  8.5 6.7 %collective-permute-start.1 = (bf16[16,4096]{1,0:T(8,128)(2,1)S(1)}, bf16[16,4096]{1,0:T(8,128)(2,1)S(1)}, u32[]{:S(2)}, u32[]{:S(2)}) collective-permute-start(bf16[16,4096]{1,0:T(8,128)(2,1)S(1)} %collective-permute-done.refs_2_), channel_id=1, source_target_pairs={{0,2},{1,5},{2,6},{3,1},{6,10},{7,3},{10,14},{11,7},{14,12},{15,11... | collective-permute-start | bytes 393224 | tf_op jit(solution)/shard_map/ppermute | solution.py:632
  11.0 6.2 %collective-permute-start.5 = (bf16[16,4096]{1,0:T(8,128)(2,1)S(1)}, bf16[16,4096]{1,0:T(8,128)(2,1)S(1)}, u32[]{:S(2)}, u32[]{:S(2)}) collective-permute-start(bf16[16,4096]{1,0:T(8,128)(2,1)S(1)} %collective-permute-done.4.refs_3_), channel_id=1, source_target_pairs={{0,4},{1,3},{2,0},{3,7},{6,2},{7,11},{10,6},{11,15},{14,10},{15,13... | collective-permute-start | bytes 393224 | tf_op jit(solution)/shard_map/ppermute | solution.py:632
  11.3 6.8 %collective-permute-start.10 = (bf16[16,4096]{1,0:T(8,128)(2,1)S(1)}, bf16[16,4096]{1,0:T(8,128)(2,1)S(1)}, u32[]{:S(2)}, u32[]{:S(2)}) collective-permute-start(bf16[16,4096]{1,0:T(8,128)(2,1)S(1)} %collective-permute-done.8.refs_4_), channel_id=1, source_target_pairs={{0,2},{1,5},{2,6},{3,1},{6,10},{7,3},{10,14},{11,7},{14,12},{15,11... | collective-permute-start | bytes 393224 | tf_op jit(solution)/shard_map/ppermute | solution.py:632
  13.0 6.8 %collective-permute-start.11 = (bf16[16,4096]{1,0:T(8,128)(2,1)S(1)}, bf16[16,4096]{1,0:T(8,128)(2,1)S(1)}, u32[]{:S(2)}, u32[]{:S(2)}) collective-permute-start(bf16[16,4096]{1,0:T(8,128)(2,1)S(1)} %collective-permute-done.9.refs_5_), channel_id=1, source_target_pairs={{0,4},{1,3},{2,0},{3,7},{6,2},{7,11},{10,6},{11,15},{14,10},{15,13... | collective-permute-start | bytes 393224 | tf_op jit(solution)/shard_map/ppermute | solution.py:632
  15.2 5.7 %collective-permute-start.2 = (bf16[16,4096]{1,0:T(8,128)(2,1)S(1)}, bf16[16,4096]{1,0:T(8,128)(2,1)S(1)}, u32[]{:S(2)}, u32[]{:S(2)}) collective-permute-start(bf16[16,4096]{1,0:T(8,128)(2,1)S(1)} %collective-permute-done.1.refs_6_), channel_id=1, source_target_pairs={{0,2},{1,5},{2,6},{3,1},{6,10},{7,3},{10,14},{11,7},{14,12},{15,11... | collective-permute-start | bytes 393224 | tf_op jit(solution)/shard_map/ppermute | solution.py:632
  17.2 6.2 %collective-permute-start.6 = (bf16[16,4096]{1,0:T(8,128)(2,1)S(1)}, bf16[16,4096]{1,0:T(8,128)(2,1)S(1)}, u32[]{:S(2)}, u32[]{:S(2)}) collective-permute-start(bf16[16,4096]{1,0:T(8,128)(2,1)S(1)} %collective-permute-done.5.refs_7_), channel_id=1, source_target_pairs={{0,4},{1,3},{2,0},{3,7},{6,2},{7,11},{10,6},{11,15},{14,10},{15,13... | collective-permute-start | bytes 393224 | tf_op jit(solution)/shard_map/ppermute | solution.py:632
  18.1 6.6 %collective-permute-start.12 = (bf16[16,4096]{1,0:T(8,128)(2,1)S(1)}, bf16[16,4096]{1,0:T(8,128)(2,1)S(1)}, u32[]{:S(2)}, u32[]{:S(2)}) collective-permute-start(bf16[16,4096]{1,0:T(8,128)(2,1)S(1)} %collective-permute-done.10.refs_8_), channel_id=1, source_target_pairs={{0,2},{1,5},{2,6},{3,1},{6,10},{7,3},{10,14},{11,7},{14,12},{15,11... | collective-permute-start | bytes 393224 | tf_op jit(solution)/shard_map/ppermute | solution.py:632
  19.8 5.0 %collective-permute-start.13 = (bf16[16,4096]{1,0:T(8,128)(2,1)S(1)}, bf16[16,4096]{1,0:T(8,128)(2,1)S(1)}, u32[]{:S(2)}, u32[]{:S(2)}) collective-permute-start(bf16[16,4096]{1,0:T(8,128)(2,1)S(1)} %collective-permute-done.11.refs_9_), channel_id=1, source_target_pairs={{0,4},{1,3},{2,0},{3,7},{6,2},{7,11},{10,6},{11,15},{14,10},{15,13... | collective-permute-start | bytes 393224 | tf_op jit(solution)/shard_map/ppermute | solution.py:632
  20.9 5.4 %collective-permute-start.3 = (bf16[16,4096]{1,0:T(8,128)(2,1)S(1)}, bf16[16,4096]{1,0:T(8,128)(2,1)S(1)}, u32[]{:S(2)}, u32[]{:S(2)}) collective-permute-start(bf16[16,4096]{1,0:T(8,128)(2,1)S(1)} %collective-permute-done.2.refs_10_), channel_id=1, source_target_pairs={{0,2},{1,5},{2,6},{3,1},{6,10},{7,3},{10,14},{11,7},{14,12},{15,11... | collective-permute-start | bytes 393224 | tf_op jit(solution)/shard_map/ppermute | solution.py:632
  23.4 5.0 %collective-permute-start.7 = (bf16[16,4096]{1,0:T(8,128)(2,1)S(1)}, bf16[16,4096]{1,0:T(8,128)(2,1)S(1)}, u32[]{:S(2)}, u32[]{:S(2)}) collective-permute-start(bf16[16,4096]{1,0:T(8,128)(2,1)S(1)} %collective-permute-done.6.refs_11_), channel_id=1, source_target_pairs={{0,4},{1,3},{2,0},{3,7},{6,2},{7,11},{10,6},{11,15},{14,10},{15,13... | collective-permute-start | bytes 393224 | tf_op jit(solution)/shard_map/ppermute | solution.py:632
  23.4 1.3 %copy-start.1 = (bf16[1,256,448]{1,2,0:T(8,128)(2,1)S(1)}, bf16[1,256,448]{1,2,0:T(8,128)(2,1)}, u32[]{:S(2)}) copy-start(bf16[1,256,448]{1,2,0:T(8,128)(2,1)} %param.5) | copy-start | bytes 688132
  29.0 1.4 %collective-permute-start.14 = (f32[64,448]{1,0:T(8,128)S(1)}, f32[64,448]{1,0:T(8,128)S(1)}, u32[]{:S(2)}, u32[]{:S(2)}) collective-permute-start(f32[64,448]{1,0:T(8,128)S(1)} %get-tuple-element.54.here_l), channel_id=1, source_target_pairs={{0,1},{1,0},{2,3},{3,2},{4,5},{5,4},{6,7},{7,6},{8,9},{9,8},{10,11... | collective-permute-start | bytes 344072 | tf_op jit(solution)/shard_map/ppermute | solution.py:641
  31.0 1.7 %collective-permute-start.15 = (f32[2,64,512]{2,1,0:T(8,128)S(1)}, f32[2,64,512]{2,1,0:T(8,128)S(1)}, u32[]{:S(2)}, u32[]{:S(2)}) collective-permute-start(f32[2,64,512]{2,1,0:T(8,128)S(1)} %get-tuple-element.60), channel_id=1, source_target_pairs={{0,1},{1,0},{2,3},{3,2},{4,5},{5,4},{6,7},{7,6},{8,9},{9,8},{10,11... | collective-permute-start | bytes 786440 | tf_op jit(solution)/shard_map/ppermute | solution.py:641
  31.8 2.1 %collective-permute-start.16 = (f32[2,64,512]{2,1,0:T(8,128)S(1)}, f32[2,64,512]{2,1,0:T(8,128)S(1)}, u32[]{:S(2)}, u32[]{:S(2)}) collective-permute-start(f32[2,64,512]{2,1,0:T(8,128)S(1)} %get-tuple-element.62), channel_id=1, source_target_pairs={{0,1},{1,0},{2,3},{3,2},{4,5},{5,4},{6,7},{7,6},{8,9},{9,8},{10,11... | collective-permute-start | bytes 786440 | tf_op jit(solution)/shard_map/ppermute | solution.py:641
  32.8 7.1 %collective-permute-start.18 = (f32[72,512]{1,0:T(8,128)S(1)}, f32[72,512]{1,0:T(8,128)S(1)}, u32[]{:S(2)}, u32[]{:S(2)}) collective-permute-start(f32[72,512]{1,0:T(8,128)S(1)} %begin_messages.1), channel_id=1, source_target_pairs={{0,8},{1,3},{2,10},{3,1},{4,12},{5,7},{6,14},{7,5},{8,0},{9,11},{1... | collective-permute-start | bytes 442376 | tf_op jit(solution)/shard_map/ppermute | solution.py:656
  33.9 11.0 %collective-permute-start.19 = (f32[72,512]{1,0:T(8,128)S(1)}, f32[72,512]{1,0:T(8,128)S(1)}, u32[]{:S(2)}, u32[]{:S(2)}) collective-permute-start(f32[72,512]{1,0:T(8,128)S(1)} %get-tuple-element.68), channel_id=1, source_target_pairs={{0,10},{1,5},{2,8},{3,7},{4,14},{5,1},{6,12},{7,3},{8,2},{9,13},{1... | collective-permute-start | bytes 442376 | tf_op jit(solution)/shard_map/ppermute | solution.py:656
  36.8 5.4 %collective-permute-start.17 = (f32[72,512]{1,0:T(8,128)S(1)}, f32[72,512]{1,0:T(8,128)S(1)}, u32[]{:S(2)}, u32[]{:S(2)}) collective-permute-start(f32[72,512]{1,0:T(8,128)S(1)} %get-tuple-element.65), channel_id=1, source_target_pairs={{1,7},{3,5},{5,3},{7,1},{9,15},{11,13},{13,11},{15,9},{17,23},{19,... | collective-permute-start | bytes 442376 | tf_op jit(solution)/shard_map/ppermute | solution.py:656
  39.9 5.6 %collective-permute-start.20 = (f32[72,512]{1,0:T(8,128)S(1)}, f32[72,512]{1,0:T(8,128)S(1)}, u32[]{:S(2)}, u32[]{:S(2)}) collective-permute-start(f32[72,512]{1,0:T(8,128)S(1)} %crossing.1), channel_id=1, source_target_pairs={{0,2},{1,13},{2,0},{3,15},{4,6},{5,9},{6,4},{7,11},{8,10},{9,5},{1... | collective-permute-start | bytes 442376 | tf_op jit(solution)/shard_map/ppermute | solution.py:656
  45.5 1.4 %collective-permute-start.21 = (f32[72,512]{1,0:T(8,128)S(1)}, f32[72,512]{1,0:T(8,128)S(1)}, u32[]{:S(2)}, u32[]{:S(2)}) collective-permute-start(f32[72,512]{1,0:T(8,128)S(1)} %core_sum.1.here), channel_id=1, source_target_pairs={{0,1},{1,0},{2,3},{3,2},{4,5},{5,4},{6,7},{7,6},{8,9},{9,8},{10,11... | collective-permute-start | bytes 442376 | tf_op jit(solution)/shard_map/ppermute | solution.py:641
  47.0 5.6 %collective-permute-start.23 = (f32[64,512]{1,0:T(8,128)S(1)}, f32[64,512]{1,0:T(8,128)S(1)}, u32[]{:S(2)}, u32[]{:S(2)}) collective-permute-start(f32[64,512]{1,0:T(8,128)S(1)} %get-tuple-element.70.share.here), channel_id=1, source_target_pairs={{0,2},{1,13},{2,0},{3,15},{4,6},{5,9},{6,4},{7,11},{8,10},{9,5},{1... | collective-permute-start | bytes 393224 | tf_op jit(solution)/shard_map/ppermute | solution.py:656
  49.7 8.3 %collective-permute-start.24 = (f32[64,512]{1,0:T(8,128)S(1)}, f32[64,512]{1,0:T(8,128)S(1)}, u32[]{:S(2)}, u32[]{:S(2)}) collective-permute-start(f32[64,512]{1,0:T(8,128)S(1)} %get-tuple-element.70.share.here), channel_id=1, source_target_pairs={{0,10},{1,5},{2,8},{3,7},{4,14},{5,1},{6,12},{7,3},{8,2},{9,13},{1... | collective-permute-start | bytes 393224 | tf_op jit(solution)/shard_map/ppermute | solution.py:656
  50.9 7.1 %collective-permute-start.22 = (f32[64,512]{1,0:T(8,128)S(1)}, f32[64,512]{1,0:T(8,128)S(1)}, u32[]{:S(2)}, u32[]{:S(2)}) collective-permute-start(f32[64,512]{1,0:T(8,128)S(1)} %get-tuple-element.70.share.here), channel_id=1, source_target_pairs={{1,7},{3,5},{5,3},{7,1},{9,15},{11,13},{13,11},{15,9},{17,23},{19,... | collective-permute-start | bytes 393224 | tf_op jit(solution)/shard_map/ppermute | solution.py:656
  52.6 7.3 %collective-permute-start.25 = (f32[64,512]{1,0:T(8,128)S(1)}, f32[64,512]{1,0:T(8,128)S(1)}, u32[]{:S(2)}, u32[]{:S(2)}) collective-permute-start(f32[64,512]{1,0:T(8,128)S(1)} %by_core.1), channel_id=1, source_target_pairs={{0,8},{1,3},{2,10},{3,1},{4,12},{5,7},{6,14},{7,5},{8,0},{9,11},{1... | collective-permute-start | bytes 393224 | tf_op jit(solution)/shard_map/ppermute | solution.py:656
  60.0 2.0 %collective-permute-start.26 = (f32[4,64,512]{2,1,0:T(8,128)S(1)}, f32[4,64,512]{2,1,0:T(8,128)S(1)}, u32[]{:S(2)}, u32[]{:S(2)}) collective-permute-start(f32[4,64,512]{2,1,0:T(8,128)S(1)} %pad_maximum_fusion), channel_id=1, source_target_pairs={{0,1},{1,0},{2,3},{3,2},{4,5},{5,4},{6,7},{7,6},{8,9},{9,8},{10,11... | collective-permute-start | bytes 1572872 | tf_op jit(solution)/shard_map/ppermute | solution.py:641

commit v11 on v10

--- a/solution.py
+++ b/solution.py
@@ -167,29 +167,34 @@
     )(*operands)
 
 
-def late_kernel(origins, first, second, terms, hidden, early_t, _, tokens, left_t):
+def late_kernel(origins, first, second, terms, hidden, early_t, _, tokens, left_t, sems):
     size = first.shape[0]
-    seen = []
-    for origin, piece in zip(origins, (first, second)):
+    seen, copies = [], []
+    for index, (origin, piece) in enumerate(zip(origins, (first, second))):
         rows = piece_rows(origin, size)
-        tokens[rows, :] = piece[...]
+        copies.append(pltpu.make_async_copy(piece, tokens.at[rows, :], sems.at[index]))
+        copies[-1].start()
         seen.append(hidden[rows, :])
     projected = fold2(nt(terms[...], jnp.concatenate([first[...], second[...]], axis=0)))
     stacked = jnp.concatenate(split2(projected), axis=0)
     left_t[...] = early_t[...] + fold2(nn(stacked, jnp.concatenate(seen, axis=0)))
+    for copy in copies:
+        copy.wait()
 
 
 def late_left(origins, pieces, terms, hidden, early_t, tokens):
     operands = [*pieces, terms, hidden, early_t, tokens]
     return pl.pallas_call(
         functools.partial(late_kernel, origins),
-        in_specs=[pl.BlockSpec(memory_space=pltpu.VMEM)] * len(operands),
-        out_specs=[pl.BlockSpec(memory_space=pltpu.VMEM)] * 2,
+        in_specs=[pl.BlockSpec(memory_space=pltpu.VMEM)] * (len(operands) - 1)
+        + [pl.BlockSpec(memory_space=pl.ANY)],
+        out_specs=[pl.BlockSpec(memory_space=pl.ANY), pl.BlockSpec(memory_space=pltpu.VMEM)],
         out_shape=[
             jax.ShapeDtypeStruct(tokens.shape, BF16),
             jax.ShapeDtypeStruct(early_t.shape, F32),
         ],
         input_output_aliases={len(operands) - 1: 0},
+        scratch_shapes=[pltpu.SemaphoreType.DMA((2,))],
         compiler_params=params(),
         cost_estimate=cost(1.0),
         name="late_left",

time: 63.9 us -> 64.2 us (level)
  no operation moved by 1% of the time
where the time goes in v11:
time: 64.2 us; the launch traced here: 64.1 us
  starting transfers between devices  30 us (47%)
  waiting for transfers between devices  18.8 us (29%)
  Pallas kernels  13.5 us (21%)
  local copies, waits for them, and re-layouts  0.96 us (1%)
  between operations  0.84 us (1%)
    ppermute x14, starting transfers between devices, ring_gather(): going[way, half] = lax.ppermute(going[way, half], ('tp', 'dp'), pairs(way))  16.7 us
    ppermute x8, starting transfers between devices, send(): return lax.ppermute(value, ('tp', 'dp'), pairs)  12.1 us
    ppermute x8, waiting for transfers between devices, send(): return lax.ppermute(value, ('tp', 'dp'), pairs)  8.03 us
    ppermute x14, waiting for transfers between devices, ring_gather(): going[way, half] = lax.ppermute(going[way, half], ('tp', 'dp'), pairs(way))  7.51 us
    pallas_call x3, Pallas kernels, finish(): pl.pallas_call(functools.partial(final_kernel, indices, side), in_specs=[...  4.39 us
    ppermute x5, waiting for transfers between devices, swap(): return lax.ppermute(value, 'dp', [(0, 1), (1, 0)])  3.24 us
    pallas_call x1, Pallas kernels, cholesky_inverse(): pl.pallas_call(inverse_kernel, in_specs=[pl.BlockSpec(memory_space=pltpu....  1.77 us
  transfers between devices with their start and end apart: 27, of which 19 were waited for; matrix products, arithmetic and copies ran while one was open for 0% of the time, Pallas kernels for 16%

profile of v11, /device:TPU:0, one launch (start us, length us, event | category | flops | bytes accessed | tf_op | source)
XLA Modules:
  0.0 64.1 jit_solution(13712400584146482364)
XLA Ops:
  0.6 0.9 %copy-done.3 = bf16[1,32,4096]{2,1,0:T(8,128)(2,1)S(1)} copy-done((bf16[1,32,4096]{2,1,0:T(8,128)(2,1)S(1)}, bf16[1,32,4096]{2,1,0:T(8,128)(2,1)}, u32[]{:S(2)}) %copy-start.3) | copy-done | bytes 262168
  1.6 3.0 %collective-permute-start = (bf16[16,4096]{1,0:T(8,128)(2,1)S(1)}, bf16[16,4096]{1,0:T(8,128)(2,1)S(1)}, u32[]{:S(2)}, u32[]{:S(2)}) collective-permute-start(bf16[16,4096]{1,0:T(8,128)(2,1)S(1)} %get-tuple-element.43.first.refs_0_), channel_id=1, source_target_pairs={{0,2},{1,5},{2,6},{3,1},{6,10},{7,3},{10,14},{11,7},{14,12},{15,11... | collective-permute-start | bytes 393224 | tf_op jit(solution)/shard_map/ppermute | solution.py:637
  4.8 1.9 %collective-permute-start.8 = (bf16[16,4096]{1,0:T(8,128)(2,1)S(1)}, bf16[16,4096]{1,0:T(8,128)(2,1)S(1)}, u32[]{:S(2)}, u32[]{:S(2)}) collective-permute-start(bf16[16,4096]{1,0:T(8,128)(2,1)S(1)} %get-tuple-element.48), channel_id=1, source_target_pairs={{0,2},{1,5},{2,6},{3,1},{6,10},{7,3},{10,14},{11,7},{14,12},{15,11... | collective-permute-start | bytes 393224 | tf_op jit(solution)/shard_map/ppermute | solution.py:637
  6.9 1.6 %collective-permute-done.refs_2_ = bf16[16,4096]{1,0:T(8,128)(2,1)S(1)} collective-permute-done((bf16[16,4096]{1,0:T(8,128)(2,1)S(1)}, bf16[16,4096]{1,0:T(8,128)(2,1)S(1)}, u32[]{:S(2)}, u32[]{:S(2)}) %collective-permute-start) | collective-permute-done | bytes 131104 | tf_op jit(solution)/shard_map/ppermute | solution.py:637
  8.5 2.5 %collective-permute-start.1 = (bf16[16,4096]{1,0:T(8,128)(2,1)S(1)}, bf16[16,4096]{1,0:T(8,128)(2,1)S(1)}, u32[]{:S(2)}, u32[]{:S(2)}) collective-permute-start(bf16[16,4096]{1,0:T(8,128)(2,1)S(1)} %collective-permute-done.refs_2_), channel_id=1, source_target_pairs={{0,2},{1,5},{2,6},{3,1},{6,10},{7,3},{10,14},{11,7},{14,12},{15,11... | collective-permute-start | bytes 393224 | tf_op jit(solution)/shard_map/ppermute | solution.py:637
  11.3 1.8 %collective-permute-start.10 = (bf16[16,4096]{1,0:T(8,128)(2,1)S(1)}, bf16[16,4096]{1,0:T(8,128)(2,1)S(1)}, u32[]{:S(2)}, u32[]{:S(2)}) collective-permute-start(bf16[16,4096]{1,0:T(8,128)(2,1)S(1)} %collective-permute-done.8.refs_4_), channel_id=1, source_target_pairs={{0,2},{1,5},{2,6},{3,1},{6,10},{7,3},{10,14},{11,7},{14,12},{15,11... | collective-permute-start | bytes 393224 | tf_op jit(solution)/shard_map/ppermute | solution.py:637
  13.0 0.9 %collective-permute-start.11 = (bf16[16,4096]{1,0:T(8,128)(2,1)S(1)}, bf16[16,4096]{1,0:T(8,128)(2,1)S(1)}, u32[]{:S(2)}, u32[]{:S(2)}) collective-permute-start(bf16[16,4096]{1,0:T(8,128)(2,1)S(1)} %collective-permute-done.9.refs_5_), channel_id=1, source_target_pairs={{0,4},{1,3},{2,0},{3,7},{6,2},{7,11},{10,6},{11,15},{14,10},{15,13... | collective-permute-start | bytes 393224 | tf_op jit(solution)/shard_map/ppermute | solution.py:637
  14.0 1.3 %collective-permute-done.1.refs_6_ = bf16[16,4096]{1,0:T(8,128)(2,1)S(1)} collective-permute-done((bf16[16,4096]{1,0:T(8,128)(2,1)S(1)}, bf16[16,4096]{1,0:T(8,128)(2,1)S(1)}, u32[]{:S(2)}, u32[]{:S(2)}) %collective-permute-start.1) | collective-permute-done | bytes 131104 | tf_op jit(solution)/shard_map/ppermute | solution.py:637
  15.2 1.9 %collective-permute-start.2 = (bf16[16,4096]{1,0:T(8,128)(2,1)S(1)}, bf16[16,4096]{1,0:T(8,128)(2,1)S(1)}, u32[]{:S(2)}, u32[]{:S(2)}) collective-permute-start(bf16[16,4096]{1,0:T(8,128)(2,1)S(1)} %collective-permute-done.1.refs_6_), channel_id=1, source_target_pairs={{0,2},{1,5},{2,6},{3,1},{6,10},{7,3},{10,14},{11,7},{14,12},{15,11... | collective-permute-start | bytes 393224 | tf_op jit(solution)/shard_map/ppermute | solution.py:637
  17.3 0.8 %collective-permute-done.10.refs_8_ = bf16[16,4096]{1,0:T(8,128)(2,1)S(1)} collective-permute-done((bf16[16,4096]{1,0:T(8,128)(2,1)S(1)}, bf16[16,4096]{1,0:T(8,128)(2,1)S(1)}, u32[]{:S(2)}, u32[]{:S(2)}) %collective-permute-start.10) | collective-permute-done | bytes 131104 | tf_op jit(solution)/shard_map/ppermute | solution.py:637
  18.1 1.4 %collective-permute-start.12 = (bf16[16,4096]{1,0:T(8,128)(2,1)S(1)}, bf16[16,4096]{1,0:T(8,128)(2,1)S(1)}, u32[]{:S(2)}, u32[]{:S(2)}) collective-permute-start(bf16[16,4096]{1,0:T(8,128)(2,1)S(1)} %collective-permute-done.10.refs_8_), channel_id=1, source_target_pairs={{0,2},{1,5},{2,6},{3,1},{6,10},{7,3},{10,14},{11,7},{14,12},{15,11... | collective-permute-start | bytes 393224 | tf_op jit(solution)/shard_map/ppermute | solution.py:637
  19.5 0.3 collective-permute-done.11.refs_9_
  19.8 0.3 collective-permute-start.13
  20.1 0.8 %collective-permute-done.2.refs_10_ = bf16[16,4096]{1,0:T(8,128)(2,1)S(1)} collective-permute-done((bf16[16,4096]{1,0:T(8,128)(2,1)S(1)}, bf16[16,4096]{1,0:T(8,128)(2,1)S(1)}, u32[]{:S(2)}, u32[]{:S(2)}) %collective-permute-start.2) | collective-permute-done | bytes 131104 | tf_op jit(solution)/shard_map/ppermute | solution.py:637
  20.9 2.5 %collective-permute-start.3 = (bf16[16,4096]{1,0:T(8,128)(2,1)S(1)}, bf16[16,4096]{1,0:T(8,128)(2,1)S(1)}, u32[]{:S(2)}, u32[]{:S(2)}) collective-permute-start(bf16[16,4096]{1,0:T(8,128)(2,1)S(1)} %collective-permute-done.2.refs_10_), channel_id=1, source_target_pairs={{0,2},{1,5},{2,6},{3,1},{6,10},{7,3},{10,14},{11,7},{14,12},{15,11... | collective-permute-start | bytes 393224 | tf_op jit(solution)/shard_map/ppermute | solution.py:637
  23.5 1.2 %residue_left.1 = (bf16[128,4096]{1,0:T(8,128)(2,1)S(1)}, f32[64,448]{1,0:T(8,128)S(1)}) custom-call(f32[64,4096]{1,0:T(8,128)S(1)} %copy-done.2, bf16[448,4096]{1,0:T(8,128)(2,1)S(1)} %bitcast.7), custom_call_target="tpu_custom_call" | custom-call | flops 2529999872 | tf_op jit(solution)/shard_map/residue_left/pallas_call | solution.py:100
  24.8 1.2 %early_left.1 = (bf16[256,4096]{1,0:T(8,128)(2,1)S(1)}, bf16[256,448]{1,0:T(8,128)(2,1)S(1)}, f32[64,448]{1,0:T(8,128)S(1)}) custom-call(bf16[16,4096]{1,0:T(8,128)(2,1)S(1)} %get-tuple-element.43.first.refs_0_, bf16[16,4096]{1,0:T(8,128)(2,1)S(1)} %get-tuple-element.45.second.refs_1_, bf16[16,4096]{1,0:T(8,128)(2,1)S(1)} %collective-permute-done.refs_2_, ...), custom_call_target="tpu_custom_call" | custom-call | flops 2300000000 | tf_op jit(solution)/shard_map/early_left/pallas_call | solution.py:155
  26.0 0.3 collective-permute-done.3.first
  26.3 2.1 %collective-permute-done.7.second = bf16[16,4096]{1,0:T(8,128)(2,1)S(1)} collective-permute-done((bf16[16,4096]{1,0:T(8,128)(2,1)S(1)}, bf16[16,4096]{1,0:T(8,128)(2,1)S(1)}, u32[]{:S(2)}, u32[]{:S(2)}) %collective-permute-start.7) | collective-permute-done | bytes 131104 | tf_op jit(solution)/shard_map/ppermute | solution.py:637
  28.4 1.0 %late_left.1 = (bf16[256,4096]{1,0:T(8,128)(2,1)S(1)}, f32[64,448]{1,0:T(8,128)S(1)}) custom-call(bf16[16,4096]{1,0:T(8,128)(2,1)S(1)} %collective-permute-done.3.first, bf16[16,4096]{1,0:T(8,128)(2,1)S(1)} %collective-permute-done.7.second, bf16[128,4096]{1,0:T(8,128)(2,1)S(1)} %get-tuple-element.47.refs_14_.terms, ...), custom_call_target="tpu_custom_call", output_to_operand_aliasing={{0}: (5, {})} | custom-call | flops 1150000000 | tf_op jit(solution)/shard_map/late_left/pallas_call | solution.py:187
  29.4 1.3 %collective-permute-done.14.other_l = f32[64,448]{1,0:T(8,128)S(1)} collective-permute-done((f32[64,448]{1,0:T(8,128)S(1)}, f32[64,448]{1,0:T(8,128)S(1)}, u32[]{:S(2)}, u32[]{:S(2)}) %collective-permute-start.14) | collective-permute-done | bytes 114720 | tf_op jit(solution)/shard_map/ppermute | solution.py:646
  30.8 0.5 given_far.1
  31.5 0.6 near_terms.1
  32.1 0.4 collective-permute-start.16
  32.5 0.5 kept_far.1
  33.1 1.1 %collective-permute-start.18 = (f32[72,512]{1,0:T(8,128)S(1)}, f32[72,512]{1,0:T(8,128)S(1)}, u32[]{:S(2)}, u32[]{:S(2)}) collective-permute-start(f32[72,512]{1,0:T(8,128)S(1)} %begin_messages.1), channel_id=1, source_target_pairs={{0,8},{1,3},{2,10},{3,1},{4,12},{5,7},{6,14},{7,5},{8,0},{9,11},{1... | collective-permute-start | bytes 442376 | tf_op jit(solution)/shard_map/ppermute | solution.py:661
  34.3 2.9 %collective-permute-start.19 = (f32[72,512]{1,0:T(8,128)S(1)}, f32[72,512]{1,0:T(8,128)S(1)}, u32[]{:S(2)}, u32[]{:S(2)}) collective-permute-start(f32[72,512]{1,0:T(8,128)S(1)} %get-tuple-element.68), channel_id=1, source_target_pairs={{0,10},{1,5},{2,8},{3,7},{4,14},{5,1},{6,12},{7,3},{8,2},{9,13},{1... | collective-permute-start | bytes 442376 | tf_op jit(solution)/shard_map/ppermute | solution.py:661
  37.1 0.7 %collective-permute-start.17 = (f32[72,512]{1,0:T(8,128)S(1)}, f32[72,512]{1,0:T(8,128)S(1)}, u32[]{:S(2)}, u32[]{:S(2)}) collective-permute-start(f32[72,512]{1,0:T(8,128)S(1)} %get-tuple-element.65), channel_id=1, source_target_pairs={{1,7},{3,5},{5,3},{7,1},{9,15},{11,13},{13,11},{15,9},{17,23},{19,... | collective-permute-start | bytes 442376 | tf_op jit(solution)/shard_map/ppermute | solution.py:661
  37.8 2.4 %collective-permute-done.18.passed.refs_0_ = f32[72,512]{1,0:T(8,128)S(1)} collective-permute-done((f32[72,512]{1,0:T(8,128)S(1)}, f32[72,512]{1,0:T(8,128)S(1)}, u32[]{:S(2)}, u32[]{:S(2)}) %collective-permute-start.18) | collective-permute-done | bytes 147488 | tf_op jit(solution)/shard_map/ppermute | solution.py:661
  40.2 1.1 %collective-permute-start.20 = (f32[72,512]{1,0:T(8,128)S(1)}, f32[72,512]{1,0:T(8,128)S(1)}, u32[]{:S(2)}, u32[]{:S(2)}) collective-permute-start(f32[72,512]{1,0:T(8,128)S(1)} %crossing.1), channel_id=1, source_target_pairs={{0,2},{1,13},{2,0},{3,15},{4,6},{5,9},{6,4},{7,11},{8,10},{9,5},{1... | collective-permute-start | bytes 442376 | tf_op jit(solution)/shard_map/ppermute | solution.py:661
  41.4 1.1 %merged.1 = f32[448,4096]{1,0:T(8,128)S(1)} custom-call(bf16[448,256]{1,0:T(8,128)(2,1)S(1)} %bitcast.14, bf16[448,4096]{1,0:T(8,128)(2,1)S(1)} %bitcast.11, bf16[256,4096]{1,0:T(8,128)(2,1)S(1)} %get-tuple-element.66.tokens), custom_call_target="tpu_custom_call" | custom-call | flops 57500000 | tf_op jit(solution)/shard_map/merged/pallas_call | solution.py:310
  42.5 2.7 %collective-permute-done.19.refs_1_ = f32[72,512]{1,0:T(8,128)S(1)} collective-permute-done((f32[72,512]{1,0:T(8,128)S(1)}, f32[72,512]{1,0:T(8,128)S(1)}, u32[]{:S(2)}, u32[]{:S(2)}) %collective-permute-start.19) | collective-permute-done | bytes 147488 | tf_op jit(solution)/shard_map/ppermute | solution.py:661
  45.2 0.5 collective-permute-done.20.refs_2_
  45.9 1.4 %collective-permute-done.21.other = f32[72,512]{1,0:T(8,128)S(1)} collective-permute-done((f32[72,512]{1,0:T(8,128)S(1)}, f32[72,512]{1,0:T(8,128)S(1)}, u32[]{:S(2)}, u32[]{:S(2)}) %collective-permute-start.21) | collective-permute-done | bytes 147488 | tf_op jit(solution)/shard_map/ppermute | solution.py:646
  47.4 2.7 %collective-permute-start.23 = (f32[64,512]{1,0:T(8,128)S(1)}, f32[64,512]{1,0:T(8,128)S(1)}, u32[]{:S(2)}, u32[]{:S(2)}) collective-permute-start(f32[64,512]{1,0:T(8,128)S(1)} %get-tuple-element.70.share.here), channel_id=1, source_target_pairs={{0,2},{1,13},{2,0},{3,15},{4,6},{5,9},{6,4},{7,11},{8,10},{9,5},{1... | collective-permute-start | bytes 393224 | tf_op jit(solution)/shard_map/ppermute | solution.py:661
  50.0 1.3 %collective-permute-start.24 = (f32[64,512]{1,0:T(8,128)S(1)}, f32[64,512]{1,0:T(8,128)S(1)}, u32[]{:S(2)}, u32[]{:S(2)}) collective-permute-start(f32[64,512]{1,0:T(8,128)S(1)} %get-tuple-element.70.share.here), channel_id=1, source_target_pairs={{0,10},{1,5},{2,8},{3,7},{4,14},{5,1},{6,12},{7,3},{8,2},{9,13},{1... | collective-permute-start | bytes 393224 | tf_op jit(solution)/shard_map/ppermute | solution.py:661
  51.3 0.7 %collective-permute-start.22 = (f32[64,512]{1,0:T(8,128)S(1)}, f32[64,512]{1,0:T(8,128)S(1)}, u32[]{:S(2)}, u32[]{:S(2)}) collective-permute-start(f32[64,512]{1,0:T(8,128)S(1)} %get-tuple-element.70.share.here), channel_id=1, source_target_pairs={{1,7},{3,5},{5,3},{7,1},{9,15},{11,13},{13,11},{15,9},{17,23},{19,... | collective-permute-start | bytes 393224 | tf_op jit(solution)/shard_map/ppermute | solution.py:661
  51.9 1.0 %collective-permute-done.23.refs_0_.there = f32[64,512]{1,0:T(8,128)S(1)} collective-permute-done((f32[64,512]{1,0:T(8,128)S(1)}, f32[64,512]{1,0:T(8,128)S(1)}, u32[]{:S(2)}, u32[]{:S(2)}) %collective-permute-start.23) | collective-permute-done | bytes 131104 | tf_op jit(solution)/shard_map/ppermute | solution.py:661
  53.0 1.9 %collective-permute-start.25 = (f32[64,512]{1,0:T(8,128)S(1)}, f32[64,512]{1,0:T(8,128)S(1)}, u32[]{:S(2)}, u32[]{:S(2)}) collective-permute-start(f32[64,512]{1,0:T(8,128)S(1)} %by_core.1), channel_id=1, source_target_pairs={{0,8},{1,3},{2,10},{3,1},{4,12},{5,7},{6,14},{7,5},{8,0},{9,11},{1... | collective-permute-start | bytes 393224 | tf_op jit(solution)/shard_map/ppermute | solution.py:661
  54.9 1.8 %cholesky_inverse.1.inverse = f32[64,64]{1,0:T(8,128)S(1)} custom-call(f32[64,64]{1,0:T(8,128)S(1)} %get-tuple-element.71.gram), custom_call_target="tpu_custom_call" | custom-call | flops 5750000128 | tf_op jit(solution)/shard_map/cholesky_inverse/pallas_call | solution.py:518
  56.6 0.8 %last_operand.1.lhs = bf16[512,256]{1,0:T(8,128)(2,1)S(1)} custom-call(f32[64,64]{1,0:T(8,128)S(1)} %cholesky_inverse.1.inverse, f32[64,448]{1,0:T(8,128)S(1)} %get-tuple-element.56.left_sum), custom_call_target="tpu_custom_call" | custom-call | flops 57500000 | tf_op jit(solution)/shard_map/last_operand/pallas_call | solution.py:549
  57.4 0.9 %collective-permute-done.24.refs_1_ = f32[64,512]{1,0:T(8,128)S(1)} collective-permute-done((f32[64,512]{1,0:T(8,128)S(1)}, f32[64,512]{1,0:T(8,128)S(1)}, u32[]{:S(2)}, u32[]{:S(2)}) %collective-permute-start.24) | collective-permute-done | bytes 131104 | tf_op jit(solution)/shard_map/ppermute | solution.py:661
  58.4 1.5 %finish.3 = (bf16[448,4096]{1,0:T(8,128)(2,1)}, f32[64,4096]{1,0:T(8,128)}) custom-call(f32[3,64,512]{2,1,0:T(8,128)S(1)} %joined.1.shares, bf16[512,256]{1,0:T(8,128)(2,1)S(1)} %last_operand.1.lhs, f32[448,4096]{1,0:T(8,128)S(1)} %merged.1), custom_call_target="tpu_custom_call" | custom-call | flops 57500000 | tf_op jit(solution)/shard_map/finish/pallas_call | solution.py:588
  59.9 0.4 collective-permute-done.25
  60.4 0.3 collective-permute-start.26
  60.7 1.1 %finish.4 = (bf16[448,4096]{1,0:T(8,128)(2,1)}, f32[64,4096]{1,0:T(8,128)}) custom-call(f32[1,64,512]{2,1,0:T(8,128)S(1)} %bitcast.16, bf16[512,256]{1,0:T(8,128)(2,1)S(1)} %last_operand.1.lhs, f32[448,4096]{1,0:T(8,128)S(1)} %merged.1, bf16[448,4096]{1,0:T(8,128)(2,1)} %get-tuple-element.78.refs_0_, ...), custom_call_target="tpu_custom_call", output_to_operand_aliasing={{0}: (3, {}), {1}: (4, {})} | custom-call | flops 57500000 | tf_op jit(solution)/shard_map/finish/pallas_call | solution.py:588
  61.8 0.5 collective-permute-done.26.shares
  62.3 1.7 %finish.5 = (bf16[448,4096]{1,0:T(8,128)(2,1)}, f32[64,4096]{1,0:T(8,128)}) custom-call(f32[4,64,512]{2,1,0:T(8,128)S(1)} %collective-permute-done.26.shares, bf16[512,256]{1,0:T(8,128)(2,1)S(1)} %last_operand.1.lhs, f32[448,4096]{1,0:T(8,128)S(1)} %merged.1, ...), custom_call_target="tpu_custom_call", output_to_operand_aliasing={{0}: (3, {}), {1}: (4, {})} | custom-call | flops 57500000 | tf_op jit(solution)/shard_map/finish/pallas_call | solution.py:588
  (36 shorter events, 1.6 us)
Async XLA Ops:
  0.6 1.0 %copy-start.3 = (bf16[1,32,4096]{2,1,0:T(8,128)(2,1)S(1)}, bf16[1,32,4096]{2,1,0:T(8,128)(2,1)}, u32[]{:S(2)}) copy-start(bf16[1,32,4096]{2,1,0:T(8,128)(2,1)} %param.4) | copy-start | bytes 786436
  1.6 6.9 %collective-permute-start = (bf16[16,4096]{1,0:T(8,128)(2,1)S(1)}, bf16[16,4096]{1,0:T(8,128)(2,1)S(1)}, u32[]{:S(2)}, u32[]{:S(2)}) collective-permute-start(bf16[16,4096]{1,0:T(8,128)(2,1)S(1)} %get-tuple-element.43.first.refs_0_), channel_id=1, source_target_pairs={{0,2},{1,5},{2,6},{3,1},{6,10},{7,3},{10,14},{11,7},{14,12},{15,11... | collective-permute-start | bytes 393224 | tf_op jit(solution)/shard_map/ppermute | solution.py:637
  4.6 18.8 %copy-start = (bf16[1,448,4096]{2,1,0:T(8,128)(2,1)S(1)}, bf16[1,448,4096]{2,1,0:T(8,128)(2,1)}, u32[]{:S(2)}) copy-start(bf16[1,448,4096]{2,1,0:T(8,128)(2,1)} %param.6) | copy-start | bytes 11010052
  4.6 18.8 %copy-start.2 = (f32[64,4096]{1,0:T(8,128)S(1)}, f32[64,4096]{1,0:T(8,128)}, u32[]{:S(2)}) copy-start(f32[64,4096]{1,0:T(8,128)} %right) | copy-start | bytes 3145732
  4.6 6.4 %collective-permute-start.4 = (bf16[16,4096]{1,0:T(8,128)(2,1)S(1)}, bf16[16,4096]{1,0:T(8,128)(2,1)S(1)}, u32[]{:S(2)}, u32[]{:S(2)}) collective-permute-start(bf16[16,4096]{1,0:T(8,128)(2,1)S(1)} %get-tuple-element.45.second.refs_1_), channel_id=1, source_target_pairs={{0,4},{1,3},{2,0},{3,7},{6,2},{7,11},{10,6},{11,15},{14,10},{15,13... | collective-permute-start | bytes 393224 | tf_op jit(solution)/shard_map/ppermute | solution.py:637
  4.8 6.5 %collective-permute-start.8 = (bf16[16,4096]{1,0:T(8,128)(2,1)S(1)}, bf16[16,4096]{1,0:T(8,128)(2,1)S(1)}, u32[]{:S(2)}, u32[]{:S(2)}) collective-permute-start(bf16[16,4096]{1,0:T(8,128)(2,1)S(1)} %get-tuple-element.48), channel_id=1, source_target_pairs={{0,2},{1,5},{2,6},{3,1},{6,10},{7,3},{10,14},{11,7},{14,12},{15,11... | collective-permute-start | bytes 393224 | tf_op jit(solution)/shard_map/ppermute | solution.py:637
  6.7 6.3 %collective-permute-start.9 = (bf16[16,4096]{1,0:T(8,128)(2,1)S(1)}, bf16[16,4096]{1,0:T(8,128)(2,1)S(1)}, u32[]{:S(2)}, u32[]{:S(2)}) collective-permute-start(bf16[16,4096]{1,0:T(8,128)(2,1)S(1)} %get-tuple-element.49), channel_id=1, source_target_pairs={{0,4},{1,3},{2,0},{3,7},{6,2},{7,11},{10,6},{11,15},{14,10},{15,13... | collective-permute-start | bytes 393224 | tf_op jit(solution)/shard_map/ppermute | solution.py:637
  8.5 6.7 %collective-permute-start.1 = (bf16[16,4096]{1,0:T(8,128)(2,1)S(1)}, bf16[16,4096]{1,0:T(8,128)(2,1)S(1)}, u32[]{:S(2)}, u32[]{:S(2)}) collective-permute-start(bf16[16,4096]{1,0:T(8,128)(2,1)S(1)} %collective-permute-done.refs_2_), channel_id=1, source_target_pairs={{0,2},{1,5},{2,6},{3,1},{6,10},{7,3},{10,14},{11,7},{14,12},{15,11... | collective-permute-start | bytes 393224 | tf_op jit(solution)/shard_map/ppermute | solution.py:637
  11.0 6.2 %collective-permute-start.5 = (bf16[16,4096]{1,0:T(8,128)(2,1)S(1)}, bf16[16,4096]{1,0:T(8,128)(2,1)S(1)}, u32[]{:S(2)}, u32[]{:S(2)}) collective-permute-start(bf16[16,4096]{1,0:T(8,128)(2,1)S(1)} %collective-permute-done.4.refs_3_), channel_id=1, source_target_pairs={{0,4},{1,3},{2,0},{3,7},{6,2},{7,11},{10,6},{11,15},{14,10},{15,13... | collective-permute-start | bytes 393224 | tf_op jit(solution)/shard_map/ppermute | solution.py:637
  11.3 6.8 %collective-permute-start.10 = (bf16[16,4096]{1,0:T(8,128)(2,1)S(1)}, bf16[16,4096]{1,0:T(8,128)(2,1)S(1)}, u32[]{:S(2)}, u32[]{:S(2)}) collective-permute-start(bf16[16,4096]{1,0:T(8,128)(2,1)S(1)} %collective-permute-done.8.refs_4_), channel_id=1, source_target_pairs={{0,2},{1,5},{2,6},{3,1},{6,10},{7,3},{10,14},{11,7},{14,12},{15,11... | collective-permute-start | bytes 393224 | tf_op jit(solution)/shard_map/ppermute | solution.py:637
  13.0 6.8 %collective-permute-start.11 = (bf16[16,4096]{1,0:T(8,128)(2,1)S(1)}, bf16[16,4096]{1,0:T(8,128)(2,1)S(1)}, u32[]{:S(2)}, u32[]{:S(2)}) collective-permute-start(bf16[16,4096]{1,0:T(8,128)(2,1)S(1)} %collective-permute-done.9.refs_5_), channel_id=1, source_target_pairs={{0,4},{1,3},{2,0},{3,7},{6,2},{7,11},{10,6},{11,15},{14,10},{15,13... | collective-permute-start | bytes 393224 | tf_op jit(solution)/shard_map/ppermute | solution.py:637
  15.2 5.7 %collective-permute-start.2 = (bf16[16,4096]{1,0:T(8,128)(2,1)S(1)}, bf16[16,4096]{1,0:T(8,128)(2,1)S(1)}, u32[]{:S(2)}, u32[]{:S(2)}) collective-permute-start(bf16[16,4096]{1,0:T(8,128)(2,1)S(1)} %collective-permute-done.1.refs_6_), channel_id=1, source_target_pairs={{0,2},{1,5},{2,6},{3,1},{6,10},{7,3},{10,14},{11,7},{14,12},{15,11... | collective-permute-start | bytes 393224 | tf_op jit(solution)/shard_map/ppermute | solution.py:637
  17.2 6.2 %collective-permute-start.6 = (bf16[16,4096]{1,0:T(8,128)(2,1)S(1)}, bf16[16,4096]{1,0:T(8,128)(2,1)S(1)}, u32[]{:S(2)}, u32[]{:S(2)}) collective-permute-start(bf16[16,4096]{1,0:T(8,128)(2,1)S(1)} %collective-permute-done.5.refs_7_), channel_id=1, source_target_pairs={{0,4},{1,3},{2,0},{3,7},{6,2},{7,11},{10,6},{11,15},{14,10},{15,13... | collective-permute-start | bytes 393224 | tf_op jit(solution)/shard_map/ppermute | solution.py:637
  18.1 6.6 %collective-permute-start.12 = (bf16[16,4096]{1,0:T(8,128)(2,1)S(1)}, bf16[16,4096]{1,0:T(8,128)(2,1)S(1)}, u32[]{:S(2)}, u32[]{:S(2)}) collective-permute-start(bf16[16,4096]{1,0:T(8,128)(2,1)S(1)} %collective-permute-done.10.refs_8_), channel_id=1, source_target_pairs={{0,2},{1,5},{2,6},{3,1},{6,10},{7,3},{10,14},{11,7},{14,12},{15,11... | collective-permute-start | bytes 393224 | tf_op jit(solution)/shard_map/ppermute | solution.py:637
  19.8 5.0 %collective-permute-start.13 = (bf16[16,4096]{1,0:T(8,128)(2,1)S(1)}, bf16[16,4096]{1,0:T(8,128)(2,1)S(1)}, u32[]{:S(2)}, u32[]{:S(2)}) collective-permute-start(bf16[16,4096]{1,0:T(8,128)(2,1)S(1)} %collective-permute-done.11.refs_9_), channel_id=1, source_target_pairs={{0,4},{1,3},{2,0},{3,7},{6,2},{7,11},{10,6},{11,15},{14,10},{15,13... | collective-permute-start | bytes 393224 | tf_op jit(solution)/shard_map/ppermute | solution.py:637
  20.9 5.4 %collective-permute-start.3 = (bf16[16,4096]{1,0:T(8,128)(2,1)S(1)}, bf16[16,4096]{1,0:T(8,128)(2,1)S(1)}, u32[]{:S(2)}, u32[]{:S(2)}) collective-permute-start(bf16[16,4096]{1,0:T(8,128)(2,1)S(1)} %collective-permute-done.2.refs_10_), channel_id=1, source_target_pairs={{0,2},{1,5},{2,6},{3,1},{6,10},{7,3},{10,14},{11,7},{14,12},{15,11... | collective-permute-start | bytes 393224 | tf_op jit(solution)/shard_map/ppermute | solution.py:637
  23.4 5.0 %collective-permute-start.7 = (bf16[16,4096]{1,0:T(8,128)(2,1)S(1)}, bf16[16,4096]{1,0:T(8,128)(2,1)S(1)}, u32[]{:S(2)}, u32[]{:S(2)}) collective-permute-start(bf16[16,4096]{1,0:T(8,128)(2,1)S(1)} %collective-permute-done.6.refs_11_), channel_id=1, source_target_pairs={{0,4},{1,3},{2,0},{3,7},{6,2},{7,11},{10,6},{11,15},{14,10},{15,13... | collective-permute-start | bytes 393224 | tf_op jit(solution)/shard_map/ppermute | solution.py:637
  23.4 1.3 %copy-start.1 = (bf16[1,256,448]{1,2,0:T(8,128)(2,1)S(1)}, bf16[1,256,448]{1,2,0:T(8,128)(2,1)}, u32[]{:S(2)}) copy-start(bf16[1,256,448]{1,2,0:T(8,128)(2,1)} %param.5) | copy-start | bytes 688132
  29.3 1.4 %collective-permute-start.14 = (f32[64,448]{1,0:T(8,128)S(1)}, f32[64,448]{1,0:T(8,128)S(1)}, u32[]{:S(2)}, u32[]{:S(2)}) collective-permute-start(f32[64,448]{1,0:T(8,128)S(1)} %get-tuple-element.54.here_l), channel_id=1, source_target_pairs={{0,1},{1,0},{2,3},{3,2},{4,5},{5,4},{6,7},{7,6},{8,9},{9,8},{10,11... | collective-permute-start | bytes 344072 | tf_op jit(solution)/shard_map/ppermute | solution.py:646
  31.3 1.7 %collective-permute-start.15 = (f32[2,64,512]{2,1,0:T(8,128)S(1)}, f32[2,64,512]{2,1,0:T(8,128)S(1)}, u32[]{:S(2)}, u32[]{:S(2)}) collective-permute-start(f32[2,64,512]{2,1,0:T(8,128)S(1)} %get-tuple-element.60), channel_id=1, source_target_pairs={{0,1},{1,0},{2,3},{3,2},{4,5},{5,4},{6,7},{7,6},{8,9},{9,8},{10,11... | collective-permute-start | bytes 786440 | tf_op jit(solution)/shard_map/ppermute | solution.py:646
  32.1 2.1 %collective-permute-start.16 = (f32[2,64,512]{2,1,0:T(8,128)S(1)}, f32[2,64,512]{2,1,0:T(8,128)S(1)}, u32[]{:S(2)}, u32[]{:S(2)}) collective-permute-start(f32[2,64,512]{2,1,0:T(8,128)S(1)} %get-tuple-element.62), channel_id=1, source_target_pairs={{0,1},{1,0},{2,3},{3,2},{4,5},{5,4},{6,7},{7,6},{8,9},{9,8},{10,11... | collective-permute-start | bytes 786440 | tf_op jit(solution)/shard_map/ppermute | solution.py:646
  33.1 7.1 %collective-permute-start.18 = (f32[72,512]{1,0:T(8,128)S(1)}, f32[72,512]{1,0:T(8,128)S(1)}, u32[]{:S(2)}, u32[]{:S(2)}) collective-permute-start(f32[72,512]{1,0:T(8,128)S(1)} %begin_messages.1), channel_id=1, source_target_pairs={{0,8},{1,3},{2,10},{3,1},{4,12},{5,7},{6,14},{7,5},{8,0},{9,11},{1... | collective-permute-start | bytes 442376 | tf_op jit(solution)/shard_map/ppermute | solution.py:661
  34.3 11.0 %collective-permute-start.19 = (f32[72,512]{1,0:T(8,128)S(1)}, f32[72,512]{1,0:T(8,128)S(1)}, u32[]{:S(2)}, u32[]{:S(2)}) collective-permute-start(f32[72,512]{1,0:T(8,128)S(1)} %get-tuple-element.68), channel_id=1, source_target_pairs={{0,10},{1,5},{2,8},{3,7},{4,14},{5,1},{6,12},{7,3},{8,2},{9,13},{1... | collective-permute-start | bytes 442376 | tf_op jit(solution)/shard_map/ppermute | solution.py:661
  37.1 5.4 %collective-permute-start.17 = (f32[72,512]{1,0:T(8,128)S(1)}, f32[72,512]{1,0:T(8,128)S(1)}, u32[]{:S(2)}, u32[]{:S(2)}) collective-permute-start(f32[72,512]{1,0:T(8,128)S(1)} %get-tuple-element.65), channel_id=1, source_target_pairs={{1,7},{3,5},{5,3},{7,1},{9,15},{11,13},{13,11},{15,9},{17,23},{19,... | collective-permute-start | bytes 442376 | tf_op jit(solution)/shard_map/ppermute | solution.py:661
  40.2 5.6 %collective-permute-start.20 = (f32[72,512]{1,0:T(8,128)S(1)}, f32[72,512]{1,0:T(8,128)S(1)}, u32[]{:S(2)}, u32[]{:S(2)}) collective-permute-start(f32[72,512]{1,0:T(8,128)S(1)} %crossing.1), channel_id=1, source_target_pairs={{0,2},{1,13},{2,0},{3,15},{4,6},{5,9},{6,4},{7,11},{8,10},{9,5},{1... | collective-permute-start | bytes 442376 | tf_op jit(solution)/shard_map/ppermute | solution.py:661
  45.8 1.4 %collective-permute-start.21 = (f32[72,512]{1,0:T(8,128)S(1)}, f32[72,512]{1,0:T(8,128)S(1)}, u32[]{:S(2)}, u32[]{:S(2)}) collective-permute-start(f32[72,512]{1,0:T(8,128)S(1)} %core_sum.1.here), channel_id=1, source_target_pairs={{0,1},{1,0},{2,3},{3,2},{4,5},{5,4},{6,7},{7,6},{8,9},{9,8},{10,11... | collective-permute-start | bytes 442376 | tf_op jit(solution)/shard_map/ppermute | solution.py:646
  47.4 5.6 %collective-permute-start.23 = (f32[64,512]{1,0:T(8,128)S(1)}, f32[64,512]{1,0:T(8,128)S(1)}, u32[]{:S(2)}, u32[]{:S(2)}) collective-permute-start(f32[64,512]{1,0:T(8,128)S(1)} %get-tuple-element.70.share.here), channel_id=1, source_target_pairs={{0,2},{1,13},{2,0},{3,15},{4,6},{5,9},{6,4},{7,11},{8,10},{9,5},{1... | collective-permute-start | bytes 393224 | tf_op jit(solution)/shard_map/ppermute | solution.py:661
  50.0 8.3 %collective-permute-start.24 = (f32[64,512]{1,0:T(8,128)S(1)}, f32[64,512]{1,0:T(8,128)S(1)}, u32[]{:S(2)}, u32[]{:S(2)}) collective-permute-start(f32[64,512]{1,0:T(8,128)S(1)} %get-tuple-element.70.share.here), channel_id=1, source_target_pairs={{0,10},{1,5},{2,8},{3,7},{4,14},{5,1},{6,12},{7,3},{8,2},{9,13},{1... | collective-permute-start | bytes 393224 | tf_op jit(solution)/shard_map/ppermute | solution.py:661
  51.3 7.1 %collective-permute-start.22 = (f32[64,512]{1,0:T(8,128)S(1)}, f32[64,512]{1,0:T(8,128)S(1)}, u32[]{:S(2)}, u32[]{:S(2)}) collective-permute-start(f32[64,512]{1,0:T(8,128)S(1)} %get-tuple-element.70.share.here), channel_id=1, source_target_pairs={{1,7},{3,5},{5,3},{7,1},{9,15},{11,13},{13,11},{15,9},{17,23},{19,... | collective-permute-start | bytes 393224 | tf_op jit(solution)/shard_map/ppermute | solution.py:661
  53.0 7.3 %collective-permute-start.25 = (f32[64,512]{1,0:T(8,128)S(1)}, f32[64,512]{1,0:T(8,128)S(1)}, u32[]{:S(2)}, u32[]{:S(2)}) collective-permute-start(f32[64,512]{1,0:T(8,128)S(1)} %by_core.1), channel_id=1, source_target_pairs={{0,8},{1,3},{2,10},{3,1},{4,12},{5,7},{6,14},{7,5},{8,0},{9,11},{1... | collective-permute-start | bytes 393224 | tf_op jit(solution)/shard_map/ppermute | solution.py:661
  60.4 2.0 %collective-permute-start.26 = (f32[4,64,512]{2,1,0:T(8,128)S(1)}, f32[4,64,512]{2,1,0:T(8,128)S(1)}, u32[]{:S(2)}, u32[]{:S(2)}) collective-permute-start(f32[4,64,512]{2,1,0:T(8,128)S(1)} %pad_maximum_fusion), channel_id=1, source_target_pairs={{0,1},{1,0},{2,3},{3,2},{4,5},{5,4},{6,7},{7,6},{8,9},{9,8},{10,11... | collective-permute-start | bytes 1572872 | tf_op jit(solution)/shard_map/ppermute | solution.py:646

commit v12 on v10

--- a/solution.py
+++ b/solution.py
@@ -167,33 +167,49 @@
     )(*operands)
 
 
-def late_kernel(origins, first, second, terms, hidden, early_t, _, tokens, left_t):
+def late_kernel(origins, first, second, terms, hidden, early_t, left_t):
     size = first.shape[0]
-    seen = []
-    for origin, piece in zip(origins, (first, second)):
-        rows = piece_rows(origin, size)
-        tokens[rows, :] = piece[...]
-        seen.append(hidden[rows, :])
+    seen = [hidden[piece_rows(origin, size), :] for origin in origins]
     projected = fold2(nt(terms[...], jnp.concatenate([first[...], second[...]], axis=0)))
     stacked = jnp.concatenate(split2(projected), axis=0)
     left_t[...] = early_t[...] + fold2(nn(stacked, jnp.concatenate(seen, axis=0)))
 
 
-def late_left(origins, pieces, terms, hidden, early_t, tokens):
-    operands = [*pieces, terms, hidden, early_t, tokens]
+def late_left(origins, pieces, terms, hidden, early_t):
+    operands = [*pieces, terms, hidden, early_t]
     return pl.pallas_call(
         functools.partial(late_kernel, origins),
         in_specs=[pl.BlockSpec(memory_space=pltpu.VMEM)] * len(operands),
-        out_specs=[pl.BlockSpec(memory_space=pltpu.VMEM)] * 2,
-        out_shape=[
-            jax.ShapeDtypeStruct(tokens.shape, BF16),
-            jax.ShapeDtypeStruct(early_t.shape, F32),
-        ],
-        input_output_aliases={len(operands) - 1: 0},
+        out_specs=pl.BlockSpec(memory_space=pltpu.VMEM),
+        out_shape=jax.ShapeDtypeStruct(early_t.shape, F32),
         compiler_params=params(),
         cost_estimate=cost(1.0),
         name="late_left",
     )(*operands)
+
+
+def insert_kernel(origins, first, second, _, tokens, sems):
+    copies = []
+    for index, (origin, piece) in enumerate(zip(origins, (first, second))):
+        rows = piece_rows(origin, piece.shape[0])
+        copies.append(pltpu.make_async_copy(piece, tokens.at[rows, :], sems.at[index]))
+        copies[-1].start()
+    for copy in copies:
+        copy.wait()
+
+
+def inserted(origins, pieces, tokens):
+    return pl.pallas_call(
+        functools.partial(insert_kernel, origins),
+        in_specs=[pl.BlockSpec(memory_space=pltpu.VMEM)] * 2 + [pl.BlockSpec(memory_space=pl.ANY)],
+        out_specs=pl.BlockSpec(memory_space=pl.ANY),
+        out_shape=jax.ShapeDtypeStruct(tokens.shape, BF16),
+        input_output_aliases={2: 0},
+        scratch_shapes=[pltpu.SemaphoreType.DMA((2,))],
+        compiler_params=params(),
+        cost_estimate=cost(0.4),
+        name="inserted",
+    )(*pieces, tokens)
 
 
 def core_of(place):
@@ -658,7 +674,9 @@
     pieces, origins, right_factor = ring_gather(shard, chips, right_factor)
     terms, residue_t = residue_left(right_factor, residue)
     tokens, hidden_rows, left_t = early_left(origins, pieces[:-2], terms, residue_t, hidden_t)
-    tokens, left_t = late_left(origins[-2:], pieces[-2:], terms, hidden_rows, left_t, tokens)
+    left_t = late_left(origins[-2:], pieces[-2:], terms, hidden_rows, left_t)
+    left_t, tokens = lax.optimization_barrier((left_t, tokens))
+    tokens = inserted(origins[-2:], pieces[-2:], tokens)
     give, left_sum, lhs, rhs = given_far(left_t, swap(left_t), hidden_t, residue, tokens, chips)
     got = swap(give)
     keep, gram = kept_far(left_sum, lhs, rhs, residue, tokens, chips)

time: 63.9 us -> 63.9 us (level)
  no operation moved by 1% of the time
where the time goes in v12:
time: 63.9 us; the launch traced here: 63.7 us
  starting transfers between devices  30 us (47%)
  waiting for transfers between devices  18.3 us (29%)
  Pallas kernels  13.5 us (21%)
  local copies, waits for them, and re-layouts  0.96 us (2%)
  between operations  0.84 us (1%)
    ppermute x14, starting transfers between devices, ring_gather(): going[way, half] = lax.ppermute(going[way, half], ('tp', 'dp'), pairs(way))  16.7 us
    ppermute x8, starting transfers between devices, send(): return lax.ppermute(value, ('tp', 'dp'), pairs)  12.2 us
    ppermute x8, waiting for transfers between devices, send(): return lax.ppermute(value, ('tp', 'dp'), pairs)  7.96 us
    ppermute x14, waiting for transfers between devices, ring_gather(): going[way, half] = lax.ppermute(going[way, half], ('tp', 'dp'), pairs(way))  7.51 us
    pallas_call x3, Pallas kernels, finish(): pl.pallas_call(functools.partial(final_kernel, indices, side), in_specs=[...  4.38 us
    ppermute x5, waiting for transfers between devices, swap(): return lax.ppermute(value, 'dp', [(0, 1), (1, 0)])  2.85 us
    pallas_call x1, Pallas kernels, cholesky_inverse(): pl.pallas_call(inverse_kernel, in_specs=[pl.BlockSpec(memory_space=pltpu....  1.77 us
  transfers between devices with their start and end apart: 27, of which 19 were waited for; matrix products, arithmetic and copies ran while one was open for 0% of the time, Pallas kernels for 16%

profile of v12, /device:TPU:0, one launch (start us, length us, event | category | flops | bytes accessed | tf_op | source)
XLA Modules:
  0.0 63.7 jit_solution(7828138293423754656)
XLA Ops:
  0.6 0.9 %copy-done.3 = bf16[1,32,4096]{2,1,0:T(8,128)(2,1)S(1)} copy-done((bf16[1,32,4096]{2,1,0:T(8,128)(2,1)S(1)}, bf16[1,32,4096]{2,1,0:T(8,128)(2,1)}, u32[]{:S(2)}) %copy-start.3) | copy-done | bytes 262168
  1.6 3.0 %collective-permute-start = (bf16[16,4096]{1,0:T(8,128)(2,1)S(1)}, bf16[16,4096]{1,0:T(8,128)(2,1)S(1)}, u32[]{:S(2)}, u32[]{:S(2)}) collective-permute-start(bf16[16,4096]{1,0:T(8,128)(2,1)S(1)} %get-tuple-element.43.first.refs_0_), channel_id=1, source_target_pairs={{0,2},{1,5},{2,6},{3,1},{6,10},{7,3},{10,14},{11,7},{14,12},{15,11... | collective-permute-start | bytes 393224 | tf_op jit(solution)/shard_map/ppermute | solution.py:648
  4.8 1.9 %collective-permute-start.8 = (bf16[16,4096]{1,0:T(8,128)(2,1)S(1)}, bf16[16,4096]{1,0:T(8,128)(2,1)S(1)}, u32[]{:S(2)}, u32[]{:S(2)}) collective-permute-start(bf16[16,4096]{1,0:T(8,128)(2,1)S(1)} %get-tuple-element.48), channel_id=1, source_target_pairs={{0,2},{1,5},{2,6},{3,1},{6,10},{7,3},{10,14},{11,7},{14,12},{15,11... | collective-permute-start | bytes 393224 | tf_op jit(solution)/shard_map/ppermute | solution.py:648
  6.9 1.6 %collective-permute-done.refs_2_ = bf16[16,4096]{1,0:T(8,128)(2,1)S(1)} collective-permute-done((bf16[16,4096]{1,0:T(8,128)(2,1)S(1)}, bf16[16,4096]{1,0:T(8,128)(2,1)S(1)}, u32[]{:S(2)}, u32[]{:S(2)}) %collective-permute-start) | collective-permute-done | bytes 131104 | tf_op jit(solution)/shard_map/ppermute | solution.py:648
  8.5 2.5 %collective-permute-start.1 = (bf16[16,4096]{1,0:T(8,128)(2,1)S(1)}, bf16[16,4096]{1,0:T(8,128)(2,1)S(1)}, u32[]{:S(2)}, u32[]{:S(2)}) collective-permute-start(bf16[16,4096]{1,0:T(8,128)(2,1)S(1)} %collective-permute-done.refs_2_), channel_id=1, source_target_pairs={{0,2},{1,5},{2,6},{3,1},{6,10},{7,3},{10,14},{11,7},{14,12},{15,11... | collective-permute-start | bytes 393224 | tf_op jit(solution)/shard_map/ppermute | solution.py:648
  11.3 1.8 %collective-permute-start.10 = (bf16[16,4096]{1,0:T(8,128)(2,1)S(1)}, bf16[16,4096]{1,0:T(8,128)(2,1)S(1)}, u32[]{:S(2)}, u32[]{:S(2)}) collective-permute-start(bf16[16,4096]{1,0:T(8,128)(2,1)S(1)} %collective-permute-done.8.refs_4_), channel_id=1, source_target_pairs={{0,2},{1,5},{2,6},{3,1},{6,10},{7,3},{10,14},{11,7},{14,12},{15,11... | collective-permute-start | bytes 393224 | tf_op jit(solution)/shard_map/ppermute | solution.py:648
  13.0 0.9 %collective-permute-start.11 = (bf16[16,4096]{1,0:T(8,128)(2,1)S(1)}, bf16[16,4096]{1,0:T(8,128)(2,1)S(1)}, u32[]{:S(2)}, u32[]{:S(2)}) collective-permute-start(bf16[16,4096]{1,0:T(8,128)(2,1)S(1)} %collective-permute-done.9.refs_5_), channel_id=1, source_target_pairs={{0,4},{1,3},{2,0},{3,7},{6,2},{7,11},{10,6},{11,15},{14,10},{15,13... | collective-permute-start | bytes 393224 | tf_op jit(solution)/shard_map/ppermute | solution.py:648
  14.0 1.3 %collective-permute-done.1.refs_6_ = bf16[16,4096]{1,0:T(8,128)(2,1)S(1)} collective-permute-done((bf16[16,4096]{1,0:T(8,128)(2,1)S(1)}, bf16[16,4096]{1,0:T(8,128)(2,1)S(1)}, u32[]{:S(2)}, u32[]{:S(2)}) %collective-permute-start.1) | collective-permute-done | bytes 131104 | tf_op jit(solution)/shard_map/ppermute | solution.py:648
  15.2 1.9 %collective-permute-start.2 = (bf16[16,4096]{1,0:T(8,128)(2,1)S(1)}, bf16[16,4096]{1,0:T(8,128)(2,1)S(1)}, u32[]{:S(2)}, u32[]{:S(2)}) collective-permute-start(bf16[16,4096]{1,0:T(8,128)(2,1)S(1)} %collective-permute-done.1.refs_6_), channel_id=1, source_target_pairs={{0,2},{1,5},{2,6},{3,1},{6,10},{7,3},{10,14},{11,7},{14,12},{15,11... | collective-permute-start | bytes 393224 | tf_op jit(solution)/shard_map/ppermute | solution.py:648
  17.3 0.8 %collective-permute-done.10.refs_8_ = bf16[16,4096]{1,0:T(8,128)(2,1)S(1)} collective-permute-done((bf16[16,4096]{1,0:T(8,128)(2,1)S(1)}, bf16[16,4096]{1,0:T(8,128)(2,1)S(1)}, u32[]{:S(2)}, u32[]{:S(2)}) %collective-permute-start.10) | collective-permute-done | bytes 131104 | tf_op jit(solution)/shard_map/ppermute | solution.py:648
  18.1 1.4 %collective-permute-start.12 = (bf16[16,4096]{1,0:T(8,128)(2,1)S(1)}, bf16[16,4096]{1,0:T(8,128)(2,1)S(1)}, u32[]{:S(2)}, u32[]{:S(2)}) collective-permute-start(bf16[16,4096]{1,0:T(8,128)(2,1)S(1)} %collective-permute-done.10.refs_8_), channel_id=1, source_target_pairs={{0,2},{1,5},{2,6},{3,1},{6,10},{7,3},{10,14},{11,7},{14,12},{15,11... | collective-permute-start | bytes 393224 | tf_op jit(solution)/shard_map/ppermute | solution.py:648
  19.8 0.3 collective-permute-start.13
  20.1 0.8 %collective-permute-done.2.refs_10_ = bf16[16,4096]{1,0:T(8,128)(2,1)S(1)} collective-permute-done((bf16[16,4096]{1,0:T(8,128)(2,1)S(1)}, bf16[16,4096]{1,0:T(8,128)(2,1)S(1)}, u32[]{:S(2)}, u32[]{:S(2)}) %collective-permute-start.2) | collective-permute-done | bytes 131104 | tf_op jit(solution)/shard_map/ppermute | solution.py:648
  20.9 2.5 %collective-permute-start.3 = (bf16[16,4096]{1,0:T(8,128)(2,1)S(1)}, bf16[16,4096]{1,0:T(8,128)(2,1)S(1)}, u32[]{:S(2)}, u32[]{:S(2)}) collective-permute-start(bf16[16,4096]{1,0:T(8,128)(2,1)S(1)} %collective-permute-done.2.refs_10_), channel_id=1, source_target_pairs={{0,2},{1,5},{2,6},{3,1},{6,10},{7,3},{10,14},{11,7},{14,12},{15,11... | collective-permute-start | bytes 393224 | tf_op jit(solution)/shard_map/ppermute | solution.py:648
  23.5 1.2 %residue_left.1 = (bf16[128,4096]{1,0:T(8,128)(2,1)S(1)}, f32[64,448]{1,0:T(8,128)S(1)}) custom-call(f32[64,4096]{1,0:T(8,128)S(1)} %copy-done.2, bf16[448,4096]{1,0:T(8,128)(2,1)S(1)} %bitcast.7), custom_call_target="tpu_custom_call" | custom-call | flops 2529999872 | tf_op jit(solution)/shard_map/residue_left/pallas_call | solution.py:100
  24.8 1.2 %early_left.1 = (bf16[256,4096]{1,0:T(8,128)(2,1)S(1)}, bf16[256,448]{1,0:T(8,128)(2,1)S(1)}, f32[64,448]{1,0:T(8,128)S(1)}) custom-call(bf16[16,4096]{1,0:T(8,128)(2,1)S(1)} %get-tuple-element.43.first.refs_0_, bf16[16,4096]{1,0:T(8,128)(2,1)S(1)} %get-tuple-element.45.second.refs_1_, bf16[16,4096]{1,0:T(8,128)(2,1)S(1)} %collective-permute-done.refs_2_, ...), custom_call_target="tpu_custom_call" | custom-call | flops 2300000000 | tf_op jit(solution)/shard_map/early_left/pallas_call | solution.py:155
  26.0 0.3 collective-permute-done.3.first
  26.3 2.1 %collective-permute-done.7.second = bf16[16,4096]{1,0:T(8,128)(2,1)S(1)} collective-permute-done((bf16[16,4096]{1,0:T(8,128)(2,1)S(1)}, bf16[16,4096]{1,0:T(8,128)(2,1)S(1)}, u32[]{:S(2)}, u32[]{:S(2)}) %collective-permute-start.7) | collective-permute-done | bytes 131104 | tf_op jit(solution)/shard_map/ppermute | solution.py:648
  28.4 0.6 late_left.1.here_l
  29.1 0.4 inserted.1.tokens
  29.5 0.9 %collective-permute-done.14.other_l = f32[64,448]{1,0:T(8,128)S(1)} collective-permute-done((f32[64,448]{1,0:T(8,128)S(1)}, f32[64,448]{1,0:T(8,128)S(1)}, u32[]{:S(2)}, u32[]{:S(2)}) %collective-permute-start.14) | collective-permute-done | bytes 114720 | tf_op jit(solution)/shard_map/ppermute | solution.py:657
  30.4 0.5 given_far.1
  31.2 0.6 near_terms.1
  31.8 0.4 collective-permute-start.16
  32.2 0.5 kept_far.1
  32.8 1.1 %collective-permute-start.18 = (f32[72,512]{1,0:T(8,128)S(1)}, f32[72,512]{1,0:T(8,128)S(1)}, u32[]{:S(2)}, u32[]{:S(2)}) collective-permute-start(f32[72,512]{1,0:T(8,128)S(1)} %begin_messages.1), channel_id=1, source_target_pairs={{0,8},{1,3},{2,10},{3,1},{4,12},{5,7},{6,14},{7,5},{8,0},{9,11},{1... | collective-permute-start | bytes 442376 | tf_op jit(solution)/shard_map/ppermute | solution.py:672
  33.9 2.9 %collective-permute-start.19 = (f32[72,512]{1,0:T(8,128)S(1)}, f32[72,512]{1,0:T(8,128)S(1)}, u32[]{:S(2)}, u32[]{:S(2)}) collective-permute-start(f32[72,512]{1,0:T(8,128)S(1)} %get-tuple-element.68), channel_id=1, source_target_pairs={{0,10},{1,5},{2,8},{3,7},{4,14},{5,1},{6,12},{7,3},{8,2},{9,13},{1... | collective-permute-start | bytes 442376 | tf_op jit(solution)/shard_map/ppermute | solution.py:672
  36.8 0.7 %collective-permute-start.17 = (f32[72,512]{1,0:T(8,128)S(1)}, f32[72,512]{1,0:T(8,128)S(1)}, u32[]{:S(2)}, u32[]{:S(2)}) collective-permute-start(f32[72,512]{1,0:T(8,128)S(1)} %get-tuple-element.65), channel_id=1, source_target_pairs={{1,7},{3,5},{5,3},{7,1},{9,15},{11,13},{13,11},{15,9},{17,23},{19,... | collective-permute-start | bytes 442376 | tf_op jit(solution)/shard_map/ppermute | solution.py:672
  37.4 2.4 %collective-permute-done.18.passed.refs_0_ = f32[72,512]{1,0:T(8,128)S(1)} collective-permute-done((f32[72,512]{1,0:T(8,128)S(1)}, f32[72,512]{1,0:T(8,128)S(1)}, u32[]{:S(2)}, u32[]{:S(2)}) %collective-permute-start.18) | collective-permute-done | bytes 147488 | tf_op jit(solution)/shard_map/ppermute | solution.py:672
  39.9 1.2 %collective-permute-start.20 = (f32[72,512]{1,0:T(8,128)S(1)}, f32[72,512]{1,0:T(8,128)S(1)}, u32[]{:S(2)}, u32[]{:S(2)}) collective-permute-start(f32[72,512]{1,0:T(8,128)S(1)} %crossing.1), channel_id=1, source_target_pairs={{0,2},{1,13},{2,0},{3,15},{4,6},{5,9},{6,4},{7,11},{8,10},{9,5},{1... | collective-permute-start | bytes 442376 | tf_op jit(solution)/shard_map/ppermute | solution.py:672
  41.1 1.1 %merged.1 = f32[448,4096]{1,0:T(8,128)S(1)} custom-call(bf16[448,256]{1,0:T(8,128)(2,1)S(1)} %bitcast.14, bf16[448,4096]{1,0:T(8,128)(2,1)S(1)} %bitcast.11, bf16[256,4096]{1,0:T(8,128)(2,1)S(1)} %inserted.1.tokens), custom_call_target="tpu_custom_call" | custom-call | flops 57500000 | tf_op jit(solution)/shard_map/merged/pallas_call | solution.py:321
  42.2 2.8 %collective-permute-done.19.refs_1_ = f32[72,512]{1,0:T(8,128)S(1)} collective-permute-done((f32[72,512]{1,0:T(8,128)S(1)}, f32[72,512]{1,0:T(8,128)S(1)}, u32[]{:S(2)}, u32[]{:S(2)}) %collective-permute-start.19) | collective-permute-done | bytes 147488 | tf_op jit(solution)/shard_map/ppermute | solution.py:672
  45.0 0.5 collective-permute-done.20.refs_2_
  45.6 1.4 %collective-permute-done.21.other = f32[72,512]{1,0:T(8,128)S(1)} collective-permute-done((f32[72,512]{1,0:T(8,128)S(1)}, f32[72,512]{1,0:T(8,128)S(1)}, u32[]{:S(2)}, u32[]{:S(2)}) %collective-permute-start.21) | collective-permute-done | bytes 147488 | tf_op jit(solution)/shard_map/ppermute | solution.py:657
  47.0 2.6 %collective-permute-start.23 = (f32[64,512]{1,0:T(8,128)S(1)}, f32[64,512]{1,0:T(8,128)S(1)}, u32[]{:S(2)}, u32[]{:S(2)}) collective-permute-start(f32[64,512]{1,0:T(8,128)S(1)} %get-tuple-element.70.share.here), channel_id=1, source_target_pairs={{0,2},{1,13},{2,0},{3,15},{4,6},{5,9},{6,4},{7,11},{8,10},{9,5},{1... | collective-permute-start | bytes 393224 | tf_op jit(solution)/shard_map/ppermute | solution.py:672
  49.6 1.3 %collective-permute-start.24 = (f32[64,512]{1,0:T(8,128)S(1)}, f32[64,512]{1,0:T(8,128)S(1)}, u32[]{:S(2)}, u32[]{:S(2)}) collective-permute-start(f32[64,512]{1,0:T(8,128)S(1)} %get-tuple-element.70.share.here), channel_id=1, source_target_pairs={{0,10},{1,5},{2,8},{3,7},{4,14},{5,1},{6,12},{7,3},{8,2},{9,13},{1... | collective-permute-start | bytes 393224 | tf_op jit(solution)/shard_map/ppermute | solution.py:672
  50.9 0.7 %collective-permute-start.22 = (f32[64,512]{1,0:T(8,128)S(1)}, f32[64,512]{1,0:T(8,128)S(1)}, u32[]{:S(2)}, u32[]{:S(2)}) collective-permute-start(f32[64,512]{1,0:T(8,128)S(1)} %get-tuple-element.70.share.here), channel_id=1, source_target_pairs={{1,7},{3,5},{5,3},{7,1},{9,15},{11,13},{13,11},{15,9},{17,23},{19,... | collective-permute-start | bytes 393224 | tf_op jit(solution)/shard_map/ppermute | solution.py:672
  51.6 1.0 %collective-permute-done.23.refs_0_.there = f32[64,512]{1,0:T(8,128)S(1)} collective-permute-done((f32[64,512]{1,0:T(8,128)S(1)}, f32[64,512]{1,0:T(8,128)S(1)}, u32[]{:S(2)}, u32[]{:S(2)}) %collective-permute-start.23) | collective-permute-done | bytes 131104 | tf_op jit(solution)/shard_map/ppermute | solution.py:672
  52.6 1.9 %collective-permute-start.25 = (f32[64,512]{1,0:T(8,128)S(1)}, f32[64,512]{1,0:T(8,128)S(1)}, u32[]{:S(2)}, u32[]{:S(2)}) collective-permute-start(f32[64,512]{1,0:T(8,128)S(1)} %by_core.1), channel_id=1, source_target_pairs={{0,8},{1,3},{2,10},{3,1},{4,12},{5,7},{6,14},{7,5},{8,0},{9,11},{1... | collective-permute-start | bytes 393224 | tf_op jit(solution)/shard_map/ppermute | solution.py:672
  54.5 1.8 %cholesky_inverse.1.inverse = f32[64,64]{1,0:T(8,128)S(1)} custom-call(f32[64,64]{1,0:T(8,128)S(1)} %get-tuple-element.71.gram), custom_call_target="tpu_custom_call" | custom-call | flops 5750000128 | tf_op jit(solution)/shard_map/cholesky_inverse/pallas_call | solution.py:529
  56.3 0.8 %last_operand.1.lhs = bf16[512,256]{1,0:T(8,128)(2,1)S(1)} custom-call(f32[64,64]{1,0:T(8,128)S(1)} %cholesky_inverse.1.inverse, f32[64,448]{1,0:T(8,128)S(1)} %get-tuple-element.56.left_sum), custom_call_target="tpu_custom_call" | custom-call | flops 57500000 | tf_op jit(solution)/shard_map/last_operand/pallas_call | solution.py:560
  57.1 0.8 %collective-permute-done.24.refs_1_ = f32[64,512]{1,0:T(8,128)S(1)} collective-permute-done((f32[64,512]{1,0:T(8,128)S(1)}, f32[64,512]{1,0:T(8,128)S(1)}, u32[]{:S(2)}, u32[]{:S(2)}) %collective-permute-start.24) | collective-permute-done | bytes 131104 | tf_op jit(solution)/shard_map/ppermute | solution.py:672
  58.0 1.5 %finish.3 = (bf16[448,4096]{1,0:T(8,128)(2,1)}, f32[64,4096]{1,0:T(8,128)}) custom-call(f32[3,64,512]{2,1,0:T(8,128)S(1)} %joined.1.shares, bf16[512,256]{1,0:T(8,128)(2,1)S(1)} %last_operand.1.lhs, f32[448,4096]{1,0:T(8,128)S(1)} %merged.1), custom_call_target="tpu_custom_call" | custom-call | flops 57500000 | tf_op jit(solution)/shard_map/finish/pallas_call | solution.py:599
  59.5 0.5 collective-permute-done.25
  60.0 0.3 collective-permute-start.26
  60.3 1.1 %finish.4 = (bf16[448,4096]{1,0:T(8,128)(2,1)}, f32[64,4096]{1,0:T(8,128)}) custom-call(f32[1,64,512]{2,1,0:T(8,128)S(1)} %bitcast.16, bf16[512,256]{1,0:T(8,128)(2,1)S(1)} %last_operand.1.lhs, f32[448,4096]{1,0:T(8,128)S(1)} %merged.1, bf16[448,4096]{1,0:T(8,128)(2,1)} %get-tuple-element.78.refs_0_, ...), custom_call_target="tpu_custom_call", output_to_operand_aliasing={{0}: (3, {}), {1}: (4, {})} | custom-call | flops 57500000 | tf_op jit(solution)/shard_map/finish/pallas_call | solution.py:599
  61.4 0.6 collective-permute-done.26.shares
  62.0 1.7 %finish.5 = (bf16[448,4096]{1,0:T(8,128)(2,1)}, f32[64,4096]{1,0:T(8,128)}) custom-call(f32[4,64,512]{2,1,0:T(8,128)S(1)} %collective-permute-done.26.shares, bf16[512,256]{1,0:T(8,128)(2,1)S(1)} %last_operand.1.lhs, f32[448,4096]{1,0:T(8,128)S(1)} %merged.1, ...), custom_call_target="tpu_custom_call", output_to_operand_aliasing={{0}: (3, {}), {1}: (4, {})} | custom-call | flops 57500000 | tf_op jit(solution)/shard_map/finish/pallas_call | solution.py:599
  (37 shorter events, 1.9 us)
Async XLA Ops:
  0.6 1.0 %copy-start.3 = (bf16[1,32,4096]{2,1,0:T(8,128)(2,1)S(1)}, bf16[1,32,4096]{2,1,0:T(8,128)(2,1)}, u32[]{:S(2)}) copy-start(bf16[1,32,4096]{2,1,0:T(8,128)(2,1)} %param.4) | copy-start | bytes 786436
  1.6 6.9 %collective-permute-start = (bf16[16,4096]{1,0:T(8,128)(2,1)S(1)}, bf16[16,4096]{1,0:T(8,128)(2,1)S(1)}, u32[]{:S(2)}, u32[]{:S(2)}) collective-permute-start(bf16[16,4096]{1,0:T(8,128)(2,1)S(1)} %get-tuple-element.43.first.refs_0_), channel_id=1, source_target_pairs={{0,2},{1,5},{2,6},{3,1},{6,10},{7,3},{10,14},{11,7},{14,12},{15,11... | collective-permute-start | bytes 393224 | tf_op jit(solution)/shard_map/ppermute | solution.py:648
  4.6 18.8 %copy-start = (bf16[1,448,4096]{2,1,0:T(8,128)(2,1)S(1)}, bf16[1,448,4096]{2,1,0:T(8,128)(2,1)}, u32[]{:S(2)}) copy-start(bf16[1,448,4096]{2,1,0:T(8,128)(2,1)} %param.6) | copy-start | bytes 11010052
  4.6 18.8 %copy-start.2 = (f32[64,4096]{1,0:T(8,128)S(1)}, f32[64,4096]{1,0:T(8,128)}, u32[]{:S(2)}) copy-start(f32[64,4096]{1,0:T(8,128)} %right) | copy-start | bytes 3145732
  4.6 6.4 %collective-permute-start.4 = (bf16[16,4096]{1,0:T(8,128)(2,1)S(1)}, bf16[16,4096]{1,0:T(8,128)(2,1)S(1)}, u32[]{:S(2)}, u32[]{:S(2)}) collective-permute-start(bf16[16,4096]{1,0:T(8,128)(2,1)S(1)} %get-tuple-element.45.second.refs_1_), channel_id=1, source_target_pairs={{0,4},{1,3},{2,0},{3,7},{6,2},{7,11},{10,6},{11,15},{14,10},{15,13... | collective-permute-start | bytes 393224 | tf_op jit(solution)/shard_map/ppermute | solution.py:648
  4.8 6.5 %collective-permute-start.8 = (bf16[16,4096]{1,0:T(8,128)(2,1)S(1)}, bf16[16,4096]{1,0:T(8,128)(2,1)S(1)}, u32[]{:S(2)}, u32[]{:S(2)}) collective-permute-start(bf16[16,4096]{1,0:T(8,128)(2,1)S(1)} %get-tuple-element.48), channel_id=1, source_target_pairs={{0,2},{1,5},{2,6},{3,1},{6,10},{7,3},{10,14},{11,7},{14,12},{15,11... | collective-permute-start | bytes 393224 | tf_op jit(solution)/shard_map/ppermute | solution.py:648
  6.7 6.3 %collective-permute-start.9 = (bf16[16,4096]{1,0:T(8,128)(2,1)S(1)}, bf16[16,4096]{1,0:T(8,128)(2,1)S(1)}, u32[]{:S(2)}, u32[]{:S(2)}) collective-permute-start(bf16[16,4096]{1,0:T(8,128)(2,1)S(1)} %get-tuple-element.49), channel_id=1, source_target_pairs={{0,4},{1,3},{2,0},{3,7},{6,2},{7,11},{10,6},{11,15},{14,10},{15,13... | collective-permute-start | bytes 393224 | tf_op jit(solution)/shard_map/ppermute | solution.py:648
  8.5 6.7 %collective-permute-start.1 = (bf16[16,4096]{1,0:T(8,128)(2,1)S(1)}, bf16[16,4096]{1,0:T(8,128)(2,1)S(1)}, u32[]{:S(2)}, u32[]{:S(2)}) collective-permute-start(bf16[16,4096]{1,0:T(8,128)(2,1)S(1)} %collective-permute-done.refs_2_), channel_id=1, source_target_pairs={{0,2},{1,5},{2,6},{3,1},{6,10},{7,3},{10,14},{11,7},{14,12},{15,11... | collective-permute-start | bytes 393224 | tf_op jit(solution)/shard_map/ppermute | solution.py:648
  11.0 6.2 %collective-permute-start.5 = (bf16[16,4096]{1,0:T(8,128)(2,1)S(1)}, bf16[16,4096]{1,0:T(8,128)(2,1)S(1)}, u32[]{:S(2)}, u32[]{:S(2)}) collective-permute-start(bf16[16,4096]{1,0:T(8,128)(2,1)S(1)} %collective-permute-done.4.refs_3_), channel_id=1, source_target_pairs={{0,4},{1,3},{2,0},{3,7},{6,2},{7,11},{10,6},{11,15},{14,10},{15,13... | collective-permute-start | bytes 393224 | tf_op jit(solution)/shard_map/ppermute | solution.py:648
  11.3 6.8 %collective-permute-start.10 = (bf16[16,4096]{1,0:T(8,128)(2,1)S(1)}, bf16[16,4096]{1,0:T(8,128)(2,1)S(1)}, u32[]{:S(2)}, u32[]{:S(2)}) collective-permute-start(bf16[16,4096]{1,0:T(8,128)(2,1)S(1)} %collective-permute-done.8.refs_4_), channel_id=1, source_target_pairs={{0,2},{1,5},{2,6},{3,1},{6,10},{7,3},{10,14},{11,7},{14,12},{15,11... | collective-permute-start | bytes 393224 | tf_op jit(solution)/shard_map/ppermute | solution.py:648
  13.0 6.8 %collective-permute-start.11 = (bf16[16,4096]{1,0:T(8,128)(2,1)S(1)}, bf16[16,4096]{1,0:T(8,128)(2,1)S(1)}, u32[]{:S(2)}, u32[]{:S(2)}) collective-permute-start(bf16[16,4096]{1,0:T(8,128)(2,1)S(1)} %collective-permute-done.9.refs_5_), channel_id=1, source_target_pairs={{0,4},{1,3},{2,0},{3,7},{6,2},{7,11},{10,6},{11,15},{14,10},{15,13... | collective-permute-start | bytes 393224 | tf_op jit(solution)/shard_map/ppermute | solution.py:648
  15.2 5.7 %collective-permute-start.2 = (bf16[16,4096]{1,0:T(8,128)(2,1)S(1)}, bf16[16,4096]{1,0:T(8,128)(2,1)S(1)}, u32[]{:S(2)}, u32[]{:S(2)}) collective-permute-start(bf16[16,4096]{1,0:T(8,128)(2,1)S(1)} %collective-permute-done.1.refs_6_), channel_id=1, source_target_pairs={{0,2},{1,5},{2,6},{3,1},{6,10},{7,3},{10,14},{11,7},{14,12},{15,11... | collective-permute-start | bytes 393224 | tf_op jit(solution)/shard_map/ppermute | solution.py:648
  17.2 6.2 %collective-permute-start.6 = (bf16[16,4096]{1,0:T(8,128)(2,1)S(1)}, bf16[16,4096]{1,0:T(8,128)(2,1)S(1)}, u32[]{:S(2)}, u32[]{:S(2)}) collective-permute-start(bf16[16,4096]{1,0:T(8,128)(2,1)S(1)} %collective-permute-done.5.refs_7_), channel_id=1, source_target_pairs={{0,4},{1,3},{2,0},{3,7},{6,2},{7,11},{10,6},{11,15},{14,10},{15,13... | collective-permute-start | bytes 393224 | tf_op jit(solution)/shard_map/ppermute | solution.py:648
  18.1 6.6 %collective-permute-start.12 = (bf16[16,4096]{1,0:T(8,128)(2,1)S(1)}, bf16[16,4096]{1,0:T(8,128)(2,1)S(1)}, u32[]{:S(2)}, u32[]{:S(2)}) collective-permute-start(bf16[16,4096]{1,0:T(8,128)(2,1)S(1)} %collective-permute-done.10.refs_8_), channel_id=1, source_target_pairs={{0,2},{1,5},{2,6},{3,1},{6,10},{7,3},{10,14},{11,7},{14,12},{15,11... | collective-permute-start | bytes 393224 | tf_op jit(solution)/shard_map/ppermute | solution.py:648
  19.8 5.0 %collective-permute-start.13 = (bf16[16,4096]{1,0:T(8,128)(2,1)S(1)}, bf16[16,4096]{1,0:T(8,128)(2,1)S(1)}, u32[]{:S(2)}, u32[]{:S(2)}) collective-permute-start(bf16[16,4096]{1,0:T(8,128)(2,1)S(1)} %collective-permute-done.11.refs_9_), channel_id=1, source_target_pairs={{0,4},{1,3},{2,0},{3,7},{6,2},{7,11},{10,6},{11,15},{14,10},{15,13... | collective-permute-start | bytes 393224 | tf_op jit(solution)/shard_map/ppermute | solution.py:648
  20.9 5.4 %collective-permute-start.3 = (bf16[16,4096]{1,0:T(8,128)(2,1)S(1)}, bf16[16,4096]{1,0:T(8,128)(2,1)S(1)}, u32[]{:S(2)}, u32[]{:S(2)}) collective-permute-start(bf16[16,4096]{1,0:T(8,128)(2,1)S(1)} %collective-permute-done.2.refs_10_), channel_id=1, source_target_pairs={{0,2},{1,5},{2,6},{3,1},{6,10},{7,3},{10,14},{11,7},{14,12},{15,11... | collective-permute-start | bytes 393224 | tf_op jit(solution)/shard_map/ppermute | solution.py:648
  23.4 5.0 %collective-permute-start.7 = (bf16[16,4096]{1,0:T(8,128)(2,1)S(1)}, bf16[16,4096]{1,0:T(8,128)(2,1)S(1)}, u32[]{:S(2)}, u32[]{:S(2)}) collective-permute-start(bf16[16,4096]{1,0:T(8,128)(2,1)S(1)} %collective-permute-done.6.refs_11_), channel_id=1, source_target_pairs={{0,4},{1,3},{2,0},{3,7},{6,2},{7,11},{10,6},{11,15},{14,10},{15,13... | collective-permute-start | bytes 393224 | tf_op jit(solution)/shard_map/ppermute | solution.py:648
  23.4 1.3 %copy-start.1 = (bf16[1,256,448]{1,2,0:T(8,128)(2,1)S(1)}, bf16[1,256,448]{1,2,0:T(8,128)(2,1)}, u32[]{:S(2)}) copy-start(bf16[1,256,448]{1,2,0:T(8,128)(2,1)} %param.5) | copy-start | bytes 688132
  29.0 1.4 %collective-permute-start.14 = (f32[64,448]{1,0:T(8,128)S(1)}, f32[64,448]{1,0:T(8,128)S(1)}, u32[]{:S(2)}, u32[]{:S(2)}) collective-permute-start(f32[64,448]{1,0:T(8,128)S(1)} %late_left.1.here_l), channel_id=1, source_target_pairs={{0,1},{1,0},{2,3},{3,2},{4,5},{5,4},{6,7},{7,6},{8,9},{9,8},{10,11... | collective-permute-start | bytes 344072 | tf_op jit(solution)/shard_map/ppermute | solution.py:657
  31.0 1.7 %collective-permute-start.15 = (f32[2,64,512]{2,1,0:T(8,128)S(1)}, f32[2,64,512]{2,1,0:T(8,128)S(1)}, u32[]{:S(2)}, u32[]{:S(2)}) collective-permute-start(f32[2,64,512]{2,1,0:T(8,128)S(1)} %get-tuple-element.60), channel_id=1, source_target_pairs={{0,1},{1,0},{2,3},{3,2},{4,5},{5,4},{6,7},{7,6},{8,9},{9,8},{10,11... | collective-permute-start | bytes 786440 | tf_op jit(solution)/shard_map/ppermute | solution.py:657
  31.8 2.1 %collective-permute-start.16 = (f32[2,64,512]{2,1,0:T(8,128)S(1)}, f32[2,64,512]{2,1,0:T(8,128)S(1)}, u32[]{:S(2)}, u32[]{:S(2)}) collective-permute-start(f32[2,64,512]{2,1,0:T(8,128)S(1)} %get-tuple-element.62), channel_id=1, source_target_pairs={{0,1},{1,0},{2,3},{3,2},{4,5},{5,4},{6,7},{7,6},{8,9},{9,8},{10,11... | collective-permute-start | bytes 786440 | tf_op jit(solution)/shard_map/ppermute | solution.py:657
  32.8 7.1 %collective-permute-start.18 = (f32[72,512]{1,0:T(8,128)S(1)}, f32[72,512]{1,0:T(8,128)S(1)}, u32[]{:S(2)}, u32[]{:S(2)}) collective-permute-start(f32[72,512]{1,0:T(8,128)S(1)} %begin_messages.1), channel_id=1, source_target_pairs={{0,8},{1,3},{2,10},{3,1},{4,12},{5,7},{6,14},{7,5},{8,0},{9,11},{1... | collective-permute-start | bytes 442376 | tf_op jit(solution)/shard_map/ppermute | solution.py:672
  33.9 11.1 %collective-permute-start.19 = (f32[72,512]{1,0:T(8,128)S(1)}, f32[72,512]{1,0:T(8,128)S(1)}, u32[]{:S(2)}, u32[]{:S(2)}) collective-permute-start(f32[72,512]{1,0:T(8,128)S(1)} %get-tuple-element.68), channel_id=1, source_target_pairs={{0,10},{1,5},{2,8},{3,7},{4,14},{5,1},{6,12},{7,3},{8,2},{9,13},{1... | collective-permute-start | bytes 442376 | tf_op jit(solution)/shard_map/ppermute | solution.py:672
  36.8 5.4 %collective-permute-start.17 = (f32[72,512]{1,0:T(8,128)S(1)}, f32[72,512]{1,0:T(8,128)S(1)}, u32[]{:S(2)}, u32[]{:S(2)}) collective-permute-start(f32[72,512]{1,0:T(8,128)S(1)} %get-tuple-element.65), channel_id=1, source_target_pairs={{1,7},{3,5},{5,3},{7,1},{9,15},{11,13},{13,11},{15,9},{17,23},{19,... | collective-permute-start | bytes 442376 | tf_op jit(solution)/shard_map/ppermute | solution.py:672
  39.9 5.6 %collective-permute-start.20 = (f32[72,512]{1,0:T(8,128)S(1)}, f32[72,512]{1,0:T(8,128)S(1)}, u32[]{:S(2)}, u32[]{:S(2)}) collective-permute-start(f32[72,512]{1,0:T(8,128)S(1)} %crossing.1), channel_id=1, source_target_pairs={{0,2},{1,13},{2,0},{3,15},{4,6},{5,9},{6,4},{7,11},{8,10},{9,5},{1... | collective-permute-start | bytes 442376 | tf_op jit(solution)/shard_map/ppermute | solution.py:672
  45.5 1.4 %collective-permute-start.21 = (f32[72,512]{1,0:T(8,128)S(1)}, f32[72,512]{1,0:T(8,128)S(1)}, u32[]{:S(2)}, u32[]{:S(2)}) collective-permute-start(f32[72,512]{1,0:T(8,128)S(1)} %core_sum.1.here), channel_id=1, source_target_pairs={{0,1},{1,0},{2,3},{3,2},{4,5},{5,4},{6,7},{7,6},{8,9},{9,8},{10,11... | collective-permute-start | bytes 442376 | tf_op jit(solution)/shard_map/ppermute | solution.py:657
  47.0 5.6 %collective-permute-start.23 = (f32[64,512]{1,0:T(8,128)S(1)}, f32[64,512]{1,0:T(8,128)S(1)}, u32[]{:S(2)}, u32[]{:S(2)}) collective-permute-start(f32[64,512]{1,0:T(8,128)S(1)} %get-tuple-element.70.share.here), channel_id=1, source_target_pairs={{0,2},{1,13},{2,0},{3,15},{4,6},{5,9},{6,4},{7,11},{8,10},{9,5},{1... | collective-permute-start | bytes 393224 | tf_op jit(solution)/shard_map/ppermute | solution.py:672
  49.6 8.3 %collective-permute-start.24 = (f32[64,512]{1,0:T(8,128)S(1)}, f32[64,512]{1,0:T(8,128)S(1)}, u32[]{:S(2)}, u32[]{:S(2)}) collective-permute-start(f32[64,512]{1,0:T(8,128)S(1)} %get-tuple-element.70.share.here), channel_id=1, source_target_pairs={{0,10},{1,5},{2,8},{3,7},{4,14},{5,1},{6,12},{7,3},{8,2},{9,13},{1... | collective-permute-start | bytes 393224 | tf_op jit(solution)/shard_map/ppermute | solution.py:672
  50.9 7.0 %collective-permute-start.22 = (f32[64,512]{1,0:T(8,128)S(1)}, f32[64,512]{1,0:T(8,128)S(1)}, u32[]{:S(2)}, u32[]{:S(2)}) collective-permute-start(f32[64,512]{1,0:T(8,128)S(1)} %get-tuple-element.70.share.here), channel_id=1, source_target_pairs={{1,7},{3,5},{5,3},{7,1},{9,15},{11,13},{13,11},{15,9},{17,23},{19,... | collective-permute-start | bytes 393224 | tf_op jit(solution)/shard_map/ppermute | solution.py:672
  52.6 7.3 %collective-permute-start.25 = (f32[64,512]{1,0:T(8,128)S(1)}, f32[64,512]{1,0:T(8,128)S(1)}, u32[]{:S(2)}, u32[]{:S(2)}) collective-permute-start(f32[64,512]{1,0:T(8,128)S(1)} %by_core.1), channel_id=1, source_target_pairs={{0,8},{1,3},{2,10},{3,1},{4,12},{5,7},{6,14},{7,5},{8,0},{9,11},{1... | collective-permute-start | bytes 393224 | tf_op jit(solution)/shard_map/ppermute | solution.py:672
  60.0 2.0 %collective-permute-start.26 = (f32[4,64,512]{2,1,0:T(8,128)S(1)}, f32[4,64,512]{2,1,0:T(8,128)S(1)}, u32[]{:S(2)}, u32[]{:S(2)}) collective-permute-start(f32[4,64,512]{2,1,0:T(8,128)S(1)} %pad_maximum_fusion), channel_id=1, source_target_pairs={{0,1},{1,0},{2,3},{3,2},{4,5},{5,4},{6,7},{7,6},{8,9},{9,8},{10,11... | collective-permute-start | bytes 1572872 | tf_op jit(solution)/shard_map/ppermute | solution.py:657
